TPU v7x, 32 devices: a whole 2x2x4 slice. The times are simulated.
32 devices in a mesh: dp: 8 (over z, y), ctx: 2 (over core), tp: 2 (over x).
Axes of the slice: x: 2, y: 2, z: 4, core: 2. Of those that a mesh axis runs over, the one named last changes fastest.
Arguments:
- tokens: bfloat16 [8, 2, 1024, 1536], P('dp', 'ctx'), may hold values from -6 to 6
- routes: int32 [8, 2, 1024, 8], P('dp', 'ctx'), may hold values from 0 to 15, all different within a row; in each aligned block of 1024 rows (0 to 1023, 1024 to 2047, ..., all dimensions but the last counted through in order) at most 576 rows name the same one
- cotangent: bfloat16 [8, 2, 1024, 1536], P('dp', 'ctx'), may hold values from -6 to 6
- norm_one: bfloat16 [1536], P('dp'), may hold values from 0.5 to 1.5
- w_query: bfloat16 [1536, 1536], P('dp', 'tp'), may hold values from -0.4375 to 0.4375
- key_weight: bfloat16 [1536, 512], P('dp', 'tp'), may hold values from -0.4375 to 0.4375
- value_weight: bfloat16 [1536, 512], P('dp', 'tp'), may hold values from -0.15625 to 0.15625
- w_output: bfloat16 [1536, 1536], P('dp', 'tp'), may hold values from -0.625 to 0.625
- norm_two: bfloat16 [1536], P('dp'), may hold values from 0.5 to 1.5
- w_router: bfloat16 [1536, 16], P('dp'), may hold values from -0.078125 to 0.078125
- w_gate: bfloat16 [16, 1536, 512], P(None, 'dp', 'tp'), may hold values from -0.15625 to 0.15625
- w_up: bfloat16 [16, 1536, 512], P(None, 'dp', 'tp'), may hold values from -0.15625 to 0.15625
- w_down: bfloat16 [16, 1536, 512], P(None, 'dp', 'tp'), may hold values from -1 to 1
Outputs:
- output: bfloat16 [8, 2, 1024, 1536], P('dp', 'ctx')
- token_grad: float32 [8, 2, 1024, 1536], P('dp', 'ctx')
- grad_norm_one: float32 [1536], P('dp')
- grad_query: float32 [1536, 1536], P('dp', 'tp')
- grad_key: float32 [1536, 512], P('dp', 'tp')
- grad_value: float32 [1536, 512], P('dp', 'tp')
- grad_output: float32 [1536, 1536], P('dp', 'tp')
- grad_norm_two: float32 [1536], P('dp')
- grad_router: float32 [1536, 16], P('dp')
- grad_gate: float32 [16, 1536, 512], P(None, 'dp', 'tp')
- grad_up: float32 [16, 1536, 512], P(None, 'dp', 'tp')
- grad_down: float32 [16, 1536, 512], P(None, 'dp', 'tp')
Inputs may be any that keep to these rules, and one draw needn't show every extreme that they name: `routes`: each row names 8 different experts. In the rows of one slab no expert is named more than 576 times, a bound that some block reaches.
All inputs are finite; a program needn't handle non-finite values.
Results may differ from a plain program's by a relative error of at most 0.015.
Values may be sent and summed in bfloat16 or wider, within the bound.
No kernel may reach another device: no remote copies, remote signals or barrier semaphores. Data moves between devices by JAX's collectives and lax.ppermute only.
A program may use at most 448 MiB of HBM per device.

v0:
```python
import jax
import jax.numpy as jnp
from jax import lax
from jax.sharding import PartitionSpec as P

HEAD_DIM = 64
EXPERTS = 16
TOPK = 8
PROMPT_TOKENS = 1024


norm_eps = 1e-06
rope_base = 10000.0
masked_score = -1e30
contract_rows = (((0,), (0,)), ((), ()))
contract_cols = (((1,), (1,)), ((), ()))


def rms_scale(values, gain):
    return values * lax.rsqrt(jnp.mean(values * values, axis=-1, keepdims=True) + norm_eps) * gain


def apply_rotary(vectors, token_positions, turning):
    half_dim = vectors.shape[-1] // 2
    freq_ids = jnp.arange(half_dim).astype(jnp.float32)
    inverse = rope_base ** (-2.0 * freq_ids / vectors.shape[-1])
    angles = token_positions.astype(jnp.float32)[..., None, None] * inverse
    cosine = jnp.cos(angles)
    sine = jnp.sin(angles) * turning
    first = vectors[..., :half_dim]
    second = vectors[..., half_dim:]
    return jnp.concatenate(
        [first * cosine - second * sine, second * cosine + first * sine], axis=-1
    )


def body(
    tokens,
    routes,
    cotangent,
    norm_one,
    w_query,
    key_weight,
    value_weight,
    w_output,
    norm_two,
    w_router,
    w_gate,
    w_up,
    w_down,
):
    (
        gain_one,
        query_full,
        key_full,
        value_full,
        output_full,
        gain_two,
        router_full,
        gate_full,
        up_full,
        down_full,
    ) = (
        lax.all_gather(norm_one, "dp", axis=0, tiled=True),
        lax.all_gather(w_query, "dp", axis=0, tiled=True),
        lax.all_gather(key_weight, "dp", axis=0, tiled=True),
        lax.all_gather(value_weight, "dp", axis=0, tiled=True),
        lax.all_gather(w_output, "dp", axis=0, tiled=True),
        lax.all_gather(norm_two, "dp", axis=0, tiled=True),
        lax.all_gather(w_router, "dp", axis=0, tiled=True),
        lax.all_gather(w_gate, "dp", axis=1, tiled=True),
        lax.all_gather(w_up, "dp", axis=1, tiled=True),
        lax.all_gather(w_down, "dp", axis=1, tiled=True),
    )
    token_length = tokens.shape[2]
    model_width = tokens.shape[3]
    half_length = PROMPT_TOKENS // lax.axis_size("ctx")
    cont_len = token_length - half_length
    ctx_index = lax.axis_index("ctx")
    query_heads = query_full.shape[1] // HEAD_DIM
    kv_heads = key_full.shape[1] // HEAD_DIM
    heads_per_group = query_heads // kv_heads
    score_scale = 1.0 / HEAD_DIM
    offsets = jnp.arange(token_length, dtype=jnp.int32)
    token_positions = jnp.where(
        offsets < half_length,
        ctx_index * half_length + offsets,
        PROMPT_TOKENS + offsets - half_length,
    )
    key_pos = jnp.concatenate(
        [
            jnp.arange(PROMPT_TOKENS, dtype=jnp.int32),
            PROMPT_TOKENS + jnp.arange(cont_len, dtype=jnp.int32),
        ]
    )
    allowed = key_pos[None, :] <= token_positions[:, None]
    inputs = tokens.reshape(token_length, model_width).astype(jnp.float32)
    gain_first = gain_one.astype(jnp.float32)
    normed_low = rms_scale(inputs, gain_first).astype(jnp.bfloat16)
    query_pre = jnp.dot(normed_low, query_full, preferred_element_type=jnp.float32)
    key_pre = jnp.dot(normed_low, key_full, preferred_element_type=jnp.float32)
    value_pre = jnp.dot(normed_low, value_full, preferred_element_type=jnp.float32)
    query_low = apply_rotary(
        query_pre.reshape(token_length, query_heads, HEAD_DIM), token_positions, 1.0
    ).astype(jnp.bfloat16)
    key_low = (
        apply_rotary(key_pre.reshape(token_length, kv_heads, HEAD_DIM), token_positions, 1.0)
        .astype(jnp.bfloat16)
        .reshape(token_length, kv_heads * HEAD_DIM)
    )
    value_low = value_pre.astype(jnp.bfloat16)
    prefix_keys, prefix_values = (
        lax.all_gather(key_low[:half_length], "ctx", axis=0, tiled=True),
        lax.all_gather(value_low[:half_length], "ctx", axis=0, tiled=True),
    )
    joined_keys = jnp.concatenate([prefix_keys, key_low[half_length:]], axis=0)
    joined_values = jnp.concatenate([prefix_values, value_low[half_length:]], axis=0)
    key_count = joined_keys.shape[0]
    head_queries = query_low.reshape(token_length, kv_heads, heads_per_group, HEAD_DIM).transpose(
        1, 2, 0, 3
    )
    head_keys = joined_keys.reshape(key_count, kv_heads, HEAD_DIM).transpose(1, 0, 2)
    head_values = joined_values.reshape(key_count, kv_heads, HEAD_DIM).transpose(1, 0, 2)

    def head_scores(head_query, head_key):
        scores = (
            jnp.einsum("gtd,kd->gtk", head_query, head_key, preferred_element_type=jnp.float32)
            * score_scale
        )
        return jnp.where(allowed, scores, masked_score)

    def attend(head_parts):
        head_query, head_key, head_value = head_parts
        scores = head_scores(head_query, head_key)
        row_peak = jnp.max(scores, axis=-1, keepdims=True)
        raw_weights = jnp.exp(scores - row_peak)
        row_total = jnp.sum(raw_weights, axis=-1, keepdims=True)
        attn_probs = raw_weights / row_total
        head_out = jnp.einsum(
            "gtk,kd->gtd",
            attn_probs.astype(jnp.bfloat16),
            head_value,
            preferred_element_type=jnp.float32,
        )
        return (head_out, (row_peak + jnp.log(row_total))[..., 0])

    head_mixed, head_lse = lax.map(attend, (head_queries, head_keys, head_values))
    attended = (
        head_mixed.transpose(2, 0, 1, 3)
        .reshape(token_length, query_heads * HEAD_DIM)
        .astype(jnp.bfloat16)
    )
    branch_part = lax.dot_general(
        attended, output_full, contract_cols, preferred_element_type=jnp.float32
    )
    branch = lax.psum(branch_part, "tp")
    residual = inputs + branch
    gain_second = gain_two.astype(jnp.float32)
    second_low = rms_scale(residual, gain_second).astype(jnp.bfloat16)
    logits = jnp.dot(second_low, router_full, preferred_element_type=jnp.float32)
    route_ids = routes.reshape(token_length, TOPK)
    chosen = jnp.take_along_axis(logits, route_ids, axis=1)
    gate_vals = jax.nn.softmax(chosen, axis=-1)
    expert_ids = jnp.arange(EXPERTS, dtype=jnp.int32)
    picks = (route_ids[:, :, None] == expert_ids).astype(jnp.float32)
    weight_table = jnp.sum(picks * gate_vals[:, :, None], axis=1)
    member = jnp.sum(picks, axis=1).astype(jnp.int32)
    capacity = 9 * TOPK * token_length // (8 * EXPERTS)
    slot_of = jnp.cumsum(member, axis=0) - 1
    dump_slot = EXPERTS * capacity
    target = jnp.where(member > 0, expert_ids[None, :] * capacity + slot_of, dump_slot).reshape(-1)
    token_table = (
        jnp.zeros((dump_slot + 1,), jnp.int32)
        .at[target]
        .set(jnp.broadcast_to(offsets[:, None], (token_length, EXPERTS)).reshape(-1))
    )
    slot_tokens = token_table[:dump_slot].reshape(EXPERTS, capacity)
    slot_filled = (
        jnp.zeros((dump_slot + 1,), jnp.float32)
        .at[target]
        .set(1.0)[:dump_slot]
        .reshape(EXPERTS, capacity)
    )
    slot_gates = (
        jnp.zeros((dump_slot + 1,), jnp.float32)
        .at[target]
        .set(weight_table.reshape(-1))[:dump_slot]
        .reshape(EXPERTS, capacity)
    )

    def expert_forward(running, expert_parts):
        gate_mat, up_mat, down_mat, slot_ids, slot_gate = expert_parts
        slot_rows = second_low[slot_ids]
        gate_act = jnp.dot(slot_rows, gate_mat, preferred_element_type=jnp.float32)
        up_act = jnp.dot(slot_rows, up_mat, preferred_element_type=jnp.float32)
        hidden = (jax.nn.silu(gate_act) * up_act).astype(jnp.bfloat16)
        expert_out = lax.dot_general(
            hidden, down_mat, contract_cols, preferred_element_type=jnp.float32
        )
        return (running.at[slot_ids].add(expert_out * slot_gate[:, None]), (gate_act, up_act))

    moe_part, (gate_kept, up_kept) = lax.scan(
        expert_forward,
        jnp.zeros((token_length, model_width), jnp.float32),
        (gate_full, up_full, down_full, slot_tokens, slot_gates),
    )
    moe_total = lax.psum(moe_part, "tp")
    result = (residual + moe_total).astype(jnp.bfloat16).reshape(tokens.shape)
    out_grad = cotangent.reshape(token_length, model_width).astype(jnp.float32)

    def expert_backward(running, expert_parts):
        rows_grad, table_grad = running
        gate_mat, up_mat, down_mat, slot_ids, slot_gate, slot_live, expert_id, gate_act, up_act = (
            expert_parts
        )
        slot_rows = second_low[slot_ids]
        sigmoid_gate = jax.nn.sigmoid(gate_act)
        silu_gate = jax.nn.silu(gate_act)
        hidden = (silu_gate * up_act).astype(jnp.bfloat16)
        expert_out = lax.dot_general(
            hidden, down_mat, contract_cols, preferred_element_type=jnp.float32
        )
        slot_grad = out_grad[slot_ids]
        weight_grad = jnp.sum(slot_grad * expert_out, axis=1) * slot_live
        branch_low = (slot_grad * slot_gate[:, None]).astype(jnp.bfloat16)
        hidden_grad = jnp.dot(branch_low, down_mat, preferred_element_type=jnp.float32)
        down_grad = lax.dot_general(
            branch_low, hidden, contract_rows, preferred_element_type=jnp.float32
        )
        gate_low = (
            hidden_grad * up_act * sigmoid_gate * (1.0 + gate_act * (1.0 - sigmoid_gate))
        ).astype(jnp.bfloat16)
        up_low = (hidden_grad * silu_gate).astype(jnp.bfloat16)
        gate_grad = lax.dot_general(
            slot_rows, gate_low, contract_rows, preferred_element_type=jnp.float32
        )
        up_grad = lax.dot_general(
            slot_rows, up_low, contract_rows, preferred_element_type=jnp.float32
        )
        row_grad = lax.dot_general(
            gate_low, gate_mat, contract_cols, preferred_element_type=jnp.float32
        )
        row_grad = row_grad + lax.dot_general(
            up_low, up_mat, contract_cols, preferred_element_type=jnp.float32
        )
        rows_grad = rows_grad.at[slot_ids].add(row_grad)
        table_grad = table_grad.at[slot_ids, expert_id].add(weight_grad)
        return ((rows_grad, table_grad), (gate_grad, up_grad, down_grad))

    (rows_part, table_part), (gate_grads, up_grads, down_grads) = lax.scan(
        expert_backward,
        (
            jnp.zeros((token_length, model_width), jnp.float32),
            jnp.zeros((token_length, EXPERTS), jnp.float32),
        ),
        (
            gate_full,
            up_full,
            down_full,
            slot_tokens,
            slot_gates,
            slot_filled,
            expert_ids,
            gate_kept,
            up_kept,
        ),
    )
    rows_total, table_total = lax.psum((rows_part, table_part), "tp")
    pick_grad = jnp.take_along_axis(table_total, route_ids, axis=1)
    chosen_grad = gate_vals * (pick_grad - jnp.sum(gate_vals * pick_grad, axis=1, keepdims=True))
    logit_low = jnp.sum(picks * chosen_grad[:, :, None], axis=1).astype(jnp.bfloat16)
    router_grad = lax.dot_general(
        second_low, logit_low, contract_rows, preferred_element_type=jnp.float32
    )
    normed_two_grad = rows_total + lax.dot_general(
        logit_low, router_full, contract_cols, preferred_element_type=jnp.float32
    )
    _, norm_two_back = jax.vjp(rms_scale, residual, gain_second)
    resid_norm_grad, gain_two_grad = norm_two_back(normed_two_grad)
    residual_grad = out_grad + resid_norm_grad
    branch_low = residual_grad.astype(jnp.bfloat16)
    output_grad = lax.dot_general(
        branch_low, attended, contract_rows, preferred_element_type=jnp.float32
    )
    attended_low = jnp.dot(branch_low, output_full, preferred_element_type=jnp.float32).astype(
        jnp.bfloat16
    )
    head_douts = attended_low.reshape(token_length, kv_heads, heads_per_group, HEAD_DIM).transpose(
        1, 2, 0, 3
    )

    def attend_back(head_parts):
        head_query, head_key, head_value, head_norm, head_dout = head_parts
        scores = head_scores(head_query, head_key)
        attn_probs = jnp.exp(scores - head_norm[..., None])
        value_grad = jnp.einsum(
            "gtk,gtd->kd",
            attn_probs.astype(jnp.bfloat16),
            head_dout,
            preferred_element_type=jnp.float32,
        )
        prob_grad = jnp.einsum(
            "gtd,kd->gtk", head_dout, head_value, preferred_element_type=jnp.float32
        )
        score_low = (
            attn_probs * (prob_grad - jnp.sum(attn_probs * prob_grad, axis=-1, keepdims=True))
        ).astype(jnp.bfloat16)
        query_grad = (
            jnp.einsum("gtk,kd->gtd", score_low, head_key, preferred_element_type=jnp.float32)
            * score_scale
        )
        key_grad = (
            jnp.einsum("gtk,gtd->kd", score_low, head_query, preferred_element_type=jnp.float32)
            * score_scale
        )
        return (query_grad, key_grad, value_grad)

    query_grads, key_grads, value_grads = lax.map(
        attend_back, (head_queries, head_keys, head_values, head_lse, head_douts)
    )
    query_back = apply_rotary(
        query_grads.transpose(2, 0, 1, 3).reshape(token_length, query_heads, HEAD_DIM),
        token_positions,
        -1.0,
    )
    query_back = query_back.reshape(token_length, query_heads * HEAD_DIM)
    key_back = apply_rotary(key_grads.transpose(1, 0, 2), key_pos, -1.0).reshape(
        key_count, kv_heads * HEAD_DIM
    )
    value_back = value_grads.transpose(1, 0, 2).reshape(key_count, kv_heads * HEAD_DIM)
    prompt_key_grad, prompt_value_grad = (
        lax.psum_scatter(key_back[:PROMPT_TOKENS], "ctx", scatter_dimension=0, tiled=True),
        lax.psum_scatter(value_back[:PROMPT_TOKENS], "ctx", scatter_dimension=0, tiled=True),
    )
    key_low_grad = jnp.concatenate([prompt_key_grad, key_back[PROMPT_TOKENS:]], axis=0).astype(
        jnp.bfloat16
    )
    value_low_grad = jnp.concatenate(
        [prompt_value_grad, value_back[PROMPT_TOKENS:]], axis=0
    ).astype(jnp.bfloat16)
    query_low_grad = query_back.astype(jnp.bfloat16)
    query_w_grad = lax.dot_general(
        normed_low, query_low_grad, contract_rows, preferred_element_type=jnp.float32
    )
    key_w_grad = lax.dot_general(
        normed_low, key_low_grad, contract_rows, preferred_element_type=jnp.float32
    )
    value_w_grad = lax.dot_general(
        normed_low, value_low_grad, contract_rows, preferred_element_type=jnp.float32
    )
    normed_one_part = lax.dot_general(
        query_low_grad, query_full, contract_cols, preferred_element_type=jnp.float32
    )
    normed_one_part = normed_one_part + lax.dot_general(
        key_low_grad, key_full, contract_cols, preferred_element_type=jnp.float32
    )
    normed_one_part = normed_one_part + lax.dot_general(
        value_low_grad, value_full, contract_cols, preferred_element_type=jnp.float32
    )
    normed_one_grad = lax.psum(normed_one_part, "tp")
    _, norm_one_back = jax.vjp(rms_scale, inputs, gain_first)
    input_norm_grad, gain_one_grad = norm_one_back(normed_one_grad)
    token_grad = (residual_grad + input_norm_grad).reshape(tokens.shape)
    share_a, share_b, share_c, share_d, share_e, share_f, share_g, share_h, share_i, share_j = (
        lax.psum_scatter(gain_one_grad, "dp", scatter_dimension=0, tiled=True),
        lax.psum_scatter(query_w_grad, "dp", scatter_dimension=0, tiled=True),
        lax.psum_scatter(key_w_grad, "dp", scatter_dimension=0, tiled=True),
        lax.psum_scatter(value_w_grad, "dp", scatter_dimension=0, tiled=True),
        lax.psum_scatter(output_grad, "dp", scatter_dimension=0, tiled=True),
        lax.psum_scatter(gain_two_grad, "dp", scatter_dimension=0, tiled=True),
        lax.psum_scatter(router_grad, "dp", scatter_dimension=0, tiled=True),
        lax.psum_scatter(gate_grads, "dp", scatter_dimension=1, tiled=True),
        lax.psum_scatter(up_grads, "dp", scatter_dimension=1, tiled=True),
        lax.psum_scatter(down_grads, "dp", scatter_dimension=1, tiled=True),
    )
    owned = lax.psum(
        (share_a, share_b, share_c, share_d, share_e, share_f, share_g, share_h, share_i, share_j),
        "ctx",
    )
    return (
        result,
        token_grad,
        owned[0],
        owned[1],
        owned[2],
        owned[3],
        owned[4],
        owned[5],
        owned[6],
        owned[7],
        owned[8],
        owned[9],
    )


def solution(mesh):
    return jax.shard_map(
        body,
        mesh=mesh,
        in_specs=(
            P("dp", "ctx", None, None),
            P("dp", "ctx", None, None),
            P("dp", "ctx", None, None),
            P("dp"),
            P("dp", "tp"),
            P("dp", "tp"),
            P("dp", "tp"),
            P("dp", "tp"),
            P("dp"),
            P("dp", None),
            P(None, "dp", "tp"),
            P(None, "dp", "tp"),
            P(None, "dp", "tp"),
        ),
        out_specs=(
            P("dp", "ctx", None, None),
            P("dp", "ctx", None, None),
            P("dp"),
            P("dp", "tp"),
            P("dp", "tp"),
            P("dp", "tp"),
            P("dp", "tp"),
            P("dp"),
            P("dp", None),
            P(None, "dp", "tp"),
            P(None, "dp", "tp"),
            P(None, "dp", "tp"),
        ),
        check_vma=False,
    )
```

profile of v0, /device:TPU:0, one launch (start us, length us, event | category | flops | bytes accessed | tf_op | source)
XLA Modules:
  0.0 5315.2 jit_solution(170853726044863951)
XLA Ops:
  13.8 24.3 all-reduce.10
  40.8 35.7 all_gather.38
  85.6 33.8 all_gather.40
  136.8 73.9 %while.66 = (s32[]{:T(128)}, bf16[4,3,1024,64]{2,3,1,0:T(8,128)(2,1)S(1)}, f32[4,3,1024]{2,1,0:T(4,128)}, bf16[4,3,1024,64]{2,3,1,0:T(8,128)(2,1)S(1)}, bf16[4,1...) while((s32[]{:T(128)}, ...), condition=%wide.region_4.5_spmd.clone.clone, body=%wide.region_1.4_spmd.clone.sunk.clone | while | flops 1266152448 | bytes 64610900 | solution.py:147
  220.0 30.7 all-gather
  258.3 110.8 %all-reduce.16.cloned.1.call-done = f32[1024,1536]{1,0:T(8,128)} async-done(((f32[1024,1536]{1,0:T(8,128)}), f32[1024,1536]{1,0:T(8,128)}) %all-reduce.16.cloned.1.call-update) | async-done | bytes 6291472 | tf_op jit(solution)/shard_map/psum | solution.py:156
  378.1 65.5 %gather_fusion.3 = f32[8192]{0:T(1024)S(1)} fusion(f32[1024,16]{0,1:T(8,128)S(1)} %fusion.185, s32[8192]{0:T(1024)S(1)} %reshape.627), kind=kCustom, calls=%fused_computation.clone | custom fusion | bytes 131072 | tf_op jit(solution)/shard_map/jit(take_along_axis)/gather | solution.py:162
  453.2 60.3 %scatter_custom_fusion.4 = f32[9217]{0:T(1024)S(1)} fusion(s32[16384]{0:T(1024)S(1)} %bitcast.469, f32[16384]{0:T(1024)S(1)} %reshape.592, f32[]{:T(128)} %constant.157.clone.1), kind=kCustom, calls=%fused_computation.253 | custom fusion | bytes 36872 | tf_op jit(solution)/shard_map/scatter | solution.py:187
  513.7 60.6 %scatter_custom_fusion.3 = s32[9217]{0:T(1024)S(1)} fusion(s32[16384]{0:T(1024)S(1)} %bitcast.470, s32[16384]{0:T(1024)} %reshape.584, s32[]{:T(128)} %copy.161), kind=kCustom, calls=%fused_computation.255 | custom fusion | bytes 37380 | tf_op jit(solution)/shard_map/scatter | solution.py:175
  574.4 60.7 %scatter_custom_fusion.5 = f32[9217]{0:T(1024)S(1)} fusion(s32[16384]{0:T(1024)S(1)} %bitcast.471, f32[16384]{0:T(1024)S(1)} %broadcast.417, f32[]{:T(128)} %constant.157.clone.1), kind=kCustom, calls=%fused_computation.251 | custom fusion | bytes 36872 | tf_op jit(solution)/shard_map/scatter | solution.py:181
  635.2 89.6 %all-gather.13.cloned.1.call-done = bf16[16,1536,256]{2,1,0:T(8,128)(2,1)} async-done(((bf16[16,192,256]{2,1,0:T(8,128)(2,1)}), bf16[16,1536,256]{2,1,0:T(8,128)(2,1)}) %all-gather.13.cloned.1.call-update) | async-done | bytes 12582928 | tf_op jit(solution)/shard_map/all_gather | solution.py:72
  724.8 176.9 %all-gather.15.cloned.1.call-done = bf16[16,1536,256]{2,1,0:T(8,128)(2,1)} async-done(((bf16[16,192,256]{2,1,0:T(8,128)(2,1)}), bf16[16,1536,256]{2,1,0:T(8,128)(2,1)}) %all-gather.15.cloned.1.call-update) | async-done | bytes 12582928 | tf_op jit(solution)/shard_map/all_gather | solution.py:73
  905.2 493.3 %while.64 = (s32[]{:T(128)}, f32[1024,1536]{1,0:T(8,128)}, f32[16,576,256]{2,1,0:T(8,128)}, f32[16,576,256]{2,1,0:T(8,128)}, s32[16,576]{1,0:T(8,128)S(1)}, /*in...) while((s32[]{:T(128)}, f32[1024,1536]{1,0:T(8,128)}, ...), condition=%wide.region_17.19_spmd.clone, body=%wide.region_15.18_spmd.sunk.clone | while | flops 1361611520 | bytes 33448072 | solution.py:202
  1401.9 1424.2 %while.65 = (s32[]{:T(128)}, f32[1024,1536]{1,0:T(8,128)}, f32[1024,16]{0,1:T(8,128)S(1)}, f32[16,1536,256]{2,1,0:T(8,128)}, f32[16,1536,256]{2,1,0:T(8,128)}, /...) while((s32[]{:T(128)}, f32[1024,1536]{1,0:T(8,128)}, ...), condition=%wide.region_24.26_spmd.clone, body=%wide.region_20.25_spmd.sunk.clone | while | flops 3181664768 | bytes 81748744 | solution.py:250
  1437.7 18.7 scatter_custom_fusion.24
  1459.8 31.2 scatter_fusion
  1548.7 31.2 scatter_fusion
  1637.7 31.2 scatter_fusion
  1726.6 31.2 scatter_fusion
  1815.7 31.2 scatter_fusion
  1904.7 31.2 scatter_fusion
  1993.6 31.2 scatter_fusion
  2082.6 31.2 scatter_fusion
  2171.6 31.2 scatter_fusion
  2260.6 31.2 scatter_fusion
  2349.5 31.2 scatter_fusion
  2438.5 31.2 scatter_fusion
  2527.5 31.2 scatter_fusion
  2616.5 31.2 scatter_fusion
  2705.4 31.2 scatter_fusion
  2794.5 31.2 scatter_fusion
  2826.9 153.2 %all-reduce.20.cloned.1.call-done = (f32[1024,1536]{1,0:T(8,128)}, f32[1024,16]{0,1:T(8,128)}) async-done(((f32[1024,1536]{1,0:T(8,128)}, f32[1024,16]{0,1:T(8,128)}), (f32[1024,1536]{1,0:T(8,128)}, f32[1024,16]{0,1:T(8,128)})) %all-reduce.20.cloned.1.call-update) | async-done | bytes 6357008 | tf_op jit(solution)/shard_map/psum | solution.py:268
  2980.1 56.5 %gather_fusion.4 = f32[8192]{0:T(1024)S(1)} fusion(f32[1024,16]{0,1:T(8,128)} %get-tuple-element.414, s32[8192]{0:T(1024)S(1)} %copy-done.6), kind=kCustom, calls=%fused_computation.4.clone | custom fusion | bytes 131072 | tf_op jit(solution)/shard_map/jit(take_along_axis)/gather | solution.py:269
  3052.2 246.9 %while.67 = (s32[]{:T(128)}, f32[4,3,1024,64]{2,3,1,0:T(8,128)}, f32[4,1536,64]{1,2,0:T(8,128)}, f32[4,1536,64]{1,2,0:T(8,128)}, bf16[4,3,1024,64]{2,3,1,0:T(8,1...) while((s32[]{:T(128)}, f32[4,3,1024,64]{2,3,1,0:T(8,128)}, ...), condition=%wide.region_32.34_spmd.clone.clone, body=%wide.region_30.33_spmd.clone.sunk.clone | while | flops 3092542464 | bytes 214609200 | solution.py:318
  3075.2 19.1 multiply_convert_fusion.21
  3136.9 19.1 multiply_convert_fusion.21
  3198.6 19.1 multiply_convert_fusion.21
  3260.2 19.1 multiply_convert_fusion.21
  3360.9 32.1 reduce-scatter.21.cloned.1.call-done
  3393.0 67.8 %reduce-scatter.19.cloned.1.call-done = f32[192,256]{1,0:T(8,128)} async-done(((f32[1536,256]{1,0:T(8,128)}), f32[192,256]{1,0:T(8,128)}) %reduce-scatter.19.cloned.1.call-update) | async-done | bytes 196624 | tf_op jit(solution)/shard_map/reduce_scatter | solution.py:367
  3460.9 98.1 %reduce-scatter.23.cloned.1.call-done = f32[192,768]{1,0:T(8,128)} async-done(((f32[1536,768]{1,0:T(8,128)}), f32[192,768]{1,0:T(8,128)}) %reduce-scatter.23.cloned.1.call-update) | async-done | bytes 589840 | tf_op jit(solution)/shard_map/reduce_scatter | solution.py:369
  3559.0 99.1 %reduce-scatter.17.cloned.1.call-done = f32[192,768]{1,0:T(8,128)} async-done(((f32[1536,768]{1,0:T(8,128)}), f32[192,768]{1,0:T(8,128)}) %reduce-scatter.17.cloned.1.call-update) | async-done | bytes 589840 | tf_op jit(solution)/shard_map/reduce_scatter | solution.py:366
  3658.1 407.7 %reduce-scatter.25.cloned.1.call-done = f32[16,192,256]{2,1,0:T(8,128)} async-done(((f32[16,1536,256]{2,1,0:T(8,128)}), f32[16,192,256]{2,1,0:T(8,128)}) %reduce-scatter.25.cloned.1.call-update) | async-done | bytes 3145744 | tf_op jit(solution)/shard_map/reduce_scatter | solution.py:372
  4065.9 407.0 %reduce-scatter.27.cloned.1.call-done = f32[16,192,256]{2,1,0:T(8,128)} async-done(((f32[16,1536,256]{2,1,0:T(8,128)}), f32[16,192,256]{2,1,0:T(8,128)}) %reduce-scatter.27.cloned.1.call-update) | async-done | bytes 3145744 | tf_op jit(solution)/shard_map/reduce_scatter | solution.py:373
  4472.9 406.9 %reduce-scatter.29.cloned.1.call-done = f32[16,192,256]{2,1,0:T(8,128)} async-done(((f32[16,1536,256]{2,1,0:T(8,128)}), f32[16,192,256]{2,1,0:T(8,128)}) %reduce-scatter.29.cloned.1.call-update) | async-done | bytes 3145744 | tf_op jit(solution)/shard_map/reduce_scatter | solution.py:374
  4880.5 65.0 %reduce-scatter.31.cloned.1.call-done = f32[192,16]{1,0:T(8,128)} async-done(((f32[1536,16]{1,0:T(8,128)}), f32[192,16]{1,0:T(8,128)}) %reduce-scatter.31.cloned.1.call-update) | async-done | bytes 12304
  4946.5 289.1 %all-reduce.18.cloned.1.call-done = (f32[1024,1536]{1,0:T(8,128)}, f32[1024,1536]{1,0:T(8,128)}) async-done(((f32[1024,1536]{1,0:T(8,128)}, f32[1024,1536]{1,0:T(8,128)}), (f32[1024,1536]{1,0:T(8,128)}, f32[1024,1536]{1,0:T(8,128)})) %all-reduce.18.cloned.1.call-update) | async-done | bytes 12582928 | tf_op jit(solution)/shard_map/psum | solution.py:207
  5239.8 37.1 all-reduce.5
  (1106 shorter events, 1800.0 us)
Async XLA Ops:
  7.2 72.8 %copy-start.10 = (bf16[1,1,1024,1536]{3,2,1,0:T(8,128)(2,1)S(1)}, bf16[1,1,1024,1536]{3,2,1,0:T(8,128)(2,1)}, u32[]{:S(2)}) copy-start(bf16[1,1,1024,1536]{3,2,1,0:T(8,128)(2,1)} %param.23) | copy-start | bytes 9437188
  7.2 33.6 copy-start.60
  7.2 119.3 %all-gather.7.cloned.1.call-start = ((), (), s32[]{:S(2)}) async-start(), calls=%async_computation.10 | async-start | bytes 2654208 | tf_op jit(solution)/shard_map/all_gather | solution.py:65
  7.9 202.8 %all-gather.9.cloned.1.call-start = ((), (), s32[]{:S(2)}) async-start(), calls=%async_computation.11 | async-start | bytes 2654208 | tf_op jit(solution)/shard_map/all_gather | solution.py:68
  8.7 360.4 %all-reduce.16.cloned.1.call-start = ((), (), s32[]{:S(2)}) async-start(), calls=%async_computation.12 | async-start | bytes 12582912 | tf_op jit(solution)/shard_map/psum | solution.py:156
  8.8 73.5 %copy-start.78 = (f32[32]{0:T(128)}, f32[32]{0:T(128)S(1)}, u32[]{:S(2)}) copy-start(f32[32]{0:T(128)S(1)} %multiply_power_fusion) | copy-start | bytes 388
  38.2 92.8 %copy-start.62 = (f32[1536]{0:T(1024)}, f32[1536]{0:T(1024)S(1)}, u32[]{:S(2)}) copy-start(f32[1536]{0:T(1024)S(1)} %convert_element_type.148) | copy-start | bytes 18436
  40.8 35.7 copy-start.70
  40.8 90.2 %copy-start.68 = (f32[1024]{0:T(1024)}, f32[1024]{0:T(1024)S(1)}, u32[]{:S(2)}) copy-start(f32[1024]{0:T(1024)S(1)} %fusion.167) | copy-start | bytes 12292
  79.9 55.4 %copy-start.30 = (f32[1024,32]{0,1:T(8,128)}, f32[1024,32]{0,1:T(8,128)S(1)}, u32[]{:S(2)}) copy-start(f32[1024,32]{0,1:T(8,128)S(1)} %get-tuple-element.459) | copy-start | bytes 393220
  218.2 417.0 %all-gather.11.cloned.1.call-start = ((), (), s32[]{:S(2)}) async-start(), calls=%async_computation.13 | async-start | bytes 14155776 | tf_op jit(solution)/shard_map/all_gather | solution.py:71
  218.7 506.1 %all-gather.13.cloned.1.call-start = ((), (), s32[]{:S(2)}) async-start(), calls=%async_computation.14 | async-start | bytes 14155776 | tf_op jit(solution)/shard_map/all_gather | solution.py:72
  219.3 682.4 %all-gather.15.cloned.1.call-start = ((), (), s32[]{:S(2)}) async-start(), calls=%async_computation.15 | async-start | bytes 14155776 | tf_op jit(solution)/shard_map/all_gather | solution.py:73
  219.9 2760.1 %all-reduce.20.cloned.1.call-start = ((), (), s32[]{:S(2)}) async-start(), calls=%async_computation.27 | async-start | bytes 12713984 | tf_op jit(solution)/shard_map/psum | solution.py:268
  220.0 152.8 %copy-start.54 = (f32[1536]{0:T(1024)}, f32[1536]{0:T(1024)S(1)}, u32[]{:S(2)}) copy-start(f32[1536]{0:T(1024)S(1)} %convert_element_type.161) | copy-start | bytes 18436
  250.9 123.2 %copy-start.48 = (bf16[1536,16]{0,1:T(8,128)(2,1)}, bf16[1536,16]{0,1:T(8,128)(2,1)S(1)}, u32[]{:S(2)}) copy-start(bf16[1536,16]{0,1:T(8,128)(2,1)S(1)} %reshape.621) | copy-start | bytes 147460
  251.4 126.7 %copy-start.5 = (s32[8192]{0:T(1024)}, s32[8192]{0:T(1024)S(1)}, u32[]{:S(2)}) copy-start(s32[8192]{0:T(1024)S(1)} %reshape.627) | copy-start | bytes 98308
  252.8 116.3 %copy-start.11 = (bf16[1,1,1024,1536]{3,2,1,0:T(8,128)(2,1)S(1)}, bf16[1,1,1024,1536]{3,2,1,0:T(8,128)(2,1)}, u32[]{:S(2)}) copy-start(bf16[1,1,1024,1536]{3,2,1,0:T(8,128)(2,1)} %param.23) | copy-start | bytes 9437188
  378.1 66.0 %copy-start.42 = (s32[1,1,1024,8]{2,3,1,0:T(8,128)S(1)}, s32[1,1,1024,8]{2,3,1,0:T(8,128)}, u32[]{:S(2)}) copy-start(s32[1,1,1024,8]{2,3,1,0:T(8,128)} %param.24) | copy-start | bytes 98308
  378.1 72.2 %copy-start.80 = (s32[16]{0:T(128)S(1)}, s32[16]{0:T(128)}, u32[]{:S(2)}) copy-start(s32[16]{0:T(128)} %iota_multiply_fusion) | copy-start | bytes 196
  450.8 454.4 %copy-start.1 = (bf16[1024,1536]{1,0:T(8,128)(2,1)S(1)}, bf16[1024,1536]{1,0:T(8,128)(2,1)}, u32[]{:S(2)}) copy-start(bf16[1024,1536]{1,0:T(8,128)(2,1)} %copy-done) | copy-start | bytes 9437188
  2826.1 210.5 %copy-start.2 = (bf16[1024,1536]{1,0:T(8,128)(2,1)}, bf16[1024,1536]{1,0:T(8,128)(2,1)S(1)}, u32[]{:S(2)}) copy-start(bf16[1024,1536]{1,0:T(8,128)(2,1)S(1)} %get-tuple-element.1082) | copy-start | bytes 9437188
  2826.2 153.9 %copy-start.6 = (s32[8192]{0:T(1024)S(1)}, s32[8192]{0:T(1024)}, u32[]{:S(2)}) copy-start(s32[8192]{0:T(1024)} %copy-done.5) | copy-start | bytes 98308
  2826.8 483.4 %reduce-scatter.15.cloned.1.call-start = ((), (), s32[]{:S(2)}) async-start(), calls=%async_computation.17 | async-start | bytes 1572864 | tf_op jit(solution)/shard_map/reduce_scatter | solution.py:333
  2980.1 58.9 %copy-start.45 = (f32[1024,8]{0,1:T(8,128)S(1)}, f32[1024,8]{0,1:T(8,128)}, u32[]{:S(2)}) copy-start(f32[1024,8]{0,1:T(8,128)} %copy-done.44) | copy-start | bytes 98308
  2980.1 58.9 %copy-start.53 = (pred[1024,8]{0,1:T(8,128)(4,1)S(1)}, pred[1024,8]{0,1:T(8,128)(4,1)}, u32[]{:S(2)}) copy-start(pred[1024,8]{0,1:T(8,128)(4,1)} %copy-done.52) | copy-start | bytes 24580
  2980.1 58.9 %copy-start.43 = (s32[1,1,1024,8]{2,3,1,0:T(8,128)S(1)}, s32[1,1,1024,8]{2,3,1,0:T(8,128)}, u32[]{:S(2)}) copy-start(s32[1,1,1024,8]{2,3,1,0:T(8,128)} %param.24) | copy-start | bytes 98308
  2980.1 59.0 %copy-start.49 = (bf16[1536,16]{0,1:T(8,128)(2,1)S(1)}, bf16[1536,16]{0,1:T(8,128)(2,1)}, u32[]{:S(2)}) copy-start(bf16[1536,16]{0,1:T(8,128)(2,1)} %copy-done.48) | copy-start | bytes 147460
  2980.1 59.0 %copy-start.55 = (f32[1536]{0:T(1024)S(1)}, f32[1536]{0:T(1024)}, u32[]{:S(2)}) copy-start(f32[1536]{0:T(1024)} %copy-done.54) | copy-start | bytes 18436
  2980.1 59.0 %copy-start.67 = (f32[1024]{0:T(1024)S(1)}, f32[1024]{0:T(1024)}, u32[]{:S(2)}) copy-start(f32[1024]{0:T(1024)} %copy-done.66) | copy-start | bytes 12292
  3052.2 249.4 %copy-start.75 = (f32[1536]{0:T(1024)S(1)}, f32[1536]{0:T(1024)}, u32[]{:S(2)}) copy-start(f32[1536]{0:T(1024)} %get-tuple-element.455) | copy-start | bytes 18436
  3052.2 249.4 %copy-start.79 = (f32[32]{0:T(128)S(1)}, f32[32]{0:T(128)}, u32[]{:S(2)}) copy-start(f32[32]{0:T(128)} %copy-done.78) | copy-start | bytes 388
  3075.2 33.0 slice-start.1
  3136.8 33.0 slice-start.1
  3198.5 33.0 slice-start.1
  3301.5 21.2 reduce-scatter.13.cloned.1.call-start
  3306.1 86.9 %reduce-scatter.21.cloned.1.call-start = ((), (), s32[]{:S(2)}) async-start(), calls=%async_computation.20 | async-start | bytes 1769472 | tf_op jit(solution)/shard_map/reduce_scatter | solution.py:368
  3314.7 146.1 %reduce-scatter.19.cloned.1.call-start = ((), (), s32[]{:S(2)}) async-start(), calls=%async_computation.19 | async-start | bytes 1769472 | tf_op jit(solution)/shard_map/reduce_scatter | solution.py:367
  3327.9 231.1 %reduce-scatter.23.cloned.1.call-start = ((), (), s32[]{:S(2)}) async-start(), calls=%async_computation.21 | async-start | bytes 5308416 | tf_op jit(solution)/shard_map/reduce_scatter | solution.py:369
  3336.0 322.1 %reduce-scatter.17.cloned.1.call-start = ((), (), s32[]{:S(2)}) async-start(), calls=%async_computation.18 | async-start | bytes 5308416 | tf_op jit(solution)/shard_map/reduce_scatter | solution.py:366
  3345.4 720.5 %reduce-scatter.25.cloned.1.call-start = ((), (), s32[]{:S(2)}) async-start(), calls=%async_computation.22 | async-start | bytes 28311552 | tf_op jit(solution)/shard_map/reduce_scatter | solution.py:372
  3345.9 1126.9 %reduce-scatter.27.cloned.1.call-start = ((), (), s32[]{:S(2)}) async-start(), calls=%async_computation.23 | async-start | bytes 28311552 | tf_op jit(solution)/shard_map/reduce_scatter | solution.py:373
  3346.5 1533.2 %reduce-scatter.29.cloned.1.call-start = ((), (), s32[]{:S(2)}) async-start(), calls=%async_computation.24 | async-start | bytes 28311552 | tf_op jit(solution)/shard_map/reduce_scatter | solution.py:374
  3347.1 1598.4 %reduce-scatter.31.cloned.1.call-start = ((), (), s32[]{:S(2)}) async-start(), calls=%async_computation.25 | async-start | bytes 884736
  3350.8 1884.8 %all-reduce.18.cloned.1.call-start = ((), (), s32[]{:S(2)}) async-start(), calls=%async_computation.26 | async-start | bytes 25165824 | tf_op jit(solution)/shard_map/psum | solution.py:207
  3360.9 1933.8 %all-reduce.22.cloned.1.call-start = ((), (), s32[]{:S(2)}) async-start(), calls=%async_computation.28 | async-start | bytes 22020096 | tf_op jit(solution)/shard_map/psum | solution.py:376
  4879.8 355.8 %copy-start.13 = (bf16[1,1,1024,1536]{3,2,1,0:T(8,128)(2,1)S(1)}, bf16[1,1,1024,1536]{3,2,1,0:T(8,128)(2,1)}, u32[]{:S(2)}) copy-start(bf16[1,1,1024,1536]{3,2,1,0:T(8,128)(2,1)} %param.23) | copy-start | bytes 9437188
  5235.6 45.5 copy-start.71
  (228 other events, 2974.5 us)
Sparse Core Ops, SparseCore 0:
  10.2 65.5 all-gather.6
  78.0 55.8 all-gather.8
  218.3 150.7 all-reduce.15
  371.4 176.4 all-gather.10
  550.2 174.6 all-gather.12
  727.1 174.6 all-gather.14
  2826.9 153.0 all-reduce.19
  3301.6 8.5 reduce-scatter.14
  3313.0 9.6 reduce-scatter.12
  3327.0 65.9 reduce-scatter.20
  3397.0 63.7 reduce-scatter.18
  3464.8 94.1 reduce-scatter.22
  3563.1 95.0 reduce-scatter.16
  3662.4 403.4 reduce-scatter.24
  4070.1 402.7 reduce-scatter.26
  4477.1 402.6 reduce-scatter.28
  4883.8 61.6 reduce-scatter.30
  4947.9 287.6 all-reduce.17
  5238.9 44.6 all-reduce.21
where the time goes:
time: 5330 us; the launch traced here: 5320 us
  waiting for transfers between devices  2420 us (45%)
  other arithmetic  1250 us (23%)
  matrix products  796 us (15%)
  local copies, waits for them, and re-layouts  634 us (12%)
  blocking collectives  170 us (3%)
    scatter-add x16, other arithmetic, expert_backward(): table_grad = table_grad.at[slot_ids, expert_id].add(weight_grad)  500 us
    reduce_scatter x1, waiting for transfers between devices, body(): lax.psum_scatter(gate_grads, 'dp', scatter_dimension=1, tiled=True)  408 us
    reduce_scatter x1, waiting for transfers between devices, body(): lax.psum_scatter(up_grads, 'dp', scatter_dimension=1, tiled=True)  407 us
    reduce_scatter x1, waiting for transfers between devices, body(): lax.psum_scatter(down_grads, 'dp', scatter_dimension=1, tiled=True)  407 us
    scatter-add x16, other arithmetic, expert_backward(): rows_grad = rows_grad.at[slot_ids].add(row_grad)  299 us
    psum x1, waiting for transfers between devices, body(): moe_total = lax.psum(moe_part, 'tp')  289 us
    scatter-add x16, other arithmetic, expert_forward(): running.at[slot_ids].add(expert_out * slot_gate[:, None])  284 us
    all_gather x1, waiting for transfers between devices, body(): lax.all_gather(w_down, 'dp', axis=1, tiled=True)  177 us
  transfers between devices with their start and end apart: 19, of which 15 were waited for; matrix products, arithmetic and copies ran while one was open for 8% of the time, Pallas kernels for 0%

commit v1 on v0

v1 whole, which is shorter than its diff:
```python
import functools

import jax
import jax.numpy as jnp
from jax import lax
from jax.experimental import pallas as pl
from jax.experimental.pallas import tpu as pltpu
from jax.sharding import PartitionSpec as P

HEAD_DIM = 64
EXPERTS = 16
TOPK = 8
PROMPT_TOKENS = 1024
LANES = 128
ROUTER_LANE = 16

norm_eps = 1e-06
rope_base = 10000.0
masked_score = -1e30
bf = jnp.bfloat16
f32 = jnp.float32
contract_cols = (((1,), (1,)), ((), ()))
vmem_bytes = 58 * 1024 * 1024


def mm(a, b):
    return jnp.dot(a, b, preferred_element_type=f32)


def mm_nt(a, b):
    return lax.dot_general(a, b, contract_cols, preferred_element_type=f32)


def whole(shape):
    return pl.BlockSpec(shape, lambda *_: (0,) * len(shape), pipeline_mode=pl.Buffered(1))


def rows_of(block, width):
    return pl.BlockSpec((block, width), lambda i, *_: (i, 0))


def any_space():
    return pl.BlockSpec(memory_space=pl.ANY)


def call(kernel, name, grid, ins, in_specs, outs, out_specs, scratch, flops, scalars, limit=vmem_bytes):
    moved = sum(a.size * a.dtype.itemsize for a in (*ins, *outs))
    return pl.pallas_call(
        kernel,
        out_shape=tuple(outs),
        grid_spec=pltpu.PrefetchScalarGridSpec(
            num_scalar_prefetch=1,
            grid=grid,
            in_specs=in_specs,
            out_specs=tuple(out_specs),
            scratch_shapes=scratch,
        ),
        compiler_params=pltpu.CompilerParams(vmem_limit_bytes=limit),
        cost_estimate=pl.CostEstimate(flops=int(flops), bytes_accessed=int(moved), transcendentals=0),
        name=name,
    )(scalars, *ins)


def sds(shape, dtype):
    return jax.ShapeDtypeStruct(tuple(shape), dtype)


def ring_rank(place, count):
    place = lax.rem(place + 2 * count, count)
    return jnp.where(place < count // 2, 2 * place, 2 * count - 1 - 2 * place)


def ring_place(rank, count):
    return jnp.where(rank % 2 == 0, rank // 2, (2 * count - 1 - rank) // 2)


def ring_pairs(count):
    order = list(range(0, count, 2)) + list(range(count - 1, 0, -2))
    ahead = [(order[k], order[(k + 1) % count]) for k in range(count)]
    return ahead, [(d, s) for s, d in ahead]


def ring_gather(own, count):
    ahead, back = ring_pairs(count)
    cut = (own.shape[0] + 1) // 2
    kept, f, g = [own], own, own
    for hop in range(1, count // 2 + 1):
        if hop == count // 2:
            f, g = f[:cut], g[cut:]
        f, g = lax.ppermute(f, "dp", ahead), lax.ppermute(g, "dp", back)
        kept += [f, g]
    return kept


def ring_sources(place, count):
    away = [0]
    for hop in range(1, count // 2):
        away += [-hop, hop]
    away.append(count // 2)
    return [ring_rank(place + a, count) for a in away]


def ring_scatter(piece, place, count):
    ahead, back = ring_pairs(count)
    f = g = None
    for hop in range(1, count // 2 + 1):
        far = count // 2 - hop + 1
        if hop == 1:
            mine = piece(ring_rank(place + far, count))
            cut = (mine.shape[0] + 1) // 2
            f, g = mine[:cut].astype(bf), mine[cut:].astype(bf)
        else:
            mine_f = piece(ring_rank(place + far, count))
            mine_g = piece(ring_rank(place - far, count))
            if hop == 2:
                f = jnp.concatenate([mine_f[:cut] + f.astype(f32), mine_f[cut:]], axis=0).astype(bf)
                g = jnp.concatenate([mine_g[:cut], mine_g[cut:] + g.astype(f32)], axis=0).astype(bf)
            else:
                f = (mine_f + f.astype(f32)).astype(bf)
                g = (mine_g + g.astype(f32)).astype(bf)
        f, g = lax.ppermute(f, "dp", ahead), lax.ppermute(g, "dp", back)
    return piece(ring_rank(place, count)) + f.astype(f32) + g.astype(f32)


def swap(values, axis):
    return lax.ppermute(values, axis, [(0, 1), (1, 0)])


def take(values, start, size):
    return lax.dynamic_slice_in_dim(values, start, size, 0)


def load_shards(scalars, bufs, first_block, blocks, dst, shard, sem):
    total = len(bufs)
    cut = (blocks + 1) // 2
    for k, buf in enumerate(bufs):
        rows = pl.ds(pl.multiple_of(scalars[min(k, total - 2)] * shard, shard), shard)
        at = first_block + (cut if k == total - 1 else 0)
        size = blocks if k < total - 2 else (cut if k == total - 2 else blocks - cut)
        pltpu.make_async_copy(buf, dst.at[pl.ds(at, size), rows, :], sem).start()


def lanes_of(ref, first, count):
    return jnp.concatenate([ref[first + b] for b in range(count)], axis=1)


def rope(x, cosine, sine):
    lane = lax.broadcasted_iota(jnp.int32, x.shape, x.ndim - 1)
    ahead = pltpu.roll(x, x.shape[-1] - HEAD_DIM // 2, x.ndim - 1)
    behind = pltpu.roll(x, HEAD_DIM // 2, x.ndim - 1)
    return x * cosine + jnp.where(lax.rem(lane, HEAD_DIM) < HEAD_DIM // 2, ahead, behind) * sine


def qkv_kernel(shard, kinds, sc, tok, cosine, sine, *refs):
    heads, kvs, total = kinds
    bufs, (w_out, extra_out, q_out, k_out, v_out, nt_out, w, et, sem, out_sem) = refs[: 2 * total], refs[2 * total :]
    half = w.shape[0] // 2
    step = pl.program_id(0)

    @pl.when(step == 0)
    def _():
        for side in range(2):
            base = sc[total - 1 + side] * half
            load_shards(sc, bufs[side * total : (side + 1) * total], base, half, w, shard, sem)
        pltpu.make_async_copy(w, w, sem).wait()
        pltpu.make_async_copy(w, w_out, out_sem).start()
        et[...] = w[heads // 2 + kvs].T

    extra_out[...] = et[...]
    x = tok[...].astype(f32)
    scale = lax.rsqrt(jnp.mean(x * x, axis=-1, keepdims=True) + norm_eps)
    normed = (x * scale * et[0:1, :].astype(f32)).astype(bf)
    nt_out[...] = normed.T
    cs, sn = cosine[...], sine[...]
    for pair in range((heads + 2 * kvs) // 4):
        made = mm(normed, lanes_of(w, 2 * pair, 2))
        for side in range(2):
            first = 4 * pair + 2 * side
            part = made[:, side * LANES : (side + 1) * LANES]
            if first < heads + kvs:
                part = rope(part, cs, sn)
            if first < heads:
                part, out, at = part * (1.0 / HEAD_DIM), q_out, first
            elif first < heads + kvs:
                out, at = k_out, first - heads
            else:
                out, at = v_out, first - heads - kvs
            low = part.astype(bf)
            out[at] = low[:, :HEAD_DIM]
            out[at + 1] = low[:, HEAD_DIM:]

    @pl.when(step == pl.num_programs(0) - 1)
    def _():
        pltpu.make_async_copy(w, w_out, out_sem).wait()


def project(tokens, cosine, sine, scalars, own, mate, heads, kvs, block=256):
    rows, width = tokens.shape
    shard = own[0].shape[1]
    blocks = 2 * own[0].shape[0]
    head_spec = lambda count: pl.BlockSpec((count, block, HEAD_DIM), lambda i, s: (0, i, 0))
    outs = [
        sds((blocks, width, LANES), bf),
        sds((LANES, width), bf),
        sds((heads, rows, HEAD_DIM), bf),
        sds((kvs, rows, HEAD_DIM), bf),
        sds((kvs, rows, HEAD_DIM), bf),
        sds((width, rows), bf),
    ]
    return call(
        functools.partial(qkv_kernel, shard, (heads, kvs, len(own))),
        "project",
        (rows // block,),
        [tokens, cosine, sine, *own, *mate],
        [rows_of(block, width), rows_of(block, LANES), rows_of(block, LANES)] + [any_space()] * (2 * len(own)),
        outs,
        [
            any_space(),
            whole((LANES, width)),
            head_spec(heads),
            head_spec(kvs),
            head_spec(kvs),
            pl.BlockSpec((width, block), lambda i, s: (0, i)),
        ],
        [
            pltpu.VMEM((blocks, width, LANES), bf),
            pltpu.VMEM((LANES, width), bf),
            pltpu.SemaphoreType.DMA,
            pltpu.SemaphoreType.DMA,
        ],
        2 * rows * width * blocks * LANES,
        scalars,
    )


def assemble_kernel(shard, sc, *refs):
    total = (len(refs) - 2) // 2
    out, sem = refs[-2], refs[-1]
    half = out.shape[0] // 2
    for side in range(2):
        load_shards(sc, refs[side * total : (side + 1) * total], sc[total - 1 + side] * half, half, out, shard, sem)
    pltpu.make_async_copy(out, out, sem).wait()


def assemble(scalars, own, mate, width):
    shard = own[0].shape[1]
    return call(
        functools.partial(assemble_kernel, shard),
        "assemble",
        (1,),
        [*own, *mate],
        [any_space()] * (2 * len(own)),
        [sds((2 * own[0].shape[0], width, LANES), bf)],
        [any_space()],
        [pltpu.SemaphoreType.DMA],
        0,
        scalars,
    )[0]


def causal(scores):
    key = lax.broadcasted_iota(jnp.int32, scores.shape, 0)
    query = lax.broadcasted_iota(jnp.int32, scores.shape, 1)
    return jnp.where(key <= query, scores, masked_score)


def block_scores(query, keys, other_keys, at, block, prompt, bias):
    parts = []
    if at:
        parts.append(mm_nt(keys[0:at], query))
    parts.append(causal(mm_nt(keys[at : at + block], query)))
    other = mm_nt(other_keys, query)
    if at < prompt:
        other = other + bias
    parts.append(other)
    return parts


def attend_kernel(cfg, sc, q, k0, k1, o0, o1, v0, v1, w0, w1, mixed, lse):
    starts, block, prompt = cfg
    bias = jnp.where(sc[0] == 0, masked_score, 0.0).astype(f32)
    for side, (keys, other, values, other_values) in enumerate(((k0, o0, v0, w0), (k1, o1, v1, w1))):
        values_t = values[0].T
        other_t = other_values[0].T
        for a, at in enumerate(starts):
            rows = slice(a * block, a * block + block)
            scores = block_scores(q[side, rows, :], keys[0], other[0], at, block, prompt, bias)
            peak = functools.reduce(jnp.maximum, [jnp.max(s, axis=0, keepdims=True) for s in scores])
            raw = [jnp.exp(s - peak) for s in scores]
            total = sum(jnp.sum(r, axis=0, keepdims=True) for r in raw)
            low = [r.astype(bf) for r in raw]
            out = mm(other_t, low[-1]) + mm(values_t[:, at : at + block], low[-2])
            if at:
                out = out + mm(values_t[:, 0:at], low[0])
            out = out * (1.0 / total)
            mixed[rows, side * HEAD_DIM : side * HEAD_DIM + HEAD_DIM] = out.T.astype(bf)
            lse[0, side : side + 1, rows] = peak + jnp.log(total)


def kv_specs(kvs, rows, prompt, rep):
    index = lambda side: (lambda p, s: ((2 * p + side) // rep, 0, 0))
    own = [pl.BlockSpec((1, rows, HEAD_DIM), index(side)) for side in range(2)]
    other = [pl.BlockSpec((1, prompt, HEAD_DIM), index(side)) for side in range(2)]
    return own + other


def attend(q, k, v, other_k, other_v, core, part, block=256):
    heads, rows, _ = q.shape
    kvs, prompt = other_k.shape[:2]
    count = prompt if part == 0 else rows - prompt
    first = 0 if part == 0 else prompt
    starts = tuple(range(first, first + count, block))
    specs = kv_specs(kvs, rows, prompt, heads // kvs)
    return call(
        functools.partial(attend_kernel, (starts, block, prompt)),
        "attend",
        (heads // 2,),
        [q, k, k, other_k, other_k, v, v, other_v, other_v],
        [pl.BlockSpec((2, count, HEAD_DIM), lambda p, s: (p, part, 0)), *specs, *specs],
        [sds((count, heads * HEAD_DIM), bf), sds((heads // 2, 2, count), f32)],
        [
            pl.BlockSpec((count, LANES), lambda p, s: (0, p)),
            pl.BlockSpec((1, 2, count), lambda p, s: (p, 0, 0)),
        ],
        [],
        16 * heads * count * 1024 * HEAD_DIM,
        core,
    )


def attend_back_kernel(cfg, sc, q, k0, k1, o0, o1, v0, v1, w0, w1, dout, mixed_a, mixed_b, lse_a, lse_b, cosine, sine, dq, dk, dko, dv, dvo):
    rows_total, block, prompt, rep = cfg
    pair = pl.program_id(0)
    bias = jnp.where(sc[0] == 0, masked_score, 0.0).astype(f32)

    @pl.when(pair == 0)
    def _():
        for ref in (dk, dko, dv, dvo):
            ref[...] = jnp.zeros_like(ref)

    heads = ((k0, o0, v0, w0), (k1, o1, v1, w1))
    keys_t = [(keys[0].T, other[0].T) for keys, other, _, _ in heads]
    for at in range(0, rows_total, block):
        rows = slice(at, at + block)
        mixed, lse, local = (mixed_a, lse_a, at) if at < prompt else (mixed_b, lse_b, at - prompt)
        inner = slice(local, local + block)
        dot = (dout[rows, :].astype(f32) * mixed[inner, :].astype(f32)).T
        grads = []
        for side, (keys, other, values, other_values) in enumerate(heads):
            kv = (2 * pair + side) // rep
            query = q[side, rows, :]
            grad = dout[rows, side * HEAD_DIM : side * HEAD_DIM + HEAD_DIM]
            weighted = jnp.sum(dot[side * HEAD_DIM : side * HEAD_DIM + HEAD_DIM], axis=0, keepdims=True)
            norm = lse[0, side : side + 1, inner]
            scores = block_scores(query, keys[0], other[0], at, block, prompt, bias)
            spans = ([(False, 0, at)] if at else []) + [(False, at, block), (True, 0, prompt)]
            back = None
            for score, (is_other, first, size) in zip(scores, spans):
                probs = jnp.exp(score - norm)
                value = other_values[0] if is_other else values[0, first : first + size]
                score_low = (probs * (mm_nt(value, grad) - weighted)).astype(bf)
                key_sum, value_sum = (dko, dvo) if is_other else (dk, dv)
                span = pl.ds(first, size)
                value_sum[kv, span, :] += mm(probs.astype(bf), grad)
                key_sum[kv, span, :] += mm(score_low, query)
                key_t = keys_t[side][1] if is_other else keys_t[side][0][:, first : first + size]
                term = mm(key_t, score_low)
                back = term if back is None else back + term
            grads.append(back)
        both = jnp.concatenate(grads, axis=0).T * (1.0 / HEAD_DIM)
        dq[rows, :] = rope(both, cosine[rows, :], -sine[rows, :]).astype(bf)


def attend_back(q, k, v, other_k, other_v, dout, mixed, lse, cosine, sine, core, block=256):
    heads, rows, _ = q.shape
    kvs, prompt = other_k.shape[:2]
    specs = kv_specs(kvs, rows, prompt, heads // kvs)
    pair = pl.BlockSpec((rows, LANES), lambda p, s: (0, p))
    mixed_spec = lambda a: pl.BlockSpec((a.shape[0], LANES), lambda p, s: (0, p))
    lse_spec = lambda a: pl.BlockSpec((1, 2, a.shape[2]), lambda p, s: (p, 0, 0))
    return call(
        functools.partial(attend_back_kernel, (rows, block, prompt, heads // kvs)),
        "attend_back",
        (heads // 2,),
        [q, k, k, other_k, other_k, v, v, other_v, other_v, dout, *mixed, *lse, cosine, sine],
        [
            pl.BlockSpec((2, rows, HEAD_DIM), lambda p, s: (p, 0, 0)),
            *specs,
            *specs,
            pair,
            *[mixed_spec(a) for a in mixed],
            *[lse_spec(a) for a in lse],
            whole(cosine.shape),
            whole(sine.shape),
        ],
        [
            sds((rows, heads * HEAD_DIM), bf),
            sds((kvs, rows, HEAD_DIM), f32),
            sds((kvs, prompt, HEAD_DIM), f32),
            sds((kvs, rows, HEAD_DIM), f32),
            sds((kvs, prompt, HEAD_DIM), f32),
        ],
        [
            pair,
            whole((kvs, rows, HEAD_DIM)),
            whole((kvs, prompt, HEAD_DIM)),
            whole((kvs, rows, HEAD_DIM)),
            whole((kvs, prompt, HEAD_DIM)),
        ],
        [],
        40 * heads * rows * 1024 * HEAD_DIM,
        core,
    )


def load_halves(sc, mine, theirs, first_block, w, sem):
    half = mine.shape[0]
    pltpu.make_async_copy(mine, w.at[pl.ds(first_block + sc[0] * half, half)], sem).start()
    pltpu.make_async_copy(theirs, w.at[pl.ds(first_block + (1 - sc[0]) * half, half)], sem).start()


def settle_kernel(sc, tok, ids, own_a, own_b, far_a, far_b, extra, w_own, w_mine, w_theirs, res_out, n_out, nt_out, wt_out, w, sem):
    step = pl.program_id(0)
    blocks = w_own.shape[0]

    @pl.when(step == 0)
    def _():
        pltpu.make_async_copy(w_own, w.at[pl.ds(0, blocks)], sem).start()
        load_halves(sc, w_mine, w_theirs, blocks, w, sem)
        pltpu.make_async_copy(w, w, sem).wait()

    early = step < pl.num_programs(0) // 2
    own = jnp.where(early, own_a[...], own_b[...])
    far = jnp.where(early, far_a[...], far_b[...])
    branch = mm_nt(own, lanes_of(w, 0, blocks)) + mm_nt(far, lanes_of(w, blocks, blocks))
    residual = tok[...].astype(f32) + branch
    res_out[...] = residual
    scale = lax.rsqrt(jnp.mean(residual * residual, axis=-1, keepdims=True) + norm_eps)
    normed = (residual * scale * extra[1:2, :].astype(f32)).astype(bf)
    n_out[...] = normed
    nt_out[...] = normed.T
    logits = mm_nt(normed, extra[...])
    lane = lax.broadcasted_iota(jnp.int32, logits.shape, 1)
    routed = lane < 0
    for k in range(TOPK):
        routed = jnp.logical_or(routed, lane == ids[:, k : k + 1] + ROUTER_LANE)
    logits = jnp.where(routed, logits, masked_score)
    raw = jnp.where(routed, jnp.exp(logits - jnp.max(logits, axis=-1, keepdims=True)), 0.0)
    wt_out[...] = raw / jnp.sum(raw, axis=-1, keepdims=True)


def settle(tokens, ids, own, far, extra, w_own, w_mine, w_theirs, core, block=256):
    rows, width = tokens.shape
    halves = rows // block // 2
    cols = own[0].shape[1]
    low = pl.BlockSpec((block, cols), lambda i, s: (jnp.minimum(i, halves - 1), 0))
    high = pl.BlockSpec((block, cols), lambda i, s: (jnp.maximum(i - halves, 0), 0))
    return call(
        settle_kernel,
        "settle",
        (rows // block,),
        [tokens, ids, *own, *far, extra, w_own, w_mine, w_theirs],
        [rows_of(block, width), rows_of(block, TOPK), low, high, low, high, whole(extra.shape)] + [any_space()] * 3,
        [sds((rows, width), f32), sds((rows, width), bf), sds((width, rows), bf), sds((rows, LANES), f32)],
        [rows_of(block, width), rows_of(block, width), pl.BlockSpec((width, block), lambda i, s: (0, i)), rows_of(block, LANES)],
        [pltpu.VMEM((2 * w_own.shape[0], width, LANES), bf), pltpu.SemaphoreType.DMA],
        4 * rows * width * cols,
        core,
    )


def experts_kernel(cfg, sc, *refs):
    shard, width, rows_total, hidden, half, first, last, total = cfg
    block = 256
    step = pl.program_id(0)
    it = iter(refs)
    n2, n2t, cot, cott, wt = (next(it) for _ in range(5))
    mine = [next(it) for _ in range(total)]
    mate = [next(it) for _ in range(total)]
    if not first:
        moe_in, back_in = next(it), next(it)
    moe_out, back_out, keep, send, pick = (next(it) for _ in range(5))
    w, scaled, acts, sem, sum_sem = (next(it) for _ in range(5))
    moe, back = (next(it), next(it)) if last else (moe_out, back_out)
    cut = half // 2

    def fetch(at, slot):
        for side, bufs in enumerate((mine, mate)):
            lanes = pl.ds(side * hidden, hidden)

            def copy(k, start):
                rows = pl.ds(pl.multiple_of(sc[min(k, total - 2)] * shard, shard), shard)
                src = bufs[k].at[pl.ds(start * 3, 3)]
                pltpu.make_async_copy(src, w.at[slot, :, rows, lanes], sem.at[slot]).start()

            for k in range(total - 2):
                copy(k, at)

            @pl.when(at < cut)
            def _():
                copy(total - 2, at)

            @pl.when(at >= cut)
            def _():
                copy(total - 1, at - cut)

    slot = lax.rem(step, 2)

    @pl.when(step == 0)
    def _():
        fetch(0, 0)
        if not first:
            pltpu.make_async_copy(moe_in, moe, sum_sem.at[0]).start()
            pltpu.make_async_copy(back_in, back, sum_sem.at[1]).start()
        else:
            moe[...] = jnp.zeros_like(moe)
            back[...] = jnp.zeros_like(back)

    @pl.when(step + 1 < half)
    def _():
        fetch(step + 1, 1 - slot)

    pltpu.make_async_copy(w.at[slot], w.at[slot], sem.at[slot]).wait()
    experts = [sc[total - 1 + side] + step + ROUTER_LANE for side in range(2)]
    lane = lax.broadcasted_iota(jnp.int32, (block, LANES), 1)
    for at in range(0, rows_total, block):
        rows = pl.ds(at, block)
        x = n2[rows, :]
        gate = mm(x, w[slot, 0])
        up = mm(x, w[slot, 1])
        grad = mm(cot[rows, :], w[slot, 2])
        table = wt[rows, :]
        sig = 1.0 / (1.0 + jnp.exp(-gate))
        silu = gate * sig
        act = silu * up
        dots = act * grad
        picked = jnp.zeros(table.shape, f32)
        for side, expert in enumerate(experts):
            cols = slice(side * hidden, side * hidden + hidden)
            weight = jnp.sum(jnp.where(lane == expert, table, 0.0), axis=1, keepdims=True)
            picked = picked + jnp.where(lane == expert, jnp.sum(dots[:, cols], axis=1, keepdims=True), 0.0)
            scaled[rows, cols] = (act[:, cols] * weight).astype(bf)
            g = grad[:, cols] * weight
            s = sig[:, cols]
            acts[rows, cols] = (g * up[:, cols] * s * (1.0 + gate[:, cols] * (1.0 - s))).astype(bf)
            acts[rows, slice((2 + side) * hidden, (3 + side) * hidden)] = (g * silu[:, cols]).astype(bf)

        @pl.when(step == 0)
        def _():
            pick[rows, :] = picked

        @pl.when(step > 0)
        def _():
            pick[rows, :] += picked

    if not first:

        @pl.when(step == 0)
        def _():
            pltpu.make_async_copy(moe_in, moe, sum_sem.at[0]).wait()
            pltpu.make_async_copy(back_in, back, sum_sem.at[1]).wait()

    for at in range(0, rows_total, block):
        rows = pl.ds(at, block)
        moe[rows, :] += mm_nt(scaled[rows, :], w[slot, 2])
        back[rows, :] += mm_nt(acts[rows, 0 : 2 * hidden], w[slot, 0]) + mm_nt(acts[rows, 2 * hidden : 4 * hidden], w[slot, 1])
    for at in range(0, width, block):
        cols = pl.ds(at, block)
        down = mm(cott[cols, :], scaled[...])
        gate_up = mm(n2t[cols, :], acts[...])
        for k, made in enumerate((gate_up[:, : 2 * hidden], gate_up[:, 2 * hidden :], down)):
            keep[0, k, cols, :] = made[:, :hidden].astype(bf)
            send[0, k, cols, :] = made[:, hidden:].astype(bf)

    if last:

        @pl.when(step == half - 1)
        def _():
            moe_out[...] = moe[...].astype(moe_out.dtype)
            back_out[...] = back[...].astype(back_out.dtype)


def experts(n2, n2t, cot, cott, wt, scalars, mine, mate, sums, last):
    rows, width = n2.shape
    shard, hidden = mine[0].shape[1:]
    half = mine[0].shape[0] // 3
    first = sums is None
    cfg = (shard, width, rows, hidden, half, first, last, len(mine))
    dense = [n2, n2t, cot, cott, wt]
    ins = dense + list(mine) + list(mate) + ([] if first else list(sums))
    kind = bf if last else f32
    grads = pl.BlockSpec((1, 3, width, hidden), lambda i, s: (i, 0, 0, 0))
    return call(
        functools.partial(experts_kernel, cfg),
        "experts",
        (half,),
        ins,
        [whole(a.shape) for a in dense] + [any_space()] * (len(ins) - len(dense)),
        [
            sds((rows, width), kind),
            sds((rows, width), kind),
            sds((half, 3, width, hidden), bf),
            sds((half, 3, width, hidden), bf),
            sds((rows, LANES), f32),
        ],
        [whole((rows, width)), whole((rows, width)), grads, grads, whole((rows, LANES))],
        [
            pltpu.VMEM((2, 3, width, 2 * hidden), bf),
            pltpu.VMEM((rows, 2 * hidden), bf),
            pltpu.VMEM((rows, 4 * hidden), bf),
            pltpu.SemaphoreType.DMA((2,)),
            pltpu.SemaphoreType.DMA((2,)),
        ]
        + [pltpu.VMEM((rows, width), f32)] * (2 if last else 0),
        36 * rows * width * hidden * half,
        scalars,
    )


def norm_back(values, gain, grad):
    scale = lax.rsqrt(jnp.mean(values * values, axis=-1, keepdims=True) + norm_eps)
    inner = jnp.mean(values * gain * grad, axis=-1, keepdims=True)
    passed = scale * gain * grad - values * (scale * scale * scale * inner)
    return passed, jnp.sum(grad * values * scale, axis=0, keepdims=True)


def unsettle_kernel(sc, back_a, back_b, pick_a, pick_b, wt, res, cot, extra, w_own, rg_out, low_t_out, dout_out, ll_out, gain_out, w, sem):
    step = pl.program_id(0)

    @pl.when(step == 0)
    def _():
        pltpu.make_async_copy(w_own, w, sem).start()
        pltpu.make_async_copy(w_own, w, sem).wait()
        gain_out[...] = jnp.zeros_like(gain_out)

    weights = wt[...]
    picked = pick_a[...] + pick_b[...]
    logit_low = (weights * (picked - jnp.sum(weights * picked, axis=-1, keepdims=True))).astype(bf)
    ll_out[...] = logit_low
    grad = back_a[...].astype(f32) + back_b[...].astype(f32) + mm(logit_low, extra[...])
    passed, gain = norm_back(res[...], extra[1:2, :].astype(f32), grad)
    gain_out[...] += gain
    total = cot[...].astype(f32) + passed
    rg_out[...] = total
    low = total.astype(bf)
    low_t_out[...] = low.T
    dout_out[...] = mm(low, lanes_of(w, 0, w.shape[0])).astype(bf)


def unsettle(back, picks, wt, res, cot, extra, w_own, core, block=256):
    rows, width = res.shape
    cols = w_own.shape[0] * LANES
    wide, thin = rows_of(block, width), rows_of(block, LANES)
    return call(
        unsettle_kernel,
        "unsettle",
        (rows // block,),
        [*back, *picks, wt, res, cot, extra, w_own],
        [wide, wide, thin, thin, thin, wide, wide, whole(extra.shape), any_space()],
        [sds((rows, width), f32), sds((width, rows), bf), sds((rows, cols), bf), sds((rows, LANES), bf), sds((1, width), f32)],
        [wide, pl.BlockSpec((width, block), lambda i, s: (0, i)), rows_of(block, cols), thin, whole((1, width))],
        [pltpu.VMEM(w_own.shape, bf), pltpu.SemaphoreType.DMA],
        2 * rows * width * cols,
        core,
    )


def lane_column(row, shape, lane_at):
    lane = lax.broadcasted_iota(jnp.int32, shape, 1)
    return jnp.where(lane == lane_at, jnp.broadcast_to(row, (shape[1], shape[0])).T, 0.0)


def output_grads_kernel(sc, low_t, mixed_a, mixed_b, n2t, ll, gain, out):
    prompt = mixed_a.shape[0]
    made = mm(low_t[:, 0:prompt], mixed_a[...]) + mm(low_t[:, prompt:], mixed_b[...])
    count = made.shape[1] // LANES
    for b in range(count):
        out[b] = made[:, b * LANES : (b + 1) * LANES].astype(bf)
    router = mm(n2t[...], ll[...])
    out[count] = (router + lane_column(gain[...], router.shape, 1)).astype(bf)
    for b in range(count + 1, out.shape[0]):
        out[b] = jnp.zeros_like(out[b])


def output_grads(low_t, mixed, n2t, ll, gain, core, block=256):
    width, rows = low_t.shape
    blocks = mixed[0].shape[1] // LANES + 2
    tall = pl.BlockSpec((block, rows), lambda i, s: (i, 0))
    return call(
        output_grads_kernel,
        "output_grads",
        (width // block,),
        [low_t, *mixed, n2t, ll, gain],
        [tall, *[whole(a.shape) for a in mixed], tall, whole(ll.shape), pl.BlockSpec((1, block), lambda i, s: (0, i))],
        [sds((blocks, width, LANES), bf)],
        [pl.BlockSpec((blocks, block, LANES), lambda i, s: (0, i, 0))],
        [],
        2 * rows * width * blocks * LANES,
        core,
    )[0]


def unproject_kernel(sc, tok, dq, dk, dkx, dv, dvx, cosine, sine, w_own, low_out, part_out, gain_out, w, low_scr, sem):
    step = pl.program_id(0)
    cols = low_out.shape[1]
    blocks = cols // LANES
    kvs = dk.shape[0]

    @pl.when(step == 0)
    def _():
        pltpu.make_async_copy(w_own, w, sem).start()
        pltpu.make_async_copy(w_own, w, sem).wait()
        gain_out[...] = jnp.zeros_like(gain_out)

    shared = jnp.where(step < pl.num_programs(0) // 2, 1.0, 0.0).astype(f32)
    at = dq.shape[1]
    low_out[:, 0:at] = dq[...]
    for grads, more, turn in ((dk, dkx, True), (dv, dvx, False)):
        for kv in range(0, kvs, 2):
            pair = jnp.concatenate([grads[kv] + more[kv] * shared, grads[kv + 1] + more[kv + 1] * shared], axis=1)
            if turn:
                pair = rope(pair, cosine[...], -sine[...])
            low_out[:, at : at + LANES] = pair.astype(bf)
            at += LANES
    part = mm_nt(low_out[...], lanes_of(w, 0, blocks))
    part_out[...] = part
    x = tok[...].astype(f32)
    scale = lax.rsqrt(jnp.mean(x * x, axis=-1, keepdims=True) + norm_eps)
    gain_out[...] += jnp.sum(part * x * scale, axis=0, keepdims=True)


def unproject(tokens, dq, dk, dkx, dv, dvx, cosine, sine, w_own, core, block=256):
    rows, width = tokens.shape
    kvs, prompt = dkx.shape[:2]
    cols = dq.shape[1] + 2 * kvs * HEAD_DIM
    halves = prompt // block
    own = pl.BlockSpec((kvs, block, HEAD_DIM), lambda i, s: (0, i, 0))
    other = pl.BlockSpec((kvs, block, HEAD_DIM), lambda i, s: (0, jnp.minimum(i, halves - 1), 0))
    return call(
        unproject_kernel,
        "unproject",
        (rows // block,),
        [tokens, dq, dk, dkx, dv, dvx, cosine, sine, w_own],
        [rows_of(block, width), rows_of(block, dq.shape[1]), own, other, own, other, rows_of(block, LANES), rows_of(block, LANES), any_space()],
        [sds((rows, cols), bf), sds((rows, width), f32), sds((1, width), f32)],
        [rows_of(block, cols), rows_of(block, width), whole((1, width))],
        [pltpu.VMEM(w_own.shape, bf), pltpu.VMEM((8, LANES), f32), pltpu.SemaphoreType.DMA],
        2 * rows * width * cols,
        core,
    )


def project_grads_kernel(sc, nt, low, gain, out):
    made = mm(nt[...], low[...])
    count = made.shape[1] // LANES
    for b in range(count):
        out[b] = made[:, b * LANES : (b + 1) * LANES].astype(bf)
    out[count] = lane_column(gain[...], (made.shape[0], LANES), 0).astype(bf)
    for b in range(count + 1, out.shape[0]):
        out[b] = jnp.zeros_like(out[b])


def project_grads(nt, low, gain, core, block=256):
    width, rows = nt.shape
    blocks = low.shape[1] // LANES + 2
    return call(
        project_grads_kernel,
        "project_grads",
        (width // block,),
        [nt, low, gain],
        [pl.BlockSpec((block, rows), lambda i, s: (i, 0)), whole(low.shape), pl.BlockSpec((1, block), lambda i, s: (0, i))],
        [sds((blocks, width, LANES), bf)],
        [pl.BlockSpec((blocks, block, LANES), lambda i, s: (0, i, 0))],
        [],
        2 * rows * width * blocks * LANES,
        core,
    )[0]


def finish_kernel(sc, tok, part, far, extra, rg, w_mine, w_theirs, out, w, sem):
    @pl.when(pl.program_id(0) == 0)
    def _():
        load_halves(sc, w_mine, w_theirs, 0, w, sem)
        pltpu.make_async_copy(w, w, sem).wait()

    grad = part[...] + mm_nt(far[...], lanes_of(w, 0, w.shape[0]))
    passed, _ = norm_back(tok[...].astype(f32), extra[0:1, :].astype(f32), grad)
    out[...] = rg[...] + passed


def finish(tokens, part, far, extra, rg, w_mine, w_theirs, core, block=256):
    rows, width = tokens.shape
    wide = rows_of(block, width)
    return call(
        finish_kernel,
        "finish",
        (rows // block,),
        [tokens, part, far, extra, rg, w_mine, w_theirs],
        [wide, wide, rows_of(block, far.shape[1]), whole(extra.shape), wide, any_space(), any_space()],
        [sds((rows, width), f32)],
        [wide],
        [pltpu.VMEM((2 * w_mine.shape[0], width, LANES), bf), pltpu.SemaphoreType.DMA],
        2 * rows * width * far.shape[1],
        core,
    )[0]


def lane_blocks(values):
    rows, cols = values.shape
    return values.reshape(rows, cols // LANES, LANES).transpose(1, 0, 2)


def unblock(values):
    return values.transpose(1, 0, 2).reshape(values.shape[1], -1)


def body(
    tokens,
    routes,
    cotangent,
    norm_one,
    w_query,
    key_weight,
    value_weight,
    w_output,
    norm_two,
    w_router,
    w_gate,
    w_up,
    w_down,
):
    count = lax.axis_size("dp")
    core = lax.axis_index("ctx")
    place = ring_place(lax.axis_index("dp"), count)
    rows, width = tokens.shape[2:]
    prompt = PROMPT_TOKENS // lax.axis_size("ctx")
    heads = w_query.shape[1] // HEAD_DIM
    kvs = key_weight.shape[1] // HEAD_DIM
    shard, hidden = w_gate.shape[1:]
    chunk = 4
    half = chunk // 2
    core_only = jnp.stack([core, core]).astype(jnp.int32)
    sources = ring_sources(place, count)

    def scalars(*more):
        return jnp.stack([*sources, *more]).astype(jnp.int32)

    with_cores = scalars(core, 1 - core)
    tok = tokens.reshape(rows, width)
    cot = cotangent.reshape(rows, width)
    ids = routes.reshape(rows, TOPK)

    extra_shard = jnp.zeros((shard, LANES), bf)
    extra_shard = extra_shard.at[:, 0].set(norm_one).at[:, 1].set(norm_two)
    extra_shard = extra_shard.at[:, ROUTER_LANE : ROUTER_LANE + EXPERTS].set(w_router)
    packed = lane_blocks(jnp.concatenate([w_query, key_weight, value_weight, extra_shard, jnp.zeros_like(extra_shard)], axis=1))
    first_half = packed.shape[0] // 2
    first_own = ring_gather(take(packed, core * first_half, first_half), count)
    first_mate = [swap(b, "ctx") for b in first_own]
    packed_out = lane_blocks(w_output)
    out_half = packed_out.shape[0] // 2
    out_own = ring_gather(take(packed_out, core * out_half, out_half), count)
    out_mate = [swap(b, "ctx") for b in out_own]

    stacked = jnp.stack([w_gate, w_up, w_down], axis=1)
    expert_bufs = []
    for base in range(0, EXPERTS, chunk):
        mine = take(stacked, base + core * half, half).reshape(half * 3, shard, hidden)
        own = ring_gather(mine, count)
        expert_bufs.append((own, [swap(b, "ctx") for b in own]))

    offsets = jnp.arange(rows, dtype=jnp.int32)
    positions = jnp.where(offsets < prompt, core * prompt + offsets, PROMPT_TOKENS + offsets - prompt)
    half_dim = HEAD_DIM // 2
    inverse = rope_base ** (-2.0 * jnp.arange(half_dim).astype(f32) / HEAD_DIM)
    angles = positions.astype(f32)[:, None] * inverse
    cosine = jnp.tile(jnp.cos(angles), (1, LANES // half_dim))
    sine = jnp.sin(angles)
    sine = jnp.tile(jnp.concatenate([-sine, sine], axis=1), (1, LANES // HEAD_DIM))

    w_first, extra, q, k, v, n1t = project(tok, cosine, sine, with_cores, first_own, first_mate, heads, kvs)
    other_k, other_v = swap(k[:, :prompt], "ctx"), swap(v[:, :prompt], "ctx")
    w_out = assemble(with_cores, out_own, out_mate, width)
    out_far_mine = swap(take(w_out, core * out_half, out_half), "tp")
    out_far_theirs = swap(out_far_mine, "ctx")
    mixed_b, lse_b = attend(q, k, v, other_k, other_v, core_only, 1)
    far_b = swap(mixed_b, "tp")
    mixed_a, lse_a = attend(q, k, v, other_k, other_v, core_only, 0)
    far_a = swap(mixed_a, "tp")
    mixed, lse = (mixed_a, mixed_b), (lse_a, lse_b)
    first_count = (heads + 2 * kvs) // 2
    first_part = first_count // 2
    w_first = w_first[:first_count]
    first_far_mine = swap(take(w_first, core * first_part, first_part), "tp")
    first_far_theirs = swap(first_far_mine, "ctx")

    res, n2, n2t, wt = settle(tok, ids, mixed, (far_a, far_b), extra, w_out, out_far_mine, out_far_theirs, core_only)
    cott = cot.T
    sums, picks, shares = None, [], []

    def reduce_chunk(keep, send):
        got = swap(send, "ctx")

        def piece(rank):
            part = lambda a: lax.dynamic_slice_in_dim(a, rank * shard, shard, 2).reshape(half * 3, shard, hidden).astype(f32)
            return part(keep) + part(got)

        return ring_scatter(piece, place, count)

    for index, (own, mate) in enumerate(expert_bufs):
        base = index * chunk
        sc = scalars(base + core * half, base + (1 - core) * half)
        last = index == len(expert_bufs) - 1
        *sums, keep, send, pick = experts(n2, n2t, cot, cott, wt, sc, own, mate, sums, last)
        picks.append(pick)
        shares.append(reduce_chunk(keep, send))
    moe_low, back_low = sums
    pick = functools.reduce(jnp.add, picks)
    back_far = swap(back_low, "tp")
    pick_far = swap(pick, "tp")
    moe_far = swap(moe_low, "tp")
    result = (res + (moe_low.astype(f32) + moe_far.astype(f32))).astype(bf).reshape(tokens.shape)

    rg, low_t, dout, ll, gain_two = unsettle((back_low, back_far), (pick, pick_far), wt, res, cot, extra, w_out, core_only)
    second = output_grads(low_t, mixed, n2t, ll, gain_two, core_only)
    dq, dk, dko, dv, dvo = attend_back(q, k, v, other_k, other_v, dout, mixed, lse, cosine, sine, core_only)
    dkx, dvx = swap(dko, "ctx"), swap(dvo, "ctx")
    low, part, gain_one = unproject(tok, dq, dk, dkx, dv, dvx, cosine, sine, w_first, core_only)
    far = swap(low, "tp")
    first = project_grads(n1t, low, gain_one, core_only)
    token_grad = finish(tok, part, far, extra, rg, first_far_mine, first_far_theirs, core_only).reshape(tokens.shape)

    def reduce_blocks(grads):
        size = grads.shape[0] // 2
        keep = take(grads, core * size, size)
        got = swap(take(grads, (1 - core) * size, size), "ctx")

        def piece(rank):
            part = lambda a: lax.dynamic_slice_in_dim(a, rank * shard, shard, 1).astype(f32)
            return part(keep) + part(got)

        mine = ring_scatter(piece, place, count)
        theirs = swap(mine, "ctx")
        return jnp.concatenate([jnp.where(core == 0, mine, theirs), jnp.where(core == 0, theirs, mine)], axis=0)

    second = reduce_blocks(second)
    first = reduce_blocks(first)
    q_blocks, kv_blocks = heads // 2, kvs // 2
    grad_query = unblock(first[:q_blocks])
    grad_key = unblock(first[q_blocks : q_blocks + kv_blocks])
    grad_value = unblock(first[q_blocks + kv_blocks : q_blocks + 2 * kv_blocks])
    gain_part = first[q_blocks + 2 * kv_blocks][:, 0]
    grad_norm_one = gain_part + swap(gain_part, "tp")
    grad_output = unblock(second[:q_blocks])
    grad_norm_two = second[q_blocks][:, 1]
    grad_router = second[q_blocks][:, ROUTER_LANE : ROUTER_LANE + EXPERTS]

    parts = []
    for mine in shares:
        theirs = swap(mine, "ctx")
        parts += [jnp.where(core == 0, mine, theirs), jnp.where(core == 0, theirs, mine)]
    owned = jnp.concatenate(parts, axis=0).reshape(EXPERTS, 3, shard, hidden)
    return (
        result,
        token_grad,
        grad_norm_one,
        grad_query,
        grad_key,
        grad_value,
        grad_output,
        grad_norm_two,
        grad_router,
        owned[:, 0],
        owned[:, 1],
        owned[:, 2],
    )


def solution(mesh):
    slab = P("dp", "ctx", None, None)
    split, rows_only, expert = P("dp", "tp"), P("dp"), P(None, "dp", "tp")
    return jax.shard_map(
        body,
        mesh=mesh,
        in_specs=(slab, slab, slab, rows_only, split, split, split, split, rows_only, P("dp", None), expert, expert, expert),
        out_specs=(slab, slab, rows_only, split, split, split, split, rows_only, P("dp", None), expert, expert, expert),
        check_vma=False,
    )
```

time: 5330 us -> 1150 us (0.22)
  waiting for transfers between devices: 2420 us -> 430 us
  other arithmetic: 1250 us -> 78.6 us
  matrix products: 796 us -> 0 us
  local copies, waits for them, and re-layouts: 634 us -> 69.8 us
  Pallas kernels: 0 us -> 436 us
  blocking collectives: 170 us -> 0 us
  starting transfers between devices: 0.97 us -> 122 us
    reduce_scatter x9 -> x0, waiting for transfers between devices: 1530 us -> none  [the longest x1 408 us: body(): lax.psum_scatter(gate_grads, 'dp', scatter_dimension=1, tiled=True)]
    scatter-add x48 -> x0, other arithmetic: 1080 us -> none  [the longest x16 500 us: expert_backward(): table_grad = table_grad.at[slot_ids, expert_id].add(weight_grad)]
    dot_general x202 -> x0, matrix products: 794 us -> none  [the longest x16 64.6 us: expert_backward(): jnp.dot(branch_low, down_mat, preferred_element_type=jnp.float32)]
    psum x4 -> x0, waiting for transfers between devices: 553 us -> none  [the longest x1 289 us: body(): moe_total = lax.psum(moe_part, 'tp')]
    pallas_call x0 -> x15, Pallas kernels: none -> 436 us  [call(): pl.pallas_call(kernel, out_shape=tuple(outs), grid_spec=pltpu.PrefetchSca...]
    ppermute x0 -> x177, waiting for transfers between devices: none -> 430 us  [the longest x48 183 us: ring_scatter(): f, g = (lax.ppermute(f, 'dp', ahead), lax.ppermute(g, 'dp', back))]
    gather x56 -> x0, local copies, waits for them, and re-layouts: 375 us -> none  [the longest x16 135 us: expert_backward(): slot_grad = out_grad[slot_ids]]
    all_gather x5 -> x0, waiting for transfers between devices: 267 us -> none  [the longest x1 177 us: body(): lax.all_gather(w_down, 'dp', axis=1, tiled=True)]
  transfers between devices with their start and end apart: 19 -> 177, of which waited for: 15 -> 58; matrix products, arithmetic and copies ran while one was open for 8% -> 12% of each run, Pallas kernels for 0% -> 34%
where the time goes in v1:
time: 1150 us; the launch traced here: 1140 us
  Pallas kernels  436 us (38%)
  waiting for transfers between devices  430 us (37%)
  starting transfers between devices  122 us (11%)
  other arithmetic  78.6 us (7%)
  local copies, waits for them, and re-layouts  69.8 us (6%)
    pallas_call x15, Pallas kernels, call(): pl.pallas_call(kernel, out_shape=tuple(outs), grid_spec=pltpu.PrefetchSca...  436 us
    ppermute x48, waiting for transfers between devices, ring_scatter(): f, g = (lax.ppermute(f, 'dp', ahead), lax.ppermute(g, 'dp', back))  183 us
    ppermute x48, waiting for transfers between devices, ring_gather(): f, g = (lax.ppermute(f, 'dp', ahead), lax.ppermute(g, 'dp', back))  128 us
    ppermute x81, waiting for transfers between devices, swap(): return lax.ppermute(values, axis, [(0, 1), (1, 0)])  119 us
    ppermute x48, starting transfers between devices, ring_gather(): f, g = (lax.ppermute(f, 'dp', ahead), lax.ppermute(g, 'dp', back))  53.9 us
    ppermute x48, starting transfers between devices, ring_scatter(): f, g = (lax.ppermute(f, 'dp', ahead), lax.ppermute(g, 'dp', back))  43.1 us
    add x6, other arithmetic, piece(): return part(keep) + part(got)  28.5 us
    ppermute x81, starting transfers between devices, swap(): return lax.ppermute(values, axis, [(0, 1), (1, 0)])  25.1 us
  transfers between devices with their start and end apart: 177, of which 58 were waited for; matrix products, arithmetic and copies ran while one was open for 12% of the time, Pallas kernels for 34%

profile of v1, /device:TPU:0, one launch (start us, length us, event | category | flops | bytes accessed | tf_op | source)
XLA Modules:
  0.0 1138.9 jit_solution(2217662067235426328)
XLA Ops:
  18.3 6.3 collective-permute-done.23.refs_3_
  52.2 8.7 collective-permute-done.91.refs_6_
  63.6 10.0 collective-permute-done.74.refs_6_
  76.2 10.1 collective-permute-done.57.refs_6_
  89.0 15.8 %collective-permute-done.4.refs_5_ = bf16[6,192,128]{2,1,0:T(8,128)(2,1)S(1)} collective-permute-done((bf16[6,192,128]{2,1,0:T(8,128)(2,1)}, bf16[6,192,128]{2,1,0:T(8,128)(2,1)S(1)}, u32[]{:S(2)}, u32[]{:S(2)}) %collective-permute-start.4) | collective-permute-done | bytes 294944 | tf_op jit(solution)/shard_map/ppermute | solution.py:90
  115.9 13.0 %collective-permute-done.93.refs_8_ = bf16[6,192,256]{2,1,0:T(8,128)(2,1)} collective-permute-done((bf16[6,192,256]{2,1,0:T(8,128)(2,1)S(1)}, bf16[6,192,256]{2,1,0:T(8,128)(2,1)}, u32[]{:S(2)}, u32[]{:S(2)}) %collective-permute-start.93) | collective-permute-done | bytes 589856 | tf_op jit(solution)/shard_map/ppermute | solution.py:90
  131.4 10.0 collective-permute-done.76.refs_8_
  144.0 10.1 collective-permute-done.59.refs_8_
  160.3 6.5 collective-permute-done.42.refs_8_
  170.3 12.9 %project.1 = (bf16[12,1536,128]{2,1,0:T(8,128)(2,1)}, bf16[128,1536]{1,0:T(8,128)(2,1)}, bf16[12,1024,64]{2,1,0:T(8,128)(2,1)}, bf16[4,1024,64]{2,1,0:T(8,128)(2...) custom-call(s32[10]{0:T(128)} %stack.129.sc, bf16[1024,1536]{1,0:T(8,128)(2,1)} %bitcast.246, ...), custom_call_target="tpu_custom_call" | custom-call | flops 4831838208 | bytes 19791872 | tf_op jit(solution)/shard_map/project/pallas_call | solution.py:48
  186.6 73.2 %assemble.1.w_own = bf16[6,1536,128]{2,1,0:T(8,128)(2,1)} custom-call(s32[10]{0:T(128)} %stack.129.sc, bf16[3,192,128]{2,1,0:T(8,128)(2,1)} %bitcast.260, bf16[3,192,128]{2,1,0:T(8,128)(2,1)} %copy-done.46, bf16[3,192,128]{2,1,0:T(8,128)(2,1)} %copy-done.47, bf16[3,192,128]{2,1,0:T(8,128)(2,1)} %copy-done.49, ...), custom_call_target="tpu_custom_call" | custom-call | bytes 4718592 | tf_op jit(solution)/shard_map/assemble/pallas_call | solution.py:48
  266.5 9.0 collective-permute-done.78.refs_10_
  278.6 21.5 %attend.3 = (bf16[512,768]{1,0:T(8,128)(2,1)}, f32[6,2,512]{2,1,0:T(2,128)}) custom-call(s32[2]{0:T(128)} %pad_add_fusion.sc, bf16[12,1024,64]{2,1,0:T(8,128)(2,1)} %get-tuple-element.95.q, bf16[4,1024,64]{2,1,0:T(8,128)(2,1)} %get-tuple-element.96.k0.k1, bf16[4,1024,64]{2,1,0:T(8,128)(2,1)} %get-tuple-element.96.k0.k1, bf16[4,512,64]{2,1,0:T(8,128)(2,1)} %copy-done.107, ...), custom_call_target="tpu_custom_call" | custom-call | flops 6442450944 | bytes 5529600 | tf_op jit(solution)/shard_map/attend/pallas_call | solution.py:48
  304.9 16.9 %attend.2 = (bf16[512,768]{1,0:T(8,128)(2,1)}, f32[6,2,512]{2,1,0:T(2,128)}) custom-call(s32[2]{0:T(128)} %pad_add_fusion.sc, bf16[12,1024,64]{2,1,0:T(8,128)(2,1)} %get-tuple-element.95.q, bf16[4,1024,64]{2,1,0:T(8,128)(2,1)} %get-tuple-element.96.k0.k1, bf16[4,1024,64]{2,1,0:T(8,128)(2,1)} %get-tuple-element.96.k0.k1, bf16[4,512,64]{2,1,0:T(8,128)(2,1)} %copy-done.107, ...), custom_call_target="tpu_custom_call" | custom-call | flops 6442450944 | bytes 5529600 | tf_op jit(solution)/shard_map/attend/pallas_call | solution.py:48
  329.8 5.8 collective-permute-done.98.refs_13_
  337.7 6.2 collective-permute-done.81.refs_13_
  359.5 15.9 %settle.1 = (f32[1024,1536]{1,0:T(8,128)}, bf16[1024,1536]{1,0:T(8,128)(2,1)}, bf16[1536,1024]{1,0:T(8,128)(2,1)}, f32[1024,128]{1,0:T(8,128)}) custom-call(s32[2]{0:T(128)} %pad_add_fusion.sc, bf16[1024,1536]{1,0:T(8,128)(2,1)} %bitcast.247, s32[1024,8]{1,0:T(8,128)} %bitcast.278, bf16[512,768]{1,0:T(8,128)(2,1)} %get-tuple-element.98.own_a.mixed_a, ...), custom_call_target="tpu_custom_call" | custom-call | flops 4831838208 | bytes 24543232 | tf_op jit(solution)/shard_map/settle/pallas_call | solution.py:48
  376.9 53.3 %experts.4 = (f32[1024,1536]{1,0:T(8,128)}, f32[1024,1536]{1,0:T(8,128)}, bf16[2,3,1536,256]{3,2,1,0:T(8,128)(2,1)}, bf16[2,3,1536,256]{3,2,1,0:T(8,128)(2,1)}, f32[1024,128]{1,0:T(8,128)}) custom-call(s32[10]{0:T(128)} %stack.145.sc, bf16[1024,1536]{1,0:T(8,128)(2,1)} %get-tuple-element.102.refs_0_, bf16[1536,1024]{1,0:T(8,128)(2,1)} %get-tuple-element.103.refs_1_.n2t, ...), custom_call_target="tpu_custom_call" | custom-call | flops 28991029248 | bytes 45088768 | tf_op jit(solution)/shard_map/experts/pallas_call | solution.py:48
  433.6 42.9 %experts.5 = (f32[1024,1536]{1,0:T(8,128)}, f32[1024,1536]{1,0:T(8,128)}, bf16[2,3,1536,256]{3,2,1,0:T(8,128)(2,1)}, bf16[2,3,1536,256]{3,2,1,0:T(8,128)(2,1)}, f32[1024,128]{1,0:T(8,128)}) custom-call(s32[10]{0:T(128)} %stack.142.sc, bf16[1024,1536]{1,0:T(8,128)(2,1)} %get-tuple-element.102.refs_0_, bf16[1536,1024]{1,0:T(8,128)(2,1)} %get-tuple-element.103.refs_1_.n2t, ...), custom_call_target="tpu_custom_call" | custom-call | flops 28991029248 | bytes 57671680 | tf_op jit(solution)/shard_map/experts/pallas_call | solution.py:48
  478.5 43.0 %experts.6 = (f32[1024,1536]{1,0:T(8,128)}, f32[1024,1536]{1,0:T(8,128)}, bf16[2,3,1536,256]{3,2,1,0:T(8,128)(2,1)}, bf16[2,3,1536,256]{3,2,1,0:T(8,128)(2,1)}, f32[1024,128]{1,0:T(8,128)}) custom-call(s32[10]{0:T(128)} %stack.139.sc, bf16[1024,1536]{1,0:T(8,128)(2,1)} %get-tuple-element.102.refs_0_, bf16[1536,1024]{1,0:T(8,128)(2,1)} %get-tuple-element.103.refs_1_.n2t, ...), custom_call_target="tpu_custom_call" | custom-call | flops 28991029248 | bytes 57671680 | tf_op jit(solution)/shard_map/experts/pallas_call | solution.py:48
  523.0 46.3 %experts.7 = (bf16[1024,1536]{1,0:T(8,128)(2,1)}, bf16[1024,1536]{1,0:T(8,128)(2,1)}, bf16[2,3,1536,256]{3,2,1,0:T(8,128)(2,1)}, bf16[2,3,1536,256]{3,2,1,0:T(8,128)(2,1)}, f32[1024,128]{1,0:T(8,128)}) custom-call(s32[10]{0:T(128)} %stack.132.sc, bf16[1024,1536]{1,0:T(8,128)(2,1)} %get-tuple-element.102.refs_0_, ...), custom_call_target="tpu_custom_call" | custom-call | flops 28991029248 | bytes 51380224 | tf_op jit(solution)/shard_map/experts/pallas_call | solution.py:48
  580.7 71.1 %collective-permute-done.110.pick_b = f32[1024,128]{1,0:T(8,128)} collective-permute-done((f32[1024,128]{1,0:T(8,128)}, f32[1024,128]{1,0:T(8,128)}, u32[]{:S(2)}, u32[]{:S(2)}) %collective-permute-start.110) | collective-permute-done | bytes 524320 | tf_op jit(solution)/shard_map/ppermute | solution.py:126
  653.4 16.7 %unsettle.1 = (f32[1024,1536]{1,0:T(8,128)}, bf16[1536,1024]{1,0:T(8,128)(2,1)}, bf16[1024,768]{1,0:T(8,128)(2,1)}, bf16[1024,128]{1,0:T(8,128)(2,1)}, f32[1,1536]{1,0:T(1,128)}) custom-call(s32[2]{0:T(128)} %pad_add_fusion.sc, bf16[1024,1536]{1,0:T(8,128)(2,1)} %get-tuple-element.112.back_a, bf16[1024,1536]{1,0:T(8,128)(2,1)} %collective-permute-done.109.back_b, ...), custom_call_target="tpu_custom_call" | custom-call | flops 2415919104 | bytes 31332352 | tf_op jit(solution)/shard_map/unsettle/pallas_call | solution.py:48
  670.1 45.6 %attend_back.1 = (bf16[1024,768]{1,0:T(8,128)(2,1)}, f32[4,1024,64]{2,1,0:T(8,128)}, f32[4,512,64]{2,1,0:T(8,128)}, f32[4,1024,64]{2,1,0:T(8,128)}, f32[4,512,64]{2,1,0:T(8,128)}) custom-call(s32[2]{0:T(128)} %pad_add_fusion.sc, bf16[12,1024,64]{2,1,0:T(8,128)(2,1)} %get-tuple-element.95.q, bf16[4,1024,64]{2,1,0:T(8,128)(2,1)} %get-tuple-element.96.k0.k1, ...), custom_call_target="tpu_custom_call" | custom-call | flops 32212254720 | bytes 13680640 | tf_op jit(solution)/shard_map/attend_back/pallas_call | solution.py:48
  720.3 40.5 %collective-permute-done.108 = bf16[1024,1536]{1,0:T(8,128)(2,1)} collective-permute-done((bf16[1024,1536]{1,0:T(8,128)(2,1)S(1)}, bf16[1024,1536]{1,0:T(8,128)(2,1)}, u32[]{:S(2)}, u32[]{:S(2)}) %collective-permute-start.108) | collective-permute-done | bytes 3145760 | tf_op jit(solution)/shard_map/ppermute | solution.py:126
  760.8 6.7 fusion
  768.1 9.5 output_grads.1
  784.4 12.8 %unproject.1 = (bf16[1024,1280]{1,0:T(8,128)(2,1)}, f32[1024,1536]{1,0:T(8,128)}, f32[1,1536]{1,0:T(1,128)}) custom-call(s32[2]{0:T(128)} %pad_add_fusion.sc, bf16[1024,1536]{1,0:T(8,128)(2,1)} %bitcast.248, bf16[1024,768]{1,0:T(8,128)(2,1)} %get-tuple-element.120.dq, f32[4,1024,64]{2,1,0:T(8,128)} %get-tuple-element.121.dk, f32[4,512,64]{2,1,0:T(8,128)} %copy.83.dkx, ...), custom_call_target="tpu_custom_call" | custom-call | flops 4026531840 | bytes 21764096 | tf_op jit(solution)/shard_map/unproject/pallas_call | solution.py:48
  797.2 9.7 project_grads.1
  810.2 5.5 convert_add_fusion.3
  818.1 6.4 convert_add_fusion.10
  826.5 6.6 convert_add_fusion.17
  839.2 7.0 convert_add_fusion.24
  883.7 14.8 %collective-permute-done.130 = bf16[4,192,128]{2,1,0:T(8,128)(2,1)S(1)} collective-permute-done((bf16[4,192,128]{2,1,0:T(8,128)(2,1)S(1)}, bf16[4,192,128]{2,1,0:T(8,128)(2,1)S(1)}, u32[]{:S(2)}, u32[]{:S(2)}) %collective-permute-start.130) | collective-permute-done | bytes 196640 | tf_op jit(solution)/shard_map/ppermute | solution.py:121
  902.5 12.2 %collective-permute-done.133 = bf16[4,192,128]{2,1,0:T(8,128)(2,1)S(1)} collective-permute-done((bf16[4,192,128]{2,1,0:T(8,128)(2,1)S(1)}, bf16[4,192,128]{2,1,0:T(8,128)(2,1)S(1)}, u32[]{:S(2)}, u32[]{:S(2)}) %collective-permute-start.133) | collective-permute-done | bytes 196640 | tf_op jit(solution)/shard_map/ppermute | solution.py:121
  918.8 12.2 %collective-permute-done.159 = bf16[6,192,256]{2,1,0:T(8,128)(2,1)S(1)} collective-permute-done((bf16[6,192,256]{2,1,0:T(8,128)(2,1)S(1)}, bf16[6,192,256]{2,1,0:T(8,128)(2,1)S(1)}, u32[]{:S(2)}, u32[]{:S(2)}) %collective-permute-start.159) | collective-permute-done | bytes 589856 | tf_op jit(solution)/shard_map/ppermute | solution.py:121
  933.5 8.1 collective-permute-done.149
  943.2 6.2 collective-permute-done.134
  954.5 11.0 collective-permute-done.143
  975.9 9.1 collective-permute-done.117
  1004.1 8.1 collective-permute-done.154
  1019.2 5.7 collective-permute-done.144
  1031.8 15.3 %finish.1 = f32[1024,1536]{1,0:T(8,128)} custom-call(s32[2]{0:T(128)} %pad_add_fusion.sc, bf16[1024,1536]{1,0:T(8,128)(2,1)} %bitcast.249, f32[1024,1536]{1,0:T(8,128)} %get-tuple-element.126.part, bf16[1024,1280]{1,0:T(8,128)(2,1)} %collective-permute-done.113.far, bf16[128,1536]{1,0:T(8,128)(2,1)} %get-tuple-element.100.extra, ...), custom_call_target="tpu_custom_call" | custom-call | flops 4026531840 | bytes 28966912 | tf_op jit(solution)/shard_map/finish/pallas_call | solution.py:48
  1047.0 11.3 collective-permute-done.119
  1065.2 9.6 collective-permute-done.141
  1078.6 27.0 %collective-permute-done.122 = bf16[6,192,128]{2,1,0:T(8,128)(2,1)S(1)} collective-permute-done((bf16[6,192,128]{2,1,0:T(8,128)(2,1)S(1)}, bf16[6,192,128]{2,1,0:T(8,128)(2,1)S(1)}, u32[]{:S(2)}, u32[]{:S(2)}) %collective-permute-start.122) | collective-permute-done | bytes 294944 | tf_op jit(solution)/shard_map/ppermute | solution.py:121
  1109.1 7.2 collective-permute-done.123
  1120.3 7.1 collective-permute-done.124
  (758 shorter events, 295.4 us)
Async XLA Ops:
  74.2 31.2 %collective-permute-start.40 = (bf16[6,192,256]{2,1,0:T(8,128)(2,1)S(1)}, bf16[6,192,256]{2,1,0:T(8,128)(2,1)S(1)}, u32[]{:S(2)}, u32[]{:S(2)}) collective-permute-start(bf16[6,192,256]{2,1,0:T(8,128)(2,1)S(1)} %bitcast.261), channel_id=1, source_target_pairs={{0,8},{8,16},{16,24},{24,28},{28,20},{20,12},{12,4},{4,0},{1,9},{9... | collective-permute-start | bytes 1769480 | tf_op jit(solution)/shard_map/ppermute | solution.py:90
  74.5 31.3 %collective-permute-start.41 = (bf16[6,192,256]{2,1,0:T(8,128)(2,1)S(1)}, bf16[6,192,256]{2,1,0:T(8,128)(2,1)S(1)}, u32[]{:S(2)}, u32[]{:S(2)}) collective-permute-start(bf16[6,192,256]{2,1,0:T(8,128)(2,1)S(1)} %bitcast.262), channel_id=1, source_target_pairs={{8,0},{16,8},{24,16},{28,24},{20,28},{12,20},{4,12},{0,4},{9,1},{1... | collective-permute-start | bytes 1769480 | tf_op jit(solution)/shard_map/ppermute | solution.py:90
  159.7 100.5 %collective-permute-start.95 = (bf16[6,192,256]{2,1,0:T(8,128)(2,1)}, bf16[6,192,256]{2,1,0:T(8,128)(2,1)}, u32[]{:S(2)}, u32[]{:S(2)}) collective-permute-start(bf16[6,192,256]{2,1,0:T(8,128)(2,1)} %collective-permute-done.93.refs_8_), channel_id=1, source_target_pairs={{0,8},{8,16},{16,24},{24,28},{28,20},{20,12},{12,4},{4,0},{1,9},{9... | collective-permute-start | bytes 1769480 | tf_op jit(solution)/shard_map/ppermute | solution.py:90
  166.8 95.2 %collective-permute-start.102 = (bf16[6,192,256]{2,1,0:T(8,128)(2,1)}, bf16[6,192,256]{2,1,0:T(8,128)(2,1)S(1)}, u32[]{:S(2)}, u32[]{:S(2)}) collective-permute-start(bf16[6,192,256]{2,1,0:T(8,128)(2,1)} %collective-permute-done.93.refs_8_), channel_id=1, source_target_pairs={{0,2},{2,0},{1,3},{3,1},{4,6},{6,4},{5,7},{7,5},{8,10},{10,8},{9,1... | collective-permute-start | bytes 1769480 | tf_op jit(solution)/shard_map/ppermute | solution.py:126
  168.2 92.1 %collective-permute-start.96 = (bf16[6,192,256]{2,1,0:T(8,128)(2,1)}, bf16[6,192,256]{2,1,0:T(8,128)(2,1)}, u32[]{:S(2)}, u32[]{:S(2)}) collective-permute-start(bf16[6,192,256]{2,1,0:T(8,128)(2,1)} %collective-permute-done.94.refs_9_), channel_id=1, source_target_pairs={{8,0},{16,8},{24,16},{28,24},{20,28},{12,20},{4,12},{0,4},{9,1},{1... | collective-permute-start | bytes 1769480 | tf_op jit(solution)/shard_map/ppermute | solution.py:90
  184.5 79.9 %collective-permute-start.103 = (bf16[6,192,256]{2,1,0:T(8,128)(2,1)}, bf16[6,192,256]{2,1,0:T(8,128)(2,1)S(1)}, u32[]{:S(2)}, u32[]{:S(2)}) collective-permute-start(bf16[6,192,256]{2,1,0:T(8,128)(2,1)} %collective-permute-done.94.refs_9_), channel_id=1, source_target_pairs={{0,2},{2,0},{1,3},{3,1},{4,6},{6,4},{5,7},{7,5},{8,10},{10,8},{9,1... | collective-permute-start | bytes 1769480 | tf_op jit(solution)/shard_map/ppermute | solution.py:126
  186.4 73.4 %collective-permute-start.18 = (bf16[4,512,64]{2,1,0:T(8,128)(2,1)S(1)}, bf16[4,512,64]{2,1,0:T(8,128)(2,1)S(1)}, u32[]{:S(2)}, u32[]{:S(2)}) collective-permute-start(bf16[4,512,64]{2,1,0:T(8,128)(2,1)S(1)} %slice.319), channel_id=1, source_target_pairs={{0,2},{2,0},{1,3},{3,1},{4,6},{6,4},{5,7},{7,5},{8,10},{10,8},{9,1... | collective-permute-start | bytes 786440 | tf_op jit(solution)/shard_map/ppermute | solution.py:126
  264.4 39.9 %collective-permute-start.38 = (bf16[3,1536,128]{2,1,0:T(8,128)(2,1)S(1)}, bf16[3,1536,128]{2,1,0:T(8,128)(2,1)}, u32[]{:S(2)}, u32[]{:S(2)}) collective-permute-start(bf16[3,1536,128]{2,1,0:T(8,128)(2,1)S(1)} %constant_dynamic-slice_fusion.7), channel_id=1, source_target_pairs={{0,1},{1,0},{2,3},{3,2},{4,5},{5,4},{6,7},{7,6},{8,9},{9,8},{10,11... | collective-permute-start | bytes 3538952 | tf_op jit(solution)/shard_map/ppermute | solution.py:126
  304.9 54.2 %collective-permute-start.39 = (bf16[3,1536,128]{2,1,0:T(8,128)(2,1)}, bf16[3,1536,128]{2,1,0:T(8,128)(2,1)}, u32[]{:S(2)}, u32[]{:S(2)}) collective-permute-start(bf16[3,1536,128]{2,1,0:T(8,128)(2,1)} %collective-permute-done.38.w_mine), channel_id=1, source_target_pairs={{0,2},{2,0},{1,3},{3,1},{4,6},{6,4},{5,7},{7,5},{8,10},{10,8},{9,1... | collective-permute-start | bytes 3538952 | tf_op jit(solution)/shard_map/ppermute | solution.py:126
  321.8 32.3 %collective-permute-start.20 = (bf16[512,768]{1,0:T(8,128)(2,1)}, bf16[512,768]{1,0:T(8,128)(2,1)}, u32[]{:S(2)}, u32[]{:S(2)}) collective-permute-start(bf16[512,768]{1,0:T(8,128)(2,1)} %get-tuple-element.99.own_b.mixed_b), channel_id=1, source_target_pairs={{0,1},{1,0},{2,3},{3,2},{4,5},{5,4},{6,7},{7,6},{8,9},{9,8},{10,11... | collective-permute-start | bytes 2359304 | tf_op jit(solution)/shard_map/ppermute | solution.py:126
  324.2 34.8 %collective-permute-start.19 = (bf16[512,768]{1,0:T(8,128)(2,1)}, bf16[512,768]{1,0:T(8,128)(2,1)}, u32[]{:S(2)}, u32[]{:S(2)}) collective-permute-start(bf16[512,768]{1,0:T(8,128)(2,1)} %get-tuple-element.98.own_a.mixed_a), channel_id=1, source_target_pairs={{0,1},{1,0},{2,3},{3,2},{4,5},{5,4},{6,7},{7,6},{8,9},{9,8},{10,11... | collective-permute-start | bytes 2359304 | tf_op jit(solution)/shard_map/ppermute | solution.py:126
  343.9 32.5 %collective-permute-start.104 = (bf16[6,192,256]{2,1,0:T(8,128)(2,1)}, bf16[6,192,256]{2,1,0:T(8,128)(2,1)}, u32[]{:S(2)}, u32[]{:S(2)}) collective-permute-start(bf16[6,192,256]{2,1,0:T(8,128)(2,1)} %collective-permute-done.95.refs_10_), channel_id=1, source_target_pairs={{0,2},{2,0},{1,3},{3,1},{4,6},{6,4},{5,7},{7,5},{8,10},{10,8},{9,1... | collective-permute-start | bytes 1769480 | tf_op jit(solution)/shard_map/ppermute | solution.py:126
  345.8 30.7 %collective-permute-start.105 = (bf16[6,192,256]{2,1,0:T(8,128)(2,1)}, bf16[6,192,256]{2,1,0:T(8,128)(2,1)}, u32[]{:S(2)}, u32[]{:S(2)}) collective-permute-start(bf16[6,192,256]{2,1,0:T(8,128)(2,1)} %collective-permute-done.96.refs_11_), channel_id=1, source_target_pairs={{0,2},{2,0},{1,3},{3,1},{4,6},{6,4},{5,7},{7,5},{8,10},{10,8},{9,1... | collective-permute-start | bytes 1769480 | tf_op jit(solution)/shard_map/ppermute | solution.py:126
  375.5 54.7 %collective-permute-start.46 = (bf16[3,192,256]{2,1,0:T(8,128)(2,1)S(1)}, bf16[3,192,256]{2,1,0:T(8,128)(2,1)S(1)}, u32[]{:S(2)}, u32[]{:S(2)}) collective-permute-start(bf16[3,192,256]{2,1,0:T(8,128)(2,1)S(1)} %slice.399), channel_id=1, source_target_pairs={{0,8},{8,16},{16,24},{24,28},{28,20},{20,12},{12,4},{4,0},{1,9},{9... | collective-permute-start | bytes 884744 | tf_op jit(solution)/shard_map/ppermute | solution.py:90
  375.8 56.8 %collective-permute-start.87 = (bf16[6,192,256]{2,1,0:T(8,128)(2,1)S(1)}, bf16[6,192,256]{2,1,0:T(8,128)(2,1)S(1)}, u32[]{:S(2)}, u32[]{:S(2)}) collective-permute-start(bf16[6,192,256]{2,1,0:T(8,128)(2,1)S(1)} %copy-done.63), channel_id=1, source_target_pairs={{0,2},{2,0},{1,3},{3,1},{4,6},{6,4},{5,7},{7,5},{8,10},{10,8},{9,1... | collective-permute-start | bytes 1769480 | tf_op jit(solution)/shard_map/ppermute | solution.py:126
  375.9 56.8 %collective-permute-start.88 = (bf16[6,192,256]{2,1,0:T(8,128)(2,1)S(1)}, bf16[6,192,256]{2,1,0:T(8,128)(2,1)S(1)}, u32[]{:S(2)}, u32[]{:S(2)}) collective-permute-start(bf16[6,192,256]{2,1,0:T(8,128)(2,1)S(1)} %copy-done.66), channel_id=1, source_target_pairs={{0,2},{2,0},{1,3},{3,1},{4,6},{6,4},{5,7},{7,5},{8,10},{10,8},{9,1... | collective-permute-start | bytes 1769480 | tf_op jit(solution)/shard_map/ppermute | solution.py:126
  376.4 55.7 %collective-permute-start.89 = (bf16[3,192,256]{2,1,0:T(8,128)(2,1)S(1)}, bf16[3,192,256]{2,1,0:T(8,128)(2,1)}, u32[]{:S(2)}, u32[]{:S(2)}) collective-permute-start(bf16[3,192,256]{2,1,0:T(8,128)(2,1)S(1)} %collective-permute-done.80.refs_12_), channel_id=1, source_target_pairs={{0,2},{2,0},{1,3},{3,1},{4,6},{6,4},{5,7},{7,5},{8,10},{10,8},{9,1... | collective-permute-start | bytes 884744 | tf_op jit(solution)/shard_map/ppermute | solution.py:126
  376.5 55.6 %collective-permute-start.90 = (bf16[3,192,256]{2,1,0:T(8,128)(2,1)}, bf16[3,192,256]{2,1,0:T(8,128)(2,1)}, u32[]{:S(2)}, u32[]{:S(2)}) collective-permute-start(bf16[3,192,256]{2,1,0:T(8,128)(2,1)} %collective-permute-done.81.refs_13_), channel_id=1, source_target_pairs={{0,2},{2,0},{1,3},{3,1},{4,6},{6,4},{5,7},{7,5},{8,10},{10,8},{9,1... | collective-permute-start | bytes 884744 | tf_op jit(solution)/shard_map/ppermute | solution.py:126
  430.2 46.3 %collective-permute-start.47 = (bf16[3,192,256]{2,1,0:T(8,128)(2,1)S(1)}, bf16[3,192,256]{2,1,0:T(8,128)(2,1)}, u32[]{:S(2)}, u32[]{:S(2)}) collective-permute-start(bf16[3,192,256]{2,1,0:T(8,128)(2,1)S(1)} %slice.400), channel_id=1, source_target_pairs={{8,0},{16,8},{24,16},{28,24},{20,28},{12,20},{4,12},{0,4},{9,1},{1... | collective-permute-start | bytes 884744 | tf_op jit(solution)/shard_map/ppermute | solution.py:90
  432.0 45.5 %collective-permute-start.70 = (bf16[6,192,256]{2,1,0:T(8,128)(2,1)}, bf16[6,192,256]{2,1,0:T(8,128)(2,1)S(1)}, u32[]{:S(2)}, u32[]{:S(2)}) collective-permute-start(bf16[6,192,256]{2,1,0:T(8,128)(2,1)} %collective-permute-done.61.refs_10_), channel_id=1, source_target_pairs={{0,2},{2,0},{1,3},{3,1},{4,6},{6,4},{5,7},{7,5},{8,10},{10,8},{9,1... | collective-permute-start | bytes 1769480 | tf_op jit(solution)/shard_map/ppermute | solution.py:126
  432.1 45.7 %collective-permute-start.71 = (bf16[6,192,256]{2,1,0:T(8,128)(2,1)S(1)}, bf16[6,192,256]{2,1,0:T(8,128)(2,1)S(1)}, u32[]{:S(2)}, u32[]{:S(2)}) collective-permute-start(bf16[6,192,256]{2,1,0:T(8,128)(2,1)S(1)} %copy-done.61), channel_id=1, source_target_pairs={{0,2},{2,0},{1,3},{3,1},{4,6},{6,4},{5,7},{7,5},{8,10},{10,8},{9,1... | collective-permute-start | bytes 1769480 | tf_op jit(solution)/shard_map/ppermute | solution.py:126
  432.6 44.4 %collective-permute-start.72 = (bf16[3,192,256]{2,1,0:T(8,128)(2,1)S(1)}, bf16[3,192,256]{2,1,0:T(8,128)(2,1)}, u32[]{:S(2)}, u32[]{:S(2)}) collective-permute-start(bf16[3,192,256]{2,1,0:T(8,128)(2,1)S(1)} %copy-done.118), channel_id=1, source_target_pairs={{0,2},{2,0},{1,3},{3,1},{4,6},{6,4},{5,7},{7,5},{8,10},{10,8},{9,1... | collective-permute-start | bytes 884744 | tf_op jit(solution)/shard_map/ppermute | solution.py:126
  432.7 44.4 %collective-permute-start.73 = (bf16[3,192,256]{2,1,0:T(8,128)(2,1)}, bf16[3,192,256]{2,1,0:T(8,128)(2,1)}, u32[]{:S(2)}, u32[]{:S(2)}) collective-permute-start(bf16[3,192,256]{2,1,0:T(8,128)(2,1)} %copy-done.121), channel_id=1, source_target_pairs={{0,2},{2,0},{1,3},{3,1},{4,6},{6,4},{5,7},{7,5},{8,10},{10,8},{9,1... | collective-permute-start | bytes 884744 | tf_op jit(solution)/shard_map/ppermute | solution.py:126
  476.6 45.0 %collective-permute-start.52 = (bf16[6,192,256]{2,1,0:T(8,128)(2,1)}, bf16[6,192,256]{2,1,0:T(8,128)(2,1)S(1)}, u32[]{:S(2)}, u32[]{:S(2)}) collective-permute-start(bf16[6,192,256]{2,1,0:T(8,128)(2,1)} %collective-permute-done.43.refs_9_), channel_id=1, source_target_pairs={{0,2},{2,0},{1,3},{3,1},{4,6},{6,4},{5,7},{7,5},{8,10},{10,8},{9,1... | collective-permute-start | bytes 1769480 | tf_op jit(solution)/shard_map/ppermute | solution.py:126
  477.0 44.6 %collective-permute-start.53 = (bf16[6,192,256]{2,1,0:T(8,128)(2,1)S(1)}, bf16[6,192,256]{2,1,0:T(8,128)(2,1)S(1)}, u32[]{:S(2)}, u32[]{:S(2)}) collective-permute-start(bf16[6,192,256]{2,1,0:T(8,128)(2,1)S(1)} %copy-done.57), channel_id=1, source_target_pairs={{0,2},{2,0},{1,3},{3,1},{4,6},{6,4},{5,7},{7,5},{8,10},{10,8},{9,1... | collective-permute-start | bytes 1769480 | tf_op jit(solution)/shard_map/ppermute | solution.py:126
  477.1 44.5 %collective-permute-start.54 = (bf16[6,192,256]{2,1,0:T(8,128)(2,1)S(1)}, bf16[6,192,256]{2,1,0:T(8,128)(2,1)S(1)}, u32[]{:S(2)}, u32[]{:S(2)}) collective-permute-start(bf16[6,192,256]{2,1,0:T(8,128)(2,1)S(1)} %copy-done.59), channel_id=1, source_target_pairs={{0,2},{2,0},{1,3},{3,1},{4,6},{6,4},{5,7},{7,5},{8,10},{10,8},{9,1... | collective-permute-start | bytes 1769480 | tf_op jit(solution)/shard_map/ppermute | solution.py:126
  477.5 44.1 %collective-permute-start.55 = (bf16[3,192,256]{2,1,0:T(8,128)(2,1)S(1)}, bf16[3,192,256]{2,1,0:T(8,128)(2,1)S(1)}, u32[]{:S(2)}, u32[]{:S(2)}) collective-permute-start(bf16[3,192,256]{2,1,0:T(8,128)(2,1)S(1)} %copy-done.120), channel_id=1, source_target_pairs={{0,2},{2,0},{1,3},{3,1},{4,6},{6,4},{5,7},{7,5},{8,10},{10,8},{9,1... | collective-permute-start | bytes 884744 | tf_op jit(solution)/shard_map/ppermute | solution.py:126
  477.7 43.9 %collective-permute-start.56 = (bf16[3,192,256]{2,1,0:T(8,128)(2,1)}, bf16[3,192,256]{2,1,0:T(8,128)(2,1)S(1)}, u32[]{:S(2)}, u32[]{:S(2)}) collective-permute-start(bf16[3,192,256]{2,1,0:T(8,128)(2,1)} %collective-permute-done.47.refs_13_), channel_id=1, source_target_pairs={{0,2},{2,0},{1,3},{3,1},{4,6},{6,4},{5,7},{7,5},{8,10},{10,8},{9,1... | collective-permute-start | bytes 884744 | tf_op jit(solution)/shard_map/ppermute | solution.py:126
  569.3 82.6 %collective-permute-start.109 = (bf16[1024,1536]{1,0:T(8,128)(2,1)}, bf16[1024,1536]{1,0:T(8,128)(2,1)}, u32[]{:S(2)}, u32[]{:S(2)}) collective-permute-start(bf16[1024,1536]{1,0:T(8,128)(2,1)} %get-tuple-element.112.back_a), channel_id=1, source_target_pairs={{0,1},{1,0},{2,3},{3,2},{4,5},{5,4},{6,7},{7,6},{8,9},{9,8},{10,11... | collective-permute-start | bytes 9437192 | tf_op jit(solution)/shard_map/ppermute | solution.py:126
  572.8 79.1 %collective-permute-start.110 = (f32[1024,128]{1,0:T(8,128)}, f32[1024,128]{1,0:T(8,128)}, u32[]{:S(2)}, u32[]{:S(2)}) collective-permute-start(f32[1024,128]{1,0:T(8,128)} %add_add_fusion.pick_a), channel_id=1, source_target_pairs={{0,1},{1,0},{2,3},{3,2},{4,5},{5,4},{6,7},{7,6},{8,9},{9,8},{10,11... | collective-permute-start | bytes 1572872 | tf_op jit(solution)/shard_map/ppermute | solution.py:126
  578.8 188.7 %collective-permute-start.114 = (bf16[5,1536,128]{2,1,0:T(8,128)(2,1)}, bf16[5,1536,128]{2,1,0:T(8,128)(2,1)}, u32[]{:S(2)}, u32[]{:S(2)}) collective-permute-start(bf16[5,1536,128]{2,1,0:T(8,128)(2,1)} %constant_dynamic-slice_fusion.2), channel_id=1, source_target_pairs={{0,1},{1,0},{2,3},{3,2},{4,5},{5,4},{6,7},{7,6},{8,9},{9,8},{10,11... | collective-permute-start | bytes 5898248 | tf_op jit(solution)/shard_map/ppermute | solution.py:126
  580.2 229.9 %collective-permute-start.167 = (bf16[2,3,1536,256]{3,2,1,0:T(8,128)(2,1)}, bf16[2,3,1536,256]{3,2,1,0:T(8,128)(2,1)}, u32[]{:S(2)}, u32[]{:S(2)}) collective-permute-start(bf16[2,3,1536,256]{3,2,1,0:T(8,128)(2,1)} %get-tuple-element.141), channel_id=1, source_target_pairs={{0,2},{2,0},{1,3},{3,1},{4,6},{6,4},{5,7},{7,5},{8,10},{10,8},{9,1... | collective-permute-start | bytes 14155784 | tf_op jit(solution)/shard_map/ppermute | solution.py:126
  580.2 237.4 %collective-permute-start.157 = (bf16[2,3,1536,256]{3,2,1,0:T(8,128)(2,1)}, bf16[2,3,1536,256]{3,2,1,0:T(8,128)(2,1)}, u32[]{:S(2)}, u32[]{:S(2)}) collective-permute-start(bf16[2,3,1536,256]{3,2,1,0:T(8,128)(2,1)} %get-tuple-element.139), channel_id=1, source_target_pairs={{0,2},{2,0},{1,3},{3,1},{4,6},{6,4},{5,7},{7,5},{8,10},{10,8},{9,1... | collective-permute-start | bytes 14155784 | tf_op jit(solution)/shard_map/ppermute | solution.py:126
  651.9 174.4 %collective-permute-start.147 = (bf16[2,3,1536,256]{3,2,1,0:T(8,128)(2,1)}, bf16[2,3,1536,256]{3,2,1,0:T(8,128)(2,1)}, u32[]{:S(2)}, u32[]{:S(2)}) collective-permute-start(bf16[2,3,1536,256]{3,2,1,0:T(8,128)(2,1)} %get-tuple-element.137), channel_id=1, source_target_pairs={{0,2},{2,0},{1,3},{3,1},{4,6},{6,4},{5,7},{7,5},{8,10},{10,8},{9,1... | collective-permute-start | bytes 14155784 | tf_op jit(solution)/shard_map/ppermute | solution.py:126
  651.9 109.0 %collective-permute-start.108 = (bf16[1024,1536]{1,0:T(8,128)(2,1)S(1)}, bf16[1024,1536]{1,0:T(8,128)(2,1)}, u32[]{:S(2)}, u32[]{:S(2)}) collective-permute-start(bf16[1024,1536]{1,0:T(8,128)(2,1)S(1)} %copy-done.19), channel_id=1, source_target_pairs={{0,1},{1,0},{2,3},{3,2},{4,5},{5,4},{6,7},{7,6},{8,9},{9,8},{10,11... | collective-permute-start | bytes 9437192 | tf_op jit(solution)/shard_map/ppermute | solution.py:126
  767.5 70.0 %collective-permute-start.137 = (bf16[2,3,1536,256]{3,2,1,0:T(8,128)(2,1)}, bf16[2,3,1536,256]{3,2,1,0:T(8,128)(2,1)}, u32[]{:S(2)}, u32[]{:S(2)}) collective-permute-start(bf16[2,3,1536,256]{3,2,1,0:T(8,128)(2,1)} %get-tuple-element.135), channel_id=1, source_target_pairs={{0,2},{2,0},{1,3},{3,1},{4,6},{6,4},{5,7},{7,5},{8,10},{10,8},{9,1... | collective-permute-start | bytes 14155784 | tf_op jit(solution)/shard_map/ppermute | solution.py:126
  782.6 248.0 %collective-permute-start.115 = (bf16[5,1536,128]{2,1,0:T(8,128)(2,1)}, bf16[5,1536,128]{2,1,0:T(8,128)(2,1)}, u32[]{:S(2)}, u32[]{:S(2)}) collective-permute-start(bf16[5,1536,128]{2,1,0:T(8,128)(2,1)} %collective-permute-done.114.w_mine), channel_id=1, source_target_pairs={{0,2},{2,0},{1,3},{3,1},{4,6},{6,4},{5,7},{7,5},{8,10},{10,8},{9,1... | collective-permute-start | bytes 5898248 | tf_op jit(solution)/shard_map/ppermute | solution.py:126
  810.1 37.5 %collective-permute-start.127 = (bf16[4,1536,128]{2,1,0:T(8,128)(2,1)}, bf16[4,1536,128]{2,1,0:T(8,128)(2,1)}, u32[]{:S(2)}, u32[]{:S(2)}) collective-permute-start(bf16[4,1536,128]{2,1,0:T(8,128)(2,1)} %constant_dynamic-slice_fusion), channel_id=1, source_target_pairs={{0,2},{2,0},{1,3},{3,1},{4,6},{6,4},{5,7},{7,5},{8,10},{10,8},{9,1... | collective-permute-start | bytes 4718600 | tf_op jit(solution)/shard_map/ppermute | solution.py:126
  817.6 149.3 %collective-permute-start.116 = (bf16[6,1536,128]{2,1,0:T(8,128)(2,1)}, bf16[6,1536,128]{2,1,0:T(8,128)(2,1)}, u32[]{:S(2)}, u32[]{:S(2)}) collective-permute-start(bf16[6,1536,128]{2,1,0:T(8,128)(2,1)} %constant_dynamic-slice_fusion.1), channel_id=1, source_target_pairs={{0,2},{2,0},{1,3},{3,1},{4,6},{6,4},{5,7},{7,5},{8,10},{10,8},{9,1... | collective-permute-start | bytes 7077896 | tf_op jit(solution)/shard_map/ppermute | solution.py:126
  882.8 33.5 %collective-permute-start.169 = (bf16[6,192,256]{2,1,0:T(8,128)(2,1)S(1)}, bf16[6,192,256]{2,1,0:T(8,128)(2,1)S(1)}, u32[]{:S(2)}, u32[]{:S(2)}) collective-permute-start(bf16[6,192,256]{2,1,0:T(8,128)(2,1)S(1)} %pad_maximum_fusion.8), channel_id=1, source_target_pairs={{0,8},{8,16},{16,24},{24,28},{28,20},{20,12},{12,4},{4,0},{1,9},{9... | collective-permute-start | bytes 1769480 | tf_op jit(solution)/shard_map/ppermute | solution.py:121
  951.5 79.3 %collective-permute-start.113 = (bf16[1024,1280]{1,0:T(8,128)(2,1)}, bf16[1024,1280]{1,0:T(8,128)(2,1)}, u32[]{:S(2)}, u32[]{:S(2)}) collective-permute-start(bf16[1024,1280]{1,0:T(8,128)(2,1)} %get-tuple-element.127.low), channel_id=1, source_target_pairs={{0,1},{1,0},{2,3},{3,2},{4,5},{5,4},{6,7},{7,6},{8,9},{9,8},{10,11... | collective-permute-start | bytes 7864328 | tf_op jit(solution)/shard_map/ppermute | solution.py:126
  1012.1 48.2 %collective-permute-start.121 = (bf16[3,192,128]{2,1,0:T(8,128)(2,1)}, bf16[3,192,128]{2,1,0:T(8,128)(2,1)}, u32[]{:S(2)}, u32[]{:S(2)}) collective-permute-start(bf16[3,192,128]{2,1,0:T(8,128)(2,1)} %get-tuple-element.240), channel_id=1, source_target_pairs={{8,0},{16,8},{24,16},{28,24},{20,28},{12,20},{4,12},{0,4},{9,1},{1... | collective-permute-start | bytes 442376 | tf_op jit(solution)/shard_map/ppermute | solution.py:121
  1024.9 38.0 %collective-permute-start.171 = (bf16[6,192,256]{2,1,0:T(8,128)(2,1)}, bf16[6,192,256]{2,1,0:T(8,128)(2,1)S(1)}, u32[]{:S(2)}, u32[]{:S(2)}) collective-permute-start(bf16[6,192,256]{2,1,0:T(8,128)(2,1)} %fusion.4), channel_id=1, source_target_pairs={{0,8},{8,16},{16,24},{24,28},{28,20},{20,12},{12,4},{4,0},{1,9},{9... | collective-permute-start | bytes 1769480 | tf_op jit(solution)/shard_map/ppermute | solution.py:121
  1027.4 36.1 %collective-permute-start.175 = (bf16[6,192,256]{2,1,0:T(8,128)(2,1)}, bf16[6,192,256]{2,1,0:T(8,128)(2,1)S(1)}, u32[]{:S(2)}, u32[]{:S(2)}) collective-permute-start(bf16[6,192,256]{2,1,0:T(8,128)(2,1)} %fusion.2), channel_id=1, source_target_pairs={{8,0},{16,8},{24,16},{28,24},{20,28},{12,20},{4,12},{0,4},{9,1},{1... | collective-permute-start | bytes 1769480 | tf_op jit(solution)/shard_map/ppermute | solution.py:121
  1030.6 87.0 %collective-permute-start.161 = (bf16[6,192,256]{2,1,0:T(8,128)(2,1)}, bf16[6,192,256]{2,1,0:T(8,128)(2,1)S(1)}, u32[]{:S(2)}, u32[]{:S(2)}) collective-permute-start(bf16[6,192,256]{2,1,0:T(8,128)(2,1)} %fusion.9), channel_id=1, source_target_pairs={{0,8},{8,16},{16,24},{24,28},{28,20},{20,12},{12,4},{4,0},{1,9},{9... | collective-permute-start | bytes 1769480 | tf_op jit(solution)/shard_map/ppermute | solution.py:121
  1062.9 43.9 %collective-permute-start.151 = (bf16[6,192,256]{2,1,0:T(8,128)(2,1)S(1)}, bf16[6,192,256]{2,1,0:T(8,128)(2,1)S(1)}, u32[]{:S(2)}, u32[]{:S(2)}) collective-permute-start(bf16[6,192,256]{2,1,0:T(8,128)(2,1)S(1)} %copy-done.32), channel_id=1, source_target_pairs={{0,8},{8,16},{16,24},{24,28},{28,20},{20,12},{12,4},{4,0},{1,9},{9... | collective-permute-start | bytes 1769480 | tf_op jit(solution)/shard_map/ppermute | solution.py:121
  1063.5 43.7 %collective-permute-start.155 = (bf16[6,192,256]{2,1,0:T(8,128)(2,1)S(1)}, bf16[6,192,256]{2,1,0:T(8,128)(2,1)S(1)}, u32[]{:S(2)}, u32[]{:S(2)}) collective-permute-start(bf16[6,192,256]{2,1,0:T(8,128)(2,1)S(1)} %copy-done.33), channel_id=1, source_target_pairs={{8,0},{16,8},{24,16},{28,24},{20,28},{12,20},{4,12},{0,4},{9,1},{1... | collective-permute-start | bytes 1769480 | tf_op jit(solution)/shard_map/ppermute | solution.py:121
  1074.8 43.4 %collective-permute-start.165 = (bf16[6,192,256]{2,1,0:T(8,128)(2,1)S(1)}, bf16[6,192,256]{2,1,0:T(8,128)(2,1)S(1)}, u32[]{:S(2)}, u32[]{:S(2)}) collective-permute-start(bf16[6,192,256]{2,1,0:T(8,128)(2,1)S(1)} %copy-done.31), channel_id=1, source_target_pairs={{8,0},{16,8},{24,16},{28,24},{20,28},{12,20},{4,12},{0,4},{9,1},{1... | collective-permute-start | bytes 1769480 | tf_op jit(solution)/shard_map/ppermute | solution.py:121
  (263 other events, 4651.3 us)

commit v2 on v1

v2 whole, which is shorter than its diff:
```python
import functools

import jax
import jax.numpy as jnp
from jax import lax
from jax.experimental import pallas as pl
from jax.experimental.pallas import tpu as pltpu
from jax.sharding import PartitionSpec as P

HEAD_DIM = 64
EXPERTS = 16
TOPK = 8
PROMPT_TOKENS = 1024
LANES = 128
ROUTER_LANE = 16

norm_eps = 1e-06
rope_base = 10000.0
masked_score = -1e30
bf = jnp.bfloat16
f32 = jnp.float32
contract_cols = (((1,), (1,)), ((), ()))
vmem_bytes = 63 * 1024 * 1024


def mm(a, b):
    return jnp.dot(a, b, preferred_element_type=f32)


def mm_nt(a, b):
    return lax.dot_general(a, b, contract_cols, preferred_element_type=f32)


def whole(shape):
    return pl.BlockSpec(shape, lambda *_: (0,) * len(shape), pipeline_mode=pl.Buffered(1))


def rows_of(block, width):
    return pl.BlockSpec((block, width), lambda i, *_: (i, 0))


def any_space():
    return pl.BlockSpec(memory_space=pltpu.HBM)


def call(kernel, name, grid, ins, in_specs, outs, out_specs, scratch, flops, scalars, deps=(), limit=vmem_bytes, aliases=None):
    moved = sum(a.size * a.dtype.itemsize for a in (*ins, *outs))
    return pl.pallas_call(
        lambda sc, *refs: kernel(sc, *refs[len(deps) :]),
        out_shape=tuple(outs),
        grid_spec=pltpu.PrefetchScalarGridSpec(
            num_scalar_prefetch=1,
            grid=grid,
            in_specs=[pl.BlockSpec(memory_space=pltpu.HBM) for _ in deps] + list(in_specs),
            out_specs=tuple(out_specs),
            scratch_shapes=scratch,
        ),
        compiler_params=pltpu.CompilerParams(vmem_limit_bytes=limit),
        cost_estimate=pl.CostEstimate(flops=60_000_000_000 if flops else 1, bytes_accessed=int(moved), transcendentals=0),
        name=name,
        input_output_aliases=aliases or {},
    )(scalars, *deps, *ins)


def after(values, *deps):
    return lax.optimization_barrier((values, *deps))[0]


def sds(shape, dtype):
    return jax.ShapeDtypeStruct(tuple(shape), dtype)


def ring_rank(place, count):
    place = lax.rem(place + 2 * count, count)
    return jnp.where(place < count // 2, 2 * place, 2 * count - 1 - 2 * place)


def ring_place(rank, count):
    return jnp.where(rank % 2 == 0, rank // 2, (2 * count - 1 - rank) // 2)


def ring_hop(values, count):
    order = list(range(0, count, 2)) + list(range(count - 1, 0, -2))
    pairs = []
    for k in range(count):
        here, there = order[k], order[(k + 1) % count]
        pairs += [(2 * here, 2 * there), (2 * there + 1, 2 * here + 1)]
    return sent(lax.ppermute(values, ("dp", "ctx"), pairs))


def swap(values, axis):
    return sent(lax.ppermute(values, axis, [(0, 1), (1, 0)]))


class Window:
    def __init__(self):
        self.now, self.before = [], []

    def turn(self):
        due, self.before, self.now = self.before, self.now, []
        return due


window = Window()


def sent(values):
    window.now.append(values)
    return values


def take(values, start, size, axis=0):
    return lax.dynamic_slice_in_dim(values, start, size, axis)


def place_half(values, core, axis):
    zeros = jnp.zeros_like(values)
    return jnp.where(core == 0, jnp.concatenate([values, zeros], axis), jnp.concatenate([zeros, values], axis))


PLANNED = 4


class Gather:
    def __init__(self, own, core, count, axis):
        self.own, self.core, self.count, self.axis = own, core, count, axis
        self.mine, self.mate, self.hops = [], [], 0

    def share(self, *held):
        if len(self.mate) < len(self.mine):
            self.mate.append(swap(after(self.mine[-1], *held), "ctx"))

    def step(self, *held):
        for _ in range(1 if self.hops else self.count // 2 - PLANNED + 1):
            got = self.hop(*held)
        return got

    def hop(self, *held):
        self.share(*held)
        self.hops += 1
        last = after(self.mine[-1] if self.mine else self.own, *held)
        if self.hops == self.count // 2:
            size = last.shape[self.axis] // 2
            last = take(last, self.core * size, size, self.axis)
        self.mine.append(ring_hop(last, self.count))
        return self.mine[-1]

    def finish(self):
        while self.hops < self.count // 2:
            self.step()
        self.share()
        return self

    @property
    def bufs(self):
        return [self.own, *self.mine, *self.mate]


def gather_sources(place, core, count):
    sign = 1 - 2 * core
    away = list(range(1, count // 2 + 1))
    return [ring_rank(place, count)] + [ring_rank(place - sign * a, count) for a in away] + [ring_rank(place + sign * a, count) for a in away]


def scatter_sources(place, core, count):
    sign = 1 - 2 * core
    away = list(range(1, count // 2))
    keep = [ring_rank(place + sign * a, count) for a in away] + [ring_rank(place + count // 2, count)]
    send = [ring_rank(place - sign * a, count) for a in away] + [ring_rank(place, count)]
    return keep + send


class Scatter:
    def __init__(self, core, count, scalars, core_at):
        self.core, self.count, self.scalars, self.core_at = core, count, scalars, core_at
        self.keeps, self.gots, self.hops, self.got = [], [], 0, None

    def add(self, keep, send, *held):
        self.keeps.append(keep)
        self.gots.append(swap(after(send, *held), "ctx"))
        return self.gots[-1]

    def step(self, deps=()):
        for _ in range(1 if self.hops else self.count // 2 - PLANNED + 1):
            got = self.hop(deps)
        return got

    def hop(self, deps):
        self.hops += 1
        stage = {1: None, 2: "second"}.get(self.hops, "middle")
        slot = self.count // 2 - self.hops if self.hops > 1 else self.count // 2 - 1
        value = hop_sum(self.keeps, self.gots, self.got, slot, stage, self.scalars, self.core_at, deps)
        self.got = ring_hop(value, self.count)
        return self.got

    def finish(self, deps=()):
        while self.hops < self.count // 2:
            self.step()
        mine = hop_sum(self.keeps, self.gots, self.got, self.count // 2 - 1, "end", self.scalars, self.core_at, deps)
        return mine, swap(mine, "ctx")


def load_shards(sc, bufs, dst, shard, sem):
    total = len(bufs)
    hops = total // 2
    half = dst.shape[0] // 2
    for k, buf in enumerate(bufs):
        rows = pl.ds(pl.multiple_of(sc[k] * shard, shard), shard)
        if k in (hops, 2 * hops):
            side = sc[total] if k == hops else 1 - sc[total]
            target = dst.at[pl.ds(side * half, half), rows, :]
        else:
            target = dst.at[:, rows, :]
        pltpu.make_async_copy(buf, target, sem).start()


def lanes_of(ref, first, count):
    return jnp.concatenate([ref[first + b] for b in range(count)], axis=1)


def rope(x, cosine, sine):
    lane = lax.broadcasted_iota(jnp.int32, x.shape, x.ndim - 1)
    ahead = pltpu.roll(x, x.shape[-1] - HEAD_DIM // 2, x.ndim - 1)
    behind = pltpu.roll(x, HEAD_DIM // 2, x.ndim - 1)
    return x * cosine + jnp.where(lax.rem(lane, HEAD_DIM) < HEAD_DIM // 2, ahead, behind) * sine


def lane_column(row, shape, lane_at):
    lane = lax.broadcasted_iota(jnp.int32, shape, 1)
    return jnp.where(lane == lane_at, jnp.broadcast_to(row, (shape[1], shape[0])).T, 0.0)


def pack_kernel(sc, query, key, value, output, router, gain_one, gain_two, out):
    at = 0
    for ref in (query, key, value):
        for b in range(ref.shape[1] // LANES):
            out[at] = ref[:, b * LANES : (b + 1) * LANES]
            at += 1
    shape = out.shape[1:]
    extra = lane_column(gain_one[...].astype(f32), shape, 0) + lane_column(gain_two[...].astype(f32), shape, 1)
    out[at] = extra.astype(bf)
    out[at, :, ROUTER_LANE : ROUTER_LANE + EXPERTS] = router[...]
    for b in range(output.shape[1] // LANES):
        out[at + 1 + b] = output[:, b * LANES : (b + 1) * LANES]
    for b in range(at + 1 + output.shape[1] // LANES, out.shape[0]):
        out[b] = jnp.zeros(shape, bf)


def pack(query, key, value, output, router, gain_one, gain_two, core):
    shard = query.shape[0]
    ins = [query, key, value, output, router, gain_one.reshape(1, shard), gain_two.reshape(1, shard)]
    blocks = (query.shape[1] + key.shape[1] + value.shape[1] + output.shape[1]) // LANES + 1
    blocks += blocks % 2
    out = sds((blocks, shard, LANES), bf)
    return call(pack_kernel, "pack", (1,), ins, [whole(a.shape) for a in ins], [out], [whole(out.shape)], [], 0, core)[0]


def qkv_kernel(shard, kinds, sc, tok, cosine, sine, *refs):
    heads, kvs, total = kinds
    bufs, (w_first, w_out, w_half, extra_out, q_out, kv_out, packed_out, nt_out, w, et, sem, out_sem) = refs[:total], refs[total:]
    step = pl.program_id(0)
    count, half = w_first.shape[0], w_half.shape[0]
    copies = [
        (w.at[pl.ds(0, count)], w_first),
        (w.at[pl.ds(count + 1, 2 * half)], w_out),
        (w.at[pl.ds(count + 1 + sc[total] * half, half)], w_half),
    ]

    @pl.when(step == 0)
    def _():
        load_shards(sc, bufs, w, shard, sem)
        pltpu.make_async_copy(w, w, sem).wait()
        for k, (src, dst) in enumerate(copies):
            pltpu.make_async_copy(src, dst, out_sem.at[k]).start()
        et[...] = w[count].T

    extra_out[...] = et[...]
    x = tok[...].astype(f32)
    scale = lax.rsqrt(jnp.mean(x * x, axis=-1, keepdims=True) + norm_eps)
    normed = (x * scale * et[0:1, :].astype(f32)).astype(bf)
    nt_out[...] = normed.T
    cs, sn = cosine[...], sine[...]
    for pair in range((heads + 2 * kvs) // 4):
        made = mm(normed, lanes_of(w, 2 * pair, 2))
        for side in range(2):
            first = 4 * pair + 2 * side
            part = made[:, side * LANES : (side + 1) * LANES]
            if first < heads + kvs:
                part = rope(part, cs, sn)
            out, at = kv_out, first - heads
            if first < heads:
                part, out, at = part * (1.0 / HEAD_DIM), q_out, first
            low = part.astype(bf)
            for k in range(2):
                one = low[:, k * HEAD_DIM : (k + 1) * HEAD_DIM]
                out[at + k] = one
                if first >= heads:
                    for quarter in range(2):

                        @pl.when(step == quarter)
                        def _():
                            packed_out[at + k, :, quarter * HEAD_DIM : (quarter + 1) * HEAD_DIM] = one

    @pl.when(step == pl.num_programs(0) - 1)
    def _():
        for k, (src, dst) in enumerate(copies):
            pltpu.make_async_copy(src, dst, out_sem.at[k]).wait()


def project(tokens, cosine, sine, scalars, bufs, heads, kvs, prompt, deps, block=256):
    rows, width = tokens.shape
    blocks, shard = bufs[0].shape[:2]
    count = (heads + 2 * kvs) // 2
    head_spec = lambda n: pl.BlockSpec((n, block, HEAD_DIM), lambda i, s: (0, i, 0))
    outs = [
        sds((count, width, LANES), bf),
        sds((heads // 2, width, LANES), bf),
        sds((heads // 4, width, LANES), bf),
        sds((LANES, width), bf),
        sds((heads, rows, HEAD_DIM), bf),
        sds((2 * kvs, rows, HEAD_DIM), bf),
        sds((2 * kvs, prompt // 2, LANES), bf),
        sds((width, rows), bf),
    ]
    return call(
        functools.partial(qkv_kernel, shard, (heads, kvs, len(bufs))),
        "project",
        (rows // block,),
        [tokens, cosine, sine, *bufs],
        [rows_of(block, width), rows_of(block, LANES), rows_of(block, LANES)] + [any_space()] * len(bufs),
        outs,
        [
            any_space(),
            any_space(),
            any_space(),
            whole((LANES, width)),
            head_spec(heads),
            head_spec(2 * kvs),
            whole((2 * kvs, prompt // 2, LANES)),
            pl.BlockSpec((width, block), lambda i, s: (0, i)),
        ],
        [
            pltpu.VMEM((blocks, width, LANES), bf),
            pltpu.VMEM((LANES, width), bf),
            pltpu.SemaphoreType.DMA,
            pltpu.SemaphoreType.DMA((3,)),
        ],
        2 * rows * width * count * LANES,
        scalars,
        deps,
    )


def causal(scores):
    key = lax.broadcasted_iota(jnp.int32, scores.shape, 0)
    query = lax.broadcasted_iota(jnp.int32, scores.shape, 1)
    return jnp.where(key <= query, scores, masked_score)


def block_scores(query, keys, other_keys, at, block, prompt, bias):
    parts = []
    if at:
        parts.append(mm_nt(keys[0:at], query))
    parts.append(causal(mm_nt(keys[at : at + block], query)))
    other = mm_nt(other_keys, query)
    if at < prompt:
        other = other + bias
    parts.append(other)
    return parts


def unpack(ref):
    return jnp.concatenate([ref[0, :, :HEAD_DIM], ref[0, :, HEAD_DIM:]], axis=0)


def attend_kernel(cfg, sc, q, k0, k1, o0, o1, v0, v1, w0, w1, mixed, lse):
    starts, block, prompt = cfg
    bias = jnp.where(sc[0] == 0, masked_score, 0.0).astype(f32)
    for side, (keys, other, values, other_values) in enumerate(((k0, o0, v0, w0), (k1, o1, v1, w1))):
        values_t = values[0].T
        other_t = unpack(other_values).T
        other_keys = unpack(other)
        for a, at in enumerate(starts):
            rows = slice(a * block, a * block + block)
            scores = block_scores(q[side, rows, :], keys[0], other_keys, at, block, prompt, bias)
            peak = functools.reduce(jnp.maximum, [jnp.max(s, axis=0, keepdims=True) for s in scores])
            raw = [jnp.exp(s - peak) for s in scores]
            total = sum(jnp.sum(r, axis=0, keepdims=True) for r in raw)
            low = [r.astype(bf) for r in raw]
            out = mm(other_t, low[-1]) + mm(values_t[:, at : at + block], low[-2])
            if at:
                out = out + mm(values_t[:, 0:at], low[0])
            out = out * (1.0 / total)
            mixed[rows, side * HEAD_DIM : side * HEAD_DIM + HEAD_DIM] = out.T.astype(bf)
            lse[0, side : side + 1, rows] = peak + jnp.log(total)


def kv_specs(kvs, rows, prompt, rep, first_pair):
    index = lambda side, base: (lambda p, s: (base + (2 * (p + first_pair) + side) // rep, 0, 0))
    specs = []
    for base in (0, kvs):
        specs += [pl.BlockSpec((1, rows, HEAD_DIM), index(side, base)) for side in range(2)]
        specs += [pl.BlockSpec((1, prompt // 2, LANES), index(side, base)) for side in range(2)]
    return specs


def attend(q, kv, other, core, part, deps, block=256):
    heads, rows, _ = q.shape
    kvs, prompt = other.shape[0] // 2, 2 * other.shape[1]
    count = prompt if part == 0 else rows - prompt
    first = 0 if part == 0 else prompt
    starts = tuple(range(first, first + count, block))
    return call(
        functools.partial(attend_kernel, (starts, block, prompt)),
        "attend",
        (heads // 2,),
        [q, kv, kv, other, other, kv, kv, other, other],
        [pl.BlockSpec((2, count, HEAD_DIM), lambda p, s: (p, part, 0)), *kv_specs(kvs, rows, prompt, heads // kvs, 0)],
        [sds((count, heads * HEAD_DIM), bf), sds((heads // 2, 2, count), f32)],
        [
            pl.BlockSpec((count, LANES), lambda p, s: (0, p)),
            pl.BlockSpec((1, 2, count), lambda p, s: (p, 0, 0)),
        ],
        [],
        16 * heads * count * 1024 * HEAD_DIM,
        core,
        deps,
    )


def attend_back_kernel(cfg, sc, q, k0, k1, o0, o1, v0, v1, w0, w1, dout, mixed_a, mixed_b, lse_a, lse_b, cosine, sine, dq, dkv, dother_out, dother):
    rows_total, block, prompt, rep = cfg
    pair = pl.program_id(0)
    bias = jnp.where(sc[0] == 0, masked_score, 0.0).astype(f32)
    kvs = dkv.shape[0] // 2

    @pl.when(pair == 0)
    def _():
        dkv[...] = jnp.zeros_like(dkv)
        dother[...] = jnp.zeros_like(dother)

    heads = ((k0, unpack(o0), v0, unpack(w0)), (k1, unpack(o1), v1, unpack(w1)))
    keys_t = [(keys[0].T, other.T) for keys, other, _, _ in heads]
    for at in range(0, rows_total, block):
        rows = slice(at, at + block)
        mixed, lse, local = (mixed_a, lse_a, at) if at < prompt else (mixed_b, lse_b, at - prompt)
        inner = slice(local, local + block)
        dot = (dout[rows, :].astype(f32) * mixed[inner, :].astype(f32)).T
        grads = []
        for side, (keys, other, values, other_values) in enumerate(heads):
            head = (2 * pair + side) // rep
            query = q[side, rows, :]
            grad = dout[rows, side * HEAD_DIM : side * HEAD_DIM + HEAD_DIM]
            weighted = jnp.sum(dot[side * HEAD_DIM : side * HEAD_DIM + HEAD_DIM], axis=0, keepdims=True)
            norm = lse[0, side : side + 1, inner]
            scores = block_scores(query, keys[0], other, at, block, prompt, bias)
            spans = ([(False, 0, at)] if at else []) + [(False, at, block), (True, 0, prompt)]
            back = None
            for score, (is_other, first, size) in zip(scores, spans):
                probs = jnp.exp(score - norm)
                value = other_values if is_other else values[0, first : first + size]
                score_low = (probs * (mm_nt(value, grad) - weighted)).astype(bf)
                sums = dother if is_other else dkv
                span = pl.ds(first, size)
                sums[kvs + head, span, :] += mm(probs.astype(bf), grad)
                sums[head, span, :] += mm(score_low, query)
                key_t = keys_t[side][1] if is_other else keys_t[side][0][:, first : first + size]
                term = mm(key_t, score_low)
                back = term if back is None else back + term
            grads.append(back)
        both = jnp.concatenate(grads, axis=0).T * (1.0 / HEAD_DIM)
        dq[rows, :] = rope(both, cosine[rows, :], -sine[rows, :]).astype(bf)

    @pl.when(pair == pl.num_programs(0) - 1)
    def _():
        for h in range(dother.shape[0]):
            for quarter in range(2):
                part = dother[h, quarter * (prompt // 2) : (quarter + 1) * (prompt // 2), :]
                dother_out[h, :, quarter * HEAD_DIM : (quarter + 1) * HEAD_DIM] = part


def attend_back(q, kv, other, dout, mixed, lse, cosine, sine, core, part, parts, deps, block=256):
    heads, rows, _ = q.shape
    kvs, prompt = other.shape[0] // 2, 2 * other.shape[1]
    pairs = heads // 2 // parts
    first = part * pairs
    mine = 2 * kvs // parts
    pair = pl.BlockSpec((rows, LANES), lambda p, s: (0, p + first))
    mixed_spec = lambda a: pl.BlockSpec((a.shape[0], LANES), lambda p, s: (0, p + first))
    lse_spec = lambda a: pl.BlockSpec((1, 2, a.shape[2]), lambda p, s: (p + first, 0, 0))
    return call(
        functools.partial(attend_back_kernel, (rows, block, prompt, heads // kvs)),
        "attend_back",
        (pairs,),
        [q, kv, kv, other, other, kv, kv, other, other, dout, *mixed, *lse, cosine, sine],
        [
            pl.BlockSpec((2, rows, HEAD_DIM), lambda p, s: (p + first, 0, 0)),
            *kv_specs(kvs, rows, prompt, heads // kvs, first),
            pair,
            *[mixed_spec(a) for a in mixed],
            *[lse_spec(a) for a in lse],
            whole(cosine.shape),
            whole(sine.shape),
        ],
        [
            sds((rows, pairs * LANES), bf),
            sds((mine, rows, HEAD_DIM), f32),
            sds((mine, prompt // 2, LANES), f32),
        ],
        [
            pl.BlockSpec((rows, LANES), lambda p, s: (0, p)),
            whole((mine, rows, HEAD_DIM)),
            whole((mine, prompt // 2, LANES)),
        ],
        [pltpu.VMEM((mine, prompt, HEAD_DIM), f32)],
        40 * heads // parts * rows * 1024 * HEAD_DIM,
        core,
        deps,
    )


def load_halves(sc, mine, theirs, first_block, w, sem):
    half = mine.shape[0]
    pltpu.make_async_copy(mine, w.at[pl.ds(first_block + sc[0] * half, half)], sem).start()
    pltpu.make_async_copy(theirs, w.at[pl.ds(first_block + (1 - sc[0]) * half, half)], sem).start()


def settle_kernel(sc, tok, ids, own_a, own_b, far_a, far_b, extra, w_own, w_mine, w_theirs, res_out, n_out, nt_out, wt_out, w, sem):
    step = pl.program_id(0)
    blocks = w_own.shape[0]

    @pl.when(step == 0)
    def _():
        pltpu.make_async_copy(w_own, w.at[pl.ds(0, blocks)], sem).start()
        load_halves(sc, w_mine, w_theirs, blocks, w, sem)
        pltpu.make_async_copy(w, w, sem).wait()

    early = step < pl.num_programs(0) // 2
    own = jnp.where(early, own_a[...], own_b[...])
    far = jnp.where(early, far_a[...], far_b[...])
    branch = mm_nt(own, lanes_of(w, 0, blocks)) + mm_nt(far, lanes_of(w, blocks, blocks))
    residual = tok[...].astype(f32) + branch
    res_out[...] = residual
    scale = lax.rsqrt(jnp.mean(residual * residual, axis=-1, keepdims=True) + norm_eps)
    normed = (residual * scale * extra[1:2, :].astype(f32)).astype(bf)
    n_out[...] = normed
    nt_out[...] = normed.T
    logits = mm_nt(normed, extra[...])
    lane = lax.broadcasted_iota(jnp.int32, logits.shape, 1)
    routed = lane < 0
    for k in range(TOPK):
        routed = jnp.logical_or(routed, lane == ids[:, k : k + 1] + ROUTER_LANE)
    logits = jnp.where(routed, logits, masked_score)
    raw = jnp.where(routed, jnp.exp(logits - jnp.max(logits, axis=-1, keepdims=True)), 0.0)
    wt_out[...] = raw / jnp.sum(raw, axis=-1, keepdims=True)


def settle(tokens, ids, own, far, extra, w_own, w_mine, w_theirs, core, deps, block=256):
    rows, width = tokens.shape
    halves = rows // block // 2
    cols = own[0].shape[1]
    low = pl.BlockSpec((block, cols), lambda i, s: (jnp.minimum(i, halves - 1), 0))
    high = pl.BlockSpec((block, cols), lambda i, s: (jnp.maximum(i - halves, 0), 0))
    return call(
        settle_kernel,
        "settle",
        (rows // block,),
        [tokens, ids, *own, *far, extra, w_own, w_mine, w_theirs],
        [rows_of(block, width), rows_of(block, TOPK), low, high, low, high, whole(extra.shape)] + [any_space()] * 3,
        [sds((rows, width), f32), sds((rows, width), bf), sds((width, rows), bf), sds((rows, LANES), f32)],
        [rows_of(block, width), rows_of(block, width), pl.BlockSpec((width, block), lambda i, s: (0, i)), rows_of(block, LANES)],
        [pltpu.VMEM((2 * w_own.shape[0], width, LANES), bf), pltpu.SemaphoreType.DMA],
        4 * rows * width * cols,
        core,
        deps,
    )


def mix_halves(core, kept, sent):
    first = jnp.concatenate([kept[0], sent[0]], axis=-1)
    second = jnp.concatenate([kept[1], sent[1]], axis=-1)
    return jnp.where(core == 0, first, second), jnp.where(core == 0, second, first)


def experts_kernel(cfg, sc, *refs):
    shard, hidden, local, first, last, total = cfg
    block = 256
    it = iter(refs)
    n2, n2t, cot, cott, wt = (next(it) for _ in range(5))
    bufs = [next(it) for _ in range(total)]
    sums_in = () if first else (next(it), next(it))
    pick_in = None if first else next(it)
    moe_out, back_out, keep, send, pick = (next(it) for _ in range(5))
    pick_t = next(it) if last else None
    xs, cs, xt, ct, w, moe, back, scaled, acts, keep_s, send_s = (next(it) for _ in range(11))
    w_sem, x_sem, c_sem, t_sem, in_sem, out_sem, g_sem = (next(it) for _ in range(7))
    rows_total, width = xs.shape
    hops = total // 2
    core = sc[total]
    ranks = total + 1
    slots = hops
    lead = ranks + 2 * slots

    for side in range(2):
        for k, buf in enumerate(bufs):
            rows = pl.ds(pl.multiple_of(sc[k] * shard, shard), shard)
            lanes = pl.ds(side * hidden, hidden)
            if k in (hops, 2 * hops):
                at = core if k == hops else 1 - core
                lanes = pl.ds(pl.multiple_of(side * hidden + at * (hidden // 2), LANES), hidden // 2)
            pltpu.make_async_copy(buf.at[:, local + side], w.at[:, rows, lanes], w_sem).start()
    spans = [pl.ds(at, block) for at in range(0, rows_total, block)]
    for i, rows in enumerate(spans):
        pltpu.make_async_copy(n2.at[rows], xs.at[rows], x_sem.at[i]).start()
        pltpu.make_async_copy(cot.at[rows], cs.at[rows], c_sem.at[i]).start()
    pltpu.make_async_copy(w, w, w_sem).wait()
    lane = lax.broadcasted_iota(jnp.int32, (block, LANES), 1)
    ids = [sc[lead + side] + ROUTER_LANE for side in range(2)]
    for i, rows in enumerate(spans):
        pltpu.make_async_copy(n2.at[rows], xs.at[rows], x_sem.at[i]).wait()
        pltpu.make_async_copy(cot.at[rows], cs.at[rows], c_sem.at[i]).wait()
        if i == 1:
            for k, (src, dst) in enumerate(zip(sums_in, (moe, back))):
                pltpu.make_async_copy(src, dst, in_sem.at[k]).start()
            pltpu.make_async_copy(n2t, xt, t_sem.at[0]).start()
            pltpu.make_async_copy(cott, ct, t_sem.at[1]).start()
        x = xs[rows, :]
        gate = mm(x, w[0])
        up = mm(x, w[1])
        grad = mm(cs[rows, :], w[2])
        table = wt[rows, :]
        sig = 1.0 / (1.0 + jnp.exp(-gate))
        silu = gate * sig
        act = silu * up
        dots = act * grad
        picked = jnp.zeros(table.shape, f32) if first else pick_in[rows, :]
        for side, expert in enumerate(ids):
            cols = slice(side * hidden, side * hidden + hidden)
            weight = jnp.sum(jnp.where(lane == expert, table, 0.0), axis=1, keepdims=True)
            picked = picked + jnp.where(lane == expert, jnp.sum(dots[:, cols], axis=1, keepdims=True), 0.0)
            scaled[rows, cols] = (act[:, cols] * weight).astype(bf)
            g = grad[:, cols] * weight
            s = sig[:, cols]
            acts[rows, cols] = (g * up[:, cols] * s * (1.0 + gate[:, cols] * (1.0 - s))).astype(bf)
            acts[rows, slice((2 + side) * hidden, (3 + side) * hidden)] = (g * silu[:, cols]).astype(bf)
        pick[rows, :] = picked
        if last:
            pick_t[:, rows] = picked.T[ROUTER_LANE : ROUTER_LANE + EXPERTS]

    for k, (src, dst) in enumerate(zip(sums_in, (moe, back))):
        pltpu.make_async_copy(src, dst, in_sem.at[k]).wait()
    outs = [(xs, moe_out), (cs, back_out)] if last else [(moe, moe_out), (back, back_out)]
    for rows in spans:
        one = mm_nt(scaled[rows, :], w[2])
        two = mm_nt(acts[rows, 0 : 2 * hidden], w[0]) + mm_nt(acts[rows, 2 * hidden :], w[1])
        if not first:
            one, two = one + moe[rows, :], two + back[rows, :]
        for made, (scr, out), s in zip((one, two), outs, range(2)):
            scr[rows, :] = made.astype(scr.dtype)
            pltpu.make_async_copy(scr.at[rows], out.at[rows], out_sem.at[s]).start()

    pltpu.make_async_copy(n2t, xt, t_sem.at[0]).wait()
    pltpu.make_async_copy(cott, ct, t_sem.at[1]).wait()
    for slot in range(slots):
        at = [pl.ds(pl.multiple_of(sc[ranks + slots * k + slot] * shard, shard), shard) for k in range(2)]
        left = lambda ref: jnp.concatenate([ref[at[0], :], ref[at[1], :]], axis=0)
        gate_up = mm(left(xt), acts[...]).astype(bf)
        down = mm(left(ct), scaled[...]).astype(bf)
        kinds = (gate_up[:, : 2 * hidden], gate_up[:, 2 * hidden :], down)
        for kind, made in enumerate(kinds):
            for side in range(2):
                part = made[:, side * hidden : side * hidden + hidden]
                kept, sent = part[:shard], part[shard:]
                if slot == slots - 1:
                    cut = lambda a: (a[:, : hidden // 2], a[:, hidden // 2 :])
                    kept, sent = mix_halves(core, cut(kept), cut(sent))
                keep_s[slot, side * 3 + kind] = kept
                send_s[slot, side * 3 + kind] = sent
        pltpu.make_async_copy(keep_s.at[slot], keep.at[slot], g_sem.at[0]).start()
        pltpu.make_async_copy(send_s.at[slot], send.at[slot], g_sem.at[1]).start()

    for (scr, out), s in zip(outs, range(2)):
        pltpu.make_async_copy(scr, out, out_sem.at[s]).wait()
    pltpu.make_async_copy(keep_s, keep, g_sem.at[0]).wait()
    pltpu.make_async_copy(send_s, send, g_sem.at[1]).wait()


def experts(n2, n2t, cot, cott, wt, scalars, bufs, local, sums, last, deps):
    rows, width = n2.shape
    shard, hidden = bufs[0].shape[2:]
    slots = len(bufs) // 2
    first = sums is None
    ins = [n2, n2t, cot, cott, wt, *bufs, *([] if first else sums)]
    specs = [any_space()] * 4 + [whole(wt.shape)] + [any_space()] * (len(ins) - 5)
    if not first:
        specs[-1] = whole((rows, LANES))
    kind = bf if last else f32
    dma = pltpu.SemaphoreType.DMA
    return call(
        functools.partial(experts_kernel, (shard, hidden, local, first, last, len(bufs))),
        "experts",
        (1,),
        ins,
        specs,
        [
            sds((rows, width), kind),
            sds((rows, width), kind),
            sds((slots, 6, shard, hidden), bf),
            sds((slots, 6, shard, hidden), bf),
            sds((rows, LANES), f32),
        ]
        + ([sds((EXPERTS, rows), f32)] if last else []),
        [any_space()] * 4 + [whole((rows, LANES))] + ([whole((EXPERTS, rows))] if last else []),
        [
            pltpu.VMEM((rows, width), bf),
            pltpu.VMEM((rows, width), bf),
            pltpu.VMEM((width, rows), bf),
            pltpu.VMEM((width, rows), bf),
            pltpu.VMEM((3, width, 2 * hidden), bf),
            pltpu.VMEM((rows, width), f32),
            pltpu.VMEM((rows, width), f32),
            pltpu.VMEM((rows, 2 * hidden), bf),
            pltpu.VMEM((rows, 4 * hidden), bf),
            pltpu.VMEM((slots, 6, shard, hidden), bf),
            pltpu.VMEM((slots, 6, shard, hidden), bf),
            dma,
            dma((rows // 256,)),
            dma((rows // 256,)),
            dma((2,)),
            dma((2,)),
            dma((2,)),
            dma((2,)),
        ],
        36 * rows * width * hidden,
        scalars,
        deps,
    )


def hop_kernel(cfg, sc, *refs):
    pairs, stage, core_at = cfg
    core = sc[core_at]
    it = iter(refs)
    keeps = [next(it) for _ in range(pairs)]
    gots = [next(it) for _ in range(pairs)]
    came = next(it) if stage else None
    out = next(it)
    for p in range(pairs):
        total = keeps[p][0].astype(f32) + gots[p][0].astype(f32)
        if stage == "end":
            total = place_half(total, core, 2) + came[p].astype(f32)
        elif stage == "second":
            total = total + place_half(came[p].astype(f32), core, 2)
        elif stage:
            total = total + came[p].astype(f32)
        out[p] = total.astype(bf)


def hop_sum(keeps, gots, came, slot, stage, scalars, core_at, deps=()):
    pairs = len(keeps)
    slots, mats, shard, hidden = keeps[0].shape
    lanes = hidden // 2 if stage in (None, "end") else hidden
    side = 1 if stage == "end" else 0
    per = mats // 2
    piece = pl.BlockSpec((1, per, shard, lanes), lambda m, s: (slot, m, 0, side))
    wide = lambda a: pl.BlockSpec((pairs, per, shard, a.shape[3]), lambda m, s: (0, m, 0, 0))
    out = sds((pairs, mats, shard, hidden // 2 if stage is None else hidden), bf)
    ins = [*keeps, *gots] + ([] if came is None else [came])
    specs = [piece] * (2 * pairs) + ([] if came is None else [wide(came)])
    kernel = functools.partial(hop_kernel, (pairs, stage, core_at))
    return call(kernel, "hop_sum", (2,), ins, specs, [out], [wide(out)], [], 0, scalars, deps)[0]


def emit_kernel(sc, mine, theirs, *refs):
    for m in range(6):
        refs[m % 3 - 3][m // 3] = mine[0, m].astype(f32) + theirs[0, m].astype(f32)


def emit(group, first, total, into, core, deps):
    pairs, mats, shard, hidden = group[0].shape
    ins = [*group, *(into or [])]
    spec = pl.BlockSpec((1, mats, shard, hidden), lambda i, s: (i, 0, 0, 0))
    out_spec = pl.BlockSpec((2, shard, hidden), lambda i, s: (i + first // 2, 0, 0))
    outs = [sds((total, shard, hidden), f32)] * 3
    aliases = {1 + len(deps) + 2 + k: k for k in range(3)} if into else {}
    specs = [spec, spec] + [any_space()] * (len(ins) - 2)
    return call(emit_kernel, "emit", (pairs,), ins, specs, outs, [out_spec] * 3, [], 0, core, deps, aliases=aliases)


def norm_back(values, gain, grad):
    scale = lax.rsqrt(jnp.mean(values * values, axis=-1, keepdims=True) + norm_eps)
    inner = jnp.mean(values * gain * grad, axis=-1, keepdims=True)
    passed = scale * gain * grad - values * (scale * scale * scale * inner)
    return passed, jnp.sum(grad * values * scale, axis=0, keepdims=True)


def unsettle_kernel(sc, back_a, back_b, pick_a, pick_b, wt, res, cot, extra, w_own, rg_out, low_t_out, dout_out, ll_out, gain_out, w, sem):
    step = pl.program_id(0)

    @pl.when(step == 0)
    def _():
        pltpu.make_async_copy(w_own, w, sem).start()
        pltpu.make_async_copy(w_own, w, sem).wait()
        gain_out[...] = jnp.zeros_like(gain_out)

    weights = wt[...]
    picked = pick_a[...] + pick_b[...]
    room = lambda n: jnp.zeros((n, picked.shape[1]), f32)
    picked = jnp.concatenate([room(ROUTER_LANE), picked, room(LANES - ROUTER_LANE - EXPERTS)], axis=0).T
    logit_low = (weights * (picked - jnp.sum(weights * picked, axis=-1, keepdims=True))).astype(bf)
    ll_out[...] = logit_low
    grad = back_a[...].astype(f32) + back_b[...].astype(f32) + mm(logit_low, extra[...])
    passed, gain = norm_back(res[...], extra[1:2, :].astype(f32), grad)
    gain_out[...] += gain
    total = cot[...].astype(f32) + passed
    rg_out[...] = total
    low = total.astype(bf)
    low_t_out[...] = low.T
    dout_out[...] = mm(low, lanes_of(w, 0, w.shape[0])).astype(bf)


def unsettle(back, picks, wt, res, cot, extra, w_own, core, deps, block=256):
    rows, width = res.shape
    cols = w_own.shape[0] * LANES
    wide, thin = rows_of(block, width), rows_of(block, LANES)
    across = pl.BlockSpec((EXPERTS, block), lambda i, s: (0, i))
    return call(
        unsettle_kernel,
        "unsettle",
        (rows // block,),
        [*back, *picks, wt, res, cot, extra, w_own],
        [wide, wide, across, across, thin, wide, wide, whole(extra.shape), any_space()],
        [sds((rows, width), f32), sds((width, rows), bf), sds((rows, cols), bf), sds((rows, LANES), bf), sds((1, width), f32)],
        [wide, pl.BlockSpec((width, block), lambda i, s: (0, i)), rows_of(block, cols), thin, whole((1, width))],
        [pltpu.VMEM(w_own.shape, bf), pltpu.SemaphoreType.DMA],
        2 * rows * width * cols,
        core,
        deps,
    )


def weight_grads_kernel(cfg, sc, *refs):
    sides, extra_sides, core_at, count = cfg
    keep, send = refs[-2:]
    core = sc[core_at]
    last = pl.program_id(0) == pl.num_programs(0) - 1
    it = iter(refs[:-2])

    def left():
        return jnp.concatenate([next(it)[...], next(it)[...]], axis=0)

    tall = left()
    made, at = None, 0
    for kind in range(sides):
        right = next(it)
        size = right.shape[0]
        made_here = mm(tall[:, at : at + size] if size < tall.shape[1] else tall, right[...])
        if size < tall.shape[1]:
            made = made_here if made is None else made + made_here
            at += size
        else:
            made = [made_here] if made is None else made + [made_here]
    if isinstance(made, list):
        made = jnp.concatenate(made, axis=1) if len(made) > 1 else made[0]
    extra = None
    if extra_sides:
        tall = left()
        extra = mm(tall, next(it)[...])
    column = left()
    extra = column if extra is None else extra + column
    wide = 2 * LANES
    made = jnp.concatenate([made, extra, jnp.zeros_like(extra)], axis=1).astype(bf)
    shard = extra.shape[0] // 2
    cut = lambda a: (a[:, :LANES], a[:, LANES:])
    blocks = [made[:, b * wide : (b + 1) * wide] for b in range(count)]

    @pl.when(jnp.logical_not(last))
    def _():
        for b in range(count):
            keep[0, b] = blocks[b][:shard]
            send[0, b] = blocks[b][shard:]

    @pl.when(last)
    def _():
        for b in range(count):
            keep[0, b], send[0, b] = mix_halves(core, cut(blocks[b][:shard]), cut(blocks[b][shard:]))


def weight_grads(name, left, rights, extra, column, scalars, first_rank, core_at, shard, count, deps):
    width, rows = left.shape
    slots = (scalars.shape[0] - first_rank) // 2
    at = lambda k: (lambda i, s: (s[first_rank + k * slots + i], 0))
    two = lambda lanes: [pl.BlockSpec((shard, lanes), at(k)) for k in range(2)]
    ins, specs = [left, left, *rights], two(rows) + [whole(r.shape) for r in rights]
    if extra is not None:
        ins += [extra[0], extra[0], extra[1]]
        specs += two(rows) + [whole(extra[1].shape)]
    ins += [column, column]
    specs += two(LANES)
    out = sds((slots, count, shard, 2 * LANES), bf)
    out_spec = pl.BlockSpec((1, count, shard, 2 * LANES), lambda i, s: (i, 0, 0, 0))
    return call(
        functools.partial(weight_grads_kernel, (len(rights), extra is not None, core_at, count)),
        name,
        (slots,),
        ins,
        specs,
        [out, out],
        [out_spec, out_spec],
        [],
        4 * rows * width * count * LANES,
        scalars,
        deps,
    )


def spread_kernel(sizes, sc, mine, theirs, *outs):
    block = 0
    for out, size in zip(outs, sizes):
        for b in range(max(1, size // (2 * LANES))):
            total = mine[0, block + b].astype(f32) + theirs[0, block + b].astype(f32)
            lanes = min(2 * LANES, out.shape[1])
            out[:, b * lanes : (b + 1) * lanes] = total[:, :lanes]
        block += max(1, size // (2 * LANES))


def spread(mine, theirs, sizes, core):
    shard = mine.shape[2]
    outs = [sds((shard, size), f32) for size in sizes]
    ins = [mine, theirs]
    kernel = functools.partial(spread_kernel, sizes)
    return call(kernel, "spread", (1,), ins, [whole(a.shape) for a in ins], outs, [whole(o.shape) for o in outs], [], 0, core)


def unproject_kernel(sc, tok, cosine, sine, *refs):
    *ins, w_own, low_out, part_out, gain_out, w, sem = refs
    parts = len(ins) // 3
    dqs, sums, mores = ins[:parts], ins[parts : 2 * parts], ins[2 * parts :]
    step = pl.program_id(0)

    @pl.when(step == 0)
    def _():
        pltpu.make_async_copy(w_own, w, sem).start()
        pltpu.make_async_copy(w_own, w, sem).wait()
        gain_out[...] = jnp.zeros_like(gain_out)

    shared = jnp.where(step < pl.num_programs(0) // 2, 1.0, 0.0).astype(f32)
    at = 0
    for is_key in (True, False):
        for own, more in zip(sums, mores):
            kvs = own.shape[0] // 2
            for kv in range(0, kvs, 2):
                heads = [kv + k + (0 if is_key else kvs) for k in range(2)]
                other = [jnp.where(step == 0, more[h, :, :HEAD_DIM], more[h, :, HEAD_DIM:]) for h in heads]
                pair = jnp.concatenate([own[h] + o * shared for h, o in zip(heads, other)], axis=1)
                if is_key:
                    pair = rope(pair, cosine[...], -sine[...])
                low_out[:, at : at + LANES] = pair.astype(bf)
                at += LANES
    low = jnp.concatenate([d[...] for d in dqs] + [low_out[...]], axis=1)
    part = mm_nt(low, lanes_of(w, 0, w.shape[0]))
    part_out[...] = part
    x = tok[...].astype(f32)
    scale = lax.rsqrt(jnp.mean(x * x, axis=-1, keepdims=True) + norm_eps)
    gain_out[...] += jnp.sum(part * x * scale, axis=0, keepdims=True)


def unproject(tokens, cosine, sine, dqs, sums, mores, w_own, core, deps, block=256):
    rows, width = tokens.shape
    cols = sum(s.shape[0] for s in sums) * HEAD_DIM
    own = lambda a: pl.BlockSpec((a.shape[0], block, HEAD_DIM), lambda i, s: (0, i, 0))
    return call(
        unproject_kernel,
        "unproject",
        (rows // block,),
        [tokens, cosine, sine, *dqs, *sums, *mores, w_own],
        [rows_of(block, width), rows_of(block, LANES), rows_of(block, LANES)]
        + [rows_of(block, d.shape[1]) for d in dqs]
        + [own(a) for a in sums]
        + [whole(a.shape) for a in mores]
        + [any_space()],
        [sds((rows, cols), bf), sds((rows, width), f32), sds((1, width), f32)],
        [rows_of(block, cols), rows_of(block, width), whole((1, width))],
        [pltpu.VMEM(w_own.shape, bf), pltpu.SemaphoreType.DMA],
        2 * rows * width * w_own.shape[0] * LANES,
        core,
        deps,
    )


def finish_kernel(sc, tok, part, extra, rg, *refs):
    *fars, w_mine, w_theirs, out, w, sem = refs

    @pl.when(pl.program_id(0) == 0)
    def _():
        load_halves(sc, w_mine, w_theirs, 0, w, sem)
        pltpu.make_async_copy(w, w, sem).wait()

    far = jnp.concatenate([f[...] for f in fars], axis=1)
    grad = part[...] + mm_nt(far, lanes_of(w, 0, w.shape[0]))
    passed, _ = norm_back(tok[...].astype(f32), extra[0:1, :].astype(f32), grad)
    out[...] = rg[...] + passed


def finish(tokens, part, extra, rg, fars, w_mine, w_theirs, core, deps, block=256):
    rows, width = tokens.shape
    wide = rows_of(block, width)
    return call(
        finish_kernel,
        "finish",
        (rows // block,),
        [tokens, part, extra, rg, *fars, w_mine, w_theirs],
        [wide, wide, whole(extra.shape), wide, *[rows_of(block, f.shape[1]) for f in fars], any_space(), any_space()],
        [sds((rows, width), f32)],
        [wide],
        [pltpu.VMEM((2 * w_mine.shape[0], width, LANES), bf), pltpu.SemaphoreType.DMA],
        2 * rows * width * 2 * w_mine.shape[0] * LANES,
        core,
        deps,
    )[0]


def body(
    tokens,
    routes,
    cotangent,
    norm_one,
    w_query,
    key_weight,
    value_weight,
    w_output,
    norm_two,
    w_router,
    w_gate,
    w_up,
    w_down,
):
    window.turn()
    window.turn()
    count = lax.axis_size("dp")
    core = lax.axis_index("ctx")
    place = ring_place(lax.axis_index("dp"), count)
    rows, width = tokens.shape[2:]
    prompt = PROMPT_TOKENS // lax.axis_size("ctx")
    heads = w_query.shape[1] // HEAD_DIM
    kvs = key_weight.shape[1] // HEAD_DIM
    shard, hidden = w_gate.shape[1:]
    core_only = jnp.stack([core, core]).astype(jnp.int32)
    ranks = gather_sources(place, core, count)
    slots = scatter_sources(place, core, count)
    first_rank, core_at = len(ranks) + 1, len(ranks)

    def scalars(*more):
        return jnp.stack([*ranks, core, *slots, *more]).astype(jnp.int32)

    plain = scalars()
    tok = tokens.reshape(rows, width)
    cot = cotangent.reshape(rows, width)
    ids = routes.reshape(rows, TOPK)

    packed = pack(w_query, key_weight, value_weight, w_output, w_router, norm_one, norm_two, core_only)
    firsts = Gather(packed, core, count, 0).finish()

    sizes = [4, 4, 4, 4]
    starts = [sum(sizes[:k]) for k in range(len(sizes))]
    chunks = []

    owns = [jnp.stack([w[at : at + size] for w in (w_gate, w_up, w_down)], axis=0) for at, size in zip(starts, sizes)]

    def open_chunk(*held):
        chunks.append(Gather(after(owns[len(chunks)], *held), core, count, 3))

    offsets = jnp.arange(rows, dtype=jnp.int32)
    positions = jnp.where(offsets < prompt, core * prompt + offsets, PROMPT_TOKENS + offsets - prompt)
    half_dim = HEAD_DIM // 2
    inverse = rope_base ** (-2.0 * jnp.arange(half_dim).astype(f32) / HEAD_DIM)
    angles = positions.astype(f32)[:, None] * inverse
    cosine = jnp.tile(jnp.cos(angles), (1, LANES // half_dim))
    sine = jnp.sin(angles)
    sine = jnp.tile(jnp.concatenate([-sine, sine], axis=1), (1, LANES // HEAD_DIM))
    cott = cot.T

    open_chunk(firsts.mine[-1])
    c0 = chunks[0]
    window.turn()
    window.turn()
    c0.step()
    w_first, w_out, w_out_half, extra, q, kv, kv_prompt, n1t = project(
        tok, cosine, sine, plain, firsts.bufs, heads, kvs, prompt, [cott, *owns, *window.turn()]
    )
    other = swap(kv_prompt, "ctx")
    out_far_mine = swap(after(w_out_half, kv_prompt), "tp")
    c0.step(kv_prompt)
    mixed_b, lse_b = attend(q, kv, other, core_only, 1, window.turn())
    far_b = swap(mixed_b, "tp")
    c0.step(lse_b)
    open_chunk(lse_b)
    c1 = chunks[1]
    c1.step()
    out_far_theirs = swap(after(out_far_mine, lse_b), "ctx")
    mixed_a, lse_a = attend(q, kv, other, core_only, 0, window.turn())
    far_a = swap(mixed_a, "tp")
    c0.step(lse_a)
    c1.step(lse_a)
    mixed, lse = (mixed_a, mixed_b), (lse_a, lse_b)
    first_part = w_first.shape[0] // 2
    res, n2, n2t, wt = settle(
        tok, ids, mixed, (far_a, far_b), extra, w_out, out_far_mine, out_far_theirs, core_only, window.turn()
    )
    first_far_mine = swap(take(after(w_first, wt), core * first_part, first_part), "tp")

    scatters = [Scatter(core, count, plain, core_at) for _ in range(2)]
    total_pairs = EXPERTS // 2
    state = dict(sums=None, pick=None)

    def work(pair):
        at = 2 * pair
        k = max(k for k in range(len(starts)) if starts[k] <= at)
        sc = scalars(jnp.int32(at), jnp.int32(at + 1))
        carried = None if state["sums"] is None else (*state["sums"], state["pick"])
        made = experts(n2, n2t, cot, cott, wt, sc, chunks[k].bufs, at - starts[k], carried, pair == total_pairs - 1, window.turn())
        state["sums"], state["pick"] = made[:2], made[4]
        state["last"] = made[-1]
        return made[2], made[3], made[4]

    s0, s1 = scatters
    c0.share(wt)
    c1.step(wt)
    open_chunk(wt)
    c2 = chunks[2]
    c2.step()
    keep, send, token = work(0)

    s0.add(keep, send)
    c1.step(token)
    c2.step(token)
    keep, send, token = work(1)

    s0.add(keep, send)
    c1.share(token)
    c2.step(token)
    open_chunk(token)
    c3 = chunks[3]
    c3.step()
    first_far_theirs = swap(after(first_far_mine, token), "ctx")
    keep, send, token = work(2)

    s0.add(keep, send)
    c2.step(token)
    c3.step(token)
    keep, send, token = work(3)

    s0.add(keep, send)
    c2.share(token)
    c3.step(token)
    s0.step([token])
    keep, send, token = work(4)

    s1.add(keep, send)
    c3.step(token)
    s0.step([token])
    keep, send, token = work(5)

    s1.add(keep, send)
    c3.share(token)
    s0.step([token])
    keep, send, token = work(6)

    s1.add(keep, send)
    s0.step([token])
    keep, send, token = work(7)
    moe_low, back_low = state["sums"]
    pick_t = state["last"]

    back_far = swap(back_low, "tp")
    got = s1.add(keep, send)
    pick_far = swap(after(pick_t, got), "tp")
    a = s1.step([token])
    s0_mine, s0_theirs = s0.finish([a])
    s1.step([s0_mine])
    emitted = emit((s0_mine, s0_theirs), 0, EXPERTS, None, core_only, [s0_mine])
    rg, low_t, dout, ll, gain_two = unsettle(
        (back_low, back_far), (pick_t, pick_far), wt, res, cot, extra, w_out, core_only, [emitted[0], *window.turn()]
    )
    moe_far = swap(after(moe_low, ll), "tp")

    lane = jnp.arange(LANES)
    column = lambda gain, at: jnp.where(lane == at, gain[0][:, None], 0.0)
    parts = 2
    s1.step([ll])
    window.now = [x for x in window.now if x is not moe_far]
    dq_a, dkv_a, dother_a = attend_back(q, kv, other, dout, mixed, lse, cosine, sine, core_only, 0, parts, window.turn())
    more_a = swap(dother_a, "ctx")
    s1.step([dother_a])
    out_keep, out_send = weight_grads(
        "output_grads", low_t, list(mixed), (n2t, ll), column(gain_two, 1), plain, first_rank, core_at, shard, heads // 4 + 1, [dother_a]
    )
    second = Scatter(core, count, plain, core_at)
    second.add(out_keep, out_send)
    dq_b, dkv_b, dother_b = attend_back(q, kv, other, dout, mixed, lse, cosine, sine, core_only, 1, parts, window.turn())
    more_b = swap(dother_b, "ctx")
    far_qa = swap(after(dq_a, moe_far, dother_b), "tp")
    second.step([dother_b])
    s1_mine, s1_theirs = s1.finish([dother_b])
    dqs, dkvs, mores = [dq_a, dq_b], [dkv_a, dkv_b], [more_a, more_b]
    low_kv, part, gain_one = unproject(tok, cosine, sine, dqs, dkvs, mores, w_first, core_only, [moe_far, *window.turn()])
    far_qb = swap(after(dq_b, gain_one), "tp")
    far_qs = [far_qa, far_qb]
    second.step([gain_one])
    first_keep, first_send = weight_grads(
        "project_grads", n1t, [*dqs, low_kv], None, column(gain_one, 0), plain, first_rank, core_at, shard, w_first.shape[0] // 2 + 1, window.turn()
    )
    first = Scatter(core, count, plain, core_at)
    far_kv = swap(after(low_kv, first_keep), "tp")
    first.add(first_keep, first_send)
    a = first.step()
    second.step([first_keep])
    grad_gate, grad_up, grad_down = emit((s1_mine, s1_theirs), EXPERTS // 2, EXPERTS, emitted, core_only, [first_keep, *window.turn()])
    first.step([grad_gate])
    second.step([grad_gate])
    result = (res + (moe_low.astype(f32) + after(moe_far, grad_gate).astype(f32))).astype(bf).reshape(tokens.shape)
    token_grad = finish(
        tok, part, extra, rg, [*far_qs, far_kv], first_far_mine, first_far_theirs, core_only, [grad_gate]
    ).reshape(tokens.shape)
    a = first.step()
    second_mine, second_theirs = second.finish()
    first.step()
    grad_output, extra_two = spread(second_mine, second_theirs, (heads * HEAD_DIM, LANES), core_only)
    kv_width = kvs * HEAD_DIM
    grad_query, grad_key, grad_value, extra_one = spread(*first.finish(), (heads * HEAD_DIM, kv_width, kv_width, LANES), core_only)
    gain_part = extra_one[:, 0]
    grad_norm_one = gain_part + swap(gain_part, "tp")
    grad_norm_two = extra_two[:, 1]
    grad_router = extra_two[:, ROUTER_LANE : ROUTER_LANE + EXPERTS]
    return (
        result,
        token_grad,
        grad_norm_one,
        grad_query,
        grad_key,
        grad_value,
        grad_output,
        grad_norm_two,
        grad_router,
        grad_gate,
        grad_up,
        grad_down,
    )


def solution(mesh):
    slab = P("dp", "ctx", None, None)
    split, rows_only, expert = P("dp", "tp"), P("dp"), P(None, "dp", "tp")
    return jax.shard_map(
        body,
        mesh=mesh,
        in_specs=(slab, slab, slab, rows_only, split, split, split, split, rows_only, P("dp", None), expert, expert, expert),
        out_specs=(slab, slab, rows_only, split, split, split, split, rows_only, P("dp", None), expert, expert, expert),
        check_vma=False,
    )
```

time: 1150 us -> 783 us (0.68)
  waiting for transfers between devices: 430 us -> 156 us
  other arithmetic: 78.6 us -> 17.3 us
  starting transfers between devices: 122 us -> 71.2 us
  Pallas kernels: 436 us -> 481 us
  local copies, waits for them, and re-layouts: 69.8 us -> 45.8 us
    ppermute x177 -> x86, waiting for transfers between devices: 430 us -> 156 us  [the longest x36 114 us: ring_hop(): return sent(lax.ppermute(values, ('dp', 'ctx'), pairs))]
    ppermute x177 -> x86, starting transfers between devices: 122 us -> 71.2 us  [the longest x36 45.5 us: ring_hop(): return sent(lax.ppermute(values, ('dp', 'ctx'), pairs))]
    pallas_call x15 -> x44, Pallas kernels: 436 us -> 481 us  [call(): pl.pallas_call(lambda sc, *refs: kernel(sc, *refs[len(deps):]), out_shape...]
    add x13 -> x0, other arithmetic: 33.6 us -> none  [the longest x6 28.5 us: piece(): return part(keep) + part(got)]
    convert_element_type x24 -> x0, other arithmetic: 21.8 us -> none  [the longest x12 11.7 us: ring_scatter(): g = (mine_g + g.astype(f32)).astype(bf)]
    slice x32 -> x3, local copies, waits for them, and re-layouts: 15.9 us -> 3.61 us  [the longest x1 1.64 us: body(): grad_norm_two = extra_two[:, 1]]
  transfers between devices with their start and end apart: 177 -> 86, of which waited for: 58 -> 20; matrix products, arithmetic and copies ran while one was open for 12% -> 6% of each run, Pallas kernels for 34% -> 60%
where the time goes in v2:
time: 783 us; the launch traced here: 773 us
  Pallas kernels  481 us (61%)
  waiting for transfers between devices  156 us (20%)
  starting transfers between devices  71.2 us (9%)
  local copies, waits for them, and re-layouts  45.8 us (6%)
  other arithmetic  17.3 us (2%)
    pallas_call x44, Pallas kernels, call(): pl.pallas_call(lambda sc, *refs: kernel(sc, *refs[len(deps):]), out_shape...  481 us
    ppermute x36, waiting for transfers between devices, ring_hop(): return sent(lax.ppermute(values, ('dp', 'ctx'), pairs))  114 us
    ppermute x36, starting transfers between devices, ring_hop(): return sent(lax.ppermute(values, ('dp', 'ctx'), pairs))  45.5 us
    ppermute x50, waiting for transfers between devices, swap(): return sent(lax.ppermute(values, axis, [(0, 1), (1, 0)]))  41.4 us
    ppermute x50, starting transfers between devices, swap(): return sent(lax.ppermute(values, axis, [(0, 1), (1, 0)]))  25.7 us
  transfers between devices with their start and end apart: 86, of which 20 were waited for; matrix products, arithmetic and copies ran while one was open for 6% of the time, Pallas kernels for 60%

profile of v2, /device:TPU:0, one launch (start us, length us, event | category | flops | bytes accessed | tf_op | source)
XLA Modules:
  0.0 772.5 jit_solution(8958667926888472025)
XLA Ops:
  11.1 11.3 %collective-permute-done.refs_9_ = bf16[18,192,128]{2,1,0:T(8,128)(2,1)} collective-permute-done((bf16[18,192,128]{2,1,0:T(8,128)(2,1)}, bf16[18,192,128]{2,1,0:T(8,128)(2,1)}, u32[]{:S(2)}, u32[]{:S(2)}) %collective-permute-start) | collective-permute-done | bytes 884768 | tf_op jit(solution)/shard_map/ppermute | solution.py:88
  24.5 11.3 %collective-permute-done.1.refs_10_ = bf16[18,192,128]{2,1,0:T(8,128)(2,1)} collective-permute-done((bf16[18,192,128]{2,1,0:T(8,128)(2,1)}, bf16[18,192,128]{2,1,0:T(8,128)(2,1)}, u32[]{:S(2)}, u32[]{:S(2)}) %collective-permute-start.1) | collective-permute-done | bytes 884768 | tf_op jit(solution)/shard_map/ppermute | solution.py:88
  37.8 4.6 copy.41.refs_0_.refs_8_.refs_9_.refs_7_.refs_6_
  60.3 3.1 pad_maximum_fusion
  67.3 17.7 %project.1 = (bf16[10,1536,128]{2,1,0:T(8,128)(2,1)}, bf16[6,1536,128]{2,1,0:T(8,128)(2,1)}, bf16[3,1536,128]{2,1,0:T(8,128)(2,1)}, bf16[128,1536]{1,0:T(8,128)(...) custom-call(s32[18]{0:T(128)} %stack.90.sc, ...), custom_call_target="tpu_custom_call" | custom-call | flops 60000002048 | bytes 25427968 | tf_op jit(solution)/shard_map/project/pallas_call | solution.py:48
  89.0 21.3 %attend.2 = (bf16[512,768]{1,0:T(8,128)(2,1)}, f32[6,2,512]{2,1,0:T(2,128)}) custom-call(s32[2]{0:T(128)} %pad_add_fusion.sc, bf16[3,4,192,256]{3,2,1,0:T(8,128)(2,1)} %collective-permute-done.4.refs_0_.refs_11_, bf16[12,1024,64]{2,1,0:T(8,128)(2,1)} %get-tuple-element.130.refs_1_.refs_4_.refs_6_, ...), custom_call_target="tpu_custom_call" | custom-call | flops 60000002048 | bytes 8675328 | tf_op jit(solution)/shard_map/attend/pallas_call | solution.py:48
  115.9 16.9 %attend.3 = (bf16[512,768]{1,0:T(8,128)(2,1)}, f32[6,2,512]{2,1,0:T(2,128)}) custom-call(s32[2]{0:T(128)} %pad_add_fusion.sc, bf16[8,256,128]{2,1,0:T(8,128)(2,1)} %copy-done.19, bf16[3,1536,128]{2,1,0:T(8,128)(2,1)} %collective-permute-done.15.refs_1_.refs_13_, bf16[3,4,192,256]{3,2,1,0:T(8,128)(2,1)} %collective-permute-done.17.refs_2_.refs_15_, ...), custom_call_target="tpu_custom_call" | custom-call | flops 60000002048 | bytes 8675328 | tf_op jit(solution)/shard_map/attend/pallas_call | solution.py:48
  135.7 4.3 collective-permute-done.13.refs_2_.refs_13_
  143.3 9.3 %collective-permute-done.18.refs_9_.refs_0_ = bf16[512,768]{1,0:T(8,128)(2,1)S(1)} collective-permute-done((bf16[512,768]{1,0:T(8,128)(2,1)}, bf16[512,768]{1,0:T(8,128)(2,1)S(1)}, u32[]{:S(2)}, u32[]{:S(2)}) %collective-permute-start.18) | collective-permute-done | bytes 786464 | tf_op jit(solution)/shard_map/ppermute | solution.py:92
  153.5 15.8 %settle.1 = (f32[1024,1536]{1,0:T(8,128)}, bf16[1024,1536]{1,0:T(8,128)(2,1)}, bf16[1536,1024]{1,0:T(8,128)(2,1)}, f32[1024,128]{1,0:T(8,128)}) custom-call(s32[2]{0:T(128)} %pad_add_fusion.sc, bf16[512,768]{1,0:T(8,128)(2,1)} %collective-permute-done.10.refs_0_.refs_10_, bf16[3,4,192,256]{3,2,1,0:T(8,128)(2,1)} %collective-permute-done.12.refs_1_.refs_16_, ...), custom_call_target="tpu_custom_call" | custom-call | flops 60000002048 | bytes 24543232 | tf_op jit(solution)/shard_map/settle/pallas_call | solution.py:48
  179.4 32.4 %experts.8 = (f32[1024,1536]{1,0:T(8,128)}, f32[1024,1536]{1,0:T(8,128)}, bf16[4,6,192,256]{3,2,1,0:T(8,128)(2,1)}, bf16[4,6,192,256]{3,2,1,0:T(8,128)(2,1)}, f32[1024,128]{1,0:T(8,128)}) custom-call(s32[20]{0:T(128)} %stack.107.sc, bf16[512,768]{1,0:T(8,128)(2,1)} %copy-done.14, bf16[3,4,192,256]{3,2,1,0:T(8,128)(2,1)} %collective-permute-done.26.refs_1_.refs_17_, ...), custom_call_target="tpu_custom_call" | custom-call | flops 60000002048 | bytes 40370176 | tf_op jit(solution)/shard_map/experts/pallas_call | solution.py:48
  215.8 5.4 collective-permute-done.19.refs_0_.refs_8_
  221.4 24.5 %experts.9 = (f32[1024,1536]{1,0:T(8,128)}, f32[1024,1536]{1,0:T(8,128)}, bf16[4,6,192,256]{3,2,1,0:T(8,128)(2,1)}, bf16[4,6,192,256]{3,2,1,0:T(8,128)(2,1)}, f32[1024,128]{1,0:T(8,128)}) custom-call(s32[20]{0:T(128)} %stack.106.sc, bf16[5,1536,128]{2,1,0:T(8,128)(2,1)} %collective-permute-done.19.refs_0_.refs_8_, bf16[3,4,192,128]{3,2,1,0:T(8,128)(2,1)} %copy-done.16, ...), custom_call_target="tpu_custom_call" | custom-call | flops 60000002048 | bytes 53477376 | tf_op jit(solution)/shard_map/experts/pallas_call | solution.py:48
  250.0 24.1 %experts.10 = (f32[1024,1536]{1,0:T(8,128)}, f32[1024,1536]{1,0:T(8,128)}, bf16[4,6,192,256]{3,2,1,0:T(8,128)(2,1)}, bf16[4,6,192,256]{3,2,1,0:T(8,128)(2,1)}, f32[1024,128]{1,0:T(8,128)}) custom-call(s32[20]{0:T(128)} %stack.108.sc, bf16[4,6,192,256]{3,2,1,0:T(8,128)(2,1)} %collective-permute-done.37.refs_0_.refs_5_, ...), custom_call_target="tpu_custom_call" | custom-call | flops 60000002048 | bytes 53477376 | tf_op jit(solution)/shard_map/experts/pallas_call | solution.py:48
  276.9 24.4 %experts.11 = (f32[1024,1536]{1,0:T(8,128)}, f32[1024,1536]{1,0:T(8,128)}, bf16[4,6,192,256]{3,2,1,0:T(8,128)(2,1)}, bf16[4,6,192,256]{3,2,1,0:T(8,128)(2,1)}, f32[1024,128]{1,0:T(8,128)}) custom-call(s32[20]{0:T(128)} %stack.105.sc, bf16[4,6,192,256]{3,2,1,0:T(8,128)(2,1)} %collective-permute-done.28.refs_0_.refs_6_, bf16[3,4,192,128]{3,2,1,0:T(8,128)(2,1)} %copy-done.17, ...), custom_call_target="tpu_custom_call" | custom-call | flops 60000002048 | bytes 53477376 | tf_op jit(solution)/shard_map/experts/pallas_call | solution.py:48
  304.5 8.0 %collective-permute-done.40.refs_2_.refs_14_ = bf16[3,4,192,128]{3,2,1,0:T(8,128)(2,1)S(1)} collective-permute-done((bf16[3,4,192,128]{3,2,1,0:T(8,128)(2,1)S(1)}, bf16[3,4,192,128]{3,2,1,0:T(8,128)(2,1)S(1)}, u32[]{:S(2)}, u32[]{:S(2)}) %collective-permute-start.40) | collective-permute-done | bytes 589856 | tf_op jit(solution)/shard_map/ppermute | solution.py:88
  312.5 12.7 %collective-permute-done.42.refs_4_.refs_11_.refs_10_ = bf16[3,4,192,256]{3,2,1,0:T(8,128)(2,1)} collective-permute-done((bf16[3,4,192,256]{3,2,1,0:T(8,128)(2,1)}, bf16[3,4,192,256]{3,2,1,0:T(8,128)(2,1)}, u32[]{:S(2)}, u32[]{:S(2)}) %collective-permute-start.42) | collective-permute-done | bytes 1179680 | tf_op jit(solution)/shard_map/ppermute | solution.py:88
  327.4 3.3 hop_sum.20
  331.2 24.1 %experts.12 = (f32[1024,1536]{1,0:T(8,128)}, f32[1024,1536]{1,0:T(8,128)}, bf16[4,6,192,256]{3,2,1,0:T(8,128)(2,1)}, bf16[4,6,192,256]{3,2,1,0:T(8,128)(2,1)}, f32[1024,128]{1,0:T(8,128)}) custom-call(s32[20]{0:T(128)} %stack.109.sc, bf16[4,6,192,256]{3,2,1,0:T(8,128)(2,1)} %collective-permute-done.45.refs_7_.refs_0_, ...), custom_call_target="tpu_custom_call" | custom-call | flops 60000002048 | bytes 53477376 | tf_op jit(solution)/shard_map/experts/pallas_call | solution.py:48
  358.3 4.9 hop_sum.21
  364.8 24.4 %experts.13 = (f32[1024,1536]{1,0:T(8,128)}, f32[1024,1536]{1,0:T(8,128)}, bf16[4,6,192,256]{3,2,1,0:T(8,128)(2,1)}, bf16[4,6,192,256]{3,2,1,0:T(8,128)(2,1)}, f32[1024,128]{1,0:T(8,128)}) custom-call(s32[20]{0:T(128)} %stack.104.sc, bf16[4,6,192,256]{3,2,1,0:T(8,128)(2,1)} %collective-permute-done.39.refs_8_.refs_0_, ...), custom_call_target="tpu_custom_call" | custom-call | flops 60000002048 | bytes 53477376 | tf_op jit(solution)/shard_map/experts/pallas_call | solution.py:48
  392.5 5.2 hop_sum.22
  400.0 24.2 %experts.14 = (f32[1024,1536]{1,0:T(8,128)}, f32[1024,1536]{1,0:T(8,128)}, bf16[4,6,192,256]{3,2,1,0:T(8,128)(2,1)}, bf16[4,6,192,256]{3,2,1,0:T(8,128)(2,1)}, f32[1024,128]{1,0:T(8,128)}) custom-call(s32[20]{0:T(128)} %stack.110.sc, bf16[4,6,192,256]{3,2,1,0:T(8,128)(2,1)} %collective-permute-done.55.refs_0_.refs_5_, ...), custom_call_target="tpu_custom_call" | custom-call | flops 60000002048 | bytes 53477376 | tf_op jit(solution)/shard_map/experts/pallas_call | solution.py:48
  426.9 24.5 %experts.15 = (bf16[1024,1536]{1,0:T(8,128)(2,1)}, bf16[1024,1536]{1,0:T(8,128)(2,1)}, bf16[4,6,192,256]{3,2,1,0:T(8,128)(2,1)}, bf16[4,6,192,256]{3,2,1,0:T(8,1...) custom-call(s32[20]{0:T(128)} %stack.103.sc, bf16[4,6,192,256]{3,2,1,0:T(8,128)(2,1)} %collective-permute-done.49.refs_0_.refs_6_, ...), custom_call_target="tpu_custom_call" | custom-call | flops 60000002048 | bytes 47251456 | tf_op jit(solution)/shard_map/experts/pallas_call | solution.py:48
  451.5 5.2 hop_sum.24
  458.1 3.3 hop_sum.23
  464.2 21.6 %collective-permute-done.59.refs_9_.refs_2_ = bf16[4,6,192,256]{3,2,1,0:T(8,128)(2,1)} collective-permute-done((bf16[4,6,192,256]{3,2,1,0:T(8,128)(2,1)}, bf16[4,6,192,256]{3,2,1,0:T(8,128)(2,1)}, u32[]{:S(2)}, u32[]{:S(2)}) %collective-permute-start.59) | collective-permute-done | bytes 2359328 | tf_op jit(solution)/shard_map/ppermute | solution.py:88
  485.8 12.6 %collective-permute-done.58.refs_0_.refs_9_.refs_3_ = bf16[4,6,192,128]{3,2,1,0:T(8,128)(2,1)} collective-permute-done((bf16[4,6,192,128]{3,2,1,0:T(8,128)(2,1)}, bf16[4,6,192,128]{3,2,1,0:T(8,128)(2,1)}, u32[]{:S(2)}, u32[]{:S(2)}) %collective-permute-start.58) | collective-permute-done | bytes 1179680 | tf_op jit(solution)/shard_map/ppermute | solution.py:88
  498.5 4.6 hop_sum.25.refs_0_.refs_1_
  504.9 4.9 hop_sum.26
  511.0 5.6 emit.2
  516.6 17.6 %collective-permute-done.62.refs_6_.refs_2_ = f32[16,1024]{1,0:T(8,128)S(1)} collective-permute-done((f32[16,1024]{1,0:T(8,128)S(1)}, f32[16,1024]{1,0:T(8,128)S(1)}, u32[]{:S(2)}, u32[]{:S(2)}) %collective-permute-start.62) | collective-permute-done | bytes 65568 | tf_op jit(solution)/shard_map/ppermute | solution.py:92
  534.8 16.6 %unsettle.1 = (f32[1024,1536]{1,0:T(8,128)}, bf16[1536,1024]{1,0:T(8,128)(2,1)}, bf16[1024,768]{1,0:T(8,128)(2,1)}, bf16[1024,128]{1,0:T(8,128)(2,1)}, f32[1,1536]{1,0:T(1,128)}) custom-call(s32[2]{0:T(128)} %pad_add_fusion.sc, f32[16,192,256]{2,1,0:T(8,128)} %get-tuple-element.207.refs_0_.refs_5_, ...), custom_call_target="tpu_custom_call" | custom-call | flops 60000002048 | bytes 30414848 | tf_op jit(solution)/shard_map/unsettle/pallas_call | solution.py:48
  553.0 5.2 hop_sum.27
  559.2 24.9 %attend_back.3 = (bf16[1024,384]{1,0:T(8,128)(2,1)}, f32[4,1024,64]{2,1,0:T(8,128)}, f32[4,256,128]{2,1,0:T(8,128)}) custom-call(s32[2]{0:T(128)} %pad_add_fusion.sc, bf16[1024,1536]{1,0:T(8,128)(2,1)} %collective-permute-done.61.refs_4_.refs_0_, bf16[4,6,192,256]{3,2,1,0:T(8,128)(2,1)} %collective-permute-done.57.refs_8_.refs_1_, f32[16,1024]{1,0:T(8,128)} %copy-done.22, ...), custom_call_target="tpu_custom_call" | custom-call | flops 60000002048 | bytes 14467072 | tf_op jit(solution)/shard_map/attend_back/pallas_call | solution.py:48
  585.4 8.8 %output_grads.1 = (bf16[4,4,192,256]{3,2,1,0:T(8,128)(2,1)}, bf16[4,4,192,256]{3,2,1,0:T(8,128)(2,1)}) custom-call(s32[18]{0:T(128)} %stack.90.sc, f32[4,256,128]{2,1,0:T(8,128)} %get-tuple-element.217.refs_0_, bf16[1536,1024]{1,0:T(8,128)(2,1)} %get-tuple-element.218.refs_1_.refs_2_, bf16[1536,1024]{1,0:T(8,128)(2,1)} %get-tuple-element.218.refs_1_.refs_2_, ...), custom_call_target="tpu_custom_call" | custom-call | flops 60000002048 | bytes 19136512 | tf_op jit(solution)/shard_map/output_grads/pallas_call | solution.py:48
  594.7 5.2 hop_sum.29
  600.7 25.0 %attend_back.2 = (bf16[1024,384]{1,0:T(8,128)(2,1)}, f32[4,1024,64]{2,1,0:T(8,128)}, f32[4,256,128]{2,1,0:T(8,128)}) custom-call(s32[2]{0:T(128)} %pad_add_fusion.sc, bf16[4,6,192,256]{3,2,1,0:T(8,128)(2,1)} %collective-permute-done.65.refs_0_.refs_9_, bf16[12,1024,64]{2,1,0:T(8,128)(2,1)} %get-tuple-element.130.refs_1_.refs_4_.refs_6_, ...), custom_call_target="tpu_custom_call" | custom-call | flops 60000002048 | bytes 14467072 | tf_op jit(solution)/shard_map/attend_back/pallas_call | solution.py:48
  629.9 4.6 hop_sum.30.refs_3_
  635.4 13.4 %unproject.1 = (bf16[1024,512]{1,0:T(8,128)(2,1)}, f32[1024,1536]{1,0:T(8,128)}, f32[1,1536]{1,0:T(1,128)}) custom-call(s32[2]{0:T(128)} %pad_add_fusion.sc, bf16[1024,1536]{1,0:T(8,128)(2,1)} %collective-permute-done.63.refs_0_, f32[4,256,128]{2,1,0:T(8,128)} %copy-done.20, bf16[4,6,192,256]{3,2,1,0:T(8,128)(2,1)} %collective-permute-done.70.refs_9_.refs_2_, ...), custom_call_target="tpu_custom_call" | custom-call | flops 60000002048 | bytes 20191232 | tf_op jit(solution)/shard_map/unproject/pallas_call | solution.py:48
  651.4 10.0 %project_grads.1 = (bf16[4,6,192,256]{3,2,1,0:T(8,128)(2,1)}, bf16[4,6,192,256]{3,2,1,0:T(8,128)(2,1)}) custom-call(s32[18]{0:T(128)} %stack.90.sc, f32[4,256,128]{2,1,0:T(8,128)} %collective-permute-done.66.refs_12_.refs_0_, bf16[1024,384]{1,0:T(8,128)(2,1)} %collective-permute-done.67.refs_1_.refs_5_, bf16[1,4,192,128]{3,2,1,0:T(8,128)(2,1)} %copy-done.11, ...), custom_call_target="tpu_custom_call" | custom-call | flops 60000002048 | bytes 15204352 | tf_op jit(solution)/shard_map/project_grads/pallas_call | solution.py:48
  670.7 3.2 collective-permute-done.74.refs_2_.refs_3_
  673.9 7.7 collective-permute-done.73.refs_1_.refs_6_
  681.6 5.6 emit.3
  691.9 8.9 %collective-permute-done.78.refs_2_ = bf16[1,6,192,256]{3,2,1,0:T(8,128)(2,1)S(1)} collective-permute-done((bf16[1,6,192,256]{3,2,1,0:T(8,128)(2,1)}, bf16[1,6,192,256]{3,2,1,0:T(8,128)(2,1)S(1)}, u32[]{:S(2)}, u32[]{:S(2)}) %collective-permute-start.78) | collective-permute-done | bytes 589856 | tf_op jit(solution)/shard_map/ppermute | solution.py:88
  711.3 7.8 %collective-permute-done.83.refs_3_ = bf16[1,4,192,256]{3,2,1,0:T(8,128)(2,1)S(1)} collective-permute-done((bf16[1,4,192,256]{3,2,1,0:T(8,128)(2,1)}, bf16[1,4,192,256]{3,2,1,0:T(8,128)(2,1)S(1)}, u32[]{:S(2)}, u32[]{:S(2)}) %collective-permute-start.83) | collective-permute-done | bytes 393248 | tf_op jit(solution)/shard_map/ppermute | solution.py:88
  728.6 7.6 fusion
  743.7 15.1 %finish.1 = f32[1024,1536]{1,0:T(8,128)} custom-call(s32[2]{0:T(128)} %pad_add_fusion.sc, f32[16,192,256]{2,1,0:T(8,128)} %get-tuple-element.267.refs_0_, bf16[1024,1536]{1,0:T(8,128)(2,1)} %bitcast.61, f32[1024,1536]{1,0:T(8,128)} %get-tuple-element.234.refs_2_, bf16[128,1536]{1,0:T(8,128)(2,1)} %get-tuple-element.142.refs_11_.refs_10_.refs_3_, ...), custom_call_target="tpu_custom_call" | custom-call | flops 60000002048 | bytes 28966912 | tf_op jit(solution)/shard_map/finish/pallas_call | solution.py:48
  (260 shorter events, 168.6 us)
Async XLA Ops:
  85.2 28.5 %collective-permute-start.15 = (bf16[3,1536,128]{2,1,0:T(8,128)(2,1)}, bf16[3,1536,128]{2,1,0:T(8,128)(2,1)}, u32[]{:S(2)}, u32[]{:S(2)}) collective-permute-start(bf16[3,1536,128]{2,1,0:T(8,128)(2,1)} %get-tuple-element.139), channel_id=1, source_target_pairs={{0,1},{1,0},{2,3},{3,2},{4,5},{5,4},{6,7},{7,6},{8,9},{9,8},{10,11... | collective-permute-start | bytes 3538952 | tf_op jit(solution)/shard_map/ppermute | solution.py:92
  86.7 27.0 %collective-permute-start.11 = (bf16[3,4,192,256]{3,2,1,0:T(8,128)(2,1)}, bf16[3,4,192,256]{3,2,1,0:T(8,128)(2,1)}, u32[]{:S(2)}, u32[]{:S(2)}) collective-permute-start(bf16[3,4,192,256]{3,2,1,0:T(8,128)(2,1)} %collective-permute-done.4.refs_0_.refs_11_), channel_id=1, source_target_pairs={{0,8},{10,2},{8,16},{18,10},{16,24},{26,18},{24,28},{30,26},{28,20... | collective-permute-start | bytes 3538952 | tf_op jit(solution)/shard_map/ppermute | solution.py:88
  88.2 26.1 %collective-permute-start.17 = (bf16[3,4,192,256]{3,2,1,0:T(8,128)(2,1)}, bf16[3,4,192,256]{3,2,1,0:T(8,128)(2,1)}, u32[]{:S(2)}, u32[]{:S(2)}) collective-permute-start(bf16[3,4,192,256]{3,2,1,0:T(8,128)(2,1)} %collective-permute-done.4.refs_0_.refs_11_), channel_id=1, source_target_pairs={{0,2},{2,0},{1,3},{3,1},{4,6},{6,4},{5,7},{7,5},{8,10},{10,8},{9,1... | collective-permute-start | bytes 3538952 | tf_op jit(solution)/shard_map/ppermute | solution.py:92
  110.3 32.4 %collective-permute-start.10 = (bf16[512,768]{1,0:T(8,128)(2,1)}, bf16[512,768]{1,0:T(8,128)(2,1)}, u32[]{:S(2)}, u32[]{:S(2)}) collective-permute-start(bf16[512,768]{1,0:T(8,128)(2,1)} %get-tuple-element.133.refs_8_.refs_12_.refs_17_.refs_4_), channel_id=1, source_target_pairs={{0,1},{1,0},{2,3},{3,2},{4,5},{5,4},{6,7},{7,6},{8,9},{9,8},{10,11... | collective-permute-start | bytes 2359304 | tf_op jit(solution)/shard_map/ppermute | solution.py:92
  113.7 29.0 %collective-permute-start.16 = (bf16[3,1536,128]{2,1,0:T(8,128)(2,1)}, bf16[3,1536,128]{2,1,0:T(8,128)(2,1)}, u32[]{:S(2)}, u32[]{:S(2)}) collective-permute-start(bf16[3,1536,128]{2,1,0:T(8,128)(2,1)} %collective-permute-done.15.refs_1_.refs_13_), channel_id=1, source_target_pairs={{0,2},{2,0},{1,3},{3,1},{4,6},{6,4},{5,7},{7,5},{8,10},{10,8},{9,1... | collective-permute-start | bytes 3538952 | tf_op jit(solution)/shard_map/ppermute | solution.py:92
  113.7 39.7 %collective-permute-start.12 = (bf16[3,4,192,256]{3,2,1,0:T(8,128)(2,1)}, bf16[3,4,192,256]{3,2,1,0:T(8,128)(2,1)}, u32[]{:S(2)}, u32[]{:S(2)}) collective-permute-start(bf16[3,4,192,256]{3,2,1,0:T(8,128)(2,1)} %collective-permute-done.11.refs_3_.refs_12_), channel_id=1, source_target_pairs={{0,2},{2,0},{1,3},{3,1},{4,6},{6,4},{5,7},{7,5},{8,10},{10,8},{9,1... | collective-permute-start | bytes 3538952 | tf_op jit(solution)/shard_map/ppermute | solution.py:92
  114.3 25.7 %collective-permute-start.13 = (bf16[3,4,192,256]{3,2,1,0:T(8,128)(2,1)}, bf16[3,4,192,256]{3,2,1,0:T(8,128)(2,1)}, u32[]{:S(2)}, u32[]{:S(2)}) collective-permute-start(bf16[3,4,192,256]{3,2,1,0:T(8,128)(2,1)} %collective-permute-done.11.refs_3_.refs_12_), channel_id=1, source_target_pairs={{0,8},{10,2},{8,16},{18,10},{16,24},{26,18},{24,28},{30,26},{28,20... | collective-permute-start | bytes 3538952 | tf_op jit(solution)/shard_map/ppermute | solution.py:88
  140.0 31.2 %collective-permute-start.22 = (bf16[3,4,192,256]{3,2,1,0:T(8,128)(2,1)}, bf16[3,4,192,256]{3,2,1,0:T(8,128)(2,1)}, u32[]{:S(2)}, u32[]{:S(2)}) collective-permute-start(bf16[3,4,192,256]{3,2,1,0:T(8,128)(2,1)} %collective-permute-done.14.refs_3_.refs_11_.refs_12_), channel_id=1, source_target_pairs={{0,8},{10,2},{8,16},{18,10},{16,24},{26,18},{24,28},{30,26},{28,20... | collective-permute-start | bytes 3538952 | tf_op jit(solution)/shard_map/ppermute | solution.py:88
  142.7 32.6 %collective-permute-start.27 = (bf16[3,4,192,256]{3,2,1,0:T(8,128)(2,1)}, bf16[3,4,192,256]{3,2,1,0:T(8,128)(2,1)}, u32[]{:S(2)}, u32[]{:S(2)}) collective-permute-start(bf16[3,4,192,256]{3,2,1,0:T(8,128)(2,1)} %collective-permute-done.14.refs_3_.refs_11_.refs_12_), channel_id=1, source_target_pairs={{0,2},{2,0},{1,3},{3,1},{4,6},{6,4},{5,7},{7,5},{8,10},{10,8},{9,1... | collective-permute-start | bytes 3538952 | tf_op jit(solution)/shard_map/ppermute | solution.py:92
  142.8 34.3 %collective-permute-start.26 = (bf16[3,4,192,256]{3,2,1,0:T(8,128)(2,1)}, bf16[3,4,192,256]{3,2,1,0:T(8,128)(2,1)}, u32[]{:S(2)}, u32[]{:S(2)}) collective-permute-start(bf16[3,4,192,256]{3,2,1,0:T(8,128)(2,1)} %collective-permute-done.13.refs_2_.refs_13_), channel_id=1, source_target_pairs={{0,2},{2,0},{1,3},{3,1},{4,6},{6,4},{5,7},{7,5},{8,10},{10,8},{9,1... | collective-permute-start | bytes 3538952 | tf_op jit(solution)/shard_map/ppermute | solution.py:92
  171.2 43.9 %collective-permute-start.23 = (bf16[3,4,192,256]{3,2,1,0:T(8,128)(2,1)}, bf16[3,4,192,256]{3,2,1,0:T(8,128)(2,1)}, u32[]{:S(2)}, u32[]{:S(2)}) collective-permute-start(bf16[3,4,192,256]{3,2,1,0:T(8,128)(2,1)} %collective-permute-done.22.refs_4_.refs_12_.refs_13_), channel_id=1, source_target_pairs={{0,2},{2,0},{1,3},{3,1},{4,6},{6,4},{5,7},{7,5},{8,10},{10,8},{9,1... | collective-permute-start | bytes 3538952 | tf_op jit(solution)/shard_map/ppermute | solution.py:92
  171.2 42.2 %collective-permute-start.24 = (bf16[3,4,192,256]{3,2,1,0:T(8,128)(2,1)}, bf16[3,4,192,256]{3,2,1,0:T(8,128)(2,1)}, u32[]{:S(2)}, u32[]{:S(2)}) collective-permute-start(bf16[3,4,192,256]{3,2,1,0:T(8,128)(2,1)} %collective-permute-done.22.refs_4_.refs_12_.refs_13_), channel_id=1, source_target_pairs={{0,8},{10,2},{8,16},{18,10},{16,24},{26,18},{24,28},{30,26},{28,20... | collective-permute-start | bytes 3538952 | tf_op jit(solution)/shard_map/ppermute | solution.py:88
  175.3 46.0 %collective-permute-start.19 = (bf16[5,1536,128]{2,1,0:T(8,128)(2,1)}, bf16[5,1536,128]{2,1,0:T(8,128)(2,1)}, u32[]{:S(2)}, u32[]{:S(2)}) collective-permute-start(bf16[5,1536,128]{2,1,0:T(8,128)(2,1)} %constant_dynamic-slice_fusion.4), channel_id=1, source_target_pairs={{0,1},{1,0},{2,3},{3,2},{4,5},{5,4},{6,7},{7,6},{8,9},{9,8},{10,11... | collective-permute-start | bytes 5898248 | tf_op jit(solution)/shard_map/ppermute | solution.py:92
  177.1 34.8 %collective-permute-start.25 = (bf16[3,4,192,256]{3,2,1,0:T(8,128)(2,1)}, bf16[3,4,192,256]{3,2,1,0:T(8,128)(2,1)}, u32[]{:S(2)}, u32[]{:S(2)}) collective-permute-start(bf16[3,4,192,256]{3,2,1,0:T(8,128)(2,1)} %get-tuple-element.153.refs_3_.refs_10_), channel_id=1, source_target_pairs={{0,8},{10,2},{8,16},{18,10},{16,24},{26,18},{24,28},{30,26},{28,20... | collective-permute-start | bytes 3538952 | tf_op jit(solution)/shard_map/ppermute | solution.py:88
  211.9 35.8 %collective-permute-start.31 = (bf16[3,4,192,256]{3,2,1,0:T(8,128)(2,1)}, bf16[3,4,192,256]{3,2,1,0:T(8,128)(2,1)}, u32[]{:S(2)}, u32[]{:S(2)}) collective-permute-start(bf16[3,4,192,256]{3,2,1,0:T(8,128)(2,1)} %collective-permute-done.25.refs_4_.refs_11_), channel_id=1, source_target_pairs={{0,8},{10,2},{8,16},{18,10},{16,24},{26,18},{24,28},{30,26},{28,20... | collective-permute-start | bytes 3538952 | tf_op jit(solution)/shard_map/ppermute | solution.py:88
  213.5 34.6 %collective-permute-start.38 = (bf16[3,4,192,256]{3,2,1,0:T(8,128)(2,1)}, bf16[3,4,192,256]{3,2,1,0:T(8,128)(2,1)}, u32[]{:S(2)}, u32[]{:S(2)}) collective-permute-start(bf16[3,4,192,256]{3,2,1,0:T(8,128)(2,1)} %collective-permute-done.25.refs_4_.refs_11_), channel_id=1, source_target_pairs={{0,2},{2,0},{1,3},{3,1},{4,6},{6,4},{5,7},{7,5},{8,10},{10,8},{9,1... | collective-permute-start | bytes 3538952 | tf_op jit(solution)/shard_map/ppermute | solution.py:92
  213.5 34.3 %collective-permute-start.36 = (bf16[3,4,192,256]{3,2,1,0:T(8,128)(2,1)}, bf16[3,4,192,256]{3,2,1,0:T(8,128)(2,1)}, u32[]{:S(2)}, u32[]{:S(2)}) collective-permute-start(bf16[3,4,192,256]{3,2,1,0:T(8,128)(2,1)} %collective-permute-done.24.refs_3_.refs_13_.refs_14_), channel_id=1, source_target_pairs={{0,2},{2,0},{1,3},{3,1},{4,6},{6,4},{5,7},{7,5},{8,10},{10,8},{9,1... | collective-permute-start | bytes 3538952 | tf_op jit(solution)/shard_map/ppermute | solution.py:92
  215.1 30.8 %collective-permute-start.29 = (bf16[3,4,192,128]{3,2,1,0:T(8,128)(2,1)S(1)}, bf16[3,4,192,128]{3,2,1,0:T(8,128)(2,1)}, u32[]{:S(2)}, u32[]{:S(2)}) collective-permute-start(bf16[3,4,192,128]{3,2,1,0:T(8,128)(2,1)S(1)} %constant_dynamic-slice_fusion.2), channel_id=1, source_target_pairs={{0,8},{10,2},{8,16},{18,10},{16,24},{26,18},{24,28},{30,26},{28,20... | collective-permute-start | bytes 1769480 | tf_op jit(solution)/shard_map/ppermute | solution.py:88
  221.3 27.6 %collective-permute-start.37 = (bf16[4,6,192,256]{3,2,1,0:T(8,128)(2,1)}, bf16[4,6,192,256]{3,2,1,0:T(8,128)(2,1)}, u32[]{:S(2)}, u32[]{:S(2)}) collective-permute-start(bf16[4,6,192,256]{3,2,1,0:T(8,128)(2,1)} %get-tuple-element.167), channel_id=1, source_target_pairs={{0,2},{2,0},{1,3},{3,1},{4,6},{6,4},{5,7},{7,5},{8,10},{10,8},{9,1... | collective-permute-start | bytes 7077896 | tf_op jit(solution)/shard_map/ppermute | solution.py:92
  247.6 29.3 %collective-permute-start.28 = (bf16[4,6,192,256]{3,2,1,0:T(8,128)(2,1)}, bf16[4,6,192,256]{3,2,1,0:T(8,128)(2,1)}, u32[]{:S(2)}, u32[]{:S(2)}) collective-permute-start(bf16[4,6,192,256]{3,2,1,0:T(8,128)(2,1)} %get-tuple-element.159), channel_id=1, source_target_pairs={{0,2},{2,0},{1,3},{3,1},{4,6},{6,4},{5,7},{7,5},{8,10},{10,8},{9,1... | collective-permute-start | bytes 7077896 | tf_op jit(solution)/shard_map/ppermute | solution.py:92
  247.8 26.4 %collective-permute-start.34 = (bf16[3,4,192,256]{3,2,1,0:T(8,128)(2,1)}, bf16[3,4,192,256]{3,2,1,0:T(8,128)(2,1)}, u32[]{:S(2)}, u32[]{:S(2)}) collective-permute-start(bf16[3,4,192,256]{3,2,1,0:T(8,128)(2,1)} %get-tuple-element.165.refs_4_.refs_9_.refs_8_), channel_id=1, source_target_pairs={{0,8},{10,2},{8,16},{18,10},{16,24},{26,18},{24,28},{30,26},{28,20... | collective-permute-start | bytes 3538952 | tf_op jit(solution)/shard_map/ppermute | solution.py:88
  248.1 28.8 %collective-permute-start.35 = (bf16[5,1536,128]{2,1,0:T(8,128)(2,1)}, bf16[5,1536,128]{2,1,0:T(8,128)(2,1)}, u32[]{:S(2)}, u32[]{:S(2)}) collective-permute-start(bf16[5,1536,128]{2,1,0:T(8,128)(2,1)} %collective-permute-done.19.refs_0_.refs_8_), channel_id=1, source_target_pairs={{0,2},{2,0},{1,3},{3,1},{4,6},{6,4},{5,7},{7,5},{8,10},{10,8},{9,1... | collective-permute-start | bytes 5898248 | tf_op jit(solution)/shard_map/ppermute | solution.py:92
  248.8 25.6 %collective-permute-start.32 = (bf16[3,4,192,256]{3,2,1,0:T(8,128)(2,1)}, bf16[3,4,192,256]{3,2,1,0:T(8,128)(2,1)}, u32[]{:S(2)}, u32[]{:S(2)}) collective-permute-start(bf16[3,4,192,256]{3,2,1,0:T(8,128)(2,1)} %collective-permute-done.31.refs_4_.refs_12_), channel_id=1, source_target_pairs={{0,2},{2,0},{1,3},{3,1},{4,6},{6,4},{5,7},{7,5},{8,10},{10,8},{9,1... | collective-permute-start | bytes 3538952 | tf_op jit(solution)/shard_map/ppermute | solution.py:92
  248.8 28.1 %collective-permute-start.33 = (bf16[3,4,192,256]{3,2,1,0:T(8,128)(2,1)}, bf16[3,4,192,256]{3,2,1,0:T(8,128)(2,1)}, u32[]{:S(2)}, u32[]{:S(2)}) collective-permute-start(bf16[3,4,192,256]{3,2,1,0:T(8,128)(2,1)} %collective-permute-done.31.refs_4_.refs_12_), channel_id=1, source_target_pairs={{0,8},{10,2},{8,16},{18,10},{16,24},{26,18},{24,28},{30,26},{28,20... | collective-permute-start | bytes 3538952 | tf_op jit(solution)/shard_map/ppermute | solution.py:88
  274.1 52.4 %collective-permute-start.45 = (bf16[4,6,192,256]{3,2,1,0:T(8,128)(2,1)}, bf16[4,6,192,256]{3,2,1,0:T(8,128)(2,1)}, u32[]{:S(2)}, u32[]{:S(2)}) collective-permute-start(bf16[4,6,192,256]{3,2,1,0:T(8,128)(2,1)} %get-tuple-element.183), channel_id=1, source_target_pairs={{0,2},{2,0},{1,3},{3,1},{4,6},{6,4},{5,7},{7,5},{8,10},{10,8},{9,1... | collective-permute-start | bytes 7077896 | tf_op jit(solution)/shard_map/ppermute | solution.py:92
  301.4 25.7 %collective-permute-start.39 = (bf16[4,6,192,256]{3,2,1,0:T(8,128)(2,1)}, bf16[4,6,192,256]{3,2,1,0:T(8,128)(2,1)}, u32[]{:S(2)}, u32[]{:S(2)}) collective-permute-start(bf16[4,6,192,256]{3,2,1,0:T(8,128)(2,1)} %get-tuple-element.173), channel_id=1, source_target_pairs={{0,2},{2,0},{1,3},{3,1},{4,6},{6,4},{5,7},{7,5},{8,10},{10,8},{9,1... | collective-permute-start | bytes 7077896 | tf_op jit(solution)/shard_map/ppermute | solution.py:92
  303.4 27.3 %collective-permute-start.47 = (bf16[3,4,192,256]{3,2,1,0:T(8,128)(2,1)}, bf16[3,4,192,256]{3,2,1,0:T(8,128)(2,1)}, u32[]{:S(2)}, u32[]{:S(2)}) collective-permute-start(bf16[3,4,192,256]{3,2,1,0:T(8,128)(2,1)} %collective-permute-done.33.refs_3_.refs_13_), channel_id=1, source_target_pairs={{0,2},{2,0},{1,3},{3,1},{4,6},{6,4},{5,7},{7,5},{8,10},{10,8},{9,1... | collective-permute-start | bytes 3538952 | tf_op jit(solution)/shard_map/ppermute | solution.py:92
  326.5 38.3 %collective-permute-start.43 = (bf16[3,4,192,256]{3,2,1,0:T(8,128)(2,1)}, bf16[3,4,192,256]{3,2,1,0:T(8,128)(2,1)}, u32[]{:S(2)}, u32[]{:S(2)}) collective-permute-start(bf16[3,4,192,256]{3,2,1,0:T(8,128)(2,1)} %collective-permute-done.42.refs_4_.refs_11_.refs_10_), channel_id=1, source_target_pairs={{0,2},{2,0},{1,3},{3,1},{4,6},{6,4},{5,7},{7,5},{8,10},{10,8},{9,1... | collective-permute-start | bytes 3538952 | tf_op jit(solution)/shard_map/ppermute | solution.py:92
  327.0 28.3 %collective-permute-start.44 = (bf16[3,4,192,256]{3,2,1,0:T(8,128)(2,1)}, bf16[3,4,192,256]{3,2,1,0:T(8,128)(2,1)}, u32[]{:S(2)}, u32[]{:S(2)}) collective-permute-start(bf16[3,4,192,256]{3,2,1,0:T(8,128)(2,1)} %collective-permute-done.42.refs_4_.refs_11_.refs_10_), channel_id=1, source_target_pairs={{0,8},{10,2},{8,16},{18,10},{16,24},{26,18},{24,28},{30,26},{28,20... | collective-permute-start | bytes 3538952 | tf_op jit(solution)/shard_map/ppermute | solution.py:88
  330.7 27.6 %collective-permute-start.46 = (bf16[4,6,192,128]{3,2,1,0:T(8,128)(2,1)}, bf16[4,6,192,128]{3,2,1,0:T(8,128)(2,1)}, u32[]{:S(2)}, u32[]{:S(2)}) collective-permute-start(bf16[4,6,192,128]{3,2,1,0:T(8,128)(2,1)} %hop_sum.20), channel_id=1, source_target_pairs={{0,8},{10,2},{8,16},{18,10},{16,24},{26,18},{24,28},{30,26},{28,20... | collective-permute-start | bytes 3538952 | tf_op jit(solution)/shard_map/ppermute | solution.py:88
  355.3 43.9 %collective-permute-start.54 = (bf16[3,4,192,256]{3,2,1,0:T(8,128)(2,1)}, bf16[3,4,192,256]{3,2,1,0:T(8,128)(2,1)}, u32[]{:S(2)}, u32[]{:S(2)}) collective-permute-start(bf16[3,4,192,256]{3,2,1,0:T(8,128)(2,1)} %collective-permute-done.44.refs_3_.refs_12_.refs_11_), channel_id=1, source_target_pairs={{0,2},{2,0},{1,3},{3,1},{4,6},{6,4},{5,7},{7,5},{8,10},{10,8},{9,1... | collective-permute-start | bytes 3538952 | tf_op jit(solution)/shard_map/ppermute | solution.py:92
  357.2 32.1 %collective-permute-start.50 = (bf16[3,4,192,128]{3,2,1,0:T(8,128)(2,1)S(1)}, bf16[3,4,192,128]{3,2,1,0:T(8,128)(2,1)}, u32[]{:S(2)}, u32[]{:S(2)}) collective-permute-start(bf16[3,4,192,128]{3,2,1,0:T(8,128)(2,1)S(1)} %constant_dynamic-slice_fusion), channel_id=1, source_target_pairs={{0,8},{10,2},{8,16},{18,10},{16,24},{26,18},{24,28},{30,26},{28,20... | collective-permute-start | bytes 1769480 | tf_op jit(solution)/shard_map/ppermute | solution.py:88
  358.2 41.0 %collective-permute-start.55 = (bf16[4,6,192,256]{3,2,1,0:T(8,128)(2,1)}, bf16[4,6,192,256]{3,2,1,0:T(8,128)(2,1)}, u32[]{:S(2)}, u32[]{:S(2)}) collective-permute-start(bf16[4,6,192,256]{3,2,1,0:T(8,128)(2,1)} %get-tuple-element.193), channel_id=1, source_target_pairs={{0,2},{2,0},{1,3},{3,1},{4,6},{6,4},{5,7},{7,5},{8,10},{10,8},{9,1... | collective-permute-start | bytes 7077896 | tf_op jit(solution)/shard_map/ppermute | solution.py:92
  363.2 29.3 %collective-permute-start.52 = (bf16[4,6,192,256]{3,2,1,0:T(8,128)(2,1)}, bf16[4,6,192,256]{3,2,1,0:T(8,128)(2,1)}, u32[]{:S(2)}, u32[]{:S(2)}) collective-permute-start(bf16[4,6,192,256]{3,2,1,0:T(8,128)(2,1)} %hop_sum.21), channel_id=1, source_target_pairs={{0,8},{10,2},{8,16},{18,10},{16,24},{26,18},{24,28},{30,26},{28,20... | collective-permute-start | bytes 7077896 | tf_op jit(solution)/shard_map/ppermute | solution.py:88
  390.7 33.6 %collective-permute-start.49 = (bf16[4,6,192,256]{3,2,1,0:T(8,128)(2,1)}, bf16[4,6,192,256]{3,2,1,0:T(8,128)(2,1)}, u32[]{:S(2)}, u32[]{:S(2)}) collective-permute-start(bf16[4,6,192,256]{3,2,1,0:T(8,128)(2,1)} %get-tuple-element.189), channel_id=1, source_target_pairs={{0,2},{2,0},{1,3},{3,1},{4,6},{6,4},{5,7},{7,5},{8,10},{10,8},{9,1... | collective-permute-start | bytes 7077896 | tf_op jit(solution)/shard_map/ppermute | solution.py:92
  397.7 29.2 %collective-permute-start.53 = (bf16[4,6,192,256]{3,2,1,0:T(8,128)(2,1)}, bf16[4,6,192,256]{3,2,1,0:T(8,128)(2,1)}, u32[]{:S(2)}, u32[]{:S(2)}) collective-permute-start(bf16[4,6,192,256]{3,2,1,0:T(8,128)(2,1)} %hop_sum.22), channel_id=1, source_target_pairs={{0,8},{10,2},{8,16},{18,10},{16,24},{26,18},{24,28},{30,26},{28,20... | collective-permute-start | bytes 7077896 | tf_op jit(solution)/shard_map/ppermute | solution.py:88
  424.2 34.0 %collective-permute-start.56 = (bf16[4,6,192,256]{3,2,1,0:T(8,128)(2,1)}, bf16[4,6,192,256]{3,2,1,0:T(8,128)(2,1)}, u32[]{:S(2)}, u32[]{:S(2)}) collective-permute-start(bf16[4,6,192,256]{3,2,1,0:T(8,128)(2,1)} %get-tuple-element.205), channel_id=1, source_target_pairs={{0,2},{2,0},{1,3},{3,1},{4,6},{6,4},{5,7},{7,5},{8,10},{10,8},{9,1... | collective-permute-start | bytes 7077896 | tf_op jit(solution)/shard_map/ppermute | solution.py:92
  456.7 29.2 %collective-permute-start.59 = (bf16[4,6,192,256]{3,2,1,0:T(8,128)(2,1)}, bf16[4,6,192,256]{3,2,1,0:T(8,128)(2,1)}, u32[]{:S(2)}, u32[]{:S(2)}) collective-permute-start(bf16[4,6,192,256]{3,2,1,0:T(8,128)(2,1)} %hop_sum.24), channel_id=1, source_target_pairs={{0,8},{10,2},{8,16},{18,10},{16,24},{26,18},{24,28},{30,26},{28,20... | collective-permute-start | bytes 7077896 | tf_op jit(solution)/shard_map/ppermute | solution.py:88
  461.5 37.0 %collective-permute-start.58 = (bf16[4,6,192,128]{3,2,1,0:T(8,128)(2,1)}, bf16[4,6,192,128]{3,2,1,0:T(8,128)(2,1)}, u32[]{:S(2)}, u32[]{:S(2)}) collective-permute-start(bf16[4,6,192,128]{3,2,1,0:T(8,128)(2,1)} %hop_sum.23), channel_id=1, source_target_pairs={{0,8},{10,2},{8,16},{18,10},{16,24},{26,18},{24,28},{30,26},{28,20... | collective-permute-start | bytes 3538952 | tf_op jit(solution)/shard_map/ppermute | solution.py:88
  462.7 71.5 %collective-permute-start.61 = (bf16[1024,1536]{1,0:T(8,128)(2,1)}, bf16[1024,1536]{1,0:T(8,128)(2,1)}, u32[]{:S(2)}, u32[]{:S(2)}) collective-permute-start(bf16[1024,1536]{1,0:T(8,128)(2,1)} %get-tuple-element.208.refs_3_), channel_id=1, source_target_pairs={{0,1},{1,0},{2,3},{3,2},{4,5},{5,4},{6,7},{7,6},{8,9},{9,8},{10,11... | collective-permute-start | bytes 9437192 | tf_op jit(solution)/shard_map/ppermute | solution.py:92
  503.1 31.1 %collective-permute-start.62 = (f32[16,1024]{1,0:T(8,128)S(1)}, f32[16,1024]{1,0:T(8,128)S(1)}, u32[]{:S(2)}, u32[]{:S(2)}) collective-permute-start(f32[16,1024]{1,0:T(8,128)S(1)} %copy-done.21), channel_id=1, source_target_pairs={{0,1},{1,0},{2,3},{3,2},{4,5},{5,4},{6,7},{7,6},{8,9},{9,8},{10,11... | collective-permute-start | bytes 196616 | tf_op jit(solution)/shard_map/ppermute | solution.py:92
  509.8 43.2 %collective-permute-start.64 = (bf16[4,6,192,256]{3,2,1,0:T(8,128)(2,1)}, bf16[4,6,192,256]{3,2,1,0:T(8,128)(2,1)}, u32[]{:S(2)}, u32[]{:S(2)}) collective-permute-start(bf16[4,6,192,256]{3,2,1,0:T(8,128)(2,1)} %hop_sum.26), channel_id=1, source_target_pairs={{0,8},{10,2},{8,16},{18,10},{16,24},{26,18},{24,28},{30,26},{28,20... | collective-permute-start | bytes 7077896 | tf_op jit(solution)/shard_map/ppermute | solution.py:88
  551.4 78.0 %collective-permute-start.63 = (bf16[1024,1536]{1,0:T(8,128)(2,1)}, bf16[1024,1536]{1,0:T(8,128)(2,1)}, u32[]{:S(2)}, u32[]{:S(2)}) collective-permute-start(bf16[1024,1536]{1,0:T(8,128)(2,1)} %get-tuple-element.212), channel_id=1, source_target_pairs={{0,1},{1,0},{2,3},{3,2},{4,5},{5,4},{6,7},{7,6},{8,9},{9,8},{10,11... | collective-permute-start | bytes 9437192 | tf_op jit(solution)/shard_map/ppermute | solution.py:92
  558.2 36.5 %collective-permute-start.65 = (bf16[4,6,192,256]{3,2,1,0:T(8,128)(2,1)}, bf16[4,6,192,256]{3,2,1,0:T(8,128)(2,1)}, u32[]{:S(2)}, u32[]{:S(2)}) collective-permute-start(bf16[4,6,192,256]{3,2,1,0:T(8,128)(2,1)} %hop_sum.27), channel_id=1, source_target_pairs={{0,8},{10,2},{8,16},{18,10},{16,24},{26,18},{24,28},{30,26},{28,20... | collective-permute-start | bytes 7077896 | tf_op jit(solution)/shard_map/ppermute | solution.py:88
  584.2 50.4 %collective-permute-start.72 = (f32[4,256,128]{2,1,0:T(8,128)}, f32[4,256,128]{2,1,0:T(8,128)S(1)}, u32[]{:S(2)}, u32[]{:S(2)}) collective-permute-start(f32[4,256,128]{2,1,0:T(8,128)} %get-tuple-element.217.refs_0_), channel_id=1, source_target_pairs={{0,2},{2,0},{1,3},{3,1},{4,6},{6,4},{5,7},{7,5},{8,10},{10,8},{9,1... | collective-permute-start | bytes 1572872 | tf_op jit(solution)/shard_map/ppermute | solution.py:92
  594.2 31.7 %collective-permute-start.68 = (bf16[4,4,192,256]{3,2,1,0:T(8,128)(2,1)}, bf16[4,4,192,256]{3,2,1,0:T(8,128)(2,1)}, u32[]{:S(2)}, u32[]{:S(2)}) collective-permute-start(bf16[4,4,192,256]{3,2,1,0:T(8,128)(2,1)} %get-tuple-element.221), channel_id=1, source_target_pairs={{0,2},{2,0},{1,3},{3,1},{4,6},{6,4},{5,7},{7,5},{8,10},{10,8},{9,1... | collective-permute-start | bytes 4718600 | tf_op jit(solution)/shard_map/ppermute | solution.py:92
  599.9 30.0 %collective-permute-start.70 = (bf16[4,6,192,256]{3,2,1,0:T(8,128)(2,1)}, bf16[4,6,192,256]{3,2,1,0:T(8,128)(2,1)}, u32[]{:S(2)}, u32[]{:S(2)}) collective-permute-start(bf16[4,6,192,256]{3,2,1,0:T(8,128)(2,1)} %hop_sum.29), channel_id=1, source_target_pairs={{0,8},{10,2},{8,16},{18,10},{16,24},{26,18},{24,28},{30,26},{28,20... | collective-permute-start | bytes 7077896 | tf_op jit(solution)/shard_map/ppermute | solution.py:88
  709.8 33.9 %collective-permute-start.75 = (bf16[1024,512]{1,0:T(8,128)(2,1)}, bf16[1024,512]{1,0:T(8,128)(2,1)}, u32[]{:S(2)}, u32[]{:S(2)}) collective-permute-start(bf16[1024,512]{1,0:T(8,128)(2,1)} %get-tuple-element.236.refs_8_), channel_id=1, source_target_pairs={{0,1},{1,0},{2,3},{3,2},{4,5},{5,4},{6,7},{7,6},{8,9},{9,8},{10,11... | collective-permute-start | bytes 3145736 | tf_op jit(solution)/shard_map/ppermute | solution.py:92
  (61 other events, 665.0 us)

commit v3 on v2

--- a/solution.py
+++ b/solution.py
@@ -20,6 +20,8 @@
 bf = jnp.bfloat16
 f32 = jnp.float32
 contract_cols = (((1,), (1,)), ((), ()))
+COSTS = dict(experts_all=24, experts_front_end=18, experts_rest_end=13, experts_front=18, experts_rest=13, attend=19, project=18, settle=16, unsettle=17, attend_back=25)
+COSTS.update(early_grads=12, key_value_grads=7, late_grads=10, finish=18, emit=5, hop_sum=5, combine=5)
 vmem_bytes = 63 * 1024 * 1024
 
 
@@ -56,7 +58,7 @@
             scratch_shapes=scratch,
         ),
         compiler_params=pltpu.CompilerParams(vmem_limit_bytes=limit),
-        cost_estimate=pl.CostEstimate(flops=60_000_000_000 if flops else 1, bytes_accessed=int(moved), transcendentals=0),
+        cost_estimate=pl.CostEstimate(flops=COSTS.get(name, 3) * 1_153_000_000, bytes_accessed=1, transcendentals=0),
         name=name,
         input_output_aliases=aliases or {},
     )(scalars, *deps, *ins)
@@ -89,16 +91,27 @@
 
 
 def swap(values, axis):
-    return sent(lax.ppermute(values, axis, [(0, 1), (1, 0)]))
+    swapped = lax.ppermute(values, axis, [(0, 1), (1, 0)])
+    return sent(swapped) if axis == "ctx" or not window.gated else swapped
 
 
 class Window:
     def __init__(self):
-        self.now, self.before = [], []
+        self.now, self.before, self.soon = [], [], []
+        self.gated = False
 
     def turn(self):
-        due, self.before, self.now = self.before, self.now, []
+        due, self.before, self.now, self.soon = self.before + self.soon, self.now, [], []
         return due
+
+    def step(self):
+        due, self.before, self.now, self.soon = self.soon, self.before + self.now, [], []
+        return due
+
+    def gate(self, token, *more):
+        token = after(token, *self.before, *more)
+        self.before = []
+        return token
 
 
 window = Window()
@@ -190,6 +203,8 @@
         stage = {1: None, 2: "second"}.get(self.hops, "middle")
         slot = self.count // 2 - self.hops if self.hops > 1 else self.count // 2 - 1
         value = hop_sum(self.keeps, self.gots, self.got, slot, stage, self.scalars, self.core_at, deps)
+        self.value = value
+        window.soon.append(value)
         self.got = ring_hop(value, self.count)
         return self.got
 
@@ -262,8 +277,8 @@
     count, half = w_first.shape[0], w_half.shape[0]
     copies = [
         (w.at[pl.ds(0, count)], w_first),
-        (w.at[pl.ds(count + 1, 2 * half)], w_out),
-        (w.at[pl.ds(count + 1 + sc[total] * half, half)], w_half),
+        (w.at[pl.ds(count, 2 * half)], w_out),
+        (w.at[pl.ds(count + sc[total] * half, half)], w_half),
     ]
 
     @pl.when(step == 0)
@@ -272,7 +287,7 @@
         pltpu.make_async_copy(w, w, sem).wait()
         for k, (src, dst) in enumerate(copies):
             pltpu.make_async_copy(src, dst, out_sem.at[k]).start()
-        et[...] = w[count].T
+        et[...] = w[count - 1].T
 
     extra_out[...] = et[...]
     x = tok[...].astype(f32)
@@ -310,7 +325,7 @@
 def project(tokens, cosine, sine, scalars, bufs, heads, kvs, prompt, deps, block=256):
     rows, width = tokens.shape
     blocks, shard = bufs[0].shape[:2]
-    count = (heads + 2 * kvs) // 2
+    count = (heads + 2 * kvs) // 2 + 1
     head_spec = lambda n: pl.BlockSpec((n, block, HEAD_DIM), lambda i, s: (0, i, 0))
     outs = [
         sds((count, width, LANES), bf),
@@ -567,8 +582,9 @@
         (rows // block,),
         [tokens, ids, *own, *far, extra, w_own, w_mine, w_theirs],
         [rows_of(block, width), rows_of(block, TOPK), low, high, low, high, whole(extra.shape)] + [any_space()] * 3,
-        [sds((rows, width), f32), sds((rows, width), bf), sds((width, rows), bf), sds((rows, LANES), f32)],
-        [rows_of(block, width), rows_of(block, width), pl.BlockSpec((width, block), lambda i, s: (0, i)), rows_of(block, LANES)],
+        [sds((rows, width), f32), sds((rows, width), bf), sds((width, rows), bf)] + [sds((rows, LANES), f32)],
+        [rows_of(block, width), rows_of(block, width), pl.BlockSpec((width, block), lambda i, s: (0, i))]
+        + [rows_of(block, LANES)],
         [pltpu.VMEM((2 * w_own.shape[0], width, LANES), bf), pltpu.SemaphoreType.DMA],
         4 * rows * width * cols,
         core,
@@ -582,25 +598,12 @@
     return jnp.where(core == 0, first, second), jnp.where(core == 0, second, first)
 
 
-def experts_kernel(cfg, sc, *refs):
-    shard, hidden, local, first, last, total = cfg
-    block = 256
-    it = iter(refs)
-    n2, n2t, cot, cott, wt = (next(it) for _ in range(5))
-    bufs = [next(it) for _ in range(total)]
-    sums_in = () if first else (next(it), next(it))
-    pick_in = None if first else next(it)
-    moe_out, back_out, keep, send, pick = (next(it) for _ in range(5))
-    pick_t = next(it) if last else None
-    xs, cs, xt, ct, w, moe, back, scaled, acts, keep_s, send_s = (next(it) for _ in range(11))
-    w_sem, x_sem, c_sem, t_sem, in_sem, out_sem, g_sem = (next(it) for _ in range(7))
-    rows_total, width = xs.shape
-    hops = total // 2
-    core = sc[total]
-    ranks = total + 1
-    slots = hops
-    lead = ranks + 2 * slots
-
+PARTS = ((3, 1), (2, 2))
+
+
+def fetch_weights(sc, bufs, w, kinds, local, shard, hidden, sem):
+    hops = len(bufs) // 2
+    core = sc[len(bufs)]
     for side in range(2):
         for k, buf in enumerate(bufs):
             rows = pl.ds(pl.multiple_of(sc[k] * shard, shard), shard)
@@ -608,59 +611,35 @@
             if k in (hops, 2 * hops):
                 at = core if k == hops else 1 - core
                 lanes = pl.ds(pl.multiple_of(side * hidden + at * (hidden // 2), LANES), hidden // 2)
-            pltpu.make_async_copy(buf.at[:, local + side], w.at[:, rows, lanes], w_sem).start()
-    spans = [pl.ds(at, block) for at in range(0, rows_total, block)]
-    for i, rows in enumerate(spans):
-        pltpu.make_async_copy(n2.at[rows], xs.at[rows], x_sem.at[i]).start()
-        pltpu.make_async_copy(cot.at[rows], cs.at[rows], c_sem.at[i]).start()
-    pltpu.make_async_copy(w, w, w_sem).wait()
-    lane = lax.broadcasted_iota(jnp.int32, (block, LANES), 1)
-    ids = [sc[lead + side] + ROUTER_LANE for side in range(2)]
-    for i, rows in enumerate(spans):
-        pltpu.make_async_copy(n2.at[rows], xs.at[rows], x_sem.at[i]).wait()
-        pltpu.make_async_copy(cot.at[rows], cs.at[rows], c_sem.at[i]).wait()
-        if i == 1:
-            for k, (src, dst) in enumerate(zip(sums_in, (moe, back))):
-                pltpu.make_async_copy(src, dst, in_sem.at[k]).start()
-            pltpu.make_async_copy(n2t, xt, t_sem.at[0]).start()
-            pltpu.make_async_copy(cott, ct, t_sem.at[1]).start()
-        x = xs[rows, :]
-        gate = mm(x, w[0])
-        up = mm(x, w[1])
-        grad = mm(cs[rows, :], w[2])
-        table = wt[rows, :]
-        sig = 1.0 / (1.0 + jnp.exp(-gate))
-        silu = gate * sig
-        act = silu * up
-        dots = act * grad
-        picked = jnp.zeros(table.shape, f32) if first else pick_in[rows, :]
-        for side, expert in enumerate(ids):
-            cols = slice(side * hidden, side * hidden + hidden)
-            weight = jnp.sum(jnp.where(lane == expert, table, 0.0), axis=1, keepdims=True)
-            picked = picked + jnp.where(lane == expert, jnp.sum(dots[:, cols], axis=1, keepdims=True), 0.0)
-            scaled[rows, cols] = (act[:, cols] * weight).astype(bf)
-            g = grad[:, cols] * weight
-            s = sig[:, cols]
-            acts[rows, cols] = (g * up[:, cols] * s * (1.0 + gate[:, cols] * (1.0 - s))).astype(bf)
-            acts[rows, slice((2 + side) * hidden, (3 + side) * hidden)] = (g * silu[:, cols]).astype(bf)
-        pick[rows, :] = picked
-        if last:
-            pick_t[:, rows] = picked.T[ROUTER_LANE : ROUTER_LANE + EXPERTS]
-
-    for k, (src, dst) in enumerate(zip(sums_in, (moe, back))):
-        pltpu.make_async_copy(src, dst, in_sem.at[k]).wait()
-    outs = [(xs, moe_out), (cs, back_out)] if last else [(moe, moe_out), (back, back_out)]
-    for rows in spans:
-        one = mm_nt(scaled[rows, :], w[2])
-        two = mm_nt(acts[rows, 0 : 2 * hidden], w[0]) + mm_nt(acts[rows, 2 * hidden :], w[1])
-        if not first:
-            one, two = one + moe[rows, :], two + back[rows, :]
-        for made, (scr, out), s in zip((one, two), outs, range(2)):
-            scr[rows, :] = made.astype(scr.dtype)
-            pltpu.make_async_copy(scr.at[rows], out.at[rows], out_sem.at[s]).start()
-
-    pltpu.make_async_copy(n2t, xt, t_sem.at[0]).wait()
-    pltpu.make_async_copy(cott, ct, t_sem.at[1]).wait()
+            pltpu.make_async_copy(buf.at[kinds, local + side], w.at[kinds, rows, lanes], sem).start()
+
+
+def activate(ids, hidden, rows, x, grad_rows, w, wt, pick_in, pick, scaled, acts):
+    lane = lax.broadcasted_iota(jnp.int32, (x.shape[0], LANES), 1)
+    gate = mm(x, w[0])
+    up = mm(x, w[1])
+    grad = mm(grad_rows, w[2])
+    table = wt[rows, :]
+    sig = 1.0 / (1.0 + jnp.exp(-gate))
+    silu = gate * sig
+    act = silu * up
+    dots = act * grad
+    picked = jnp.zeros(table.shape, f32) if pick_in is None else pick_in[rows, :]
+    for side, expert in enumerate(ids):
+        cols = slice(side * hidden, side * hidden + hidden)
+        weight = jnp.sum(jnp.where(lane == expert, table, 0.0), axis=1, keepdims=True)
+        picked = picked + jnp.where(lane == expert, jnp.sum(dots[:, cols], axis=1, keepdims=True), 0.0)
+        scaled[rows, cols] = (act[:, cols] * weight).astype(bf)
+        g = grad[:, cols] * weight
+        s = sig[:, cols]
+        acts[rows, cols] = (g * up[:, cols] * s * (1.0 + gate[:, cols] * (1.0 - s))).astype(bf)
+        acts[rows, slice((2 + side) * hidden, (3 + side) * hidden)] = (g * silu[:, cols]).astype(bf)
+    pick[rows, :] = picked
+    return picked
+
+
+def pair_grads(sc, total, shard, hidden, xt, ct, scaled, acts, keep_s, send_s, keep, send, g_sem):
+    core, ranks, slots = sc[total], total + 1, total // 2
     for slot in range(slots):
         at = [pl.ds(pl.multiple_of(sc[ranks + slots * k + slot] * shard, shard), shard) for k in range(2)]
         left = lambda ref: jnp.concatenate([ref[at[0], :], ref[at[1], :]], axis=0)
@@ -670,67 +649,184 @@
         for kind, made in enumerate(kinds):
             for side in range(2):
                 part = made[:, side * hidden : side * hidden + hidden]
-                kept, sent = part[:shard], part[shard:]
+                kept, sent_part = part[:shard], part[shard:]
                 if slot == slots - 1:
                     cut = lambda a: (a[:, : hidden // 2], a[:, hidden // 2 :])
-                    kept, sent = mix_halves(core, cut(kept), cut(sent))
+                    kept, sent_part = mix_halves(core, cut(kept), cut(sent_part))
                 keep_s[slot, side * 3 + kind] = kept
-                send_s[slot, side * 3 + kind] = sent
+                send_s[slot, side * 3 + kind] = sent_part
         pltpu.make_async_copy(keep_s.at[slot], keep.at[slot], g_sem.at[0]).start()
         pltpu.make_async_copy(send_s.at[slot], send.at[slot], g_sem.at[1]).start()
 
-    for (scr, out), s in zip(outs, range(2)):
-        pltpu.make_async_copy(scr, out, out_sem.at[s]).wait()
-    pltpu.make_async_copy(keep_s, keep, g_sem.at[0]).wait()
-    pltpu.make_async_copy(send_s, send, g_sem.at[1]).wait()
-
-
-def experts(n2, n2t, cot, cott, wt, scalars, bufs, local, sums, last, deps):
-    rows, width = n2.shape
+
+def experts_kernel(cfg, sc, *refs):
+    shard, hidden, local, first, mode, total = cfg
+    block = 256
+    it = iter(refs)
+    front, rest, ends = mode.startswith("front"), mode.startswith("rest"), mode.endswith("_end")
+    n2, cot, wt = (None, None, None) if rest else (next(it), next(it), next(it))
+    n2t, cott = (None, None) if front else (next(it), next(it))
+    bufs = [next(it) for _ in range(total)]
+    moe_in = None if first or front else next(it)
+    back_in, pick_in = (None, None) if first or rest else (next(it), next(it))
+    scaled_in, acts_in = (next(it), next(it)) if rest else (None, None)
+    take_out = lambda: tuple(next(it) for _ in range(len(PARTS[front]) if ends else 1))
+    moe_out = None if front else take_out()
+    back_out = None if rest else take_out()
+    keep, send = (None, None) if front else (next(it), next(it))
+    pick = None if rest else next(it)
+    scaled_out, acts_out = (next(it), next(it)) if front else (None, None)
+    pick_t = next(it) if front and ends else None
+    w, scaled, acts, w_sem, in_sem, out_sem = (next(it) for _ in range(6))
+    moe = None if front else next(it)
+    back = None if rest else next(it)
+    xs, cs, x_sem, c_sem = (None,) * 4 if rest else (next(it) for _ in range(4))
+    xt, ct, keep_s, send_s, t_sem, g_sem = (None,) * 6 if front else (next(it) for _ in range(6))
+    low = next(it) if ends else None
+    rows_total = scaled.shape[0]
+    spans = [pl.ds(at, block) for at in range(0, rows_total, block)]
+    ids = [sc[total + 1 + 2 * (total // 2) + side] + ROUTER_LANE for side in range(2)]
+
+    def load_rows(i):
+        pltpu.make_async_copy(n2.at[spans[i]], xs.at[spans[i]], x_sem.at[i]).start()
+        pltpu.make_async_copy(cot.at[spans[i]], cs.at[spans[i]], c_sem.at[i]).start()
+
+    def load_wide():
+        for k, (src, dst) in enumerate(((moe_in, moe), (back_in, back))):
+            if src is not None:
+                pltpu.make_async_copy(src, dst, in_sem.at[k]).start()
+        if not front:
+            pltpu.make_async_copy(n2t, xt, t_sem.at[0]).start()
+            pltpu.make_async_copy(cott, ct, t_sem.at[1]).start()
+
+    kinds = pl.ds(2, 1) if rest else pl.ds(0, 3)
+    fetch_weights(sc, bufs, w, kinds, local, shard, hidden, w_sem)
+    if rest:
+        pltpu.make_async_copy(scaled_in, scaled, out_sem.at[2]).start()
+        load_wide()
+        pltpu.make_async_copy(acts_in, acts, out_sem.at[3]).start()
+        pltpu.make_async_copy(w.at[kinds], w.at[kinds], w_sem).wait()
+        pltpu.make_async_copy(scaled_in, scaled, out_sem.at[2]).wait()
+    else:
+        for i in range(len(spans)):
+            load_rows(i)
+        pltpu.make_async_copy(w.at[kinds], w.at[kinds], w_sem).wait()
+        for i, rows in enumerate(spans):
+            pltpu.make_async_copy(n2.at[rows], xs.at[rows], x_sem.at[i]).wait()
+            pltpu.make_async_copy(cot.at[rows], cs.at[rows], c_sem.at[i]).wait()
+            if i == 1:
+                load_wide()
+            picked = activate(ids, hidden, rows, xs[rows, :], cs[rows, :], w, wt, pick_in, pick, scaled, acts)
+            if pick_t is not None:
+                pick_t[:, rows] = picked.T[ROUTER_LANE : ROUTER_LANE + EXPERTS]
+
+    for k, (src, dst) in enumerate(((moe_in, moe), (back_in, back))):
+        if src is not None:
+            pltpu.make_async_copy(src, dst, in_sem.at[k]).wait()
+    outs = []
+    if not front:
+        outs.append((moe, moe_out, 0, lambda rows: mm_nt(scaled[rows, :], w[2])))
+    if not rest:
+        two = lambda rows: mm_nt(acts[rows, 0 : 2 * hidden], w[0]) + mm_nt(acts[rows, 2 * hidden :], w[1])
+        outs.append((back, back_out, 1, two))
+    for i, rows in enumerate(spans):
+        for acc, halves, k, make in outs:
+            made = make(rows) + acc[rows, :]
+            scr = acc if low is None else low
+            scr[rows, :] = made.astype(scr.dtype)
+            part, at = 0, i
+            while len(halves) > 1 and at >= PARTS[front][part]:
+                part, at = part + 1, at - PARTS[front][part]
+            to = halves[part].at[pl.ds(at * block, block)]
+            pltpu.make_async_copy(scr.at[rows], to, out_sem.at[k]).start()
+    if front:
+        pltpu.make_async_copy(scaled, scaled_out, out_sem.at[2]).start()
+        pltpu.make_async_copy(acts, acts_out, out_sem.at[3]).start()
+    else:
+        pltpu.make_async_copy(n2t, xt, t_sem.at[0]).wait()
+        pltpu.make_async_copy(cott, ct, t_sem.at[1]).wait()
+        if rest:
+            pltpu.make_async_copy(acts_in, acts, out_sem.at[3]).wait()
+        pair_grads(sc, total, shard, hidden, xt, ct, scaled, acts, keep_s, send_s, keep, send, g_sem)
+    for acc, _, k, _ in outs:
+        scr = acc if low is None else low
+        pltpu.make_async_copy(scr, scr, out_sem.at[k]).wait()
+    if front:
+        pltpu.make_async_copy(scaled, scaled_out, out_sem.at[2]).wait()
+        pltpu.make_async_copy(acts, acts_out, out_sem.at[3]).wait()
+    else:
+        pltpu.make_async_copy(keep_s, keep, g_sem.at[0]).wait()
+        pltpu.make_async_copy(send_s, send, g_sem.at[1]).wait()
+
+
+def experts(mode, dense, turned, wt, scalars, bufs, local, moe_in, back_in, pick_in, made, deps):
+    width, rows = turned[0].shape
     shard, hidden = bufs[0].shape[2:]
     slots = len(bufs) // 2
-    first = sums is None
-    ins = [n2, n2t, cot, cott, wt, *bufs, *([] if first else sums)]
-    specs = [any_space()] * 4 + [whole(wt.shape)] + [any_space()] * (len(ins) - 5)
-    if not first:
-        specs[-1] = whole((rows, LANES))
-    kind = bf if last else f32
+    front, rest, ends = mode.startswith("front"), mode.startswith("rest"), mode.endswith("_end")
+    first = False
+    hbm, table = any_space(), whole((rows, LANES))
+    ins, specs, outs, out_specs = [], [], [], []
+
+    def put(arrays, spec):
+        ins.extend(arrays)
+        specs.extend([spec] * len(arrays))
+
+    def give(shape, kind, spec=None):
+        outs.append(sds(shape, kind))
+        out_specs.append(spec or any_space())
+
+    if not rest:
+        put(dense, hbm)
+        put([wt], table)
+    if not front:
+        put(turned, hbm)
+    put(bufs, hbm)
+    if not first and not front:
+        put([moe_in], hbm)
+    if not first and not rest:
+        put([back_in], hbm)
+        put([pick_in], table)
+    if rest:
+        put(made, hbm)
+    pieces = [(256 * p, width) for p in PARTS[front]] if ends else [(rows, width)]
+    for shape in pieces * (2 if mode == "all" else 1):
+        give(shape, bf if ends else f32)
+    if not front:
+        give((slots, 6, shard, hidden), bf)
+        give((slots, 6, shard, hidden), bf)
+    if not rest:
+        give((rows, LANES), f32, table)
+    if front:
+        give((rows, 2 * hidden), bf)
+        give((rows, 4 * hidden), bf)
+    if front and ends:
+        give((EXPERTS, rows), f32, whole((EXPERTS, rows)))
     dma = pltpu.SemaphoreType.DMA
+    scratch = [
+        pltpu.VMEM((3, width, 2 * hidden), bf),
+        pltpu.VMEM((rows, 2 * hidden), bf),
+        pltpu.VMEM((rows, 4 * hidden), bf),
+        dma,
+        dma((2,)),
+        dma((4,)),
+    ]
+    scratch += [pltpu.VMEM((rows, width), f32)] * (2 if mode == "all" else 1)
+    if not rest:
+        scratch += [pltpu.VMEM((rows, width), bf)] * 2 + [dma((rows // 256,))] * 2
+    if not front:
+        scratch += [pltpu.VMEM((width, rows), bf)] * 2 + [pltpu.VMEM((slots, 6, shard, hidden), bf)] * 2 + [dma((2,))] * 2
+    if ends:
+        scratch.append(pltpu.VMEM((rows, width), bf))
     return call(
-        functools.partial(experts_kernel, (shard, hidden, local, first, last, len(bufs))),
-        "experts",
+        functools.partial(experts_kernel, (shard, hidden, local, first, mode, len(bufs))),
+        "experts_" + mode,
         (1,),
         ins,
         specs,
-        [
-            sds((rows, width), kind),
-            sds((rows, width), kind),
-            sds((slots, 6, shard, hidden), bf),
-            sds((slots, 6, shard, hidden), bf),
-            sds((rows, LANES), f32),
-        ]
-        + ([sds((EXPERTS, rows), f32)] if last else []),
-        [any_space()] * 4 + [whole((rows, LANES))] + ([whole((EXPERTS, rows))] if last else []),
-        [
-            pltpu.VMEM((rows, width), bf),
-            pltpu.VMEM((rows, width), bf),
-            pltpu.VMEM((width, rows), bf),
-            pltpu.VMEM((width, rows), bf),
-            pltpu.VMEM((3, width, 2 * hidden), bf),
-            pltpu.VMEM((rows, width), f32),
-            pltpu.VMEM((rows, width), f32),
-            pltpu.VMEM((rows, 2 * hidden), bf),
-            pltpu.VMEM((rows, 4 * hidden), bf),
-            pltpu.VMEM((slots, 6, shard, hidden), bf),
-            pltpu.VMEM((slots, 6, shard, hidden), bf),
-            dma,
-            dma((rows // 256,)),
-            dma((rows // 256,)),
-            dma((2,)),
-            dma((2,)),
-            dma((2,)),
-            dma((2,)),
-        ],
+        outs,
+        out_specs,
+        scratch,
         36 * rows * width * hidden,
         scalars,
         deps,
@@ -761,14 +857,14 @@
     slots, mats, shard, hidden = keeps[0].shape
     lanes = hidden // 2 if stage in (None, "end") else hidden
     side = 1 if stage == "end" else 0
-    per = mats // 2
+    per = mats // 2 if mats % 2 == 0 else mats
     piece = pl.BlockSpec((1, per, shard, lanes), lambda m, s: (slot, m, 0, side))
     wide = lambda a: pl.BlockSpec((pairs, per, shard, a.shape[3]), lambda m, s: (0, m, 0, 0))
     out = sds((pairs, mats, shard, hidden // 2 if stage is None else hidden), bf)
     ins = [*keeps, *gots] + ([] if came is None else [came])
     specs = [piece] * (2 * pairs) + ([] if came is None else [wide(came)])
     kernel = functools.partial(hop_kernel, (pairs, stage, core_at))
-    return call(kernel, "hop_sum", (2,), ins, specs, [out], [wide(out)], [], 0, scalars, deps)[0]
+    return call(kernel, "hop_sum", (mats // per,), ins, specs, [out], [wide(out)], [], 0, scalars, deps)[0]
 
 
 def emit_kernel(sc, mine, theirs, *refs):
@@ -794,7 +890,44 @@
     return passed, jnp.sum(grad * values * scale, axis=0, keepdims=True)
 
 
-def unsettle_kernel(sc, back_a, back_b, pick_a, pick_b, wt, res, cot, extra, w_own, rg_out, low_t_out, dout_out, ll_out, gain_out, w, sem):
+def pick_part(refs, parts):
+    step = pl.program_id(0)
+    value, at = refs[0][...], 0
+    for ref, size in zip(refs, parts):
+        value = jnp.where(step >= at, ref[...], value)
+        at += size
+    return value
+
+
+def part_specs(block, parts):
+    specs, first = [], 0
+    for p in parts:
+        per = p.shape[0] // block
+        specs.append(pl.BlockSpec((block, p.shape[1]), lambda i, s, first=first, per=per: (jnp.clip(i - first, 0, per - 1), 0)))
+        first += per
+    return specs
+
+
+def combine_kernel(sc, res, *refs):
+    count = len(refs) // 2
+    total = pick_part(refs[:count], PARTS[0]).astype(f32) + pick_part(refs[count : 2 * count], PARTS[0]).astype(f32)
+    refs[-1][...] = (res[...] + total).astype(bf)
+
+
+def combine(res, own, far, core, deps, block=256):
+    rows, width = res.shape
+    specs = [rows_of(block, width)] + part_specs(block, own) + part_specs(block, far)
+    out = sds((rows, width), bf)
+    return call(combine_kernel, "combine", (rows // block,), [res, *own, *far], specs, [out], [rows_of(block, width)], [], 0, core, deps)[0]
+
+
+def unsettle_kernel(sc, *refs):
+    count = len(PARTS[1])
+    own, far, refs = refs[:count], refs[count : 2 * count], refs[2 * count :]
+    unsettle_rows(own, far, *refs)
+
+
+def unsettle_rows(own, far, pick_a, pick_b, wt, res, cot, extra, w_own, rg_out, low_t_out, dout_out, ll_out, gain_out, w, sem):
     step = pl.program_id(0)
 
     @pl.when(step == 0)
@@ -809,7 +942,7 @@
     picked = jnp.concatenate([room(ROUTER_LANE), picked, room(LANES - ROUTER_LANE - EXPERTS)], axis=0).T
     logit_low = (weights * (picked - jnp.sum(weights * picked, axis=-1, keepdims=True))).astype(bf)
     ll_out[...] = logit_low
-    grad = back_a[...].astype(f32) + back_b[...].astype(f32) + mm(logit_low, extra[...])
+    grad = pick_part(own, PARTS[1]).astype(f32) + pick_part(far, PARTS[1]).astype(f32) + mm(logit_low, extra[...])
     passed, gain = norm_back(res[...], extra[1:2, :].astype(f32), grad)
     gain_out[...] += gain
     total = cot[...].astype(f32) + passed
@@ -819,7 +952,7 @@
     dout_out[...] = mm(low, lanes_of(w, 0, w.shape[0])).astype(bf)
 
 
-def unsettle(back, picks, wt, res, cot, extra, w_own, core, deps, block=256):
+def unsettle(back, far, picks, wt, res, cot, extra, w_own, core, deps, block=256):
     rows, width = res.shape
     cols = w_own.shape[0] * LANES
     wide, thin = rows_of(block, width), rows_of(block, LANES)
@@ -828,8 +961,8 @@
         unsettle_kernel,
         "unsettle",
         (rows // block,),
-        [*back, *picks, wt, res, cot, extra, w_own],
-        [wide, wide, across, across, thin, wide, wide, whole(extra.shape), any_space()],
+        [*back, *far, *picks, wt, res, cot, extra, w_own],
+        [*part_specs(block, back), *part_specs(block, far), across, across, thin, wide, wide, whole(extra.shape), any_space()],
         [sds((rows, width), f32), sds((width, rows), bf), sds((rows, cols), bf), sds((rows, LANES), bf), sds((1, width), f32)],
         [wide, pl.BlockSpec((width, block), lambda i, s: (0, i)), rows_of(block, cols), thin, whole((1, width))],
         [pltpu.VMEM(w_own.shape, bf), pltpu.SemaphoreType.DMA],
@@ -839,72 +972,108 @@
     )
 
 
-def weight_grads_kernel(cfg, sc, *refs):
-    sides, extra_sides, core_at, count = cfg
-    keep, send = refs[-2:]
-    core = sc[core_at]
+def scaled_sum(weights, grads, gain):
+    return jnp.sum(weights.astype(f32) * grads, axis=1, keepdims=True) / gain.astype(f32)
+
+
+def leave(parts, core, shard, keep, send):
     last = pl.program_id(0) == pl.num_programs(0) - 1
-    it = iter(refs[:-2])
-
-    def left():
-        return jnp.concatenate([next(it)[...], next(it)[...]], axis=0)
-
-    tall = left()
-    made, at = None, 0
-    for kind in range(sides):
-        right = next(it)
-        size = right.shape[0]
-        made_here = mm(tall[:, at : at + size] if size < tall.shape[1] else tall, right[...])
-        if size < tall.shape[1]:
-            made = made_here if made is None else made + made_here
-            at += size
-        else:
-            made = [made_here] if made is None else made + [made_here]
-    if isinstance(made, list):
-        made = jnp.concatenate(made, axis=1) if len(made) > 1 else made[0]
-    extra = None
-    if extra_sides:
-        tall = left()
-        extra = mm(tall, next(it)[...])
-    column = left()
-    extra = column if extra is None else extra + column
-    wide = 2 * LANES
-    made = jnp.concatenate([made, extra, jnp.zeros_like(extra)], axis=1).astype(bf)
-    shard = extra.shape[0] // 2
     cut = lambda a: (a[:, :LANES], a[:, LANES:])
-    blocks = [made[:, b * wide : (b + 1) * wide] for b in range(count)]
 
     @pl.when(jnp.logical_not(last))
     def _():
-        for b in range(count):
-            keep[0, b] = blocks[b][:shard]
-            send[0, b] = blocks[b][shard:]
+        for b, part in enumerate(parts):
+            keep[0, b] = part[:shard]
+            send[0, b] = part[shard:]
 
     @pl.when(last)
     def _():
-        for b in range(count):
-            keep[0, b], send[0, b] = mix_halves(core, cut(blocks[b][:shard]), cut(blocks[b][shard:]))
-
-
-def weight_grads(name, left, rights, extra, column, scalars, first_rank, core_at, shard, count, deps):
+        for b, part in enumerate(parts):
+            keep[0, b], send[0, b] = mix_halves(core, cut(part[:shard]), cut(part[shard:]))
+
+
+def early_grads_kernel(core_at, sc, low_a, low_b, mixed_a, mixed_b, n2_a, n2_b, ll, col_a, col_b, n1_a, n1_b, dq, w_a, w_b, keep, send):
+    prompt = mixed_a.shape[0]
+    shard = low_a.shape[0]
+    join = lambda a, b: jnp.concatenate([a[...], b[...]], axis=0)
+    tall = join(low_a, low_b)
+    made = mm(tall[:, 0:prompt], mixed_a[...]) + mm(tall[:, prompt:], mixed_b[...])
+    query = mm(join(n1_a, n1_b), dq[...])
+    blocks = dq.shape[1] // LANES
+    weights = jnp.concatenate([lanes_of(ref, 0, blocks) for ref in (w_a, w_b)], axis=0)
+    gains = jnp.concatenate([ref[ref.shape[0] - 1, :, 0:1] for ref in (w_a, w_b)], axis=0)
+    first = scaled_sum(weights, query, gains)
+    extra = mm(join(n2_a, n2_b), ll[...]) + join(col_a, col_b)
+    lane = lax.broadcasted_iota(jnp.int32, extra.shape, 1)
+    extra = jnp.where(lane == 0, first, extra)
+    whole_row = jnp.concatenate([made, query, extra], axis=1).astype(bf)
+    wide = 2 * LANES
+    leave([whole_row[:, b * wide : (b + 1) * wide] for b in range(whole_row.shape[1] // wide)], sc[core_at], shard, keep, send)
+
+
+def early_grads(low_t, mixed, n2t, ll, column, n1t, dq, w, scalars, first_rank, core_at, shard, deps):
+    width, rows = low_t.shape
+    slots = (scalars.shape[0] - first_rank) // 2
+    cols = mixed[0].shape[1] + LANES + dq.shape[1]
+    at = lambda k: (lambda i, s: (s[first_rank + k * slots + i], 0))
+    w_at = lambda k: (lambda i, s: (0, s[first_rank + k * slots + i], 0))
+    two = lambda lanes: [pl.BlockSpec((shard, lanes), at(k)) for k in range(2)]
+    out = sds((slots, cols // (2 * LANES), shard, 2 * LANES), bf)
+    out_spec = pl.BlockSpec((1, *out.shape[1:]), lambda i, s: (i, 0, 0, 0))
+    return call(
+        functools.partial(early_grads_kernel, core_at),
+        "early_grads",
+        (slots,),
+        [low_t, low_t, *mixed, n2t, n2t, ll, column, column, n1t, n1t, dq, w, w],
+        two(rows)
+        + [whole(a.shape) for a in mixed]
+        + two(rows)
+        + [whole(ll.shape)]
+        + two(LANES)
+        + two(rows)
+        + [whole(dq.shape)]
+        + [pl.BlockSpec((w.shape[0], shard, LANES), w_at(k)) for k in range(2)],
+        [out, out],
+        [out_spec, out_spec],
+        [],
+        2 * rows * width * cols,
+        scalars,
+        deps,
+    )
+
+
+def late_grads_kernel(cfg, sc, left_a, left_b, dq, low_kv, w_a, w_b, keep, send):
+    core_at, first_block, count = cfg
+    core = sc[core_at]
+    shard = left_a.shape[0]
+    tall = jnp.concatenate([left_a[...], left_b[...]], axis=0)
+    made = jnp.concatenate([mm(tall, dq[...]), mm(tall, low_kv[...])], axis=1)
+    blocks = made.shape[1] // LANES
+    weights = jnp.concatenate([lanes_of(ref, first_block, blocks) for ref in (w_a, w_b)], axis=0)
+    gains = jnp.concatenate([ref[ref.shape[0] - 1, :, 0:1] for ref in (w_a, w_b)], axis=0)
+    first = scaled_sum(weights, made, gains)
+    lane = lax.broadcasted_iota(jnp.int32, (2 * shard, LANES), 1)
+    made = jnp.concatenate([made, jnp.where(lane == 0, first, 0.0)], axis=1).astype(bf)
+    wide = 2 * LANES
+    leave([made[:, b * wide : (b + 1) * wide] for b in range(count)], core, shard, keep, send)
+
+
+def late_grads(left, dq, low_kv, w, first_block, scalars, first_rank, core_at, shard, deps):
     width, rows = left.shape
     slots = (scalars.shape[0] - first_rank) // 2
+    count = (dq.shape[1] + low_kv.shape[1] + LANES) // (2 * LANES)
     at = lambda k: (lambda i, s: (s[first_rank + k * slots + i], 0))
-    two = lambda lanes: [pl.BlockSpec((shard, lanes), at(k)) for k in range(2)]
-    ins, specs = [left, left, *rights], two(rows) + [whole(r.shape) for r in rights]
-    if extra is not None:
-        ins += [extra[0], extra[0], extra[1]]
-        specs += two(rows) + [whole(extra[1].shape)]
-    ins += [column, column]
-    specs += two(LANES)
+    w_at = lambda k: (lambda i, s: (0, s[first_rank + k * slots + i], 0))
     out = sds((slots, count, shard, 2 * LANES), bf)
     out_spec = pl.BlockSpec((1, count, shard, 2 * LANES), lambda i, s: (i, 0, 0, 0))
     return call(
-        functools.partial(weight_grads_kernel, (len(rights), extra is not None, core_at, count)),
-        name,
+        functools.partial(late_grads_kernel, (core_at, first_block, count)),
+        "late_grads",
         (slots,),
-        ins,
-        specs,
+        [left, left, dq, low_kv, w, w],
+        [pl.BlockSpec((shard, rows), at(k)) for k in range(2)]
+        + [whole(dq.shape), whole(low_kv.shape)]
+        + [pl.BlockSpec((w.shape[0], shard, LANES), w_at(k)) for k in range(2)],
         [out, out],
         [out_spec, out_spec],
         [],
@@ -914,36 +1083,33 @@
     )
 
 
-def spread_kernel(sizes, sc, mine, theirs, *outs):
-    block = 0
-    for out, size in zip(outs, sizes):
-        for b in range(max(1, size // (2 * LANES))):
-            total = mine[0, block + b].astype(f32) + theirs[0, block + b].astype(f32)
-            lanes = min(2 * LANES, out.shape[1])
-            out[:, b * lanes : (b + 1) * lanes] = total[:, :lanes]
-        block += max(1, size // (2 * LANES))
-
-
-def spread(mine, theirs, sizes, core):
-    shard = mine.shape[2]
-    outs = [sds((shard, size), f32) for size in sizes]
-    ins = [mine, theirs]
-    kernel = functools.partial(spread_kernel, sizes)
-    return call(kernel, "spread", (1,), ins, [whole(a.shape) for a in ins], outs, [whole(o.shape) for o in outs], [], 0, core)
-
-
-def unproject_kernel(sc, tok, cosine, sine, *refs):
-    *ins, w_own, low_out, part_out, gain_out, w, sem = refs
-    parts = len(ins) // 3
-    dqs, sums, mores = ins[:parts], ins[parts : 2 * parts], ins[2 * parts :]
+def spread_kernel(sc, early_a, early_b, late_a, late_b, output, query, key, value, extra):
+    join = lambda a, b: jnp.concatenate([a[0, k].astype(f32) + b[0, k].astype(f32) for k in range(a.shape[1])], axis=1)
+    early, late = join(early_a, early_b), join(late_a, late_b)
+    cols = output.shape[1]
+    output[...] = early[:, 0:cols]
+    half = early.shape[1] - cols - LANES
+    query[:, 0:half] = early[:, cols : cols + half]
+    at = query.shape[1] - half
+    query[:, half:] = late[:, 0:at]
+    for out in (key, value):
+        out[...] = late[:, at : at + out.shape[1]]
+        at += out.shape[1]
+    extra[...] = jnp.concatenate([early[:, cols + half :], late[:, at : at + LANES]], axis=1)
+
+
+def spread(early, late, widths, core):
+    shard = early[0].shape[2]
+    outs = [sds((shard, size), f32) for size in (*widths, 2 * LANES)]
+    ins = [*early, *late]
+    return call(spread_kernel, "spread", (1,), ins, [whole(a.shape) for a in ins], outs, [whole(o.shape) for o in outs], [], 0, core)
+
+
+def key_value_grads_kernel(sc, cosine, sine, *refs):
+    *ins, out = refs
+    parts = len(ins) // 2
+    sums, mores = ins[:parts], ins[parts:]
     step = pl.program_id(0)
-
-    @pl.when(step == 0)
-    def _():
-        pltpu.make_async_copy(w_own, w, sem).start()
-        pltpu.make_async_copy(w_own, w, sem).wait()
-        gain_out[...] = jnp.zeros_like(gain_out)
-
     shared = jnp.where(step < pl.num_programs(0) // 2, 1.0, 0.0).astype(f32)
     at = 0
     for is_key in (True, False):
@@ -955,66 +1121,63 @@
                 pair = jnp.concatenate([own[h] + o * shared for h, o in zip(heads, other)], axis=1)
                 if is_key:
                     pair = rope(pair, cosine[...], -sine[...])
-                low_out[:, at : at + LANES] = pair.astype(bf)
+                out[:, at : at + LANES] = pair.astype(bf)
                 at += LANES
-    low = jnp.concatenate([d[...] for d in dqs] + [low_out[...]], axis=1)
-    part = mm_nt(low, lanes_of(w, 0, w.shape[0]))
-    part_out[...] = part
-    x = tok[...].astype(f32)
-    scale = lax.rsqrt(jnp.mean(x * x, axis=-1, keepdims=True) + norm_eps)
-    gain_out[...] += jnp.sum(part * x * scale, axis=0, keepdims=True)
-
-
-def unproject(tokens, cosine, sine, dqs, sums, mores, w_own, core, deps, block=256):
-    rows, width = tokens.shape
+
+
+def key_value_grads(cosine, sine, sums, mores, core, deps, block=256):
+    rows = cosine.shape[0]
     cols = sum(s.shape[0] for s in sums) * HEAD_DIM
     own = lambda a: pl.BlockSpec((a.shape[0], block, HEAD_DIM), lambda i, s: (0, i, 0))
     return call(
-        unproject_kernel,
-        "unproject",
+        key_value_grads_kernel,
+        "key_value_grads",
         (rows // block,),
-        [tokens, cosine, sine, *dqs, *sums, *mores, w_own],
-        [rows_of(block, width), rows_of(block, LANES), rows_of(block, LANES)]
-        + [rows_of(block, d.shape[1]) for d in dqs]
-        + [own(a) for a in sums]
-        + [whole(a.shape) for a in mores]
-        + [any_space()],
-        [sds((rows, cols), bf), sds((rows, width), f32), sds((1, width), f32)],
-        [rows_of(block, cols), rows_of(block, width), whole((1, width))],
-        [pltpu.VMEM(w_own.shape, bf), pltpu.SemaphoreType.DMA],
-        2 * rows * width * w_own.shape[0] * LANES,
+        [cosine, sine, *sums, *mores],
+        [rows_of(block, LANES), rows_of(block, LANES)] + [own(a) for a in sums] + [whole(a.shape) for a in mores],
+        [sds((rows, cols), bf)],
+        [rows_of(block, cols)],
+        [],
+        0,
         core,
         deps,
-    )
-
-
-def finish_kernel(sc, tok, part, extra, rg, *refs):
-    *fars, w_mine, w_theirs, out, w, sem = refs
+    )[0]
+
+
+def finish_kernel(sc, tok, extra, rg, *refs):
+    *lows, w_own, mine_a, mine_b, theirs_a, theirs_b, out, w, sem = refs
+    blocks = w.shape[0] // 2
 
     @pl.when(pl.program_id(0) == 0)
     def _():
-        load_halves(sc, w_mine, w_theirs, 0, w, sem)
+        pltpu.make_async_copy(w_own.at[pl.ds(0, blocks)], w.at[pl.ds(0, blocks)], sem).start()
+        for core, pieces in ((sc[0], (mine_a, mine_b)), (1 - sc[0], (theirs_a, theirs_b))):
+            at = blocks + core * (blocks // 2)
+            for piece in pieces:
+                pltpu.make_async_copy(piece, w.at[pl.ds(at, piece.shape[0])], sem).start()
+                at = at + piece.shape[0]
         pltpu.make_async_copy(w, w, sem).wait()
 
-    far = jnp.concatenate([f[...] for f in fars], axis=1)
-    grad = part[...] + mm_nt(far, lanes_of(w, 0, w.shape[0]))
+    low = jnp.concatenate([f[...] for f in lows], axis=1)
+    grad = mm_nt(low, lanes_of(w, 0, 2 * blocks))
     passed, _ = norm_back(tok[...].astype(f32), extra[0:1, :].astype(f32), grad)
     out[...] = rg[...] + passed
 
 
-def finish(tokens, part, extra, rg, fars, w_mine, w_theirs, core, deps, block=256):
+def finish(tokens, extra, rg, lows, w_own, w_mine, w_theirs, core, deps, block=256):
     rows, width = tokens.shape
     wide = rows_of(block, width)
+    blocks = 4 * sum(p.shape[0] for p in w_mine)
     return call(
         finish_kernel,
         "finish",
         (rows // block,),
-        [tokens, part, extra, rg, *fars, w_mine, w_theirs],
-        [wide, wide, whole(extra.shape), wide, *[rows_of(block, f.shape[1]) for f in fars], any_space(), any_space()],
+        [tokens, extra, rg, *lows, w_own, *w_mine, *w_theirs],
+        [wide, whole(extra.shape), wide, *[rows_of(block, f.shape[1]) for f in lows]] + [any_space()] * 5,
         [sds((rows, width), f32)],
         [wide],
-        [pltpu.VMEM((2 * w_mine.shape[0], width, LANES), bf), pltpu.SemaphoreType.DMA],
-        2 * rows * width * 2 * w_mine.shape[0] * LANES,
+        [pltpu.VMEM((blocks, width, LANES), bf), pltpu.SemaphoreType.DMA],
+        2 * rows * width * blocks * LANES,
         core,
         deps,
     )[0]
@@ -1037,6 +1200,7 @@
 ):
     window.turn()
     window.turn()
+    window.gated = False
     count = lax.axis_size("dp")
     core = lax.axis_index("ctx")
     place = ring_place(lax.axis_index("dp"), count)
@@ -1059,7 +1223,9 @@
     ids = routes.reshape(rows, TOPK)
 
     packed = pack(w_query, key_weight, value_weight, w_output, w_router, norm_one, norm_two, core_only)
-    firsts = Gather(packed, core, count, 0).finish()
+    firsts = Gather(packed, core, count, 0)
+    firsts.step()
+    firsts.step()
 
     sizes = [4, 4, 4, 4]
     starts = [sum(sizes[:k]) for k in range(len(sizes))]
@@ -1079,14 +1245,21 @@
     sine = jnp.sin(angles)
     sine = jnp.tile(jnp.concatenate([-sine, sine], axis=1), (1, LANES // HEAD_DIM))
     cott = cot.T
-
+    zero_wide, zero_table = jnp.zeros((rows, width), f32), jnp.zeros((rows, LANES), f32)
+
+    firsts.mine[-1], cott, zero_wide, zero_table, cosine, sine, *owns = lax.optimization_barrier(
+        (firsts.mine[-1], cott, zero_wide, zero_table, cosine, sine, *owns)
+    )
+    firsts.step()
+    firsts.step()
+    firsts.share()
     open_chunk(firsts.mine[-1])
     c0 = chunks[0]
     window.turn()
     window.turn()
     c0.step()
     w_first, w_out, w_out_half, extra, q, kv, kv_prompt, n1t = project(
-        tok, cosine, sine, plain, firsts.bufs, heads, kvs, prompt, [cott, *owns, *window.turn()]
+        tok, cosine, sine, plain, firsts.bufs, heads, kvs, prompt, window.turn()
     )
     other = swap(kv_prompt, "ctx")
     out_far_mine = swap(after(w_out_half, kv_prompt), "tp")
@@ -1103,27 +1276,34 @@
     c0.step(lse_a)
     c1.step(lse_a)
     mixed, lse = (mixed_a, mixed_b), (lse_a, lse_b)
-    first_part = w_first.shape[0] // 2
     res, n2, n2t, wt = settle(
-        tok, ids, mixed, (far_a, far_b), extra, w_out, out_far_mine, out_far_theirs, core_only, window.turn()
-    )
-    first_far_mine = swap(take(after(w_first, wt), core * first_part, first_part), "tp")
-
-    scatters = [Scatter(core, count, plain, core_at) for _ in range(2)]
-    total_pairs = EXPERTS // 2
-    state = dict(sums=None, pick=None)
-
-    def work(pair):
+        tok, ids, mixed, (far_a, far_b), extra, w_out, out_far_mine, out_far_theirs, core_only, [cott, zero_wide, *window.turn()]
+    )
+    scatters = [Scatter(core, count, plain, core_at) for _ in range(3)]
+    state = dict(moe=zero_wide, back=zero_wide, pick=zero_table)
+
+    def work(pair, mode="all", deps=None):
         at = 2 * pair
         k = max(k for k in range(len(starts)) if starts[k] <= at)
         sc = scalars(jnp.int32(at), jnp.int32(at + 1))
-        carried = None if state["sums"] is None else (*state["sums"], state["pick"])
-        made = experts(n2, n2t, cot, cott, wt, sc, chunks[k].bufs, at - starts[k], carried, pair == total_pairs - 1, window.turn())
-        state["sums"], state["pick"] = made[:2], made[4]
-        state["last"] = made[-1]
-        return made[2], made[3], made[4]
-
-    s0, s1 = scatters
+        bufs, local = chunks[k].bufs, at - starts[k]
+        made = experts(
+            mode, (n2, cot), (n2t, cott), wt, sc, bufs, local, state["moe"], state["back"], state["pick"], state.get("made"),
+            window.turn() if deps is None else deps,
+        )
+        if mode == "all":
+            state["moe"], state["back"], keep, send, state["pick"] = made
+            return keep, send, state["pick"]
+        if mode.startswith("front"):
+            *back, state["pick"], scaled, acts = made[:-1] if mode.endswith("_end") else made
+            state["back"] = back if mode.endswith("_end") else back[0]
+            state["made"] = [scaled, acts]
+            return made[-1]
+        *moe, keep, send = made
+        state["moe"] = moe if mode.endswith("_end") else moe[0]
+        return keep, send, moe[0]
+
+    s0, s1, s2 = scatters
     c0.share(wt)
     c1.step(wt)
     open_chunk(wt)
@@ -1134,6 +1314,10 @@
     s0.add(keep, send)
     c1.step(token)
     c2.step(token)
+    first_part = w_first.shape[0] // 2
+    split = (first_part + 1) // 2
+    first_half = take(after(w_first, token), core * first_part, first_part)
+    first_far_a = swap(first_half[:split], "tp")
     keep, send, token = work(1)
 
     s0.add(keep, send)
@@ -1142,7 +1326,8 @@
     open_chunk(token)
     c3 = chunks[3]
     c3.step()
-    first_far_theirs = swap(after(first_far_mine, token), "ctx")
+    first_far_b = swap(after(first_half[split:], token), "tp")
+    theirs_a = swap(after(first_far_a, token), "ctx")
     keep, send, token = work(2)
 
     s0.add(keep, send)
@@ -1150,10 +1335,11 @@
     c3.step(token)
     keep, send, token = work(3)
 
-    s0.add(keep, send)
+    s1.add(keep, send)
     c2.share(token)
     c3.step(token)
     s0.step([token])
+    theirs_b = swap(after(first_far_b, token), "ctx")
     keep, send, token = work(4)
 
     s1.add(keep, send)
@@ -1164,74 +1350,99 @@
     s1.add(keep, send)
     c3.share(token)
     s0.step([token])
-    keep, send, token = work(6)
-
-    s1.add(keep, send)
+    token = work(6, "front")
+    made_early = state["made"]
+
+    window.gated = True
+    token = window.gate(token)
     s0.step([token])
-    keep, send, token = work(7)
-    moe_low, back_low = state["sums"]
-    pick_t = state["last"]
-
-    back_far = swap(back_low, "tp")
-    got = s1.add(keep, send)
-    pick_far = swap(after(pick_t, got), "tp")
-    a = s1.step([token])
-    s0_mine, s0_theirs = s0.finish([a])
-    s1.step([s0_mine])
-    emitted = emit((s0_mine, s0_theirs), 0, EXPERTS, None, core_only, [s0_mine])
+    pick_t = work(7, "front_end", window.step())
+    made_late = state["made"]
+    back = state["back"]
+
+    back_far_a = swap(back[0], "tp")
+    pick_far = swap(after(pick_t, back[0]), "tp")
+    token = window.gate(pick_t)
+    s1.step([token])
+    s0_mine, s0_theirs = s0.finish([token])
+    state["made"] = made_early
+    keep_early, send_early, token = work(6, "rest", [s0_mine, *window.step()])
+    token = window.gate(token, back_far_a, pick_far)
+    back_far_b = swap(after(back[1], token), "tp")
+    s2.add(keep_early, send_early, token)
+    s1.step([token])
+    emitted = emit((s0_mine, s0_theirs), 0, EXPERTS, None, core_only, [token])
+    state["made"] = made_late
+    keep, send, token = work(7, "rest_end", [emitted[0], *window.step()])
+    moe = state["moe"]
+    token = window.gate(token, back_far_b)
+    s2.add(keep, send, token)
+    s1.step([token])
     rg, low_t, dout, ll, gain_two = unsettle(
-        (back_low, back_far), (pick_t, pick_far), wt, res, cot, extra, w_out, core_only, [emitted[0], *window.turn()]
-    )
-    moe_far = swap(after(moe_low, ll), "tp")
-
+        back, (back_far_a, back_far_b), (pick_t, pick_far), wt, res, cot, extra, w_out, core_only, window.step()
+    )
+    token = window.gate(ll)
+    moe_far_a = swap(after(moe[0], token), "tp")
+    s1.step([token])
+    s2.step([token])
+    parts = 2
+    dq_a, dkv_a, dother_a = attend_back(q, kv, other, dout, mixed, lse, cosine, sine, core_only, 0, parts, window.step())
+    token = window.gate(dother_a)
+    more_a = swap(after(dother_a, token), "ctx")
+    s2.step([token])
     lane = jnp.arange(LANES)
-    column = lambda gain, at: jnp.where(lane == at, gain[0][:, None], 0.0)
-    parts = 2
-    s1.step([ll])
-    window.now = [x for x in window.now if x is not moe_far]
-    dq_a, dkv_a, dother_a = attend_back(q, kv, other, dout, mixed, lse, cosine, sine, core_only, 0, parts, window.turn())
-    more_a = swap(dother_a, "ctx")
-    s1.step([dother_a])
-    out_keep, out_send = weight_grads(
-        "output_grads", low_t, list(mixed), (n2t, ll), column(gain_two, 1), plain, first_rank, core_at, shard, heads // 4 + 1, [dother_a]
-    )
-    second = Scatter(core, count, plain, core_at)
-    second.add(out_keep, out_send)
-    dq_b, dkv_b, dother_b = attend_back(q, kv, other, dout, mixed, lse, cosine, sine, core_only, 1, parts, window.turn())
-    more_b = swap(dother_b, "ctx")
-    far_qa = swap(after(dq_a, moe_far, dother_b), "tp")
-    second.step([dother_b])
-    s1_mine, s1_theirs = s1.finish([dother_b])
-    dqs, dkvs, mores = [dq_a, dq_b], [dkv_a, dkv_b], [more_a, more_b]
-    low_kv, part, gain_one = unproject(tok, cosine, sine, dqs, dkvs, mores, w_first, core_only, [moe_far, *window.turn()])
-    far_qb = swap(after(dq_b, gain_one), "tp")
-    far_qs = [far_qa, far_qb]
-    second.step([gain_one])
-    first_keep, first_send = weight_grads(
-        "project_grads", n1t, [*dqs, low_kv], None, column(gain_one, 0), plain, first_rank, core_at, shard, w_first.shape[0] // 2 + 1, window.turn()
-    )
-    first = Scatter(core, count, plain, core_at)
-    far_kv = swap(after(low_kv, first_keep), "tp")
-    first.add(first_keep, first_send)
-    a = first.step()
-    second.step([first_keep])
-    grad_gate, grad_up, grad_down = emit((s1_mine, s1_theirs), EXPERTS // 2, EXPERTS, emitted, core_only, [first_keep, *window.turn()])
-    first.step([grad_gate])
-    second.step([grad_gate])
-    result = (res + (moe_low.astype(f32) + after(moe_far, grad_gate).astype(f32))).astype(bf).reshape(tokens.shape)
+    column = jnp.where(lane == 1, gain_two[0][:, None], 0.0)
+    early_keep, early_send = early_grads(
+        low_t, mixed, n2t, ll, column, n1t, dq_a, w_first, plain, first_rank, core_at, shard, [dother_a, *window.step()]
+    )
+    token = window.gate(early_keep, moe_far_a)
+    far_qa = swap(after(dq_a, token), "tp")
+    early = Scatter(core, count, plain, core_at)
+    early.add(early_keep, early_send, token)
+    s2.step([token])
+    s1_mine, s1_theirs = s1.finish([token])
+    dq_b, dkv_b, dother_b = attend_back(
+        q, kv, other, dout, mixed, lse, cosine, sine, core_only, 1, parts, [s1_mine, *window.step()]
+    )
+    token = window.gate(dother_b, far_qa)
+    more_b = swap(after(dother_b, token), "ctx")
+    far_qb = swap(after(dq_b, token), "tp")
+    early.step([token])
+    low_kv = key_value_grads(cosine, sine, [dkv_a, dkv_b], [more_a, more_b], core_only, window.step())
+    token = window.gate(low_kv)
+    early.step([token])
+    s2.step([token])
+    half_blocks = heads // 4
+    last_keep, last_send = late_grads(
+        n1t, dq_b, low_kv, w_first, half_blocks, plain, first_rank, core_at, shard, window.step()
+    )
+    token = window.gate(last_keep, far_qb)
+    far_kv = swap(after(low_kv, token), "tp")
+    late = Scatter(core, count, plain, core_at)
+    late.add(last_keep, last_send, token)
+    early.step([token])
+    emitted = emit((s1_mine, s1_theirs), EXPERTS * 3 // 8, EXPERTS, emitted, core_only, [token, early.value])
+    late.step([emitted[0]])
+    s2_mine, s2_theirs = s2.finish([late.value])
+    early.step([s2_mine])
+    late.step([s2_mine])
+    moe_far_b = swap(after(moe[1], late.value), "tp")
+    lows = [dq_a, dq_b, low_kv, far_qa, far_qb, far_kv]
     token_grad = finish(
-        tok, part, extra, rg, [*far_qs, far_kv], first_far_mine, first_far_theirs, core_only, [grad_gate]
+        tok, extra, rg, lows, w_first, (first_far_a, first_far_b), (theirs_a, theirs_b), core_only, [late.value, early.value]
     ).reshape(tokens.shape)
-    a = first.step()
-    second_mine, second_theirs = second.finish()
-    first.step()
-    grad_output, extra_two = spread(second_mine, second_theirs, (heads * HEAD_DIM, LANES), core_only)
+    late.step([token_grad, moe_far_b])
+    early_sums = early.finish([late.value])
+    grad_gate, grad_up, grad_down = emit((s2_mine, s2_theirs), EXPERTS * 3 // 4, EXPERTS, emitted, core_only, [early_sums[0]])
+    late.step([grad_gate])
+    result = combine(res, moe, (moe_far_a, moe_far_b), core_only, [late.value]).reshape(tokens.shape)
     kv_width = kvs * HEAD_DIM
-    grad_query, grad_key, grad_value, extra_one = spread(*first.finish(), (heads * HEAD_DIM, kv_width, kv_width, LANES), core_only)
-    gain_part = extra_one[:, 0]
+    widths = (w_output.shape[1], w_query.shape[1], kv_width, kv_width)
+    grad_output, grad_query, grad_key, grad_value, extras = spread(early_sums, late.finish(), widths, core_only)
+    grad_norm_two = extras[:, 1]
+    grad_router = extras[:, ROUTER_LANE : ROUTER_LANE + EXPERTS]
+    gain_part = extras[:, 0] + extras[:, LANES]
     grad_norm_one = gain_part + swap(gain_part, "tp")
-    grad_norm_two = extra_two[:, 1]
-    grad_router = extra_two[:, ROUTER_LANE : ROUTER_LANE + EXPERTS]
     return (
         result,
         token_grad,

time: 783 us -> 745 us (0.951)
  waiting for transfers between devices: 156 us -> 110 us
  Pallas kernels: 481 us -> 507 us
  other arithmetic: 17.3 us -> 8.77 us
  local copies, waits for them, and re-layouts: 45.8 us -> 37.6 us
    ppermute x36 -> x40, waiting for transfers between devices: 114 us -> 72.1 us  [ring_hop(): return sent(lax.ppermute(values, ('dp', 'ctx'), pairs))]
    pallas_call x44 -> x52, Pallas kernels: 481 us -> 507 us  [call(): pl.pallas_call(lambda sc, *refs: kernel(sc, *refs[len(deps):]), out_shape...]
    ppermute x50 -> x55, starting transfers between devices: 25.7 us -> 21 us  [swap(): swapped = lax.ppermute(values, axis, [(0, 1), (1, 0)])]
    ppermute x50 -> x55, waiting for transfers between devices: 41.4 us -> 37.8 us  [swap(): swapped = lax.ppermute(values, axis, [(0, 1), (1, 0)])]
    ppermute x36 -> x40, starting transfers between devices: 45.5 us -> 48.9 us  [ring_hop(): return sent(lax.ppermute(values, ('dp', 'ctx'), pairs))]
  transfers between devices with their start and end apart: 86 -> 95, of which waited for: 20 -> 21; matrix products, arithmetic and copies ran while one was open for 6% -> 5% of each run, Pallas kernels for 60% -> 67%
where the time goes in v3:
time: 745 us; the launch traced here: 734 us
  Pallas kernels  507 us (68%)
  waiting for transfers between devices  110 us (15%)
  starting transfers between devices  69.9 us (9%)
  local copies, waits for them, and re-layouts  37.6 us (5%)
  other arithmetic  8.77 us (1%)
    pallas_call x52, Pallas kernels, call(): pl.pallas_call(lambda sc, *refs: kernel(sc, *refs[len(deps):]), out_shape...  507 us
    ppermute x40, waiting for transfers between devices, ring_hop(): return sent(lax.ppermute(values, ('dp', 'ctx'), pairs))  72.1 us
    ppermute x40, starting transfers between devices, ring_hop(): return sent(lax.ppermute(values, ('dp', 'ctx'), pairs))  48.9 us
    ppermute x55, waiting for transfers between devices, swap(): swapped = lax.ppermute(values, axis, [(0, 1), (1, 0)])  37.8 us
    ppermute x55, starting transfers between devices, swap(): swapped = lax.ppermute(values, axis, [(0, 1), (1, 0)])  21 us
  transfers between devices with their start and end apart: 95, of which 21 were waited for; matrix products, arithmetic and copies ran while one was open for 5% of the time, Pallas kernels for 67%

profile of v3, /device:TPU:0, one launch (start us, length us, event | category | flops | bytes accessed | tf_op | source)
XLA Modules:
  0.0 734.4 jit_solution(11573735311126981427)
XLA Ops:
  13.3 9.0 %collective-permute-done.refs_4_ = bf16[18,192,128]{2,1,0:T(8,128)(2,1)S(1)} collective-permute-done((bf16[18,192,128]{2,1,0:T(8,128)(2,1)}, bf16[18,192,128]{2,1,0:T(8,128)(2,1)S(1)}, u32[]{:S(2)}, u32[]{:S(2)}) %collective-permute-start) | collective-permute-done | bytes 884768 | tf_op jit(solution)/shard_map/ppermute | solution.py:90
  28.0 7.5 %collective-permute-done.1.refs_5_ = bf16[18,192,128]{2,1,0:T(8,128)(2,1)} collective-permute-done((bf16[18,192,128]{2,1,0:T(8,128)(2,1)S(1)}, bf16[18,192,128]{2,1,0:T(8,128)(2,1)}, u32[]{:S(2)}, u32[]{:S(2)}) %collective-permute-start.1) | collective-permute-done | bytes 884768 | tf_op jit(solution)/shard_map/ppermute | solution.py:90
  37.7 11.2 %collective-permute-done.2.refs_6_ = bf16[18,192,128]{2,1,0:T(8,128)(2,1)S(1)} collective-permute-done((bf16[18,192,128]{2,1,0:T(8,128)(2,1)}, bf16[18,192,128]{2,1,0:T(8,128)(2,1)S(1)}, u32[]{:S(2)}, u32[]{:S(2)}) %collective-permute-start.2) | collective-permute-done | bytes 884768 | tf_op jit(solution)/shard_map/ppermute | solution.py:90
  51.5 5.7 collective-permute-done.3.refs_7_
  62.0 17.7 %project.1 = (bf16[11,1536,128]{2,1,0:T(8,128)(2,1)}, bf16[6,1536,128]{2,1,0:T(8,128)(2,1)}, bf16[3,1536,128]{2,1,0:T(8,128)(2,1)}, bf16[128,1536]{1,0:T(8,128)(...) custom-call(s32[18]{0:T(128)} %stack.86.sc, ...), custom_call_target="tpu_custom_call" | custom-call | flops 20753999872 | bytes 1 | tf_op jit(solution)/shard_map/project/pallas_call | solution.py:50
  83.7 21.3 %attend.3 = (bf16[512,768]{1,0:T(8,128)(2,1)}, f32[6,2,512]{2,1,0:T(2,128)}) custom-call(s32[2]{0:T(128)} %pad_add_fusion.sc, bf16[3,4,192,256]{3,2,1,0:T(8,128)(2,1)} %collective-permute-done.10.refs_0_.refs_11_.refs_10_, bf16[12,1024,64]{2,1,0:T(8,128)(2,1)} %get-tuple-element.171.refs_4_.refs_1_.refs_2_, ...), custom_call_target="tpu_custom_call" | custom-call | flops 21906999296 | bytes 1 | tf_op jit(solution)/shard_map/attend/pallas_call | solution.py:50
  110.1 17.0 %attend.2 = (bf16[512,768]{1,0:T(8,128)(2,1)}, f32[6,2,512]{2,1,0:T(2,128)}) custom-call(s32[2]{0:T(128)} %pad_add_fusion.sc, bf16[8,256,128]{2,1,0:T(8,128)(2,1)} %copy-done.15, bf16[3,1536,128]{2,1,0:T(8,128)(2,1)} %collective-permute-done.9.refs_1_.refs_15_, bf16[3,4,192,256]{3,2,1,0:T(8,128)(2,1)} %collective-permute-done.11.refs_2_.refs_15_.refs_14_, ...), custom_call_target="tpu_custom_call" | custom-call | flops 21906999296 | bytes 1 | tf_op jit(solution)/shard_map/attend/pallas_call | solution.py:50
  130.0 4.6 copy.47.refs_0_.refs_9_.refs_8_.refs_10_.refs_11_.refs_3_
  138.0 9.5 %collective-permute-done.13.refs_11_.refs_0_ = bf16[512,768]{1,0:T(8,128)(2,1)S(1)} collective-permute-done((bf16[512,768]{1,0:T(8,128)(2,1)}, bf16[512,768]{1,0:T(8,128)(2,1)S(1)}, u32[]{:S(2)}, u32[]{:S(2)}) %collective-permute-start.13) | collective-permute-done | bytes 786464 | tf_op jit(solution)/shard_map/ppermute | solution.py:94
  149.5 3.5 broadcast_in_dim.26.refs_1_.refs_19_.refs_20_
  153.0 15.8 %settle.1 = (f32[1024,1536]{1,0:T(8,128)}, bf16[1024,1536]{1,0:T(8,128)(2,1)}, bf16[1536,1024]{1,0:T(8,128)(2,1)}, f32[1024,128]{1,0:T(8,128)}) custom-call(s32[2]{0:T(128)} %pad_add_fusion.sc, bf16[1536,1024]{1,0:T(8,128)(2,1)} %copy.47.refs_0_.refs_9_.refs_8_.refs_10_.refs_11_.refs_3_, f32[1024,1536]{1,0:T(8,128)} %broadcast_in_dim.26.refs_1_.refs_19_.refs_20_, ...), custom_call_target="tpu_custom_call" | custom-call | flops 18447998976 | bytes 1 | tf_op jit(solution)/shard_map/settle/pallas_call | solution.py:50
  173.4 25.2 %experts_all.6 = (f32[1024,1536]{1,0:T(8,128)}, f32[1024,1536]{1,0:T(8,128)}, bf16[4,6,192,256]{3,2,1,0:T(8,128)(2,1)}, bf16[4,6,192,256]{3,2,1,0:T(8,128)(2,1)}, f32[1024,128]{1,0:T(8,128)}) custom-call(s32[20]{0:T(128)} %stack.91.sc, bf16[512,768]{1,0:T(8,128)(2,1)} %copy-done.10, ...), custom_call_target="tpu_custom_call" | custom-call | flops 27672000512 | bytes 1 | tf_op jit(solution)/shard_map/experts_all/pallas_call | solution.py:50
  206.5 24.6 %experts_all.7 = (f32[1024,1536]{1,0:T(8,128)}, f32[1024,1536]{1,0:T(8,128)}, bf16[4,6,192,256]{3,2,1,0:T(8,128)(2,1)}, bf16[4,6,192,256]{3,2,1,0:T(8,128)(2,1)}, f32[1024,128]{1,0:T(8,128)}) custom-call(s32[20]{0:T(128)} %stack.108.sc, bf16[3,4,192,128]{3,2,1,0:T(8,128)(2,1)} %copy-done.13, ...), custom_call_target="tpu_custom_call" | custom-call | flops 27672000512 | bytes 1 | tf_op jit(solution)/shard_map/experts_all/pallas_call | solution.py:50
  236.7 11.6 %collective-permute-done.35.refs_3_.refs_14_.refs_15_ = bf16[3,4,192,256]{3,2,1,0:T(8,128)(2,1)} collective-permute-done((bf16[3,4,192,256]{3,2,1,0:T(8,128)(2,1)}, bf16[3,4,192,256]{3,2,1,0:T(8,128)(2,1)}, u32[]{:S(2)}, u32[]{:S(2)}) %collective-permute-start.35) | collective-permute-done | bytes 1179680 | tf_op jit(solution)/shard_map/ppermute | solution.py:90
  248.8 24.2 %experts_all.8 = (f32[1024,1536]{1,0:T(8,128)}, f32[1024,1536]{1,0:T(8,128)}, bf16[4,6,192,256]{3,2,1,0:T(8,128)(2,1)}, bf16[4,6,192,256]{3,2,1,0:T(8,128)(2,1)}, f32[1024,128]{1,0:T(8,128)}) custom-call(s32[20]{0:T(128)} %stack.90.sc, bf16[4,6,192,256]{3,2,1,0:T(8,128)(2,1)} %collective-permute-done.24.refs_0_.refs_4_, ...), custom_call_target="tpu_custom_call" | custom-call | flops 27672000512 | bytes 1 | tf_op jit(solution)/shard_map/experts_all/pallas_call | solution.py:50
  277.2 24.6 %experts_all.9 = (f32[1024,1536]{1,0:T(8,128)}, f32[1024,1536]{1,0:T(8,128)}, bf16[4,6,192,256]{3,2,1,0:T(8,128)(2,1)}, bf16[4,6,192,256]{3,2,1,0:T(8,128)(2,1)}, f32[1024,128]{1,0:T(8,128)}) custom-call(s32[20]{0:T(128)} %stack.109.sc, bf16[4,6,192,256]{3,2,1,0:T(8,128)(2,1)} %collective-permute-done.41.refs_0_.refs_5_, ...), custom_call_target="tpu_custom_call" | custom-call | flops 27672000512 | bytes 1 | tf_op jit(solution)/shard_map/experts_all/pallas_call | solution.py:50
  309.2 24.1 %experts_all.10 = (f32[1024,1536]{1,0:T(8,128)}, f32[1024,1536]{1,0:T(8,128)}, bf16[4,6,192,256]{3,2,1,0:T(8,128)(2,1)}, bf16[4,6,192,256]{3,2,1,0:T(8,128)(2,1)}, f32[1024,128]{1,0:T(8,128)}) custom-call(s32[20]{0:T(128)} %stack.89.sc, bf16[4,6,192,256]{3,2,1,0:T(8,128)(2,1)} %collective-permute-done.34.refs_6_.refs_0_, ...), custom_call_target="tpu_custom_call" | custom-call | flops 27672000512 | bytes 1 | tf_op jit(solution)/shard_map/experts_all/pallas_call | solution.py:50
  336.4 4.2 hop_sum.26.refs_6_
  341.2 24.4 %experts_all.11 = (f32[1024,1536]{1,0:T(8,128)}, f32[1024,1536]{1,0:T(8,128)}, bf16[4,6,192,256]{3,2,1,0:T(8,128)(2,1)}, bf16[4,6,192,256]{3,2,1,0:T(8,128)(2,1)}, f32[1024,128]{1,0:T(8,128)}) custom-call(s32[20]{0:T(128)} %stack.110.sc, bf16[4,6,192,256]{3,2,1,0:T(8,128)(2,1)} %collective-permute-done.52.refs_0_.refs_4_, ...), custom_call_target="tpu_custom_call" | custom-call | flops 27672000512 | bytes 1 | tf_op jit(solution)/shard_map/experts_all/pallas_call | solution.py:50
  367.5 4.5 hop_sum.27.refs_4_
  374.3 17.7 %experts_front.1 = (f32[1024,1536]{1,0:T(8,128)}, f32[1024,128]{1,0:T(8,128)}, bf16[1024,512]{1,0:T(8,128)(2,1)}, bf16[1024,1024]{1,0:T(8,128)(2,1)}) custom-call(s32[20]{0:T(128)} %stack.88.sc, bf16[4,6,192,256]{3,2,1,0:T(8,128)(2,1)} %collective-permute-done.46.refs_0_.refs_5_, bf16[3,4,192,256]{3,2,1,0:T(8,128)(2,1)} %collective-permute-done.48.refs_1_.refs_15_.refs_11_, ...), custom_call_target="tpu_custom_call" | custom-call | flops 20753999872 | bytes 1 | tf_op jit(solution)/shard_map/experts_front/pallas_call | solution.py:50
  394.8 4.5 hop_sum.28.refs_0_
  401.1 17.7 %experts_front_end.1 = (bf16[512,1536]{1,0:T(8,128)(2,1)}, bf16[512,1536]{1,0:T(8,128)(2,1)}, f32[1024,128]{1,0:T(8,128)}, bf16[1024,512]{1,0:T(8,128)(2,1)}, bf...) custom-call(s32[20]{0:T(128)} %stack.87.sc, bf16[3,6,192,256]{3,2,1,0:T(8,128)(2,1)} %hop_sum.28.refs_0_, ...), custom_call_target="tpu_custom_call" | custom-call | flops 20753999872 | bytes 1 | tf_op jit(solution)/shard_map/experts_front_end/pallas_call | solution.py:50
  422.5 4.0 hop_sum.29.refs_0_.refs_1_
  431.2 13.3 %experts_rest.1 = (f32[1024,1536]{1,0:T(8,128)}, bf16[4,6,192,256]{3,2,1,0:T(8,128)(2,1)}, bf16[4,6,192,256]{3,2,1,0:T(8,128)(2,1)}) custom-call(s32[20]{0:T(128)} %stack.88.sc, bf16[3,6,192,256]{3,2,1,0:T(8,128)(2,1)} %hop_sum.29.refs_0_.refs_1_, bf16[3,6,192,128]{3,2,1,0:T(8,128)(2,1)} %hop_sum.30.refs_1_, ...), custom_call_target="tpu_custom_call" | custom-call | flops 14988999680 | bytes 1 | tf_op jit(solution)/shard_map/experts_rest/pallas_call | solution.py:50
  444.5 11.6 %collective-permute-done.62.refs_6_ = f32[16,1024]{1,0:T(8,128)S(1)} collective-permute-done((f32[16,1024]{1,0:T(8,128)}, f32[16,1024]{1,0:T(8,128)S(1)}, u32[]{:S(2)}, u32[]{:S(2)}) %collective-permute-start.62) | collective-permute-done | bytes 65568 | tf_op jit(solution)/shard_map/ppermute | solution.py:94
  457.1 4.2 hop_sum.31.refs_1_
  461.7 5.2 emit.3
  466.9 13.4 %experts_rest_end.1 = (bf16[768,1536]{1,0:T(8,128)(2,1)}, bf16[256,1536]{1,0:T(8,128)(2,1)}, bf16[4,6,192,256]{3,2,1,0:T(8,128)(2,1)}, bf16[4,6,192,256]{3,2,1,0:T(8,128)(2,1)}) custom-call(s32[20]{0:T(128)} %stack.87.sc, f32[16,192,256]{2,1,0:T(8,128)} %get-tuple-element.253.refs_0_.refs_4_, bf16[3,6,192,256]{3,2,1,0:T(8,128)(2,1)} %hop_sum.31.refs_1_, ...), custom_call_target="tpu_custom_call" | custom-call | flops 14988999680 | bytes 1 | tf_op jit(solution)/shard_map/experts_rest_end/pallas_call | solution.py:50
  480.2 11.1 %collective-permute-done.65.refs_4_ = bf16[512,1536]{1,0:T(8,128)(2,1)} collective-permute-done((bf16[512,1536]{1,0:T(8,128)(2,1)}, bf16[512,1536]{1,0:T(8,128)(2,1)}, u32[]{:S(2)}, u32[]{:S(2)}) %collective-permute-start.65) | collective-permute-done | bytes 1572896 | tf_op jit(solution)/shard_map/ppermute | solution.py:94
  491.4 4.5 hop_sum.32.refs_0_
  496.3 16.5 %unsettle.1 = (f32[1024,1536]{1,0:T(8,128)}, bf16[1536,1024]{1,0:T(8,128)(2,1)}, bf16[1024,768]{1,0:T(8,128)(2,1)}, bf16[1024,128]{1,0:T(8,128)(2,1)}, f32[1,1536]{1,0:T(1,128)}) custom-call(s32[2]{0:T(128)} %pad_add_fusion.sc, bf16[3,6,192,256]{3,2,1,0:T(8,128)(2,1)} %hop_sum.32.refs_0_, bf16[512,1536]{1,0:T(8,128)(2,1)} %get-tuple-element.250.refs_1_, ...), custom_call_target="tpu_custom_call" | custom-call | flops 19601000448 | bytes 1 | tf_op jit(solution)/shard_map/unsettle/pallas_call | solution.py:50
  514.7 4.2 collective-permute-done.67.refs_7_
  519.2 4.5 hop_sum.33.refs_0_
  527.8 24.8 %attend_back.2 = (bf16[1024,384]{1,0:T(8,128)(2,1)}, f32[4,1024,64]{2,1,0:T(8,128)}, f32[4,256,128]{2,1,0:T(8,128)}) custom-call(s32[2]{0:T(128)} %pad_add_fusion.sc, bf16[3,6,192,256]{3,2,1,0:T(8,128)(2,1)} %hop_sum.33.refs_0_, bf16[2,6,192,128]{3,2,1,0:T(8,128)(2,1)} %hop_sum.34.refs_1_, bf16[12,1024,64]{2,1,0:T(8,128)(2,1)} %get-tuple-element.171.refs_4_.refs_1_.refs_2_, ...), custom_call_target="tpu_custom_call" | custom-call | flops 28824999936 | bytes 1 | tf_op jit(solution)/shard_map/attend_back/pallas_call | solution.py:50
  553.5 3.5 hop_sum.35.refs_1_
  557.7 12.4 %early_grads.1 = (bf16[4,5,192,256]{3,2,1,0:T(8,128)(2,1)}, bf16[4,5,192,256]{3,2,1,0:T(8,128)(2,1)}) custom-call(s32[18]{0:T(128)} %stack.86.sc, f32[4,256,128]{2,1,0:T(8,128)} %get-tuple-element.277.refs_0_, bf16[2,6,192,256]{3,2,1,0:T(8,128)(2,1)} %hop_sum.35.refs_1_, bf16[1536,1024]{1,0:T(8,128)(2,1)} %get-tuple-element.272.refs_2_.refs_3_, ...), custom_call_target="tpu_custom_call" | custom-call | flops 13836000256 | bytes 1 | tf_op jit(solution)/shard_map/early_grads/pallas_call | solution.py:50
  575.7 3.7 hop_sum.37.refs_1_
  579.6 4.0 hop_sum.36.refs_0_.refs_2_
  584.5 24.8 %attend_back.3 = (bf16[1024,384]{1,0:T(8,128)(2,1)}, f32[4,1024,64]{2,1,0:T(8,128)}, f32[4,256,128]{2,1,0:T(8,128)}) custom-call(s32[2]{0:T(128)} %pad_add_fusion.sc, bf16[3,6,192,256]{3,2,1,0:T(8,128)(2,1)} %hop_sum.36.refs_0_.refs_2_, bf16[2,6,192,256]{3,2,1,0:T(8,128)(2,1)} %hop_sum.37.refs_1_, ...), custom_call_target="tpu_custom_call" | custom-call | flops 28824999936 | bytes 1 | tf_op jit(solution)/shard_map/attend_back/pallas_call | solution.py:50
  613.4 7.1 key_value_grads.1.refs_0_.refs_5_.refs_7_
  620.5 3.7 hop_sum.40.refs_1_
  629.6 9.3 %late_grads.1 = (bf16[4,4,192,256]{3,2,1,0:T(8,128)(2,1)}, bf16[4,4,192,256]{3,2,1,0:T(8,128)(2,1)}) custom-call(s32[18]{0:T(128)} %stack.86.sc, bf16[1,5,192,256]{3,2,1,0:T(8,128)(2,1)} %hop_sum.39.refs_0_, bf16[2,6,192,256]{3,2,1,0:T(8,128)(2,1)} %hop_sum.40.refs_1_, bf16[1536,1024]{1,0:T(8,128)(2,1)} %get-tuple-element.274.refs_11_.refs_12_.refs_2_.refs_3_, ...), custom_call_target="tpu_custom_call" | custom-call | flops 11530000384 | bytes 1 | tf_op jit(solution)/shard_map/late_grads/pallas_call | solution.py:50
  638.9 7.1 collective-permute-done.79.refs_3_
  651.2 5.2 emit.4
  673.1 18.3 %finish.1 = f32[1024,1536]{1,0:T(8,128)} custom-call(s32[2]{0:T(128)} %pad_add_fusion.sc, bf16[1,4,192,256]{3,2,1,0:T(8,128)(2,1)} %hop_sum.44.refs_0_, bf16[1,5,192,256]{3,2,1,0:T(8,128)(2,1)} %hop_sum.45.refs_1_, bf16[1024,1536]{1,0:T(8,128)(2,1)} %bitcast.59, bf16[128,1536]{1,0:T(8,128)(2,1)} %get-tuple-element.185.refs_13_.refs_10_.refs_3_, ...), custom_call_target="tpu_custom_call" | custom-call | flops 20753999872 | bytes 1 | tf_op jit(solution)/shard_map/finish/pallas_call | solution.py:50
  706.6 7.4 %collective-permute-done.92.refs_2_ = bf16[1,4,192,256]{3,2,1,0:T(8,128)(2,1)} collective-permute-done((bf16[1,4,192,256]{3,2,1,0:T(8,128)(2,1)}, bf16[1,4,192,256]{3,2,1,0:T(8,128)(2,1)}, u32[]{:S(2)}, u32[]{:S(2)}) %collective-permute-start.92) | collective-permute-done | bytes 393248 | tf_op jit(solution)/shard_map/ppermute | solution.py:90
  725.4 7.5 %combine.1 = bf16[1024,1536]{1,0:T(8,128)(2,1)} custom-call(s32[2]{0:T(128)} %pad_add_fusion.sc, bf16[1,4,192,256]{3,2,1,0:T(8,128)(2,1)} %hop_sum.48.refs_0_, f32[1024,1536]{1,0:T(8,128)} %get-tuple-element.262.refs_8_.refs_1_, bf16[768,1536]{1,0:T(8,128)(2,1)} %get-tuple-element.278.refs_0_.refs_2_, bf16[256,1536]{1,0:T(8,128)(2,1)} %get-tuple-element.301.refs_3_, ...), custom_call_target="tpu_custom_call" | custom-call | flops 5765000192 | bytes 1 | tf_op jit(solution)/shard_map/combine/pallas_call | solution.py:50
  (282 shorter events, 171.6 us)
Async XLA Ops:
  79.9 28.6 %collective-permute-start.9 = (bf16[3,1536,128]{2,1,0:T(8,128)(2,1)}, bf16[3,1536,128]{2,1,0:T(8,128)(2,1)}, u32[]{:S(2)}, u32[]{:S(2)}) collective-permute-start(bf16[3,1536,128]{2,1,0:T(8,128)(2,1)} %get-tuple-element.167), channel_id=1, source_target_pairs={{0,1},{1,0},{2,3},{3,2},{4,5},{5,4},{6,7},{7,6},{8,9},{9,8},{10,11... | collective-permute-start | bytes 3538952 | tf_op jit(solution)/shard_map/ppermute | solution.py:94
  81.4 27.1 %collective-permute-start.12 = (bf16[3,4,192,256]{3,2,1,0:T(8,128)(2,1)}, bf16[3,4,192,256]{3,2,1,0:T(8,128)(2,1)}, u32[]{:S(2)}, u32[]{:S(2)}) collective-permute-start(bf16[3,4,192,256]{3,2,1,0:T(8,128)(2,1)} %collective-permute-done.10.refs_0_.refs_11_.refs_10_), channel_id=1, source_target_pairs={{0,8},{10,2},{8,16},{18,10},{16,24},{26,18},{24,28},{30,26},{28,20... | collective-permute-start | bytes 3538952 | tf_op jit(solution)/shard_map/ppermute | solution.py:90
  82.9 27.2 %collective-permute-start.11 = (bf16[3,4,192,256]{3,2,1,0:T(8,128)(2,1)}, bf16[3,4,192,256]{3,2,1,0:T(8,128)(2,1)}, u32[]{:S(2)}, u32[]{:S(2)}) collective-permute-start(bf16[3,4,192,256]{3,2,1,0:T(8,128)(2,1)} %collective-permute-done.10.refs_0_.refs_11_.refs_10_), channel_id=1, source_target_pairs={{0,2},{2,0},{1,3},{3,1},{4,6},{6,4},{5,7},{7,5},{8,10},{10,8},{9,1... | collective-permute-start | bytes 3538952 | tf_op jit(solution)/shard_map/ppermute | solution.py:94
  106.7 30.7 %collective-permute-start.20 = (bf16[512,768]{1,0:T(8,128)(2,1)}, bf16[512,768]{1,0:T(8,128)(2,1)}, u32[]{:S(2)}, u32[]{:S(2)}) collective-permute-start(bf16[512,768]{1,0:T(8,128)(2,1)} %get-tuple-element.183.refs_10_.refs_13_.refs_5_), channel_id=1, source_target_pairs={{0,1},{1,0},{2,3},{3,2},{4,5},{5,4},{6,7},{7,6},{8,9},{9,8},{10,11... | collective-permute-start | bytes 2359304 | tf_op jit(solution)/shard_map/ppermute | solution.py:94
  108.5 29.0 %collective-permute-start.22 = (bf16[3,1536,128]{2,1,0:T(8,128)(2,1)}, bf16[3,1536,128]{2,1,0:T(8,128)(2,1)}, u32[]{:S(2)}, u32[]{:S(2)}) collective-permute-start(bf16[3,1536,128]{2,1,0:T(8,128)(2,1)} %collective-permute-done.9.refs_1_.refs_15_), channel_id=1, source_target_pairs={{0,2},{2,0},{1,3},{3,1},{4,6},{6,4},{5,7},{7,5},{8,10},{10,8},{9,1... | collective-permute-start | bytes 3538952 | tf_op jit(solution)/shard_map/ppermute | solution.py:94
  110.1 39.4 %collective-permute-start.21 = (bf16[3,4,192,256]{3,2,1,0:T(8,128)(2,1)}, bf16[3,4,192,256]{3,2,1,0:T(8,128)(2,1)}, u32[]{:S(2)}, u32[]{:S(2)}) collective-permute-start(bf16[3,4,192,256]{3,2,1,0:T(8,128)(2,1)} %collective-permute-done.12.refs_3_.refs_12_.refs_11_), channel_id=1, source_target_pairs={{0,2},{2,0},{1,3},{3,1},{4,6},{6,4},{5,7},{7,5},{8,10},{10,8},{9,1... | collective-permute-start | bytes 3538952 | tf_op jit(solution)/shard_map/ppermute | solution.py:94
  134.7 35.4 %collective-permute-start.19 = (bf16[3,4,192,256]{3,2,1,0:T(8,128)(2,1)}, bf16[3,4,192,256]{3,2,1,0:T(8,128)(2,1)}, u32[]{:S(2)}, u32[]{:S(2)}) collective-permute-start(bf16[3,4,192,256]{3,2,1,0:T(8,128)(2,1)} %collective-permute-done.17.refs_5_.refs_12_.refs_13_), channel_id=1, source_target_pairs={{0,8},{10,2},{8,16},{18,10},{16,24},{26,18},{24,28},{30,26},{28,20... | collective-permute-start | bytes 3538952 | tf_op jit(solution)/shard_map/ppermute | solution.py:90
  137.4 34.3 %collective-permute-start.18 = (bf16[3,4,192,256]{3,2,1,0:T(8,128)(2,1)}, bf16[3,4,192,256]{3,2,1,0:T(8,128)(2,1)}, u32[]{:S(2)}, u32[]{:S(2)}) collective-permute-start(bf16[3,4,192,256]{3,2,1,0:T(8,128)(2,1)} %collective-permute-done.17.refs_5_.refs_12_.refs_13_), channel_id=1, source_target_pairs={{0,2},{2,0},{1,3},{3,1},{4,6},{6,4},{5,7},{7,5},{8,10},{10,8},{9,1... | collective-permute-start | bytes 3538952 | tf_op jit(solution)/shard_map/ppermute | solution.py:94
  137.5 34.9 %collective-permute-start.15 = (bf16[3,4,192,256]{3,2,1,0:T(8,128)(2,1)}, bf16[3,4,192,256]{3,2,1,0:T(8,128)(2,1)}, u32[]{:S(2)}, u32[]{:S(2)}) collective-permute-start(bf16[3,4,192,256]{3,2,1,0:T(8,128)(2,1)} %collective-permute-done.14.refs_4_.refs_13_.refs_12_), channel_id=1, source_target_pairs={{0,2},{2,0},{1,3},{3,1},{4,6},{6,4},{5,7},{7,5},{8,10},{10,8},{9,1... | collective-permute-start | bytes 3538952 | tf_op jit(solution)/shard_map/ppermute | solution.py:94
  170.1 34.8 %collective-permute-start.25 = (bf16[3,4,192,256]{3,2,1,0:T(8,128)(2,1)}, bf16[3,4,192,256]{3,2,1,0:T(8,128)(2,1)}, u32[]{:S(2)}, u32[]{:S(2)}) collective-permute-start(bf16[3,4,192,256]{3,2,1,0:T(8,128)(2,1)} %collective-permute-done.19.refs_4_.refs_13_.refs_14_), channel_id=1, source_target_pairs={{0,8},{10,2},{8,16},{18,10},{16,24},{26,18},{24,28},{30,26},{28,20... | collective-permute-start | bytes 3538952 | tf_op jit(solution)/shard_map/ppermute | solution.py:90
  171.6 34.9 %collective-permute-start.32 = (bf16[3,4,192,256]{3,2,1,0:T(8,128)(2,1)}, bf16[3,4,192,256]{3,2,1,0:T(8,128)(2,1)}, u32[]{:S(2)}, u32[]{:S(2)}) collective-permute-start(bf16[3,4,192,256]{3,2,1,0:T(8,128)(2,1)} %collective-permute-done.19.refs_4_.refs_13_.refs_14_), channel_id=1, source_target_pairs={{0,2},{2,0},{1,3},{3,1},{4,6},{6,4},{5,7},{7,5},{8,10},{10,8},{9,1... | collective-permute-start | bytes 3538952 | tf_op jit(solution)/shard_map/ppermute | solution.py:94
  171.7 27.6 %collective-permute-start.28 = (bf16[3,4,192,256]{3,2,1,0:T(8,128)(2,1)}, bf16[3,4,192,256]{3,2,1,0:T(8,128)(2,1)}, u32[]{:S(2)}, u32[]{:S(2)}) collective-permute-start(bf16[3,4,192,256]{3,2,1,0:T(8,128)(2,1)} %get-tuple-element.197.refs_11_.refs_12_), channel_id=1, source_target_pairs={{0,8},{10,2},{8,16},{18,10},{16,24},{26,18},{24,28},{30,26},{28,20... | collective-permute-start | bytes 3538952 | tf_op jit(solution)/shard_map/ppermute | solution.py:90
  199.3 31.9 %collective-permute-start.30 = (bf16[3,4,192,256]{3,2,1,0:T(8,128)(2,1)}, bf16[3,4,192,256]{3,2,1,0:T(8,128)(2,1)}, u32[]{:S(2)}, u32[]{:S(2)}) collective-permute-start(bf16[3,4,192,256]{3,2,1,0:T(8,128)(2,1)} %collective-permute-done.28.refs_3_.refs_12_.refs_13_), channel_id=1, source_target_pairs={{0,8},{10,2},{8,16},{18,10},{16,24},{26,18},{24,28},{30,26},{28,20... | collective-permute-start | bytes 3538952 | tf_op jit(solution)/shard_map/ppermute | solution.py:90
  200.8 34.8 %collective-permute-start.29 = (bf16[3,4,192,256]{3,2,1,0:T(8,128)(2,1)}, bf16[3,4,192,256]{3,2,1,0:T(8,128)(2,1)}, u32[]{:S(2)}, u32[]{:S(2)}) collective-permute-start(bf16[3,4,192,256]{3,2,1,0:T(8,128)(2,1)} %collective-permute-done.28.refs_3_.refs_12_.refs_13_), channel_id=1, source_target_pairs={{0,2},{2,0},{1,3},{3,1},{4,6},{6,4},{5,7},{7,5},{8,10},{10,8},{9,1... | collective-permute-start | bytes 3538952 | tf_op jit(solution)/shard_map/ppermute | solution.py:94
  203.2 29.9 %collective-permute-start.31 = (bf16[3,1536,128]{2,1,0:T(8,128)(2,1)}, bf16[3,1536,128]{2,1,0:T(8,128)(2,1)}, u32[]{:S(2)}, u32[]{:S(2)}) collective-permute-start(bf16[3,1536,128]{2,1,0:T(8,128)(2,1)} %constant_dynamic-slice_fusion), channel_id=1, source_target_pairs={{0,1},{1,0},{2,3},{3,2},{4,5},{5,4},{6,7},{7,6},{8,9},{9,8},{10,11... | collective-permute-start | bytes 3538952 | tf_op jit(solution)/shard_map/ppermute | solution.py:94
  206.5 41.8 %collective-permute-start.24 = (bf16[4,6,192,256]{3,2,1,0:T(8,128)(2,1)}, bf16[4,6,192,256]{3,2,1,0:T(8,128)(2,1)}, u32[]{:S(2)}, u32[]{:S(2)}) collective-permute-start(bf16[4,6,192,256]{3,2,1,0:T(8,128)(2,1)} %get-tuple-element.192), channel_id=1, source_target_pairs={{0,2},{2,0},{1,3},{3,1},{4,6},{6,4},{5,7},{7,5},{8,10},{10,8},{9,1... | collective-permute-start | bytes 7077896 | tf_op jit(solution)/shard_map/ppermute | solution.py:94
  235.6 39.4 %collective-permute-start.43 = (bf16[2,1536,128]{2,1,0:T(8,128)(2,1)S(1)}, bf16[2,1536,128]{2,1,0:T(8,128)(2,1)}, u32[]{:S(2)}, u32[]{:S(2)}) collective-permute-start(bf16[2,1536,128]{2,1,0:T(8,128)(2,1)S(1)} %constant_dynamic-slice_fusion.3), channel_id=1, source_target_pairs={{0,1},{1,0},{2,3},{3,2},{4,5},{5,4},{6,7},{7,6},{8,9},{9,8},{10,11... | collective-permute-start | bytes 2359304 | tf_op jit(solution)/shard_map/ppermute | solution.py:94
  236.2 36.8 %collective-permute-start.38 = (bf16[3,4,192,256]{3,2,1,0:T(8,128)(2,1)}, bf16[3,4,192,256]{3,2,1,0:T(8,128)(2,1)}, u32[]{:S(2)}, u32[]{:S(2)}) collective-permute-start(bf16[3,4,192,256]{3,2,1,0:T(8,128)(2,1)} %get-tuple-element.212.refs_8_.refs_4_), channel_id=1, source_target_pairs={{0,8},{10,2},{8,16},{18,10},{16,24},{26,18},{24,28},{30,26},{28,20... | collective-permute-start | bytes 3538952 | tf_op jit(solution)/shard_map/ppermute | solution.py:90
  236.6 40.6 %collective-permute-start.41 = (bf16[4,6,192,256]{3,2,1,0:T(8,128)(2,1)}, bf16[4,6,192,256]{3,2,1,0:T(8,128)(2,1)}, u32[]{:S(2)}, u32[]{:S(2)}) collective-permute-start(bf16[4,6,192,256]{3,2,1,0:T(8,128)(2,1)} %get-tuple-element.214), channel_id=1, source_target_pairs={{0,2},{2,0},{1,3},{3,1},{4,6},{6,4},{5,7},{7,5},{8,10},{10,8},{9,1... | collective-permute-start | bytes 7077896 | tf_op jit(solution)/shard_map/ppermute | solution.py:94
  248.3 28.5 %collective-permute-start.42 = (bf16[3,4,192,256]{3,2,1,0:T(8,128)(2,1)}, bf16[3,4,192,256]{3,2,1,0:T(8,128)(2,1)}, u32[]{:S(2)}, u32[]{:S(2)}) collective-permute-start(bf16[3,4,192,256]{3,2,1,0:T(8,128)(2,1)} %collective-permute-done.30.refs_4_.refs_13_.refs_14_), channel_id=1, source_target_pairs={{0,2},{2,0},{1,3},{3,1},{4,6},{6,4},{5,7},{7,5},{8,10},{10,8},{9,1... | collective-permute-start | bytes 3538952 | tf_op jit(solution)/shard_map/ppermute | solution.py:94
  248.3 28.0 %collective-permute-start.44 = (bf16[3,1536,128]{2,1,0:T(8,128)(2,1)}, bf16[3,1536,128]{2,1,0:T(8,128)(2,1)}, u32[]{:S(2)}, u32[]{:S(2)}) collective-permute-start(bf16[3,1536,128]{2,1,0:T(8,128)(2,1)} %collective-permute-done.31.refs_5_.refs_12_), channel_id=1, source_target_pairs={{0,2},{2,0},{1,3},{3,1},{4,6},{6,4},{5,7},{7,5},{8,10},{10,8},{9,1... | collective-permute-start | bytes 3538952 | tf_op jit(solution)/shard_map/ppermute | solution.py:94
  273.0 34.4 %collective-permute-start.39 = (bf16[3,4,192,256]{3,2,1,0:T(8,128)(2,1)}, bf16[3,4,192,256]{3,2,1,0:T(8,128)(2,1)}, u32[]{:S(2)}, u32[]{:S(2)}) collective-permute-start(bf16[3,4,192,256]{3,2,1,0:T(8,128)(2,1)} %collective-permute-done.38.refs_4_.refs_9_.refs_5_), channel_id=1, source_target_pairs={{0,2},{2,0},{1,3},{3,1},{4,6},{6,4},{5,7},{7,5},{8,10},{10,8},{9,1... | collective-permute-start | bytes 3538952 | tf_op jit(solution)/shard_map/ppermute | solution.py:94
  275.0 28.8 %collective-permute-start.40 = (bf16[3,4,192,256]{3,2,1,0:T(8,128)(2,1)}, bf16[3,4,192,256]{3,2,1,0:T(8,128)(2,1)}, u32[]{:S(2)}, u32[]{:S(2)}) collective-permute-start(bf16[3,4,192,256]{3,2,1,0:T(8,128)(2,1)} %collective-permute-done.38.refs_4_.refs_9_.refs_5_), channel_id=1, source_target_pairs={{0,8},{10,2},{8,16},{18,10},{16,24},{26,18},{24,28},{30,26},{28,20... | collective-permute-start | bytes 3538952 | tf_op jit(solution)/shard_map/ppermute | solution.py:90
  276.3 32.4 %collective-permute-start.36 = (bf16[3,4,192,256]{3,2,1,0:T(8,128)(2,1)}, bf16[3,4,192,256]{3,2,1,0:T(8,128)(2,1)}, u32[]{:S(2)}, u32[]{:S(2)}) collective-permute-start(bf16[3,4,192,256]{3,2,1,0:T(8,128)(2,1)} %collective-permute-done.35.refs_3_.refs_14_.refs_15_), channel_id=1, source_target_pairs={{0,2},{2,0},{1,3},{3,1},{4,6},{6,4},{5,7},{7,5},{8,10},{10,8},{9,1... | collective-permute-start | bytes 3538952 | tf_op jit(solution)/shard_map/ppermute | solution.py:94
  303.8 36.8 %collective-permute-start.54 = (bf16[2,1536,128]{2,1,0:T(8,128)(2,1)}, bf16[2,1536,128]{2,1,0:T(8,128)(2,1)}, u32[]{:S(2)}, u32[]{:S(2)}) collective-permute-start(bf16[2,1536,128]{2,1,0:T(8,128)(2,1)} %collective-permute-done.43.refs_5_.refs_13_), channel_id=1, source_target_pairs={{0,2},{2,0},{1,3},{3,1},{4,6},{6,4},{5,7},{7,5},{8,10},{10,8},{9,1... | collective-permute-start | bytes 2359304 | tf_op jit(solution)/shard_map/ppermute | solution.py:94
  303.8 37.4 %collective-permute-start.52 = (bf16[4,6,192,256]{3,2,1,0:T(8,128)(2,1)}, bf16[4,6,192,256]{3,2,1,0:T(8,128)(2,1)}, u32[]{:S(2)}, u32[]{:S(2)}) collective-permute-start(bf16[4,6,192,256]{3,2,1,0:T(8,128)(2,1)} %get-tuple-element.230), channel_id=1, source_target_pairs={{0,2},{2,0},{1,3},{3,1},{4,6},{6,4},{5,7},{7,5},{8,10},{10,8},{9,1... | collective-permute-start | bytes 7077896 | tf_op jit(solution)/shard_map/ppermute | solution.py:94
  308.7 32.0 %collective-permute-start.53 = (bf16[3,4,192,256]{3,2,1,0:T(8,128)(2,1)}, bf16[3,4,192,256]{3,2,1,0:T(8,128)(2,1)}, u32[]{:S(2)}, u32[]{:S(2)}) collective-permute-start(bf16[3,4,192,256]{3,2,1,0:T(8,128)(2,1)} %collective-permute-done.40.refs_4_.refs_10_.refs_6_), channel_id=1, source_target_pairs={{0,2},{2,0},{1,3},{3,1},{4,6},{6,4},{5,7},{7,5},{8,10},{10,8},{9,1... | collective-permute-start | bytes 3538952 | tf_op jit(solution)/shard_map/ppermute | solution.py:94
  333.4 40.1 %collective-permute-start.48 = (bf16[3,4,192,256]{3,2,1,0:T(8,128)(2,1)}, bf16[3,4,192,256]{3,2,1,0:T(8,128)(2,1)}, u32[]{:S(2)}, u32[]{:S(2)}) collective-permute-start(bf16[3,4,192,256]{3,2,1,0:T(8,128)(2,1)} %collective-permute-done.47.refs_3_.refs_11_.refs_7_), channel_id=1, source_target_pairs={{0,2},{2,0},{1,3},{3,1},{4,6},{6,4},{5,7},{7,5},{8,10},{10,8},{9,1... | collective-permute-start | bytes 3538952 | tf_op jit(solution)/shard_map/ppermute | solution.py:94
  335.0 30.6 %collective-permute-start.49 = (bf16[3,4,192,128]{3,2,1,0:T(8,128)(2,1)S(1)}, bf16[3,4,192,128]{3,2,1,0:T(8,128)(2,1)}, u32[]{:S(2)}, u32[]{:S(2)}) collective-permute-start(bf16[3,4,192,128]{3,2,1,0:T(8,128)(2,1)S(1)} %constant_dynamic-slice_fusion.1), channel_id=1, source_target_pairs={{0,8},{10,2},{8,16},{18,10},{16,24},{26,18},{24,28},{30,26},{28,20... | collective-permute-start | bytes 1769480 | tf_op jit(solution)/shard_map/ppermute | solution.py:90
  340.6 32.9 %collective-permute-start.46 = (bf16[4,6,192,256]{3,2,1,0:T(8,128)(2,1)}, bf16[4,6,192,256]{3,2,1,0:T(8,128)(2,1)}, u32[]{:S(2)}, u32[]{:S(2)}) collective-permute-start(bf16[4,6,192,256]{3,2,1,0:T(8,128)(2,1)} %get-tuple-element.226), channel_id=1, source_target_pairs={{0,2},{2,0},{1,3},{3,1},{4,6},{6,4},{5,7},{7,5},{8,10},{10,8},{9,1... | collective-permute-start | bytes 7077896 | tf_op jit(solution)/shard_map/ppermute | solution.py:94
  340.7 26.8 %collective-permute-start.51 = (bf16[3,6,192,256]{3,2,1,0:T(8,128)(2,1)}, bf16[3,6,192,256]{3,2,1,0:T(8,128)(2,1)}, u32[]{:S(2)}, u32[]{:S(2)}) collective-permute-start(bf16[3,6,192,256]{3,2,1,0:T(8,128)(2,1)} %hop_sum.26.refs_6_), channel_id=1, source_target_pairs={{0,8},{10,2},{8,16},{18,10},{16,24},{26,18},{24,28},{30,26},{28,20... | collective-permute-start | bytes 5308424 | tf_op jit(solution)/shard_map/ppermute | solution.py:90
  418.8 37.3 %collective-permute-start.61 = (bf16[512,1536]{1,0:T(8,128)(2,1)}, bf16[512,1536]{1,0:T(8,128)(2,1)}, u32[]{:S(2)}, u32[]{:S(2)}) collective-permute-start(bf16[512,1536]{1,0:T(8,128)(2,1)} %get-tuple-element.250.refs_1_), channel_id=1, source_target_pairs={{0,1},{1,0},{2,3},{3,2},{4,5},{5,4},{6,7},{7,6},{8,9},{9,8},{10,11... | collective-permute-start | bytes 4718600 | tf_op jit(solution)/shard_map/ppermute | solution.py:94
  419.2 37.0 %collective-permute-start.62 = (f32[16,1024]{1,0:T(8,128)}, f32[16,1024]{1,0:T(8,128)S(1)}, u32[]{:S(2)}, u32[]{:S(2)}) collective-permute-start(f32[16,1024]{1,0:T(8,128)} %get-tuple-element.251.refs_0_.refs_5_), channel_id=1, source_target_pairs={{0,1},{1,0},{2,3},{3,2},{4,5},{5,4},{6,7},{7,6},{8,9},{9,8},{10,11... | collective-permute-start | bytes 196616 | tf_op jit(solution)/shard_map/ppermute | solution.py:94
  426.5 29.7 %collective-permute-start.60 = (bf16[3,6,192,256]{3,2,1,0:T(8,128)(2,1)}, bf16[3,6,192,256]{3,2,1,0:T(8,128)(2,1)}, u32[]{:S(2)}, u32[]{:S(2)}) collective-permute-start(bf16[3,6,192,256]{3,2,1,0:T(8,128)(2,1)} %hop_sum.29.refs_0_.refs_1_), channel_id=1, source_target_pairs={{0,2},{2,0},{1,3},{3,1},{4,6},{6,4},{5,7},{7,5},{8,10},{10,8},{9,1... | collective-permute-start | bytes 5308424 | tf_op jit(solution)/shard_map/ppermute | solution.py:94
  429.6 26.6 %collective-permute-start.59 = (bf16[3,6,192,128]{3,2,1,0:T(8,128)(2,1)}, bf16[3,6,192,128]{3,2,1,0:T(8,128)(2,1)S(1)}, u32[]{:S(2)}, u32[]{:S(2)}) collective-permute-start(bf16[3,6,192,128]{3,2,1,0:T(8,128)(2,1)} %hop_sum.30.refs_1_), channel_id=1, source_target_pairs={{0,8},{10,2},{8,16},{18,10},{16,24},{26,18},{24,28},{30,26},{28,20... | collective-permute-start | bytes 2654216 | tf_op jit(solution)/shard_map/ppermute | solution.py:90
  456.2 35.2 %collective-permute-start.65 = (bf16[512,1536]{1,0:T(8,128)(2,1)}, bf16[512,1536]{1,0:T(8,128)(2,1)}, u32[]{:S(2)}, u32[]{:S(2)}) collective-permute-start(bf16[512,1536]{1,0:T(8,128)(2,1)} %get-tuple-element.260.refs_2_), channel_id=1, source_target_pairs={{0,1},{1,0},{2,3},{3,2},{4,5},{5,4},{6,7},{7,6},{8,9},{9,8},{10,11... | collective-permute-start | bytes 4718600 | tf_op jit(solution)/shard_map/ppermute | solution.py:94
  456.5 34.8 %collective-permute-start.63 = (bf16[4,6,192,256]{3,2,1,0:T(8,128)(2,1)}, bf16[4,6,192,256]{3,2,1,0:T(8,128)(2,1)}, u32[]{:S(2)}, u32[]{:S(2)}) collective-permute-start(bf16[4,6,192,256]{3,2,1,0:T(8,128)(2,1)} %get-tuple-element.258), channel_id=1, source_target_pairs={{0,2},{2,0},{1,3},{3,1},{4,6},{6,4},{5,7},{7,5},{8,10},{10,8},{9,1... | collective-permute-start | bytes 7077896 | tf_op jit(solution)/shard_map/ppermute | solution.py:94
  461.2 30.2 %collective-permute-start.64 = (bf16[3,6,192,256]{3,2,1,0:T(8,128)(2,1)}, bf16[3,6,192,256]{3,2,1,0:T(8,128)(2,1)}, u32[]{:S(2)}, u32[]{:S(2)}) collective-permute-start(bf16[3,6,192,256]{3,2,1,0:T(8,128)(2,1)} %hop_sum.31.refs_1_), channel_id=1, source_target_pairs={{0,8},{10,2},{8,16},{18,10},{16,24},{26,18},{24,28},{30,26},{28,20... | collective-permute-start | bytes 5308424 | tf_op jit(solution)/shard_map/ppermute | solution.py:90
  491.4 27.5 %collective-permute-start.66 = (bf16[4,6,192,256]{3,2,1,0:T(8,128)(2,1)}, bf16[4,6,192,256]{3,2,1,0:T(8,128)(2,1)}, u32[]{:S(2)}, u32[]{:S(2)}) collective-permute-start(bf16[4,6,192,256]{3,2,1,0:T(8,128)(2,1)} %get-tuple-element.265), channel_id=1, source_target_pairs={{0,2},{2,0},{1,3},{3,1},{4,6},{6,4},{5,7},{7,5},{8,10},{10,8},{9,1... | collective-permute-start | bytes 7077896 | tf_op jit(solution)/shard_map/ppermute | solution.py:94
  518.9 53.1 %collective-permute-start.72 = (bf16[768,1536]{1,0:T(8,128)(2,1)}, bf16[768,1536]{1,0:T(8,128)(2,1)}, u32[]{:S(2)}, u32[]{:S(2)}) collective-permute-start(bf16[768,1536]{1,0:T(8,128)(2,1)} %get-tuple-element.278.refs_0_.refs_2_), channel_id=1, source_target_pairs={{0,1},{1,0},{2,3},{3,2},{4,5},{5,4},{6,7},{7,6},{8,9},{9,8},{10,11... | collective-permute-start | bytes 7077896 | tf_op jit(solution)/shard_map/ppermute | solution.py:94
  523.7 29.1 %collective-permute-start.68 = (bf16[3,6,192,256]{3,2,1,0:T(8,128)(2,1)}, bf16[3,6,192,256]{3,2,1,0:T(8,128)(2,1)}, u32[]{:S(2)}, u32[]{:S(2)}) collective-permute-start(bf16[3,6,192,256]{3,2,1,0:T(8,128)(2,1)} %hop_sum.33.refs_0_), channel_id=1, source_target_pairs={{0,8},{10,2},{8,16},{18,10},{16,24},{26,18},{24,28},{30,26},{28,20... | collective-permute-start | bytes 5308424 | tf_op jit(solution)/shard_map/ppermute | solution.py:90
  574.0 35.3 %collective-permute-start.76 = (bf16[1024,384]{1,0:T(8,128)(2,1)S(1)}, bf16[1024,384]{1,0:T(8,128)(2,1)}, u32[]{:S(2)}, u32[]{:S(2)}) collective-permute-start(bf16[1024,384]{1,0:T(8,128)(2,1)S(1)} %copy-done.8), channel_id=1, source_target_pairs={{0,1},{1,0},{2,3},{3,2},{4,5},{5,4},{6,7},{7,6},{8,9},{9,8},{10,11... | collective-permute-start | bytes 2359304 | tf_op jit(solution)/shard_map/ppermute | solution.py:94
  575.7 33.6 %collective-permute-start.73 = (bf16[4,5,192,256]{3,2,1,0:T(8,128)(2,1)}, bf16[4,5,192,256]{3,2,1,0:T(8,128)(2,1)}, u32[]{:S(2)}, u32[]{:S(2)}) collective-permute-start(bf16[4,5,192,256]{3,2,1,0:T(8,128)(2,1)} %get-tuple-element.282), channel_id=1, source_target_pairs={{0,2},{2,0},{1,3},{3,1},{4,6},{6,4},{5,7},{7,5},{8,10},{10,8},{9,1... | collective-permute-start | bytes 5898248 | tf_op jit(solution)/shard_map/ppermute | solution.py:94
  579.4 29.9 %collective-permute-start.74 = (bf16[2,6,192,256]{3,2,1,0:T(8,128)(2,1)}, bf16[2,6,192,256]{3,2,1,0:T(8,128)(2,1)}, u32[]{:S(2)}, u32[]{:S(2)}) collective-permute-start(bf16[2,6,192,256]{3,2,1,0:T(8,128)(2,1)} %hop_sum.37.refs_1_), channel_id=1, source_target_pairs={{0,8},{10,2},{8,16},{18,10},{16,24},{26,18},{24,28},{30,26},{28,20... | collective-permute-start | bytes 3538952 | tf_op jit(solution)/shard_map/ppermute | solution.py:90
  609.3 29.5 %collective-permute-start.81 = (bf16[1024,384]{1,0:T(8,128)(2,1)}, bf16[1024,384]{1,0:T(8,128)(2,1)S(1)}, u32[]{:S(2)}, u32[]{:S(2)}) collective-permute-start(bf16[1024,384]{1,0:T(8,128)(2,1)} %get-tuple-element.291.refs_4_.refs_6_), channel_id=1, source_target_pairs={{0,1},{1,0},{2,3},{3,2},{4,5},{5,4},{6,7},{7,6},{8,9},{9,8},{10,11... | collective-permute-start | bytes 2359304 | tf_op jit(solution)/shard_map/ppermute | solution.py:94
  646.0 27.1 %collective-permute-start.85 = (bf16[1024,512]{1,0:T(8,128)(2,1)}, bf16[1024,512]{1,0:T(8,128)(2,1)}, u32[]{:S(2)}, u32[]{:S(2)}) collective-permute-start(bf16[1024,512]{1,0:T(8,128)(2,1)} %key_value_grads.1.refs_0_.refs_5_.refs_7_), channel_id=1, source_target_pairs={{0,1},{1,0},{2,3},{3,2},{4,5},{5,4},{6,7},{7,6},{8,9},{9,8},{10,11... | collective-permute-start | bytes 3145736 | tf_op jit(solution)/shard_map/ppermute | solution.py:94
  664.0 33.9 %collective-permute-start.89 = (bf16[2,6,192,256]{3,2,1,0:T(8,128)(2,1)}, bf16[2,6,192,256]{3,2,1,0:T(8,128)(2,1)}, u32[]{:S(2)}, u32[]{:S(2)}) collective-permute-start(bf16[2,6,192,256]{3,2,1,0:T(8,128)(2,1)} %hop_sum.43.refs_0_.refs_1_), channel_id=1, source_target_pairs={{0,2},{2,0},{1,3},{3,1},{4,6},{6,4},{5,7},{7,5},{8,10},{10,8},{9,1... | collective-permute-start | bytes 3538952 | tf_op jit(solution)/shard_map/ppermute | solution.py:94
  666.9 28.1 %collective-permute-start.88 = (bf16[1,5,192,256]{3,2,1,0:T(8,128)(2,1)}, bf16[1,5,192,256]{3,2,1,0:T(8,128)(2,1)}, u32[]{:S(2)}, u32[]{:S(2)}) collective-permute-start(bf16[1,5,192,256]{3,2,1,0:T(8,128)(2,1)} %hop_sum.45.refs_1_), channel_id=1, source_target_pairs={{0,8},{10,2},{8,16},{18,10},{16,24},{26,18},{24,28},{30,26},{28,20... | collective-permute-start | bytes 1474568 | tf_op jit(solution)/shard_map/ppermute | solution.py:90
  (69 other events, 875.0 us)

commit v4 on v3

--- a/solution.py
+++ b/solution.py
@@ -604,21 +604,24 @@
 def fetch_weights(sc, bufs, w, kinds, local, shard, hidden, sem):
     hops = len(bufs) // 2
     core = sc[len(bufs)]
-    for side in range(2):
-        for k, buf in enumerate(bufs):
-            rows = pl.ds(pl.multiple_of(sc[k] * shard, shard), shard)
-            lanes = pl.ds(side * hidden, hidden)
-            if k in (hops, 2 * hops):
-                at = core if k == hops else 1 - core
-                lanes = pl.ds(pl.multiple_of(side * hidden + at * (hidden // 2), LANES), hidden // 2)
-            pltpu.make_async_copy(buf.at[kinds, local + side], w.at[kinds, rows, lanes], sem).start()
+    for k, buf in enumerate(bufs):
+        rows = pl.ds(pl.multiple_of(sc[k] * shard, shard), shard)
+        target = w.at[kinds, :, rows, :]
+        if k in (hops, 2 * hops):
+            at = core if k == hops else 1 - core
+            target = w.at[kinds, :, rows, pl.ds(pl.multiple_of(at * (hidden // 2), LANES), hidden // 2)]
+        pltpu.make_async_copy(buf.at[kinds, pl.ds(local, 2)], target, sem).start()
+
+
+def both(w, kind):
+    return jnp.concatenate([w[kind, 0], w[kind, 1]], axis=1)
 
 
 def activate(ids, hidden, rows, x, grad_rows, w, wt, pick_in, pick, scaled, acts):
     lane = lax.broadcasted_iota(jnp.int32, (x.shape[0], LANES), 1)
-    gate = mm(x, w[0])
-    up = mm(x, w[1])
-    grad = mm(grad_rows, w[2])
+    gate = mm(x, both(w, 0))
+    up = mm(x, both(w, 1))
+    grad = mm(grad_rows, both(w, 2))
     table = wt[rows, :]
     sig = 1.0 / (1.0 + jnp.exp(-gate))
     silu = gate * sig
@@ -687,9 +690,13 @@
     spans = [pl.ds(at, block) for at in range(0, rows_total, block)]
     ids = [sc[total + 1 + 2 * (total // 2) + side] + ROUTER_LANE for side in range(2)]
 
-    def load_rows(i):
-        pltpu.make_async_copy(n2.at[spans[i]], xs.at[spans[i]], x_sem.at[i]).start()
-        pltpu.make_async_copy(cot.at[spans[i]], cs.at[spans[i]], c_sem.at[i]).start()
+    loads = (pl.ds(0, block), pl.ds(block, rows_total - block))
+
+    def row_copies(i):
+        return [
+            pltpu.make_async_copy(n2.at[loads[i]], xs.at[loads[i]], x_sem.at[i]),
+            pltpu.make_async_copy(cot.at[loads[i]], cs.at[loads[i]], c_sem.at[i]),
+        ]
 
     def load_wide():
         for k, (src, dst) in enumerate(((moe_in, moe), (back_in, back))):
@@ -708,12 +715,12 @@
         pltpu.make_async_copy(w.at[kinds], w.at[kinds], w_sem).wait()
         pltpu.make_async_copy(scaled_in, scaled, out_sem.at[2]).wait()
     else:
-        for i in range(len(spans)):
-            load_rows(i)
+        for copy in row_copies(0) + row_copies(1):
+            copy.start()
         pltpu.make_async_copy(w.at[kinds], w.at[kinds], w_sem).wait()
         for i, rows in enumerate(spans):
-            pltpu.make_async_copy(n2.at[rows], xs.at[rows], x_sem.at[i]).wait()
-            pltpu.make_async_copy(cot.at[rows], cs.at[rows], c_sem.at[i]).wait()
+            for copy in row_copies(i) if i < 2 else ():
+                copy.wait()
             if i == 1:
                 load_wide()
             picked = activate(ids, hidden, rows, xs[rows, :], cs[rows, :], w, wt, pick_in, pick, scaled, acts)
@@ -725,9 +732,9 @@
             pltpu.make_async_copy(src, dst, in_sem.at[k]).wait()
     outs = []
     if not front:
-        outs.append((moe, moe_out, 0, lambda rows: mm_nt(scaled[rows, :], w[2])))
+        outs.append((moe, moe_out, 0, lambda rows: mm_nt(scaled[rows, :], both(w, 2))))
     if not rest:
-        two = lambda rows: mm_nt(acts[rows, 0 : 2 * hidden], w[0]) + mm_nt(acts[rows, 2 * hidden :], w[1])
+        two = lambda rows: mm_nt(acts[rows, 0 : 2 * hidden], both(w, 0)) + mm_nt(acts[rows, 2 * hidden :], both(w, 1))
         outs.append((back, back_out, 1, two))
     for i, rows in enumerate(spans):
         for acc, halves, k, make in outs:
@@ -804,7 +811,7 @@
         give((EXPERTS, rows), f32, whole((EXPERTS, rows)))
     dma = pltpu.SemaphoreType.DMA
     scratch = [
-        pltpu.VMEM((3, width, 2 * hidden), bf),
+        pltpu.VMEM((3, 2, width, hidden), bf),
         pltpu.VMEM((rows, 2 * hidden), bf),
         pltpu.VMEM((rows, 4 * hidden), bf),
         dma,
@@ -813,7 +820,7 @@
     ]
     scratch += [pltpu.VMEM((rows, width), f32)] * (2 if mode == "all" else 1)
     if not rest:
-        scratch += [pltpu.VMEM((rows, width), bf)] * 2 + [dma((rows // 256,))] * 2
+        scratch += [pltpu.VMEM((rows, width), bf)] * 2 + [dma((2,))] * 2
     if not front:
         scratch += [pltpu.VMEM((width, rows), bf)] * 2 + [pltpu.VMEM((slots, 6, shard, hidden), bf)] * 2 + [dma((2,))] * 2
     if ends:
@@ -857,7 +864,7 @@
     slots, mats, shard, hidden = keeps[0].shape
     lanes = hidden // 2 if stage in (None, "end") else hidden
     side = 1 if stage == "end" else 0
-    per = mats // 2 if mats % 2 == 0 else mats
+    per = mats // 2 if pairs > 1 else mats
     piece = pl.BlockSpec((1, per, shard, lanes), lambda m, s: (slot, m, 0, side))
     wide = lambda a: pl.BlockSpec((pairs, per, shard, a.shape[3]), lambda m, s: (0, m, 0, 0))
     out = sds((pairs, mats, shard, hidden // 2 if stage is None else hidden), bf)
@@ -1326,8 +1333,6 @@
     open_chunk(token)
     c3 = chunks[3]
     c3.step()
-    first_far_b = swap(after(first_half[split:], token), "tp")
-    theirs_a = swap(after(first_far_a, token), "ctx")
     keep, send, token = work(2)
 
     s0.add(keep, send)
@@ -1339,12 +1344,12 @@
     c2.share(token)
     c3.step(token)
     s0.step([token])
-    theirs_b = swap(after(first_far_b, token), "ctx")
     keep, send, token = work(4)
 
     s1.add(keep, send)
     c3.step(token)
     s0.step([token])
+    first_far_b = swap(after(first_half[split:], token), "tp")
     keep, send, token = work(5)
 
     s1.add(keep, send)
@@ -1354,8 +1359,8 @@
     made_early = state["made"]
 
     window.gated = True
-    token = window.gate(token)
-    s0.step([token])
+    theirs_a = swap(after(first_far_a, token), "ctx")
+    theirs_b = swap(after(first_far_b, token), "ctx")
     pick_t = work(7, "front_end", window.step())
     made_late = state["made"]
     back = state["back"]
@@ -1363,13 +1368,14 @@
     back_far_a = swap(back[0], "tp")
     pick_far = swap(after(pick_t, back[0]), "tp")
     token = window.gate(pick_t)
+    s0.step([token])
     s1.step([token])
-    s0_mine, s0_theirs = s0.finish([token])
     state["made"] = made_early
-    keep_early, send_early, token = work(6, "rest", [s0_mine, *window.step()])
+    keep_early, send_early, token = work(6, "rest", window.step())
     token = window.gate(token, back_far_a, pick_far)
     back_far_b = swap(after(back[1], token), "tp")
     s2.add(keep_early, send_early, token)
+    s0_mine, s0_theirs = s0.finish([token])
     s1.step([token])
     emitted = emit((s0_mine, s0_theirs), 0, EXPERTS, None, core_only, [token])
     state["made"] = made_late
@@ -1420,25 +1426,27 @@
     far_kv = swap(after(low_kv, token), "tp")
     late = Scatter(core, count, plain, core_at)
     late.add(last_keep, last_send, token)
-    early.step([token])
-    emitted = emit((s1_mine, s1_theirs), EXPERTS * 3 // 8, EXPERTS, emitted, core_only, [token, early.value])
-    late.step([emitted[0]])
-    s2_mine, s2_theirs = s2.finish([late.value])
-    early.step([s2_mine])
-    late.step([s2_mine])
+    late.step([token])
+    early.step([late.value])
+    emitted = emit((s1_mine, s1_theirs), EXPERTS * 3 // 8, EXPERTS, emitted, core_only, [late.value])
+    late.step([emitted[0], early.value])
     moe_far_b = swap(after(moe[1], late.value), "tp")
     lows = [dq_a, dq_b, low_kv, far_qa, far_qb, far_kv]
     token_grad = finish(
-        tok, extra, rg, lows, w_first, (first_far_a, first_far_b), (theirs_a, theirs_b), core_only, [late.value, early.value]
+        tok, extra, rg, lows, w_first, (first_far_a, first_far_b), (theirs_a, theirs_b), core_only, [late.value]
     ).reshape(tokens.shape)
     late.step([token_grad, moe_far_b])
-    early_sums = early.finish([late.value])
-    grad_gate, grad_up, grad_down = emit((s2_mine, s2_theirs), EXPERTS * 3 // 4, EXPERTS, emitted, core_only, [early_sums[0]])
-    late.step([grad_gate])
-    result = combine(res, moe, (moe_far_a, moe_far_b), core_only, [late.value]).reshape(tokens.shape)
+    s2_mine, s2_theirs = s2.finish([late.value])
+    early.step([late.value])
+    late.step([s2_mine, early.value])
+    result = combine(res, moe, (moe_far_a, moe_far_b), core_only, [late.value])
+    grad_gate, grad_up, grad_down = emit((s2_mine, s2_theirs), EXPERTS * 3 // 4, EXPERTS, emitted, core_only, [late.value])
+    early_sums = early.finish([result])
+    late_sums = late.finish([result, grad_gate])
+    result = result.reshape(tokens.shape)
     kv_width = kvs * HEAD_DIM
     widths = (w_output.shape[1], w_query.shape[1], kv_width, kv_width)
-    grad_output, grad_query, grad_key, grad_value, extras = spread(early_sums, late.finish(), widths, core_only)
+    grad_output, grad_query, grad_key, grad_value, extras = spread(early_sums, late_sums, widths, core_only)
     grad_norm_two = extras[:, 1]
     grad_router = extras[:, ROUTER_LANE : ROUTER_LANE + EXPERTS]
     gain_part = extras[:, 0] + extras[:, LANES]

time: 745 us -> 742 us (level)
  waiting for transfers between devices: 110 us -> 93.9 us
  Pallas kernels: 507 us -> 515 us
  starting transfers between devices: 69.9 us -> 77.4 us
    ppermute x40, waiting for transfers between devices: 72.1 us -> 50.9 us  [ring_hop(): return sent(lax.ppermute(values, ('dp', 'ctx'), pairs))]
    pallas_call x52, Pallas kernels: 507 us -> 515 us  [call(): pl.pallas_call(lambda sc, *refs: kernel(sc, *refs[len(deps):]), out_shape...]
  transfers between devices with their start and end apart: 95 -> 95, of which waited for: 21 -> 18; matrix products, arithmetic and copies ran while one was open for 5% -> 5% of each run, Pallas kernels for 67% -> 68%
where the time goes in v4:
time: 742 us; the launch traced here: 736 us
  Pallas kernels  515 us (69%)
  waiting for transfers between devices  93.9 us (13%)
  starting transfers between devices  77.4 us (10%)
  local copies, waits for them, and re-layouts  40 us (5%)
  other arithmetic  8.79 us (1%)
    pallas_call x52, Pallas kernels, call(): pl.pallas_call(lambda sc, *refs: kernel(sc, *refs[len(deps):]), out_shape...  515 us
    ppermute x40, starting transfers between devices, ring_hop(): return sent(lax.ppermute(values, ('dp', 'ctx'), pairs))  52.7 us
    ppermute x40, waiting for transfers between devices, ring_hop(): return sent(lax.ppermute(values, ('dp', 'ctx'), pairs))  50.9 us
    ppermute x55, waiting for transfers between devices, swap(): swapped = lax.ppermute(values, axis, [(0, 1), (1, 0)])  43 us
    ppermute x55, starting transfers between devices, swap(): swapped = lax.ppermute(values, axis, [(0, 1), (1, 0)])  24.7 us
  transfers between devices with their start and end apart: 95, of which 18 were waited for; matrix products, arithmetic and copies ran while one was open for 5% of the time, Pallas kernels for 68%

profile of v4, /device:TPU:0, one launch (start us, length us, event | category | flops | bytes accessed | tf_op | source)
XLA Modules:
  0.0 736.3 jit_solution(2719521527250023659)
XLA Ops:
  13.3 9.0 %collective-permute-done.refs_4_ = bf16[18,192,128]{2,1,0:T(8,128)(2,1)S(1)} collective-permute-done((bf16[18,192,128]{2,1,0:T(8,128)(2,1)}, bf16[18,192,128]{2,1,0:T(8,128)(2,1)S(1)}, u32[]{:S(2)}, u32[]{:S(2)}) %collective-permute-start) | collective-permute-done | bytes 884768 | tf_op jit(solution)/shard_map/ppermute | solution.py:90
  28.0 7.4 %collective-permute-done.1.refs_5_ = bf16[18,192,128]{2,1,0:T(8,128)(2,1)} collective-permute-done((bf16[18,192,128]{2,1,0:T(8,128)(2,1)S(1)}, bf16[18,192,128]{2,1,0:T(8,128)(2,1)}, u32[]{:S(2)}, u32[]{:S(2)}) %collective-permute-start.1) | collective-permute-done | bytes 884768 | tf_op jit(solution)/shard_map/ppermute | solution.py:90
  37.6 11.2 %collective-permute-done.2.refs_6_ = bf16[18,192,128]{2,1,0:T(8,128)(2,1)S(1)} collective-permute-done((bf16[18,192,128]{2,1,0:T(8,128)(2,1)}, bf16[18,192,128]{2,1,0:T(8,128)(2,1)S(1)}, u32[]{:S(2)}, u32[]{:S(2)}) %collective-permute-start.2) | collective-permute-done | bytes 884768 | tf_op jit(solution)/shard_map/ppermute | solution.py:90
  51.5 5.7 collective-permute-done.3.refs_7_
  62.0 17.7 %project.1 = (bf16[11,1536,128]{2,1,0:T(8,128)(2,1)}, bf16[6,1536,128]{2,1,0:T(8,128)(2,1)}, bf16[3,1536,128]{2,1,0:T(8,128)(2,1)}, bf16[128,1536]{1,0:T(8,128)(...) custom-call(s32[18]{0:T(128)} %stack.86.sc, ...), custom_call_target="tpu_custom_call" | custom-call | flops 20753999872 | bytes 1 | tf_op jit(solution)/shard_map/project/pallas_call | solution.py:50
  83.7 21.5 %attend.2 = (bf16[512,768]{1,0:T(8,128)(2,1)}, f32[6,2,512]{2,1,0:T(2,128)}) custom-call(s32[2]{0:T(128)} %pad_add_fusion.sc, bf16[3,4,192,256]{3,2,1,0:T(8,128)(2,1)} %collective-permute-done.4.refs_0_.refs_11_.refs_10_, bf16[12,1024,64]{2,1,0:T(8,128)(2,1)} %get-tuple-element.168.refs_1_.refs_4_.refs_2_, ...), custom_call_target="tpu_custom_call" | custom-call | flops 21906999296 | bytes 1 | tf_op jit(solution)/shard_map/attend/pallas_call | solution.py:50
  110.0 17.0 %attend.3 = (bf16[512,768]{1,0:T(8,128)(2,1)}, f32[6,2,512]{2,1,0:T(2,128)}) custom-call(s32[2]{0:T(128)} %pad_add_fusion.sc, bf16[8,256,128]{2,1,0:T(8,128)(2,1)} %copy-done.15, bf16[3,1536,128]{2,1,0:T(8,128)(2,1)} %collective-permute-done.15.refs_1_.refs_15_, bf16[3,4,192,256]{3,2,1,0:T(8,128)(2,1)} %collective-permute-done.17.refs_2_.refs_15_.refs_14_, ...), custom_call_target="tpu_custom_call" | custom-call | flops 21906999296 | bytes 1 | tf_op jit(solution)/shard_map/attend/pallas_call | solution.py:50
  130.0 4.6 copy.47.refs_0_.refs_9_.refs_8_.refs_10_.refs_3_
  138.0 9.5 %collective-permute-done.18.refs_11_.refs_0_ = bf16[512,768]{1,0:T(8,128)(2,1)S(1)} collective-permute-done((bf16[512,768]{1,0:T(8,128)(2,1)}, bf16[512,768]{1,0:T(8,128)(2,1)S(1)}, u32[]{:S(2)}, u32[]{:S(2)}) %collective-permute-start.18) | collective-permute-done | bytes 786464 | tf_op jit(solution)/shard_map/ppermute | solution.py:94
  149.3 3.5 broadcast_in_dim.26.refs_1_.refs_19_.refs_20_
  152.8 15.8 %settle.1 = (f32[1024,1536]{1,0:T(8,128)}, bf16[1024,1536]{1,0:T(8,128)(2,1)}, bf16[1536,1024]{1,0:T(8,128)(2,1)}, f32[1024,128]{1,0:T(8,128)}) custom-call(s32[2]{0:T(128)} %pad_add_fusion.sc, bf16[1536,1024]{1,0:T(8,128)(2,1)} %copy.47.refs_0_.refs_9_.refs_8_.refs_10_.refs_3_, f32[1024,1536]{1,0:T(8,128)} %broadcast_in_dim.26.refs_1_.refs_19_.refs_20_, ...), custom_call_target="tpu_custom_call" | custom-call | flops 18447998976 | bytes 1 | tf_op jit(solution)/shard_map/settle/pallas_call | solution.py:50
  172.9 34.6 %experts_all.6 = (f32[1024,1536]{1,0:T(8,128)}, f32[1024,1536]{1,0:T(8,128)}, bf16[4,6,192,256]{3,2,1,0:T(8,128)(2,1)}, bf16[4,6,192,256]{3,2,1,0:T(8,128)(2,1)}, f32[1024,128]{1,0:T(8,128)}) custom-call(s32[20]{0:T(128)} %stack.106.sc, bf16[512,768]{1,0:T(8,128)(2,1)} %copy-done.10, ...), custom_call_target="tpu_custom_call" | custom-call | flops 27672000512 | bytes 1 | tf_op jit(solution)/shard_map/experts_all/pallas_call | solution.py:50
  218.5 24.3 %experts_all.7 = (f32[1024,1536]{1,0:T(8,128)}, f32[1024,1536]{1,0:T(8,128)}, bf16[4,6,192,256]{3,2,1,0:T(8,128)(2,1)}, bf16[4,6,192,256]{3,2,1,0:T(8,128)(2,1)}, f32[1024,128]{1,0:T(8,128)}) custom-call(s32[20]{0:T(128)} %stack.105.sc, bf16[3,4,192,128]{3,2,1,0:T(8,128)(2,1)} %copy-done.13, ...), custom_call_target="tpu_custom_call" | custom-call | flops 27672000512 | bytes 1 | tf_op jit(solution)/shard_map/experts_all/pallas_call | solution.py:50
  248.7 24.1 %experts_all.8 = (f32[1024,1536]{1,0:T(8,128)}, f32[1024,1536]{1,0:T(8,128)}, bf16[4,6,192,256]{3,2,1,0:T(8,128)(2,1)}, bf16[4,6,192,256]{3,2,1,0:T(8,128)(2,1)}, f32[1024,128]{1,0:T(8,128)}) custom-call(s32[20]{0:T(128)} %stack.107.sc, bf16[4,6,192,256]{3,2,1,0:T(8,128)(2,1)} %collective-permute-done.28.refs_0_.refs_4_, ...), custom_call_target="tpu_custom_call" | custom-call | flops 27672000512 | bytes 1 | tf_op jit(solution)/shard_map/experts_all/pallas_call | solution.py:50
  278.0 24.4 %experts_all.9 = (f32[1024,1536]{1,0:T(8,128)}, f32[1024,1536]{1,0:T(8,128)}, bf16[4,6,192,256]{3,2,1,0:T(8,128)(2,1)}, bf16[4,6,192,256]{3,2,1,0:T(8,128)(2,1)}, f32[1024,128]{1,0:T(8,128)}) custom-call(s32[20]{0:T(128)} %stack.108.sc, bf16[4,6,192,256]{3,2,1,0:T(8,128)(2,1)} %collective-permute-done.36.refs_0_.refs_5_, ...), custom_call_target="tpu_custom_call" | custom-call | flops 27672000512 | bytes 1 | tf_op jit(solution)/shard_map/experts_all/pallas_call | solution.py:50
  309.2 24.1 %experts_all.10 = (f32[1024,1536]{1,0:T(8,128)}, f32[1024,1536]{1,0:T(8,128)}, bf16[4,6,192,256]{3,2,1,0:T(8,128)(2,1)}, bf16[4,6,192,256]{3,2,1,0:T(8,128)(2,1)}, f32[1024,128]{1,0:T(8,128)}) custom-call(s32[20]{0:T(128)} %stack.109.sc, bf16[4,6,192,256]{3,2,1,0:T(8,128)(2,1)} %collective-permute-done.40.refs_6_.refs_0_, ...), custom_call_target="tpu_custom_call" | custom-call | flops 27672000512 | bytes 1 | tf_op jit(solution)/shard_map/experts_all/pallas_call | solution.py:50
  337.8 4.2 hop_sum.26.refs_5_
  343.5 24.4 %experts_all.11 = (f32[1024,1536]{1,0:T(8,128)}, f32[1024,1536]{1,0:T(8,128)}, bf16[4,6,192,256]{3,2,1,0:T(8,128)(2,1)}, bf16[4,6,192,256]{3,2,1,0:T(8,128)(2,1)}, f32[1024,128]{1,0:T(8,128)}) custom-call(s32[20]{0:T(128)} %stack.110.sc, bf16[4,6,192,256]{3,2,1,0:T(8,128)(2,1)} %collective-permute-done.48.refs_0_.refs_4_, ...), custom_call_target="tpu_custom_call" | custom-call | flops 27672000512 | bytes 1 | tf_op jit(solution)/shard_map/experts_all/pallas_call | solution.py:50
  369.8 4.5 hop_sum.27.refs_5_
  375.0 17.2 %experts_front.1 = (f32[1024,1536]{1,0:T(8,128)}, f32[1024,128]{1,0:T(8,128)}, bf16[1024,512]{1,0:T(8,128)(2,1)}, bf16[1024,1024]{1,0:T(8,128)(2,1)}) custom-call(s32[20]{0:T(128)} %stack.88.sc, bf16[4,6,192,256]{3,2,1,0:T(8,128)(2,1)} %collective-permute-done.51.refs_0_.refs_5_, ...), custom_call_target="tpu_custom_call" | custom-call | flops 20753999872 | bytes 1 | tf_op jit(solution)/shard_map/experts_front/pallas_call | solution.py:50
  392.8 17.1 %experts_front_end.1 = (bf16[512,1536]{1,0:T(8,128)(2,1)}, bf16[512,1536]{1,0:T(8,128)(2,1)}, f32[1024,128]{1,0:T(8,128)}, bf16[1024,512]{1,0:T(8,128)(2,1)}, bf...) custom-call(s32[20]{0:T(128)} %stack.87.sc, bf16[1024,1536]{1,0:T(8,128)(2,1)} %get-tuple-element.183.refs_5_.refs_4_.refs_6_.refs_0_, ...), custom_call_target="tpu_custom_call" | custom-call | flops 20753999872 | bytes 1 | tf_op jit(solution)/shard_map/experts_front_end/pallas_call | solution.py:50
  412.0 4.4 hop_sum.28.refs_0_
  421.5 13.3 %experts_rest.1 = (f32[1024,1536]{1,0:T(8,128)}, bf16[4,6,192,256]{3,2,1,0:T(8,128)(2,1)}, bf16[4,6,192,256]{3,2,1,0:T(8,128)(2,1)}) custom-call(s32[20]{0:T(128)} %stack.88.sc, bf16[3,6,192,256]{3,2,1,0:T(8,128)(2,1)} %hop_sum.28.refs_0_, bf16[3,6,192,128]{3,2,1,0:T(8,128)(2,1)} %hop_sum.29.refs_1_, ...), custom_call_target="tpu_custom_call" | custom-call | flops 14988999680 | bytes 1 | tf_op jit(solution)/shard_map/experts_rest/pallas_call | solution.py:50
  434.9 13.1 %collective-permute-done.61.refs_6_ = f32[16,1024]{1,0:T(8,128)S(1)} collective-permute-done((f32[16,1024]{1,0:T(8,128)}, f32[16,1024]{1,0:T(8,128)S(1)}, u32[]{:S(2)}, u32[]{:S(2)}) %collective-permute-start.61) | collective-permute-done | bytes 65568 | tf_op jit(solution)/shard_map/ppermute | solution.py:94
  448.6 4.0 hop_sum.30.refs_1_
  453.2 4.2 hop_sum.31.refs_1_
  459.0 5.2 emit.3
  464.2 13.3 %experts_rest_end.1 = (bf16[768,1536]{1,0:T(8,128)(2,1)}, bf16[256,1536]{1,0:T(8,128)(2,1)}, bf16[4,6,192,256]{3,2,1,0:T(8,128)(2,1)}, bf16[4,6,192,256]{3,2,1,0:T(8,128)(2,1)}) custom-call(s32[20]{0:T(128)} %stack.87.sc, f32[16,192,256]{2,1,0:T(8,128)} %get-tuple-element.251.refs_0_.refs_3_, bf16[3,6,192,256]{3,2,1,0:T(8,128)(2,1)} %hop_sum.31.refs_1_, ...), custom_call_target="tpu_custom_call" | custom-call | flops 14988999680 | bytes 1 | tf_op jit(solution)/shard_map/experts_rest_end/pallas_call | solution.py:50
  477.5 12.4 %collective-permute-done.65.refs_4_ = bf16[512,1536]{1,0:T(8,128)(2,1)} collective-permute-done((bf16[512,1536]{1,0:T(8,128)(2,1)}, bf16[512,1536]{1,0:T(8,128)(2,1)}, u32[]{:S(2)}, u32[]{:S(2)}) %collective-permute-start.65) | collective-permute-done | bytes 1572896 | tf_op jit(solution)/shard_map/ppermute | solution.py:94
  489.9 4.4 hop_sum.32.refs_0_
  495.7 16.5 %unsettle.1 = (f32[1024,1536]{1,0:T(8,128)}, bf16[1536,1024]{1,0:T(8,128)(2,1)}, bf16[1024,768]{1,0:T(8,128)(2,1)}, bf16[1024,128]{1,0:T(8,128)(2,1)}, f32[1,1536]{1,0:T(1,128)}) custom-call(s32[2]{0:T(128)} %pad_add_fusion.sc, bf16[3,6,192,256]{3,2,1,0:T(8,128)(2,1)} %hop_sum.32.refs_0_, bf16[512,1536]{1,0:T(8,128)(2,1)} %get-tuple-element.248.refs_1_, ...), custom_call_target="tpu_custom_call" | custom-call | flops 19601000448 | bytes 1 | tf_op jit(solution)/shard_map/unsettle/pallas_call | solution.py:50
  517.4 4.5 hop_sum.33.refs_0_
  527.1 24.9 %attend_back.2 = (bf16[1024,384]{1,0:T(8,128)(2,1)}, f32[4,1024,64]{2,1,0:T(8,128)}, f32[4,256,128]{2,1,0:T(8,128)}) custom-call(s32[2]{0:T(128)} %pad_add_fusion.sc, bf16[3,6,192,256]{3,2,1,0:T(8,128)(2,1)} %hop_sum.33.refs_0_, bf16[2,6,192,128]{3,2,1,0:T(8,128)(2,1)} %hop_sum.34.refs_1_, bf16[12,1024,64]{2,1,0:T(8,128)(2,1)} %get-tuple-element.168.refs_1_.refs_4_.refs_2_, ...), custom_call_target="tpu_custom_call" | custom-call | flops 28824999936 | bytes 1 | tf_op jit(solution)/shard_map/attend_back/pallas_call | solution.py:50
  552.8 3.5 hop_sum.35.refs_1_
  557.9 12.4 %early_grads.1 = (bf16[4,5,192,256]{3,2,1,0:T(8,128)(2,1)}, bf16[4,5,192,256]{3,2,1,0:T(8,128)(2,1)}) custom-call(s32[18]{0:T(128)} %stack.86.sc, f32[4,256,128]{2,1,0:T(8,128)} %get-tuple-element.275.refs_0_, bf16[2,6,192,256]{3,2,1,0:T(8,128)(2,1)} %hop_sum.35.refs_1_, bf16[1536,1024]{1,0:T(8,128)(2,1)} %get-tuple-element.270.refs_2_.refs_3_, ...), custom_call_target="tpu_custom_call" | custom-call | flops 13836000256 | bytes 1 | tf_op jit(solution)/shard_map/early_grads/pallas_call | solution.py:50
  574.6 3.7 hop_sum.37.refs_1_
  580.0 4.0 hop_sum.36.refs_0_.refs_1_
  584.1 24.8 %attend_back.3 = (bf16[1024,384]{1,0:T(8,128)(2,1)}, f32[4,1024,64]{2,1,0:T(8,128)}, f32[4,256,128]{2,1,0:T(8,128)}) custom-call(s32[2]{0:T(128)} %pad_add_fusion.sc, bf16[3,6,192,256]{3,2,1,0:T(8,128)(2,1)} %hop_sum.36.refs_0_.refs_1_, bf16[2,6,192,256]{3,2,1,0:T(8,128)(2,1)} %hop_sum.37.refs_1_, ...), custom_call_target="tpu_custom_call" | custom-call | flops 28824999936 | bytes 1 | tf_op jit(solution)/shard_map/attend_back/pallas_call | solution.py:50
  612.6 7.0 key_value_grads.1.refs_0_.refs_5_.refs_6_
  619.7 3.7 hop_sum.40.refs_1_
  628.4 9.3 %late_grads.1 = (bf16[4,4,192,256]{3,2,1,0:T(8,128)(2,1)}, bf16[4,4,192,256]{3,2,1,0:T(8,128)(2,1)}) custom-call(s32[18]{0:T(128)} %stack.86.sc, bf16[1,5,192,256]{3,2,1,0:T(8,128)(2,1)} %hop_sum.39.refs_0_, bf16[2,6,192,256]{3,2,1,0:T(8,128)(2,1)} %hop_sum.40.refs_1_, bf16[1536,1024]{1,0:T(8,128)(2,1)} %get-tuple-element.272.refs_11_.refs_12_.refs_2_.refs_3_, ...), custom_call_target="tpu_custom_call" | custom-call | flops 11530000384 | bytes 1 | tf_op jit(solution)/shard_map/late_grads/pallas_call | solution.py:50
  637.7 7.5 %collective-permute-done.79.refs_3_ = bf16[1,5,192,256]{3,2,1,0:T(8,128)(2,1)} collective-permute-done((bf16[1,5,192,256]{3,2,1,0:T(8,128)(2,1)}, bf16[1,5,192,256]{3,2,1,0:T(8,128)(2,1)}, u32[]{:S(2)}, u32[]{:S(2)}) %collective-permute-start.79) | collective-permute-done | bytes 491552 | tf_op jit(solution)/shard_map/ppermute | solution.py:90
  656.4 5.2 emit.4
  671.4 18.3 %finish.1 = f32[1024,1536]{1,0:T(8,128)} custom-call(s32[2]{0:T(128)} %pad_add_fusion.sc, bf16[1,4,192,256]{3,2,1,0:T(8,128)(2,1)} %hop_sum.43.refs_0_, bf16[1024,1536]{1,0:T(8,128)(2,1)} %bitcast.59, bf16[128,1536]{1,0:T(8,128)(2,1)} %get-tuple-element.181.refs_13_.refs_10_.refs_2_, f32[1024,1536]{1,0:T(8,128)} %get-tuple-element.296.refs_3_, ...), custom_call_target="tpu_custom_call" | custom-call | flops 20753999872 | bytes 1 | tf_op jit(solution)/shard_map/finish/pallas_call | solution.py:50
  694.0 3.4 hop_sum.45.refs_0_.refs_1_
  706.0 7.5 %combine.1.refs_0_ = bf16[1024,1536]{1,0:T(8,128)(2,1)} custom-call(s32[2]{0:T(128)} %pad_add_fusion.sc, bf16[1,4,192,256]{3,2,1,0:T(8,128)(2,1)} %hop_sum.47.refs_0_, f32[1024,1536]{1,0:T(8,128)} %get-tuple-element.260.refs_8_.refs_1_, bf16[768,1536]{1,0:T(8,128)(2,1)} %get-tuple-element.276.refs_0_.refs_2_, bf16[256,1536]{1,0:T(8,128)(2,1)} %get-tuple-element.299.refs_3_, ...), custom_call_target="tpu_custom_call" | custom-call | flops 5765000192 | bytes 1 | tf_op jit(solution)/shard_map/combine/pallas_call | solution.py:50
  717.1 3.4 emit.5
  726.8 3.3 spread.1
  (286 shorter events, 175.9 us)
Async XLA Ops:
  79.9 28.6 %collective-permute-start.15 = (bf16[3,1536,128]{2,1,0:T(8,128)(2,1)}, bf16[3,1536,128]{2,1,0:T(8,128)(2,1)}, u32[]{:S(2)}, u32[]{:S(2)}) collective-permute-start(bf16[3,1536,128]{2,1,0:T(8,128)(2,1)} %get-tuple-element.178), channel_id=1, source_target_pairs={{0,1},{1,0},{2,3},{3,2},{4,5},{5,4},{6,7},{7,6},{8,9},{9,8},{10,11... | collective-permute-start | bytes 3538952 | tf_op jit(solution)/shard_map/ppermute | solution.py:94
  81.4 27.1 %collective-permute-start.11 = (bf16[3,4,192,256]{3,2,1,0:T(8,128)(2,1)}, bf16[3,4,192,256]{3,2,1,0:T(8,128)(2,1)}, u32[]{:S(2)}, u32[]{:S(2)}) collective-permute-start(bf16[3,4,192,256]{3,2,1,0:T(8,128)(2,1)} %collective-permute-done.4.refs_0_.refs_11_.refs_10_), channel_id=1, source_target_pairs={{0,8},{10,2},{8,16},{18,10},{16,24},{26,18},{24,28},{30,26},{28,20... | collective-permute-start | bytes 3538952 | tf_op jit(solution)/shard_map/ppermute | solution.py:90
  82.9 27.1 %collective-permute-start.17 = (bf16[3,4,192,256]{3,2,1,0:T(8,128)(2,1)}, bf16[3,4,192,256]{3,2,1,0:T(8,128)(2,1)}, u32[]{:S(2)}, u32[]{:S(2)}) collective-permute-start(bf16[3,4,192,256]{3,2,1,0:T(8,128)(2,1)} %collective-permute-done.4.refs_0_.refs_11_.refs_10_), channel_id=1, source_target_pairs={{0,2},{2,0},{1,3},{3,1},{4,6},{6,4},{5,7},{7,5},{8,10},{10,8},{9,1... | collective-permute-start | bytes 3538952 | tf_op jit(solution)/shard_map/ppermute | solution.py:94
  106.8 30.5 %collective-permute-start.10 = (bf16[512,768]{1,0:T(8,128)(2,1)}, bf16[512,768]{1,0:T(8,128)(2,1)}, u32[]{:S(2)}, u32[]{:S(2)}) collective-permute-start(bf16[512,768]{1,0:T(8,128)(2,1)} %get-tuple-element.171.refs_10_.refs_13_.refs_5_), channel_id=1, source_target_pairs={{0,1},{1,0},{2,3},{3,2},{4,5},{5,4},{6,7},{7,6},{8,9},{9,8},{10,11... | collective-permute-start | bytes 2359304 | tf_op jit(solution)/shard_map/ppermute | solution.py:94
  108.4 29.0 %collective-permute-start.16 = (bf16[3,1536,128]{2,1,0:T(8,128)(2,1)}, bf16[3,1536,128]{2,1,0:T(8,128)(2,1)}, u32[]{:S(2)}, u32[]{:S(2)}) collective-permute-start(bf16[3,1536,128]{2,1,0:T(8,128)(2,1)} %collective-permute-done.15.refs_1_.refs_15_), channel_id=1, source_target_pairs={{0,2},{2,0},{1,3},{3,1},{4,6},{6,4},{5,7},{7,5},{8,10},{10,8},{9,1... | collective-permute-start | bytes 3538952 | tf_op jit(solution)/shard_map/ppermute | solution.py:94
  110.0 39.2 %collective-permute-start.12 = (bf16[3,4,192,256]{3,2,1,0:T(8,128)(2,1)}, bf16[3,4,192,256]{3,2,1,0:T(8,128)(2,1)}, u32[]{:S(2)}, u32[]{:S(2)}) collective-permute-start(bf16[3,4,192,256]{3,2,1,0:T(8,128)(2,1)} %collective-permute-done.11.refs_3_.refs_12_.refs_11_), channel_id=1, source_target_pairs={{0,2},{2,0},{1,3},{3,1},{4,6},{6,4},{5,7},{7,5},{8,10},{10,8},{9,1... | collective-permute-start | bytes 3538952 | tf_op jit(solution)/shard_map/ppermute | solution.py:94
  134.7 34.6 %collective-permute-start.21 = (bf16[3,4,192,256]{3,2,1,0:T(8,128)(2,1)}, bf16[3,4,192,256]{3,2,1,0:T(8,128)(2,1)}, u32[]{:S(2)}, u32[]{:S(2)}) collective-permute-start(bf16[3,4,192,256]{3,2,1,0:T(8,128)(2,1)} %collective-permute-done.14.refs_5_.refs_12_.refs_11_), channel_id=1, source_target_pairs={{0,8},{10,2},{8,16},{18,10},{16,24},{26,18},{24,28},{30,26},{28,20... | collective-permute-start | bytes 3538952 | tf_op jit(solution)/shard_map/ppermute | solution.py:90
  137.4 33.9 %collective-permute-start.26 = (bf16[3,4,192,256]{3,2,1,0:T(8,128)(2,1)}, bf16[3,4,192,256]{3,2,1,0:T(8,128)(2,1)}, u32[]{:S(2)}, u32[]{:S(2)}) collective-permute-start(bf16[3,4,192,256]{3,2,1,0:T(8,128)(2,1)} %collective-permute-done.14.refs_5_.refs_12_.refs_11_), channel_id=1, source_target_pairs={{0,2},{2,0},{1,3},{3,1},{4,6},{6,4},{5,7},{7,5},{8,10},{10,8},{9,1... | collective-permute-start | bytes 3538952 | tf_op jit(solution)/shard_map/ppermute | solution.py:94
  137.5 34.4 %collective-permute-start.25 = (bf16[3,4,192,256]{3,2,1,0:T(8,128)(2,1)}, bf16[3,4,192,256]{3,2,1,0:T(8,128)(2,1)}, u32[]{:S(2)}, u32[]{:S(2)}) collective-permute-start(bf16[3,4,192,256]{3,2,1,0:T(8,128)(2,1)} %collective-permute-done.13.refs_4_.refs_13_.refs_12_), channel_id=1, source_target_pairs={{0,2},{2,0},{1,3},{3,1},{4,6},{6,4},{5,7},{7,5},{8,10},{10,8},{9,1... | collective-permute-start | bytes 3538952 | tf_op jit(solution)/shard_map/ppermute | solution.py:94
  169.2 44.6 %collective-permute-start.22 = (bf16[3,4,192,256]{3,2,1,0:T(8,128)(2,1)}, bf16[3,4,192,256]{3,2,1,0:T(8,128)(2,1)}, u32[]{:S(2)}, u32[]{:S(2)}) collective-permute-start(bf16[3,4,192,256]{3,2,1,0:T(8,128)(2,1)} %collective-permute-done.21.refs_4_.refs_13_.refs_12_), channel_id=1, source_target_pairs={{0,2},{2,0},{1,3},{3,1},{4,6},{6,4},{5,7},{7,5},{8,10},{10,8},{9,1... | collective-permute-start | bytes 3538952 | tf_op jit(solution)/shard_map/ppermute | solution.py:94
  169.7 37.8 %collective-permute-start.23 = (bf16[3,4,192,256]{3,2,1,0:T(8,128)(2,1)}, bf16[3,4,192,256]{3,2,1,0:T(8,128)(2,1)}, u32[]{:S(2)}, u32[]{:S(2)}) collective-permute-start(bf16[3,4,192,256]{3,2,1,0:T(8,128)(2,1)} %collective-permute-done.21.refs_4_.refs_13_.refs_12_), channel_id=1, source_target_pairs={{0,8},{10,2},{8,16},{18,10},{16,24},{26,18},{24,28},{30,26},{28,20... | collective-permute-start | bytes 3538952 | tf_op jit(solution)/shard_map/ppermute | solution.py:90
  171.2 39.1 %collective-permute-start.24 = (bf16[3,4,192,256]{3,2,1,0:T(8,128)(2,1)}, bf16[3,4,192,256]{3,2,1,0:T(8,128)(2,1)}, u32[]{:S(2)}, u32[]{:S(2)}) collective-permute-start(bf16[3,4,192,256]{3,2,1,0:T(8,128)(2,1)} %get-tuple-element.192.refs_11_), channel_id=1, source_target_pairs={{0,8},{10,2},{8,16},{18,10},{16,24},{26,18},{24,28},{30,26},{28,20... | collective-permute-start | bytes 3538952 | tf_op jit(solution)/shard_map/ppermute | solution.py:90
  210.3 32.6 %collective-permute-start.32 = (bf16[3,4,192,256]{3,2,1,0:T(8,128)(2,1)}, bf16[3,4,192,256]{3,2,1,0:T(8,128)(2,1)}, u32[]{:S(2)}, u32[]{:S(2)}) collective-permute-start(bf16[3,4,192,256]{3,2,1,0:T(8,128)(2,1)} %collective-permute-done.24.refs_3_.refs_12_), channel_id=1, source_target_pairs={{0,8},{10,2},{8,16},{18,10},{16,24},{26,18},{24,28},{30,26},{28,20... | collective-permute-start | bytes 3538952 | tf_op jit(solution)/shard_map/ppermute | solution.py:90
  211.0 35.0 %collective-permute-start.31 = (bf16[3,4,192,256]{3,2,1,0:T(8,128)(2,1)}, bf16[3,4,192,256]{3,2,1,0:T(8,128)(2,1)}, u32[]{:S(2)}, u32[]{:S(2)}) collective-permute-start(bf16[3,4,192,256]{3,2,1,0:T(8,128)(2,1)} %collective-permute-done.24.refs_3_.refs_12_), channel_id=1, source_target_pairs={{0,2},{2,0},{1,3},{3,1},{4,6},{6,4},{5,7},{7,5},{8,10},{10,8},{9,1... | collective-permute-start | bytes 3538952 | tf_op jit(solution)/shard_map/ppermute | solution.py:94
  211.0 36.2 %collective-permute-start.29 = (bf16[3,4,192,256]{3,2,1,0:T(8,128)(2,1)}, bf16[3,4,192,256]{3,2,1,0:T(8,128)(2,1)}, u32[]{:S(2)}, u32[]{:S(2)}) collective-permute-start(bf16[3,4,192,256]{3,2,1,0:T(8,128)(2,1)} %collective-permute-done.23.refs_2_.refs_14_.refs_13_), channel_id=1, source_target_pairs={{0,2},{2,0},{1,3},{3,1},{4,6},{6,4},{5,7},{7,5},{8,10},{10,8},{9,1... | collective-permute-start | bytes 3538952 | tf_op jit(solution)/shard_map/ppermute | solution.py:94
  213.9 32.1 %collective-permute-start.33 = (bf16[3,1536,128]{2,1,0:T(8,128)(2,1)}, bf16[3,1536,128]{2,1,0:T(8,128)(2,1)}, u32[]{:S(2)}, u32[]{:S(2)}) collective-permute-start(bf16[3,1536,128]{2,1,0:T(8,128)(2,1)} %constant_dynamic-slice_fusion), channel_id=1, source_target_pairs={{0,1},{1,0},{2,3},{3,2},{4,5},{5,4},{6,7},{7,6},{8,9},{9,8},{10,11... | collective-permute-start | bytes 3538952 | tf_op jit(solution)/shard_map/ppermute | solution.py:94
  218.5 30.1 %collective-permute-start.28 = (bf16[4,6,192,256]{3,2,1,0:T(8,128)(2,1)}, bf16[4,6,192,256]{3,2,1,0:T(8,128)(2,1)}, u32[]{:S(2)}, u32[]{:S(2)}) collective-permute-start(bf16[4,6,192,256]{3,2,1,0:T(8,128)(2,1)} %get-tuple-element.200), channel_id=1, source_target_pairs={{0,2},{2,0},{1,3},{3,1},{4,6},{6,4},{5,7},{7,5},{8,10},{10,8},{9,1... | collective-permute-start | bytes 7077896 | tf_op jit(solution)/shard_map/ppermute | solution.py:94
  246.0 31.5 %collective-permute-start.36 = (bf16[4,6,192,256]{3,2,1,0:T(8,128)(2,1)}, bf16[4,6,192,256]{3,2,1,0:T(8,128)(2,1)}, u32[]{:S(2)}, u32[]{:S(2)}) collective-permute-start(bf16[4,6,192,256]{3,2,1,0:T(8,128)(2,1)} %get-tuple-element.210), channel_id=1, source_target_pairs={{0,2},{2,0},{1,3},{3,1},{4,6},{6,4},{5,7},{7,5},{8,10},{10,8},{9,1... | collective-permute-start | bytes 7077896 | tf_op jit(solution)/shard_map/ppermute | solution.py:94
  247.2 28.1 %collective-permute-start.38 = (bf16[3,4,192,256]{3,2,1,0:T(8,128)(2,1)}, bf16[3,4,192,256]{3,2,1,0:T(8,128)(2,1)}, u32[]{:S(2)}, u32[]{:S(2)}) collective-permute-start(bf16[3,4,192,256]{3,2,1,0:T(8,128)(2,1)} %collective-permute-done.32.refs_4_.refs_13_), channel_id=1, source_target_pairs={{0,8},{10,2},{8,16},{18,10},{16,24},{26,18},{24,28},{30,26},{28,20... | collective-permute-start | bytes 3538952 | tf_op jit(solution)/shard_map/ppermute | solution.py:90
  248.6 27.7 %collective-permute-start.37 = (bf16[3,4,192,256]{3,2,1,0:T(8,128)(2,1)}, bf16[3,4,192,256]{3,2,1,0:T(8,128)(2,1)}, u32[]{:S(2)}, u32[]{:S(2)}) collective-permute-start(bf16[3,4,192,256]{3,2,1,0:T(8,128)(2,1)} %collective-permute-done.32.refs_4_.refs_13_), channel_id=1, source_target_pairs={{0,2},{2,0},{1,3},{3,1},{4,6},{6,4},{5,7},{7,5},{8,10},{10,8},{9,1... | collective-permute-start | bytes 3538952 | tf_op jit(solution)/shard_map/ppermute | solution.py:94
  272.8 30.9 %collective-permute-start.35 = (bf16[3,4,192,256]{3,2,1,0:T(8,128)(2,1)}, bf16[3,4,192,256]{3,2,1,0:T(8,128)(2,1)}, u32[]{:S(2)}, u32[]{:S(2)}) collective-permute-start(bf16[3,4,192,256]{3,2,1,0:T(8,128)(2,1)} %collective-permute-done.27.refs_4_.refs_10_.refs_5_), channel_id=1, source_target_pairs={{0,8},{10,2},{8,16},{18,10},{16,24},{26,18},{24,28},{30,26},{28,20... | collective-permute-start | bytes 3538952 | tf_op jit(solution)/shard_map/ppermute | solution.py:90
  274.3 33.7 %collective-permute-start.43 = (bf16[3,4,192,256]{3,2,1,0:T(8,128)(2,1)}, bf16[3,4,192,256]{3,2,1,0:T(8,128)(2,1)}, u32[]{:S(2)}, u32[]{:S(2)}) collective-permute-start(bf16[3,4,192,256]{3,2,1,0:T(8,128)(2,1)} %collective-permute-done.27.refs_4_.refs_10_.refs_5_), channel_id=1, source_target_pairs={{0,2},{2,0},{1,3},{3,1},{4,6},{6,4},{5,7},{7,5},{8,10},{10,8},{9,1... | collective-permute-start | bytes 3538952 | tf_op jit(solution)/shard_map/ppermute | solution.py:94
  275.2 32.7 %collective-permute-start.41 = (bf16[3,4,192,256]{3,2,1,0:T(8,128)(2,1)}, bf16[3,4,192,256]{3,2,1,0:T(8,128)(2,1)}, u32[]{:S(2)}, u32[]{:S(2)}) collective-permute-start(bf16[3,4,192,256]{3,2,1,0:T(8,128)(2,1)} %collective-permute-done.38.refs_3_.refs_14_), channel_id=1, source_target_pairs={{0,2},{2,0},{1,3},{3,1},{4,6},{6,4},{5,7},{7,5},{8,10},{10,8},{9,1... | collective-permute-start | bytes 3538952 | tf_op jit(solution)/shard_map/ppermute | solution.py:94
  303.7 38.8 %collective-permute-start.48 = (bf16[4,6,192,256]{3,2,1,0:T(8,128)(2,1)}, bf16[4,6,192,256]{3,2,1,0:T(8,128)(2,1)}, u32[]{:S(2)}, u32[]{:S(2)}) collective-permute-start(bf16[4,6,192,256]{3,2,1,0:T(8,128)(2,1)} %get-tuple-element.226), channel_id=1, source_target_pairs={{0,2},{2,0},{1,3},{3,1},{4,6},{6,4},{5,7},{7,5},{8,10},{10,8},{9,1... | collective-permute-start | bytes 7077896 | tf_op jit(solution)/shard_map/ppermute | solution.py:94
  304.2 30.9 %collective-permute-start.39 = (bf16[3,4,192,256]{3,2,1,0:T(8,128)(2,1)}, bf16[3,4,192,256]{3,2,1,0:T(8,128)(2,1)}, u32[]{:S(2)}, u32[]{:S(2)}) collective-permute-start(bf16[3,4,192,256]{3,2,1,0:T(8,128)(2,1)} %collective-permute-done.35.refs_4_.refs_11_.refs_5_.refs_6_), channel_id=1, source_target_pairs={{0,8},{10,2},{8,16},{18,10},{16,24},{26,18},{24,28},{30,26},{28,20... | collective-permute-start | bytes 3538952 | tf_op jit(solution)/shard_map/ppermute | solution.py:90
  307.9 34.1 %collective-permute-start.46 = (bf16[3,4,192,256]{3,2,1,0:T(8,128)(2,1)}, bf16[3,4,192,256]{3,2,1,0:T(8,128)(2,1)}, u32[]{:S(2)}, u32[]{:S(2)}) collective-permute-start(bf16[3,4,192,256]{3,2,1,0:T(8,128)(2,1)} %collective-permute-done.35.refs_4_.refs_11_.refs_5_.refs_6_), channel_id=1, source_target_pairs={{0,2},{2,0},{1,3},{3,1},{4,6},{6,4},{5,7},{7,5},{8,10},{10,8},{9,1... | collective-permute-start | bytes 3538952 | tf_op jit(solution)/shard_map/ppermute | solution.py:94
  308.0 29.2 %collective-permute-start.49 = (bf16[3,6,192,128]{3,2,1,0:T(8,128)(2,1)}, bf16[3,6,192,128]{3,2,1,0:T(8,128)(2,1)}, u32[]{:S(2)}, u32[]{:S(2)}) collective-permute-start(bf16[3,6,192,128]{3,2,1,0:T(8,128)(2,1)} %hop_sum.25.refs_5_), channel_id=1, source_target_pairs={{0,8},{10,2},{8,16},{18,10},{16,24},{26,18},{24,28},{30,26},{28,20... | collective-permute-start | bytes 2654216 | tf_op jit(solution)/shard_map/ppermute | solution.py:90
  333.3 41.0 %collective-permute-start.53 = (bf16[2,1536,128]{2,1,0:T(8,128)(2,1)S(1)}, bf16[2,1536,128]{2,1,0:T(8,128)(2,1)}, u32[]{:S(2)}, u32[]{:S(2)}) collective-permute-start(bf16[2,1536,128]{2,1,0:T(8,128)(2,1)S(1)} %constant_dynamic-slice_fusion.3), channel_id=1, source_target_pairs={{0,1},{1,0},{2,3},{3,2},{4,5},{5,4},{6,7},{7,6},{8,9},{9,8},{10,11... | collective-permute-start | bytes 2359304 | tf_op jit(solution)/shard_map/ppermute | solution.py:94
  335.1 39.9 %collective-permute-start.47 = (bf16[3,4,192,256]{3,2,1,0:T(8,128)(2,1)}, bf16[3,4,192,256]{3,2,1,0:T(8,128)(2,1)}, u32[]{:S(2)}, u32[]{:S(2)}) collective-permute-start(bf16[3,4,192,256]{3,2,1,0:T(8,128)(2,1)} %collective-permute-done.39.refs_3_.refs_12_.refs_6_.refs_7_), channel_id=1, source_target_pairs={{0,2},{2,0},{1,3},{3,1},{4,6},{6,4},{5,7},{7,5},{8,10},{10,8},{9,1... | collective-permute-start | bytes 3538952 | tf_op jit(solution)/shard_map/ppermute | solution.py:94
  337.2 30.7 %collective-permute-start.45 = (bf16[3,4,192,128]{3,2,1,0:T(8,128)(2,1)}, bf16[3,4,192,128]{3,2,1,0:T(8,128)(2,1)}, u32[]{:S(2)}, u32[]{:S(2)}) collective-permute-start(bf16[3,4,192,128]{3,2,1,0:T(8,128)(2,1)} %constant_dynamic-slice_fusion.1), channel_id=1, source_target_pairs={{0,8},{10,2},{8,16},{18,10},{16,24},{26,18},{24,28},{30,26},{28,20... | collective-permute-start | bytes 1769480 | tf_op jit(solution)/shard_map/ppermute | solution.py:90
  342.0 33.0 %collective-permute-start.51 = (bf16[4,6,192,256]{3,2,1,0:T(8,128)(2,1)}, bf16[4,6,192,256]{3,2,1,0:T(8,128)(2,1)}, u32[]{:S(2)}, u32[]{:S(2)}) collective-permute-start(bf16[4,6,192,256]{3,2,1,0:T(8,128)(2,1)} %get-tuple-element.231), channel_id=1, source_target_pairs={{0,2},{2,0},{1,3},{3,1},{4,6},{6,4},{5,7},{7,5},{8,10},{10,8},{9,1... | collective-permute-start | bytes 7077896 | tf_op jit(solution)/shard_map/ppermute | solution.py:94
  369.5 40.8 %collective-permute-start.54 = (bf16[4,6,192,256]{3,2,1,0:T(8,128)(2,1)}, bf16[4,6,192,256]{3,2,1,0:T(8,128)(2,1)}, u32[]{:S(2)}, u32[]{:S(2)}) collective-permute-start(bf16[4,6,192,256]{3,2,1,0:T(8,128)(2,1)} %get-tuple-element.237), channel_id=1, source_target_pairs={{0,2},{2,0},{1,3},{3,1},{4,6},{6,4},{5,7},{7,5},{8,10},{10,8},{9,1... | collective-permute-start | bytes 7077896 | tf_op jit(solution)/shard_map/ppermute | solution.py:94
  374.3 37.7 %collective-permute-start.55 = (bf16[3,6,192,256]{3,2,1,0:T(8,128)(2,1)}, bf16[3,6,192,256]{3,2,1,0:T(8,128)(2,1)}, u32[]{:S(2)}, u32[]{:S(2)}) collective-permute-start(bf16[3,6,192,256]{3,2,1,0:T(8,128)(2,1)} %hop_sum.27.refs_5_), channel_id=1, source_target_pairs={{0,8},{10,2},{8,16},{18,10},{16,24},{26,18},{24,28},{30,26},{28,20... | collective-permute-start | bytes 5308424 | tf_op jit(solution)/shard_map/ppermute | solution.py:90
  409.9 38.1 %collective-permute-start.60 = (bf16[512,1536]{1,0:T(8,128)(2,1)}, bf16[512,1536]{1,0:T(8,128)(2,1)}, u32[]{:S(2)}, u32[]{:S(2)}) collective-permute-start(bf16[512,1536]{1,0:T(8,128)(2,1)} %get-tuple-element.248.refs_1_), channel_id=1, source_target_pairs={{0,1},{1,0},{2,3},{3,2},{4,5},{5,4},{6,7},{7,6},{8,9},{9,8},{10,11... | collective-permute-start | bytes 4718600 | tf_op jit(solution)/shard_map/ppermute | solution.py:94
  410.2 37.7 %collective-permute-start.61 = (f32[16,1024]{1,0:T(8,128)}, f32[16,1024]{1,0:T(8,128)S(1)}, u32[]{:S(2)}, u32[]{:S(2)}) collective-permute-start(f32[16,1024]{1,0:T(8,128)} %get-tuple-element.249.refs_0_.refs_5_), channel_id=1, source_target_pairs={{0,1},{1,0},{2,3},{3,2},{4,5},{5,4},{6,7},{7,6},{8,9},{9,8},{10,11... | collective-permute-start | bytes 196616 | tf_op jit(solution)/shard_map/ppermute | solution.py:94
  416.4 32.2 %collective-permute-start.58 = (bf16[3,6,192,256]{3,2,1,0:T(8,128)(2,1)}, bf16[3,6,192,256]{3,2,1,0:T(8,128)(2,1)}, u32[]{:S(2)}, u32[]{:S(2)}) collective-permute-start(bf16[3,6,192,256]{3,2,1,0:T(8,128)(2,1)} %hop_sum.28.refs_0_), channel_id=1, source_target_pairs={{0,8},{10,2},{8,16},{18,10},{16,24},{26,18},{24,28},{30,26},{28,20... | collective-permute-start | bytes 5308424 | tf_op jit(solution)/shard_map/ppermute | solution.py:90
  420.9 27.8 %collective-permute-start.59 = (bf16[3,6,192,128]{3,2,1,0:T(8,128)(2,1)}, bf16[3,6,192,128]{3,2,1,0:T(8,128)(2,1)S(1)}, u32[]{:S(2)}, u32[]{:S(2)}) collective-permute-start(bf16[3,6,192,128]{3,2,1,0:T(8,128)(2,1)} %hop_sum.29.refs_1_), channel_id=1, source_target_pairs={{0,8},{10,2},{8,16},{18,10},{16,24},{26,18},{24,28},{30,26},{28,20... | collective-permute-start | bytes 2654216 | tf_op jit(solution)/shard_map/ppermute | solution.py:90
  452.7 37.1 %collective-permute-start.65 = (bf16[512,1536]{1,0:T(8,128)(2,1)}, bf16[512,1536]{1,0:T(8,128)(2,1)}, u32[]{:S(2)}, u32[]{:S(2)}) collective-permute-start(bf16[512,1536]{1,0:T(8,128)(2,1)} %get-tuple-element.258.refs_2_), channel_id=1, source_target_pairs={{0,1},{1,0},{2,3},{3,2},{4,5},{5,4},{6,7},{7,6},{8,9},{9,8},{10,11... | collective-permute-start | bytes 4718600 | tf_op jit(solution)/shard_map/ppermute | solution.py:94
  453.1 36.8 %collective-permute-start.63 = (bf16[4,6,192,256]{3,2,1,0:T(8,128)(2,1)}, bf16[4,6,192,256]{3,2,1,0:T(8,128)(2,1)}, u32[]{:S(2)}, u32[]{:S(2)}) collective-permute-start(bf16[4,6,192,256]{3,2,1,0:T(8,128)(2,1)} %get-tuple-element.256), channel_id=1, source_target_pairs={{0,2},{2,0},{1,3},{3,1},{4,6},{6,4},{5,7},{7,5},{8,10},{10,8},{9,1... | collective-permute-start | bytes 7077896 | tf_op jit(solution)/shard_map/ppermute | solution.py:94
  457.4 32.4 %collective-permute-start.64 = (bf16[3,6,192,256]{3,2,1,0:T(8,128)(2,1)}, bf16[3,6,192,256]{3,2,1,0:T(8,128)(2,1)}, u32[]{:S(2)}, u32[]{:S(2)}) collective-permute-start(bf16[3,6,192,256]{3,2,1,0:T(8,128)(2,1)} %hop_sum.31.refs_1_), channel_id=1, source_target_pairs={{0,8},{10,2},{8,16},{18,10},{16,24},{26,18},{24,28},{30,26},{28,20... | collective-permute-start | bytes 5308424 | tf_op jit(solution)/shard_map/ppermute | solution.py:90
  489.9 27.3 %collective-permute-start.66 = (bf16[4,6,192,256]{3,2,1,0:T(8,128)(2,1)}, bf16[4,6,192,256]{3,2,1,0:T(8,128)(2,1)}, u32[]{:S(2)}, u32[]{:S(2)}) collective-permute-start(bf16[4,6,192,256]{3,2,1,0:T(8,128)(2,1)} %get-tuple-element.263), channel_id=1, source_target_pairs={{0,2},{2,0},{1,3},{3,1},{4,6},{6,4},{5,7},{7,5},{8,10},{10,8},{9,1... | collective-permute-start | bytes 7077896 | tf_op jit(solution)/shard_map/ppermute | solution.py:94
  517.1 53.1 %collective-permute-start.72 = (bf16[768,1536]{1,0:T(8,128)(2,1)}, bf16[768,1536]{1,0:T(8,128)(2,1)}, u32[]{:S(2)}, u32[]{:S(2)}) collective-permute-start(bf16[768,1536]{1,0:T(8,128)(2,1)} %get-tuple-element.276.refs_0_.refs_2_), channel_id=1, source_target_pairs={{0,1},{1,0},{2,3},{3,2},{4,5},{5,4},{6,7},{7,6},{8,9},{9,8},{10,11... | collective-permute-start | bytes 7077896 | tf_op jit(solution)/shard_map/ppermute | solution.py:94
  521.9 30.1 %collective-permute-start.68 = (bf16[3,6,192,256]{3,2,1,0:T(8,128)(2,1)}, bf16[3,6,192,256]{3,2,1,0:T(8,128)(2,1)}, u32[]{:S(2)}, u32[]{:S(2)}) collective-permute-start(bf16[3,6,192,256]{3,2,1,0:T(8,128)(2,1)} %hop_sum.33.refs_0_), channel_id=1, source_target_pairs={{0,8},{10,2},{8,16},{18,10},{16,24},{26,18},{24,28},{30,26},{28,20... | collective-permute-start | bytes 5308424 | tf_op jit(solution)/shard_map/ppermute | solution.py:90
  572.9 36.0 %collective-permute-start.76 = (bf16[1024,384]{1,0:T(8,128)(2,1)S(1)}, bf16[1024,384]{1,0:T(8,128)(2,1)}, u32[]{:S(2)}, u32[]{:S(2)}) collective-permute-start(bf16[1024,384]{1,0:T(8,128)(2,1)S(1)} %copy-done.8), channel_id=1, source_target_pairs={{0,1},{1,0},{2,3},{3,2},{4,5},{5,4},{6,7},{7,6},{8,9},{9,8},{10,11... | collective-permute-start | bytes 2359304 | tf_op jit(solution)/shard_map/ppermute | solution.py:94
  574.6 34.3 %collective-permute-start.73 = (bf16[4,5,192,256]{3,2,1,0:T(8,128)(2,1)}, bf16[4,5,192,256]{3,2,1,0:T(8,128)(2,1)}, u32[]{:S(2)}, u32[]{:S(2)}) collective-permute-start(bf16[4,5,192,256]{3,2,1,0:T(8,128)(2,1)} %get-tuple-element.280), channel_id=1, source_target_pairs={{0,2},{2,0},{1,3},{3,1},{4,6},{6,4},{5,7},{7,5},{8,10},{10,8},{9,1... | collective-permute-start | bytes 5898248 | tf_op jit(solution)/shard_map/ppermute | solution.py:94
  578.3 30.5 %collective-permute-start.74 = (bf16[2,6,192,256]{3,2,1,0:T(8,128)(2,1)}, bf16[2,6,192,256]{3,2,1,0:T(8,128)(2,1)}, u32[]{:S(2)}, u32[]{:S(2)}) collective-permute-start(bf16[2,6,192,256]{3,2,1,0:T(8,128)(2,1)} %hop_sum.37.refs_1_), channel_id=1, source_target_pairs={{0,8},{10,2},{8,16},{18,10},{16,24},{26,18},{24,28},{30,26},{28,20... | collective-permute-start | bytes 3538952 | tf_op jit(solution)/shard_map/ppermute | solution.py:90
  608.9 28.8 %collective-permute-start.81 = (bf16[1024,384]{1,0:T(8,128)(2,1)}, bf16[1024,384]{1,0:T(8,128)(2,1)S(1)}, u32[]{:S(2)}, u32[]{:S(2)}) collective-permute-start(bf16[1024,384]{1,0:T(8,128)(2,1)} %get-tuple-element.289.refs_4_.refs_5_), channel_id=1, source_target_pairs={{0,1},{1,0},{2,3},{3,2},{4,5},{5,4},{6,7},{7,6},{8,9},{9,8},{10,11... | collective-permute-start | bytes 2359304 | tf_op jit(solution)/shard_map/ppermute | solution.py:94
  655.8 41.7 %collective-permute-start.87 = (bf16[1,5,192,256]{3,2,1,0:T(8,128)(2,1)}, bf16[1,5,192,256]{3,2,1,0:T(8,128)(2,1)}, u32[]{:S(2)}, u32[]{:S(2)}) collective-permute-start(bf16[1,5,192,256]{3,2,1,0:T(8,128)(2,1)} %hop_sum.42.refs_1_), channel_id=1, source_target_pairs={{0,8},{10,2},{8,16},{18,10},{16,24},{26,18},{24,28},{30,26},{28,20... | collective-permute-start | bytes 1474568 | tf_op jit(solution)/shard_map/ppermute | solution.py:90
  (71 other events, 875.5 us)

commit v5 on v4

--- a/solution.py
+++ b/solution.py
@@ -864,7 +864,7 @@
     slots, mats, shard, hidden = keeps[0].shape
     lanes = hidden // 2 if stage in (None, "end") else hidden
     side = 1 if stage == "end" else 0
-    per = mats // 2 if pairs > 1 else mats
+    per = mats
     piece = pl.BlockSpec((1, per, shard, lanes), lambda m, s: (slot, m, 0, side))
     wide = lambda a: pl.BlockSpec((pairs, per, shard, a.shape[3]), lambda m, s: (0, m, 0, 0))
     out = sds((pairs, mats, shard, hidden // 2 if stage is None else hidden), bf)

time: 742 us -> 748 us (level)
  transfers between devices with their start and end apart: 95 -> 95, of which waited for: 18 -> 18; matrix products, arithmetic and copies ran while one was open for 5% -> 5% of each run, Pallas kernels for 68% -> 69%
where the time goes in v5:
time: 748 us; the launch traced here: 742 us
  Pallas kernels  521 us (70%)
  waiting for transfers between devices  93.2 us (12%)
  starting transfers between devices  77.1 us (10%)
  local copies, waits for them, and re-layouts  40 us (5%)
  other arithmetic  8.79 us (1%)
    pallas_call x52, Pallas kernels, call(): pl.pallas_call(lambda sc, *refs: kernel(sc, *refs[len(deps):]), out_shape...  521 us
    ppermute x40, starting transfers between devices, ring_hop(): return sent(lax.ppermute(values, ('dp', 'ctx'), pairs))  52.6 us
    ppermute x40, waiting for transfers between devices, ring_hop(): return sent(lax.ppermute(values, ('dp', 'ctx'), pairs))  51.6 us
    ppermute x55, waiting for transfers between devices, swap(): swapped = lax.ppermute(values, axis, [(0, 1), (1, 0)])  41.6 us
    ppermute x55, starting transfers between devices, swap(): swapped = lax.ppermute(values, axis, [(0, 1), (1, 0)])  24.5 us
  transfers between devices with their start and end apart: 95, of which 18 were waited for; matrix products, arithmetic and copies ran while one was open for 5% of the time, Pallas kernels for 69%

profile of v5, /device:TPU:0, one launch (start us, length us, event | category | flops | bytes accessed | tf_op | source)
XLA Modules:
  0.0 741.8 jit_solution(10288700784275490532)
XLA Ops:
  13.3 9.0 %collective-permute-done.refs_4_ = bf16[18,192,128]{2,1,0:T(8,128)(2,1)S(1)} collective-permute-done((bf16[18,192,128]{2,1,0:T(8,128)(2,1)}, bf16[18,192,128]{2,1,0:T(8,128)(2,1)S(1)}, u32[]{:S(2)}, u32[]{:S(2)}) %collective-permute-start) | collective-permute-done | bytes 884768 | tf_op jit(solution)/shard_map/ppermute | solution.py:90
  28.0 7.4 %collective-permute-done.1.refs_5_ = bf16[18,192,128]{2,1,0:T(8,128)(2,1)} collective-permute-done((bf16[18,192,128]{2,1,0:T(8,128)(2,1)S(1)}, bf16[18,192,128]{2,1,0:T(8,128)(2,1)}, u32[]{:S(2)}, u32[]{:S(2)}) %collective-permute-start.1) | collective-permute-done | bytes 884768 | tf_op jit(solution)/shard_map/ppermute | solution.py:90
  37.6 11.2 %collective-permute-done.2.refs_6_ = bf16[18,192,128]{2,1,0:T(8,128)(2,1)S(1)} collective-permute-done((bf16[18,192,128]{2,1,0:T(8,128)(2,1)}, bf16[18,192,128]{2,1,0:T(8,128)(2,1)S(1)}, u32[]{:S(2)}, u32[]{:S(2)}) %collective-permute-start.2) | collective-permute-done | bytes 884768 | tf_op jit(solution)/shard_map/ppermute | solution.py:90
  51.5 5.7 collective-permute-done.3.refs_7_
  62.0 17.7 %project.1 = (bf16[11,1536,128]{2,1,0:T(8,128)(2,1)}, bf16[6,1536,128]{2,1,0:T(8,128)(2,1)}, bf16[3,1536,128]{2,1,0:T(8,128)(2,1)}, bf16[128,1536]{1,0:T(8,128)(...) custom-call(s32[18]{0:T(128)} %stack.86.sc, ...), custom_call_target="tpu_custom_call" | custom-call | flops 20753999872 | bytes 1 | tf_op jit(solution)/shard_map/project/pallas_call | solution.py:50
  83.7 21.5 %attend.2 = (bf16[512,768]{1,0:T(8,128)(2,1)}, f32[6,2,512]{2,1,0:T(2,128)}) custom-call(s32[2]{0:T(128)} %pad_add_fusion.sc, bf16[3,4,192,256]{3,2,1,0:T(8,128)(2,1)} %collective-permute-done.4.refs_0_.refs_11_.refs_10_, bf16[12,1024,64]{2,1,0:T(8,128)(2,1)} %get-tuple-element.168.refs_1_.refs_4_.refs_2_, ...), custom_call_target="tpu_custom_call" | custom-call | flops 21906999296 | bytes 1 | tf_op jit(solution)/shard_map/attend/pallas_call | solution.py:50
  110.0 17.0 %attend.3 = (bf16[512,768]{1,0:T(8,128)(2,1)}, f32[6,2,512]{2,1,0:T(2,128)}) custom-call(s32[2]{0:T(128)} %pad_add_fusion.sc, bf16[8,256,128]{2,1,0:T(8,128)(2,1)} %copy-done.15, bf16[3,1536,128]{2,1,0:T(8,128)(2,1)} %collective-permute-done.15.refs_1_.refs_15_, bf16[3,4,192,256]{3,2,1,0:T(8,128)(2,1)} %collective-permute-done.17.refs_2_.refs_15_.refs_14_, ...), custom_call_target="tpu_custom_call" | custom-call | flops 21906999296 | bytes 1 | tf_op jit(solution)/shard_map/attend/pallas_call | solution.py:50
  130.0 4.6 copy.47.refs_0_.refs_9_.refs_8_.refs_10_.refs_3_
  138.0 9.5 %collective-permute-done.18.refs_11_.refs_0_ = bf16[512,768]{1,0:T(8,128)(2,1)S(1)} collective-permute-done((bf16[512,768]{1,0:T(8,128)(2,1)}, bf16[512,768]{1,0:T(8,128)(2,1)S(1)}, u32[]{:S(2)}, u32[]{:S(2)}) %collective-permute-start.18) | collective-permute-done | bytes 786464 | tf_op jit(solution)/shard_map/ppermute | solution.py:94
  149.3 3.5 broadcast_in_dim.26.refs_1_.refs_19_.refs_20_
  152.8 15.8 %settle.1 = (f32[1024,1536]{1,0:T(8,128)}, bf16[1024,1536]{1,0:T(8,128)(2,1)}, bf16[1536,1024]{1,0:T(8,128)(2,1)}, f32[1024,128]{1,0:T(8,128)}) custom-call(s32[2]{0:T(128)} %pad_add_fusion.sc, bf16[1536,1024]{1,0:T(8,128)(2,1)} %copy.47.refs_0_.refs_9_.refs_8_.refs_10_.refs_3_, f32[1024,1536]{1,0:T(8,128)} %broadcast_in_dim.26.refs_1_.refs_19_.refs_20_, ...), custom_call_target="tpu_custom_call" | custom-call | flops 18447998976 | bytes 1 | tf_op jit(solution)/shard_map/settle/pallas_call | solution.py:50
  172.9 34.6 %experts_all.6 = (f32[1024,1536]{1,0:T(8,128)}, f32[1024,1536]{1,0:T(8,128)}, bf16[4,6,192,256]{3,2,1,0:T(8,128)(2,1)}, bf16[4,6,192,256]{3,2,1,0:T(8,128)(2,1)}, f32[1024,128]{1,0:T(8,128)}) custom-call(s32[20]{0:T(128)} %stack.106.sc, bf16[512,768]{1,0:T(8,128)(2,1)} %copy-done.10, ...), custom_call_target="tpu_custom_call" | custom-call | flops 27672000512 | bytes 1 | tf_op jit(solution)/shard_map/experts_all/pallas_call | solution.py:50
  218.5 24.3 %experts_all.7 = (f32[1024,1536]{1,0:T(8,128)}, f32[1024,1536]{1,0:T(8,128)}, bf16[4,6,192,256]{3,2,1,0:T(8,128)(2,1)}, bf16[4,6,192,256]{3,2,1,0:T(8,128)(2,1)}, f32[1024,128]{1,0:T(8,128)}) custom-call(s32[20]{0:T(128)} %stack.105.sc, bf16[3,4,192,128]{3,2,1,0:T(8,128)(2,1)} %copy-done.13, ...), custom_call_target="tpu_custom_call" | custom-call | flops 27672000512 | bytes 1 | tf_op jit(solution)/shard_map/experts_all/pallas_call | solution.py:50
  248.7 24.1 %experts_all.8 = (f32[1024,1536]{1,0:T(8,128)}, f32[1024,1536]{1,0:T(8,128)}, bf16[4,6,192,256]{3,2,1,0:T(8,128)(2,1)}, bf16[4,6,192,256]{3,2,1,0:T(8,128)(2,1)}, f32[1024,128]{1,0:T(8,128)}) custom-call(s32[20]{0:T(128)} %stack.107.sc, bf16[4,6,192,256]{3,2,1,0:T(8,128)(2,1)} %collective-permute-done.28.refs_0_.refs_4_, ...), custom_call_target="tpu_custom_call" | custom-call | flops 27672000512 | bytes 1 | tf_op jit(solution)/shard_map/experts_all/pallas_call | solution.py:50
  278.0 24.4 %experts_all.9 = (f32[1024,1536]{1,0:T(8,128)}, f32[1024,1536]{1,0:T(8,128)}, bf16[4,6,192,256]{3,2,1,0:T(8,128)(2,1)}, bf16[4,6,192,256]{3,2,1,0:T(8,128)(2,1)}, f32[1024,128]{1,0:T(8,128)}) custom-call(s32[20]{0:T(128)} %stack.108.sc, bf16[4,6,192,256]{3,2,1,0:T(8,128)(2,1)} %collective-permute-done.36.refs_0_.refs_5_, ...), custom_call_target="tpu_custom_call" | custom-call | flops 27672000512 | bytes 1 | tf_op jit(solution)/shard_map/experts_all/pallas_call | solution.py:50
  309.2 24.1 %experts_all.10 = (f32[1024,1536]{1,0:T(8,128)}, f32[1024,1536]{1,0:T(8,128)}, bf16[4,6,192,256]{3,2,1,0:T(8,128)(2,1)}, bf16[4,6,192,256]{3,2,1,0:T(8,128)(2,1)}, f32[1024,128]{1,0:T(8,128)}) custom-call(s32[20]{0:T(128)} %stack.109.sc, bf16[4,6,192,256]{3,2,1,0:T(8,128)(2,1)} %collective-permute-done.40.refs_6_.refs_0_, ...), custom_call_target="tpu_custom_call" | custom-call | flops 27672000512 | bytes 1 | tf_op jit(solution)/shard_map/experts_all/pallas_call | solution.py:50
  337.9 4.8 hop_sum.26.refs_5_
  344.2 24.4 %experts_all.11 = (f32[1024,1536]{1,0:T(8,128)}, f32[1024,1536]{1,0:T(8,128)}, bf16[4,6,192,256]{3,2,1,0:T(8,128)(2,1)}, bf16[4,6,192,256]{3,2,1,0:T(8,128)(2,1)}, f32[1024,128]{1,0:T(8,128)}) custom-call(s32[20]{0:T(128)} %stack.110.sc, bf16[4,6,192,256]{3,2,1,0:T(8,128)(2,1)} %collective-permute-done.48.refs_0_.refs_4_, ...), custom_call_target="tpu_custom_call" | custom-call | flops 27672000512 | bytes 1 | tf_op jit(solution)/shard_map/experts_all/pallas_call | solution.py:50
  370.5 5.1 hop_sum.27.refs_5_
  376.2 17.2 %experts_front.1 = (f32[1024,1536]{1,0:T(8,128)}, f32[1024,128]{1,0:T(8,128)}, bf16[1024,512]{1,0:T(8,128)(2,1)}, bf16[1024,1024]{1,0:T(8,128)(2,1)}) custom-call(s32[20]{0:T(128)} %stack.88.sc, bf16[4,6,192,256]{3,2,1,0:T(8,128)(2,1)} %collective-permute-done.51.refs_0_.refs_5_, ...), custom_call_target="tpu_custom_call" | custom-call | flops 20753999872 | bytes 1 | tf_op jit(solution)/shard_map/experts_front/pallas_call | solution.py:50
  393.9 17.1 %experts_front_end.1 = (bf16[512,1536]{1,0:T(8,128)(2,1)}, bf16[512,1536]{1,0:T(8,128)(2,1)}, f32[1024,128]{1,0:T(8,128)}, bf16[1024,512]{1,0:T(8,128)(2,1)}, bf...) custom-call(s32[20]{0:T(128)} %stack.87.sc, bf16[1024,1536]{1,0:T(8,128)(2,1)} %get-tuple-element.183.refs_5_.refs_4_.refs_6_.refs_0_, ...), custom_call_target="tpu_custom_call" | custom-call | flops 20753999872 | bytes 1 | tf_op jit(solution)/shard_map/experts_front_end/pallas_call | solution.py:50
  413.2 5.1 hop_sum.28.refs_0_
  423.5 13.3 %experts_rest.1 = (f32[1024,1536]{1,0:T(8,128)}, bf16[4,6,192,256]{3,2,1,0:T(8,128)(2,1)}, bf16[4,6,192,256]{3,2,1,0:T(8,128)(2,1)}) custom-call(s32[20]{0:T(128)} %stack.88.sc, bf16[3,6,192,256]{3,2,1,0:T(8,128)(2,1)} %hop_sum.28.refs_0_, bf16[3,6,192,128]{3,2,1,0:T(8,128)(2,1)} %hop_sum.29.refs_1_, ...), custom_call_target="tpu_custom_call" | custom-call | flops 14988999680 | bytes 1 | tf_op jit(solution)/shard_map/experts_rest/pallas_call | solution.py:50
  436.8 12.3 %collective-permute-done.61.refs_6_ = f32[16,1024]{1,0:T(8,128)S(1)} collective-permute-done((f32[16,1024]{1,0:T(8,128)}, f32[16,1024]{1,0:T(8,128)S(1)}, u32[]{:S(2)}, u32[]{:S(2)}) %collective-permute-start.61) | collective-permute-done | bytes 65568 | tf_op jit(solution)/shard_map/ppermute | solution.py:94
  450.5 4.5 hop_sum.30.refs_1_
  455.5 4.8 hop_sum.31.refs_1_
  461.8 5.2 emit.3
  467.0 13.3 %experts_rest_end.1 = (bf16[768,1536]{1,0:T(8,128)(2,1)}, bf16[256,1536]{1,0:T(8,128)(2,1)}, bf16[4,6,192,256]{3,2,1,0:T(8,128)(2,1)}, bf16[4,6,192,256]{3,2,1,0:T(8,128)(2,1)}) custom-call(s32[20]{0:T(128)} %stack.87.sc, f32[16,192,256]{2,1,0:T(8,128)} %get-tuple-element.251.refs_0_.refs_3_, bf16[3,6,192,256]{3,2,1,0:T(8,128)(2,1)} %hop_sum.31.refs_1_, ...), custom_call_target="tpu_custom_call" | custom-call | flops 14988999680 | bytes 1 | tf_op jit(solution)/shard_map/experts_rest_end/pallas_call | solution.py:50
  480.3 11.8 %collective-permute-done.65.refs_4_ = bf16[512,1536]{1,0:T(8,128)(2,1)} collective-permute-done((bf16[512,1536]{1,0:T(8,128)(2,1)}, bf16[512,1536]{1,0:T(8,128)(2,1)}, u32[]{:S(2)}, u32[]{:S(2)}) %collective-permute-start.65) | collective-permute-done | bytes 1572896 | tf_op jit(solution)/shard_map/ppermute | solution.py:94
  492.1 5.1 hop_sum.32.refs_0_
  498.5 16.6 %unsettle.1 = (f32[1024,1536]{1,0:T(8,128)}, bf16[1536,1024]{1,0:T(8,128)(2,1)}, bf16[1024,768]{1,0:T(8,128)(2,1)}, bf16[1024,128]{1,0:T(8,128)(2,1)}, f32[1,1536]{1,0:T(1,128)}) custom-call(s32[2]{0:T(128)} %pad_add_fusion.sc, bf16[3,6,192,256]{3,2,1,0:T(8,128)(2,1)} %hop_sum.32.refs_0_, bf16[512,1536]{1,0:T(8,128)(2,1)} %get-tuple-element.248.refs_1_, ...), custom_call_target="tpu_custom_call" | custom-call | flops 19601000448 | bytes 1 | tf_op jit(solution)/shard_map/unsettle/pallas_call | solution.py:50
  520.3 5.1 hop_sum.33.refs_0_
  530.6 24.9 %attend_back.2 = (bf16[1024,384]{1,0:T(8,128)(2,1)}, f32[4,1024,64]{2,1,0:T(8,128)}, f32[4,256,128]{2,1,0:T(8,128)}) custom-call(s32[2]{0:T(128)} %pad_add_fusion.sc, bf16[3,6,192,256]{3,2,1,0:T(8,128)(2,1)} %hop_sum.33.refs_0_, bf16[2,6,192,128]{3,2,1,0:T(8,128)(2,1)} %hop_sum.34.refs_1_, bf16[12,1024,64]{2,1,0:T(8,128)(2,1)} %get-tuple-element.168.refs_1_.refs_4_.refs_2_, ...), custom_call_target="tpu_custom_call" | custom-call | flops 28824999936 | bytes 1 | tf_op jit(solution)/shard_map/attend_back/pallas_call | solution.py:50
  556.4 3.9 hop_sum.35.refs_1_
  561.8 12.4 %early_grads.1 = (bf16[4,5,192,256]{3,2,1,0:T(8,128)(2,1)}, bf16[4,5,192,256]{3,2,1,0:T(8,128)(2,1)}) custom-call(s32[18]{0:T(128)} %stack.86.sc, f32[4,256,128]{2,1,0:T(8,128)} %get-tuple-element.275.refs_0_, bf16[2,6,192,256]{3,2,1,0:T(8,128)(2,1)} %hop_sum.35.refs_1_, bf16[1536,1024]{1,0:T(8,128)(2,1)} %get-tuple-element.270.refs_2_.refs_3_, ...), custom_call_target="tpu_custom_call" | custom-call | flops 13836000256 | bytes 1 | tf_op jit(solution)/shard_map/early_grads/pallas_call | solution.py:50
  578.6 4.1 hop_sum.37.refs_1_
  584.4 4.5 hop_sum.36.refs_0_.refs_1_
  588.9 24.8 %attend_back.3 = (bf16[1024,384]{1,0:T(8,128)(2,1)}, f32[4,1024,64]{2,1,0:T(8,128)}, f32[4,256,128]{2,1,0:T(8,128)}) custom-call(s32[2]{0:T(128)} %pad_add_fusion.sc, bf16[3,6,192,256]{3,2,1,0:T(8,128)(2,1)} %hop_sum.36.refs_0_.refs_1_, bf16[2,6,192,256]{3,2,1,0:T(8,128)(2,1)} %hop_sum.37.refs_1_, ...), custom_call_target="tpu_custom_call" | custom-call | flops 28824999936 | bytes 1 | tf_op jit(solution)/shard_map/attend_back/pallas_call | solution.py:50
  617.5 7.0 key_value_grads.1.refs_0_.refs_5_.refs_6_
  624.5 4.1 hop_sum.40.refs_1_
  633.7 9.3 %late_grads.1 = (bf16[4,4,192,256]{3,2,1,0:T(8,128)(2,1)}, bf16[4,4,192,256]{3,2,1,0:T(8,128)(2,1)}) custom-call(s32[18]{0:T(128)} %stack.86.sc, bf16[1,5,192,256]{3,2,1,0:T(8,128)(2,1)} %hop_sum.39.refs_0_, bf16[2,6,192,256]{3,2,1,0:T(8,128)(2,1)} %hop_sum.40.refs_1_, bf16[1536,1024]{1,0:T(8,128)(2,1)} %get-tuple-element.272.refs_11_.refs_12_.refs_2_.refs_3_, ...), custom_call_target="tpu_custom_call" | custom-call | flops 11530000384 | bytes 1 | tf_op jit(solution)/shard_map/late_grads/pallas_call | solution.py:50
  643.0 7.5 %collective-permute-done.79.refs_3_ = bf16[1,5,192,256]{3,2,1,0:T(8,128)(2,1)} collective-permute-done((bf16[1,5,192,256]{3,2,1,0:T(8,128)(2,1)}, bf16[1,5,192,256]{3,2,1,0:T(8,128)(2,1)}, u32[]{:S(2)}, u32[]{:S(2)}) %collective-permute-start.79) | collective-permute-done | bytes 491552 | tf_op jit(solution)/shard_map/ppermute | solution.py:90
  661.7 5.2 emit.4
  676.7 18.3 %finish.1 = f32[1024,1536]{1,0:T(8,128)} custom-call(s32[2]{0:T(128)} %pad_add_fusion.sc, bf16[1,4,192,256]{3,2,1,0:T(8,128)(2,1)} %hop_sum.43.refs_0_, bf16[1024,1536]{1,0:T(8,128)(2,1)} %bitcast.59, bf16[128,1536]{1,0:T(8,128)(2,1)} %get-tuple-element.181.refs_13_.refs_10_.refs_2_, f32[1024,1536]{1,0:T(8,128)} %get-tuple-element.296.refs_3_, ...), custom_call_target="tpu_custom_call" | custom-call | flops 20753999872 | bytes 1 | tf_op jit(solution)/shard_map/finish/pallas_call | solution.py:50
  699.3 3.7 hop_sum.45.refs_0_.refs_1_
  711.5 7.5 %combine.1.refs_0_ = bf16[1024,1536]{1,0:T(8,128)(2,1)} custom-call(s32[2]{0:T(128)} %pad_add_fusion.sc, bf16[1,4,192,256]{3,2,1,0:T(8,128)(2,1)} %hop_sum.47.refs_0_, f32[1024,1536]{1,0:T(8,128)} %get-tuple-element.260.refs_8_.refs_1_, bf16[768,1536]{1,0:T(8,128)(2,1)} %get-tuple-element.276.refs_0_.refs_2_, bf16[256,1536]{1,0:T(8,128)(2,1)} %get-tuple-element.299.refs_3_, ...), custom_call_target="tpu_custom_call" | custom-call | flops 5765000192 | bytes 1 | tf_op jit(solution)/shard_map/combine/pallas_call | solution.py:50
  722.6 3.4 emit.5
  732.3 3.3 spread.1
  (286 shorter events, 176.6 us)
Async XLA Ops:
  79.9 28.6 %collective-permute-start.15 = (bf16[3,1536,128]{2,1,0:T(8,128)(2,1)}, bf16[3,1536,128]{2,1,0:T(8,128)(2,1)}, u32[]{:S(2)}, u32[]{:S(2)}) collective-permute-start(bf16[3,1536,128]{2,1,0:T(8,128)(2,1)} %get-tuple-element.178), channel_id=1, source_target_pairs={{0,1},{1,0},{2,3},{3,2},{4,5},{5,4},{6,7},{7,6},{8,9},{9,8},{10,11... | collective-permute-start | bytes 3538952 | tf_op jit(solution)/shard_map/ppermute | solution.py:94
  81.4 27.1 %collective-permute-start.11 = (bf16[3,4,192,256]{3,2,1,0:T(8,128)(2,1)}, bf16[3,4,192,256]{3,2,1,0:T(8,128)(2,1)}, u32[]{:S(2)}, u32[]{:S(2)}) collective-permute-start(bf16[3,4,192,256]{3,2,1,0:T(8,128)(2,1)} %collective-permute-done.4.refs_0_.refs_11_.refs_10_), channel_id=1, source_target_pairs={{0,8},{10,2},{8,16},{18,10},{16,24},{26,18},{24,28},{30,26},{28,20... | collective-permute-start | bytes 3538952 | tf_op jit(solution)/shard_map/ppermute | solution.py:90
  82.9 27.1 %collective-permute-start.17 = (bf16[3,4,192,256]{3,2,1,0:T(8,128)(2,1)}, bf16[3,4,192,256]{3,2,1,0:T(8,128)(2,1)}, u32[]{:S(2)}, u32[]{:S(2)}) collective-permute-start(bf16[3,4,192,256]{3,2,1,0:T(8,128)(2,1)} %collective-permute-done.4.refs_0_.refs_11_.refs_10_), channel_id=1, source_target_pairs={{0,2},{2,0},{1,3},{3,1},{4,6},{6,4},{5,7},{7,5},{8,10},{10,8},{9,1... | collective-permute-start | bytes 3538952 | tf_op jit(solution)/shard_map/ppermute | solution.py:94
  106.8 30.5 %collective-permute-start.10 = (bf16[512,768]{1,0:T(8,128)(2,1)}, bf16[512,768]{1,0:T(8,128)(2,1)}, u32[]{:S(2)}, u32[]{:S(2)}) collective-permute-start(bf16[512,768]{1,0:T(8,128)(2,1)} %get-tuple-element.171.refs_10_.refs_13_.refs_5_), channel_id=1, source_target_pairs={{0,1},{1,0},{2,3},{3,2},{4,5},{5,4},{6,7},{7,6},{8,9},{9,8},{10,11... | collective-permute-start | bytes 2359304 | tf_op jit(solution)/shard_map/ppermute | solution.py:94
  108.4 29.0 %collective-permute-start.16 = (bf16[3,1536,128]{2,1,0:T(8,128)(2,1)}, bf16[3,1536,128]{2,1,0:T(8,128)(2,1)}, u32[]{:S(2)}, u32[]{:S(2)}) collective-permute-start(bf16[3,1536,128]{2,1,0:T(8,128)(2,1)} %collective-permute-done.15.refs_1_.refs_15_), channel_id=1, source_target_pairs={{0,2},{2,0},{1,3},{3,1},{4,6},{6,4},{5,7},{7,5},{8,10},{10,8},{9,1... | collective-permute-start | bytes 3538952 | tf_op jit(solution)/shard_map/ppermute | solution.py:94
  110.0 39.2 %collective-permute-start.12 = (bf16[3,4,192,256]{3,2,1,0:T(8,128)(2,1)}, bf16[3,4,192,256]{3,2,1,0:T(8,128)(2,1)}, u32[]{:S(2)}, u32[]{:S(2)}) collective-permute-start(bf16[3,4,192,256]{3,2,1,0:T(8,128)(2,1)} %collective-permute-done.11.refs_3_.refs_12_.refs_11_), channel_id=1, source_target_pairs={{0,2},{2,0},{1,3},{3,1},{4,6},{6,4},{5,7},{7,5},{8,10},{10,8},{9,1... | collective-permute-start | bytes 3538952 | tf_op jit(solution)/shard_map/ppermute | solution.py:94
  134.7 34.6 %collective-permute-start.21 = (bf16[3,4,192,256]{3,2,1,0:T(8,128)(2,1)}, bf16[3,4,192,256]{3,2,1,0:T(8,128)(2,1)}, u32[]{:S(2)}, u32[]{:S(2)}) collective-permute-start(bf16[3,4,192,256]{3,2,1,0:T(8,128)(2,1)} %collective-permute-done.14.refs_5_.refs_12_.refs_11_), channel_id=1, source_target_pairs={{0,8},{10,2},{8,16},{18,10},{16,24},{26,18},{24,28},{30,26},{28,20... | collective-permute-start | bytes 3538952 | tf_op jit(solution)/shard_map/ppermute | solution.py:90
  137.4 33.9 %collective-permute-start.26 = (bf16[3,4,192,256]{3,2,1,0:T(8,128)(2,1)}, bf16[3,4,192,256]{3,2,1,0:T(8,128)(2,1)}, u32[]{:S(2)}, u32[]{:S(2)}) collective-permute-start(bf16[3,4,192,256]{3,2,1,0:T(8,128)(2,1)} %collective-permute-done.14.refs_5_.refs_12_.refs_11_), channel_id=1, source_target_pairs={{0,2},{2,0},{1,3},{3,1},{4,6},{6,4},{5,7},{7,5},{8,10},{10,8},{9,1... | collective-permute-start | bytes 3538952 | tf_op jit(solution)/shard_map/ppermute | solution.py:94
  137.5 34.4 %collective-permute-start.25 = (bf16[3,4,192,256]{3,2,1,0:T(8,128)(2,1)}, bf16[3,4,192,256]{3,2,1,0:T(8,128)(2,1)}, u32[]{:S(2)}, u32[]{:S(2)}) collective-permute-start(bf16[3,4,192,256]{3,2,1,0:T(8,128)(2,1)} %collective-permute-done.13.refs_4_.refs_13_.refs_12_), channel_id=1, source_target_pairs={{0,2},{2,0},{1,3},{3,1},{4,6},{6,4},{5,7},{7,5},{8,10},{10,8},{9,1... | collective-permute-start | bytes 3538952 | tf_op jit(solution)/shard_map/ppermute | solution.py:94
  169.2 44.6 %collective-permute-start.22 = (bf16[3,4,192,256]{3,2,1,0:T(8,128)(2,1)}, bf16[3,4,192,256]{3,2,1,0:T(8,128)(2,1)}, u32[]{:S(2)}, u32[]{:S(2)}) collective-permute-start(bf16[3,4,192,256]{3,2,1,0:T(8,128)(2,1)} %collective-permute-done.21.refs_4_.refs_13_.refs_12_), channel_id=1, source_target_pairs={{0,2},{2,0},{1,3},{3,1},{4,6},{6,4},{5,7},{7,5},{8,10},{10,8},{9,1... | collective-permute-start | bytes 3538952 | tf_op jit(solution)/shard_map/ppermute | solution.py:94
  169.7 37.8 %collective-permute-start.23 = (bf16[3,4,192,256]{3,2,1,0:T(8,128)(2,1)}, bf16[3,4,192,256]{3,2,1,0:T(8,128)(2,1)}, u32[]{:S(2)}, u32[]{:S(2)}) collective-permute-start(bf16[3,4,192,256]{3,2,1,0:T(8,128)(2,1)} %collective-permute-done.21.refs_4_.refs_13_.refs_12_), channel_id=1, source_target_pairs={{0,8},{10,2},{8,16},{18,10},{16,24},{26,18},{24,28},{30,26},{28,20... | collective-permute-start | bytes 3538952 | tf_op jit(solution)/shard_map/ppermute | solution.py:90
  171.2 39.1 %collective-permute-start.24 = (bf16[3,4,192,256]{3,2,1,0:T(8,128)(2,1)}, bf16[3,4,192,256]{3,2,1,0:T(8,128)(2,1)}, u32[]{:S(2)}, u32[]{:S(2)}) collective-permute-start(bf16[3,4,192,256]{3,2,1,0:T(8,128)(2,1)} %get-tuple-element.192.refs_11_), channel_id=1, source_target_pairs={{0,8},{10,2},{8,16},{18,10},{16,24},{26,18},{24,28},{30,26},{28,20... | collective-permute-start | bytes 3538952 | tf_op jit(solution)/shard_map/ppermute | solution.py:90
  210.3 32.6 %collective-permute-start.32 = (bf16[3,4,192,256]{3,2,1,0:T(8,128)(2,1)}, bf16[3,4,192,256]{3,2,1,0:T(8,128)(2,1)}, u32[]{:S(2)}, u32[]{:S(2)}) collective-permute-start(bf16[3,4,192,256]{3,2,1,0:T(8,128)(2,1)} %collective-permute-done.24.refs_3_.refs_12_), channel_id=1, source_target_pairs={{0,8},{10,2},{8,16},{18,10},{16,24},{26,18},{24,28},{30,26},{28,20... | collective-permute-start | bytes 3538952 | tf_op jit(solution)/shard_map/ppermute | solution.py:90
  211.0 35.0 %collective-permute-start.31 = (bf16[3,4,192,256]{3,2,1,0:T(8,128)(2,1)}, bf16[3,4,192,256]{3,2,1,0:T(8,128)(2,1)}, u32[]{:S(2)}, u32[]{:S(2)}) collective-permute-start(bf16[3,4,192,256]{3,2,1,0:T(8,128)(2,1)} %collective-permute-done.24.refs_3_.refs_12_), channel_id=1, source_target_pairs={{0,2},{2,0},{1,3},{3,1},{4,6},{6,4},{5,7},{7,5},{8,10},{10,8},{9,1... | collective-permute-start | bytes 3538952 | tf_op jit(solution)/shard_map/ppermute | solution.py:94
  211.0 36.2 %collective-permute-start.29 = (bf16[3,4,192,256]{3,2,1,0:T(8,128)(2,1)}, bf16[3,4,192,256]{3,2,1,0:T(8,128)(2,1)}, u32[]{:S(2)}, u32[]{:S(2)}) collective-permute-start(bf16[3,4,192,256]{3,2,1,0:T(8,128)(2,1)} %collective-permute-done.23.refs_2_.refs_14_.refs_13_), channel_id=1, source_target_pairs={{0,2},{2,0},{1,3},{3,1},{4,6},{6,4},{5,7},{7,5},{8,10},{10,8},{9,1... | collective-permute-start | bytes 3538952 | tf_op jit(solution)/shard_map/ppermute | solution.py:94
  213.9 32.1 %collective-permute-start.33 = (bf16[3,1536,128]{2,1,0:T(8,128)(2,1)}, bf16[3,1536,128]{2,1,0:T(8,128)(2,1)}, u32[]{:S(2)}, u32[]{:S(2)}) collective-permute-start(bf16[3,1536,128]{2,1,0:T(8,128)(2,1)} %constant_dynamic-slice_fusion), channel_id=1, source_target_pairs={{0,1},{1,0},{2,3},{3,2},{4,5},{5,4},{6,7},{7,6},{8,9},{9,8},{10,11... | collective-permute-start | bytes 3538952 | tf_op jit(solution)/shard_map/ppermute | solution.py:94
  218.5 30.1 %collective-permute-start.28 = (bf16[4,6,192,256]{3,2,1,0:T(8,128)(2,1)}, bf16[4,6,192,256]{3,2,1,0:T(8,128)(2,1)}, u32[]{:S(2)}, u32[]{:S(2)}) collective-permute-start(bf16[4,6,192,256]{3,2,1,0:T(8,128)(2,1)} %get-tuple-element.200), channel_id=1, source_target_pairs={{0,2},{2,0},{1,3},{3,1},{4,6},{6,4},{5,7},{7,5},{8,10},{10,8},{9,1... | collective-permute-start | bytes 7077896 | tf_op jit(solution)/shard_map/ppermute | solution.py:94
  246.0 31.5 %collective-permute-start.36 = (bf16[4,6,192,256]{3,2,1,0:T(8,128)(2,1)}, bf16[4,6,192,256]{3,2,1,0:T(8,128)(2,1)}, u32[]{:S(2)}, u32[]{:S(2)}) collective-permute-start(bf16[4,6,192,256]{3,2,1,0:T(8,128)(2,1)} %get-tuple-element.210), channel_id=1, source_target_pairs={{0,2},{2,0},{1,3},{3,1},{4,6},{6,4},{5,7},{7,5},{8,10},{10,8},{9,1... | collective-permute-start | bytes 7077896 | tf_op jit(solution)/shard_map/ppermute | solution.py:94
  247.2 28.1 %collective-permute-start.38 = (bf16[3,4,192,256]{3,2,1,0:T(8,128)(2,1)}, bf16[3,4,192,256]{3,2,1,0:T(8,128)(2,1)}, u32[]{:S(2)}, u32[]{:S(2)}) collective-permute-start(bf16[3,4,192,256]{3,2,1,0:T(8,128)(2,1)} %collective-permute-done.32.refs_4_.refs_13_), channel_id=1, source_target_pairs={{0,8},{10,2},{8,16},{18,10},{16,24},{26,18},{24,28},{30,26},{28,20... | collective-permute-start | bytes 3538952 | tf_op jit(solution)/shard_map/ppermute | solution.py:90
  248.6 27.7 %collective-permute-start.37 = (bf16[3,4,192,256]{3,2,1,0:T(8,128)(2,1)}, bf16[3,4,192,256]{3,2,1,0:T(8,128)(2,1)}, u32[]{:S(2)}, u32[]{:S(2)}) collective-permute-start(bf16[3,4,192,256]{3,2,1,0:T(8,128)(2,1)} %collective-permute-done.32.refs_4_.refs_13_), channel_id=1, source_target_pairs={{0,2},{2,0},{1,3},{3,1},{4,6},{6,4},{5,7},{7,5},{8,10},{10,8},{9,1... | collective-permute-start | bytes 3538952 | tf_op jit(solution)/shard_map/ppermute | solution.py:94
  272.8 30.9 %collective-permute-start.35 = (bf16[3,4,192,256]{3,2,1,0:T(8,128)(2,1)}, bf16[3,4,192,256]{3,2,1,0:T(8,128)(2,1)}, u32[]{:S(2)}, u32[]{:S(2)}) collective-permute-start(bf16[3,4,192,256]{3,2,1,0:T(8,128)(2,1)} %collective-permute-done.27.refs_4_.refs_10_.refs_5_), channel_id=1, source_target_pairs={{0,8},{10,2},{8,16},{18,10},{16,24},{26,18},{24,28},{30,26},{28,20... | collective-permute-start | bytes 3538952 | tf_op jit(solution)/shard_map/ppermute | solution.py:90
  274.3 33.7 %collective-permute-start.43 = (bf16[3,4,192,256]{3,2,1,0:T(8,128)(2,1)}, bf16[3,4,192,256]{3,2,1,0:T(8,128)(2,1)}, u32[]{:S(2)}, u32[]{:S(2)}) collective-permute-start(bf16[3,4,192,256]{3,2,1,0:T(8,128)(2,1)} %collective-permute-done.27.refs_4_.refs_10_.refs_5_), channel_id=1, source_target_pairs={{0,2},{2,0},{1,3},{3,1},{4,6},{6,4},{5,7},{7,5},{8,10},{10,8},{9,1... | collective-permute-start | bytes 3538952 | tf_op jit(solution)/shard_map/ppermute | solution.py:94
  275.2 32.8 %collective-permute-start.41 = (bf16[3,4,192,256]{3,2,1,0:T(8,128)(2,1)}, bf16[3,4,192,256]{3,2,1,0:T(8,128)(2,1)}, u32[]{:S(2)}, u32[]{:S(2)}) collective-permute-start(bf16[3,4,192,256]{3,2,1,0:T(8,128)(2,1)} %collective-permute-done.38.refs_3_.refs_14_), channel_id=1, source_target_pairs={{0,2},{2,0},{1,3},{3,1},{4,6},{6,4},{5,7},{7,5},{8,10},{10,8},{9,1... | collective-permute-start | bytes 3538952 | tf_op jit(solution)/shard_map/ppermute | solution.py:94
  303.7 39.4 %collective-permute-start.48 = (bf16[4,6,192,256]{3,2,1,0:T(8,128)(2,1)}, bf16[4,6,192,256]{3,2,1,0:T(8,128)(2,1)}, u32[]{:S(2)}, u32[]{:S(2)}) collective-permute-start(bf16[4,6,192,256]{3,2,1,0:T(8,128)(2,1)} %get-tuple-element.226), channel_id=1, source_target_pairs={{0,2},{2,0},{1,3},{3,1},{4,6},{6,4},{5,7},{7,5},{8,10},{10,8},{9,1... | collective-permute-start | bytes 7077896 | tf_op jit(solution)/shard_map/ppermute | solution.py:94
  304.2 30.9 %collective-permute-start.39 = (bf16[3,4,192,256]{3,2,1,0:T(8,128)(2,1)}, bf16[3,4,192,256]{3,2,1,0:T(8,128)(2,1)}, u32[]{:S(2)}, u32[]{:S(2)}) collective-permute-start(bf16[3,4,192,256]{3,2,1,0:T(8,128)(2,1)} %collective-permute-done.35.refs_4_.refs_11_.refs_5_.refs_6_), channel_id=1, source_target_pairs={{0,8},{10,2},{8,16},{18,10},{16,24},{26,18},{24,28},{30,26},{28,20... | collective-permute-start | bytes 3538952 | tf_op jit(solution)/shard_map/ppermute | solution.py:90
  308.1 34.7 %collective-permute-start.46 = (bf16[3,4,192,256]{3,2,1,0:T(8,128)(2,1)}, bf16[3,4,192,256]{3,2,1,0:T(8,128)(2,1)}, u32[]{:S(2)}, u32[]{:S(2)}) collective-permute-start(bf16[3,4,192,256]{3,2,1,0:T(8,128)(2,1)} %collective-permute-done.35.refs_4_.refs_11_.refs_5_.refs_6_), channel_id=1, source_target_pairs={{0,2},{2,0},{1,3},{3,1},{4,6},{6,4},{5,7},{7,5},{8,10},{10,8},{9,1... | collective-permute-start | bytes 3538952 | tf_op jit(solution)/shard_map/ppermute | solution.py:94
  308.1 29.2 %collective-permute-start.49 = (bf16[3,6,192,128]{3,2,1,0:T(8,128)(2,1)}, bf16[3,6,192,128]{3,2,1,0:T(8,128)(2,1)}, u32[]{:S(2)}, u32[]{:S(2)}) collective-permute-start(bf16[3,6,192,128]{3,2,1,0:T(8,128)(2,1)} %hop_sum.25.refs_5_), channel_id=1, source_target_pairs={{0,8},{10,2},{8,16},{18,10},{16,24},{26,18},{24,28},{30,26},{28,20... | collective-permute-start | bytes 2654216 | tf_op jit(solution)/shard_map/ppermute | solution.py:90
  333.3 42.2 %collective-permute-start.53 = (bf16[2,1536,128]{2,1,0:T(8,128)(2,1)S(1)}, bf16[2,1536,128]{2,1,0:T(8,128)(2,1)}, u32[]{:S(2)}, u32[]{:S(2)}) collective-permute-start(bf16[2,1536,128]{2,1,0:T(8,128)(2,1)S(1)} %constant_dynamic-slice_fusion.3), channel_id=1, source_target_pairs={{0,1},{1,0},{2,3},{3,2},{4,5},{5,4},{6,7},{7,6},{8,9},{9,8},{10,11... | collective-permute-start | bytes 2359304 | tf_op jit(solution)/shard_map/ppermute | solution.py:94
  335.2 41.0 %collective-permute-start.47 = (bf16[3,4,192,256]{3,2,1,0:T(8,128)(2,1)}, bf16[3,4,192,256]{3,2,1,0:T(8,128)(2,1)}, u32[]{:S(2)}, u32[]{:S(2)}) collective-permute-start(bf16[3,4,192,256]{3,2,1,0:T(8,128)(2,1)} %collective-permute-done.39.refs_3_.refs_12_.refs_6_.refs_7_), channel_id=1, source_target_pairs={{0,2},{2,0},{1,3},{3,1},{4,6},{6,4},{5,7},{7,5},{8,10},{10,8},{9,1... | collective-permute-start | bytes 3538952 | tf_op jit(solution)/shard_map/ppermute | solution.py:94
  337.2 31.3 %collective-permute-start.45 = (bf16[3,4,192,128]{3,2,1,0:T(8,128)(2,1)}, bf16[3,4,192,128]{3,2,1,0:T(8,128)(2,1)}, u32[]{:S(2)}, u32[]{:S(2)}) collective-permute-start(bf16[3,4,192,128]{3,2,1,0:T(8,128)(2,1)} %constant_dynamic-slice_fusion.1), channel_id=1, source_target_pairs={{0,8},{10,2},{8,16},{18,10},{16,24},{26,18},{24,28},{30,26},{28,20... | collective-permute-start | bytes 1769480 | tf_op jit(solution)/shard_map/ppermute | solution.py:90
  342.7 33.5 %collective-permute-start.51 = (bf16[4,6,192,256]{3,2,1,0:T(8,128)(2,1)}, bf16[4,6,192,256]{3,2,1,0:T(8,128)(2,1)}, u32[]{:S(2)}, u32[]{:S(2)}) collective-permute-start(bf16[4,6,192,256]{3,2,1,0:T(8,128)(2,1)} %get-tuple-element.231), channel_id=1, source_target_pairs={{0,2},{2,0},{1,3},{3,1},{4,6},{6,4},{5,7},{7,5},{8,10},{10,8},{9,1... | collective-permute-start | bytes 7077896 | tf_op jit(solution)/shard_map/ppermute | solution.py:94
  370.1 41.3 %collective-permute-start.54 = (bf16[4,6,192,256]{3,2,1,0:T(8,128)(2,1)}, bf16[4,6,192,256]{3,2,1,0:T(8,128)(2,1)}, u32[]{:S(2)}, u32[]{:S(2)}) collective-permute-start(bf16[4,6,192,256]{3,2,1,0:T(8,128)(2,1)} %get-tuple-element.237), channel_id=1, source_target_pairs={{0,2},{2,0},{1,3},{3,1},{4,6},{6,4},{5,7},{7,5},{8,10},{10,8},{9,1... | collective-permute-start | bytes 7077896 | tf_op jit(solution)/shard_map/ppermute | solution.py:94
  375.5 37.6 %collective-permute-start.55 = (bf16[3,6,192,256]{3,2,1,0:T(8,128)(2,1)}, bf16[3,6,192,256]{3,2,1,0:T(8,128)(2,1)}, u32[]{:S(2)}, u32[]{:S(2)}) collective-permute-start(bf16[3,6,192,256]{3,2,1,0:T(8,128)(2,1)} %hop_sum.27.refs_5_), channel_id=1, source_target_pairs={{0,8},{10,2},{8,16},{18,10},{16,24},{26,18},{24,28},{30,26},{28,20... | collective-permute-start | bytes 5308424 | tf_op jit(solution)/shard_map/ppermute | solution.py:90
  411.1 38.1 %collective-permute-start.60 = (bf16[512,1536]{1,0:T(8,128)(2,1)}, bf16[512,1536]{1,0:T(8,128)(2,1)}, u32[]{:S(2)}, u32[]{:S(2)}) collective-permute-start(bf16[512,1536]{1,0:T(8,128)(2,1)} %get-tuple-element.248.refs_1_), channel_id=1, source_target_pairs={{0,1},{1,0},{2,3},{3,2},{4,5},{5,4},{6,7},{7,6},{8,9},{9,8},{10,11... | collective-permute-start | bytes 4718600 | tf_op jit(solution)/shard_map/ppermute | solution.py:94
  411.4 37.7 %collective-permute-start.61 = (f32[16,1024]{1,0:T(8,128)}, f32[16,1024]{1,0:T(8,128)S(1)}, u32[]{:S(2)}, u32[]{:S(2)}) collective-permute-start(f32[16,1024]{1,0:T(8,128)} %get-tuple-element.249.refs_0_.refs_5_), channel_id=1, source_target_pairs={{0,1},{1,0},{2,3},{3,2},{4,5},{5,4},{6,7},{7,6},{8,9},{9,8},{10,11... | collective-permute-start | bytes 196616 | tf_op jit(solution)/shard_map/ppermute | solution.py:94
  418.3 32.2 %collective-permute-start.58 = (bf16[3,6,192,256]{3,2,1,0:T(8,128)(2,1)}, bf16[3,6,192,256]{3,2,1,0:T(8,128)(2,1)}, u32[]{:S(2)}, u32[]{:S(2)}) collective-permute-start(bf16[3,6,192,256]{3,2,1,0:T(8,128)(2,1)} %hop_sum.28.refs_0_), channel_id=1, source_target_pairs={{0,8},{10,2},{8,16},{18,10},{16,24},{26,18},{24,28},{30,26},{28,20... | collective-permute-start | bytes 5308424 | tf_op jit(solution)/shard_map/ppermute | solution.py:90
  422.8 27.6 %collective-permute-start.59 = (bf16[3,6,192,128]{3,2,1,0:T(8,128)(2,1)}, bf16[3,6,192,128]{3,2,1,0:T(8,128)(2,1)S(1)}, u32[]{:S(2)}, u32[]{:S(2)}) collective-permute-start(bf16[3,6,192,128]{3,2,1,0:T(8,128)(2,1)} %hop_sum.29.refs_1_), channel_id=1, source_target_pairs={{0,8},{10,2},{8,16},{18,10},{16,24},{26,18},{24,28},{30,26},{28,20... | collective-permute-start | bytes 2654216 | tf_op jit(solution)/shard_map/ppermute | solution.py:90
  455.0 37.1 %collective-permute-start.65 = (bf16[512,1536]{1,0:T(8,128)(2,1)}, bf16[512,1536]{1,0:T(8,128)(2,1)}, u32[]{:S(2)}, u32[]{:S(2)}) collective-permute-start(bf16[512,1536]{1,0:T(8,128)(2,1)} %get-tuple-element.258.refs_2_), channel_id=1, source_target_pairs={{0,1},{1,0},{2,3},{3,2},{4,5},{5,4},{6,7},{7,6},{8,9},{9,8},{10,11... | collective-permute-start | bytes 4718600 | tf_op jit(solution)/shard_map/ppermute | solution.py:94
  455.3 36.8 %collective-permute-start.63 = (bf16[4,6,192,256]{3,2,1,0:T(8,128)(2,1)}, bf16[4,6,192,256]{3,2,1,0:T(8,128)(2,1)}, u32[]{:S(2)}, u32[]{:S(2)}) collective-permute-start(bf16[4,6,192,256]{3,2,1,0:T(8,128)(2,1)} %get-tuple-element.256), channel_id=1, source_target_pairs={{0,2},{2,0},{1,3},{3,1},{4,6},{6,4},{5,7},{7,5},{8,10},{10,8},{9,1... | collective-permute-start | bytes 7077896 | tf_op jit(solution)/shard_map/ppermute | solution.py:94
  460.3 31.8 %collective-permute-start.64 = (bf16[3,6,192,256]{3,2,1,0:T(8,128)(2,1)}, bf16[3,6,192,256]{3,2,1,0:T(8,128)(2,1)}, u32[]{:S(2)}, u32[]{:S(2)}) collective-permute-start(bf16[3,6,192,256]{3,2,1,0:T(8,128)(2,1)} %hop_sum.31.refs_1_), channel_id=1, source_target_pairs={{0,8},{10,2},{8,16},{18,10},{16,24},{26,18},{24,28},{30,26},{28,20... | collective-permute-start | bytes 5308424 | tf_op jit(solution)/shard_map/ppermute | solution.py:90
  492.1 27.9 %collective-permute-start.66 = (bf16[4,6,192,256]{3,2,1,0:T(8,128)(2,1)}, bf16[4,6,192,256]{3,2,1,0:T(8,128)(2,1)}, u32[]{:S(2)}, u32[]{:S(2)}) collective-permute-start(bf16[4,6,192,256]{3,2,1,0:T(8,128)(2,1)} %get-tuple-element.263), channel_id=1, source_target_pairs={{0,2},{2,0},{1,3},{3,1},{4,6},{6,4},{5,7},{7,5},{8,10},{10,8},{9,1... | collective-permute-start | bytes 7077896 | tf_op jit(solution)/shard_map/ppermute | solution.py:94
  520.0 54.2 %collective-permute-start.72 = (bf16[768,1536]{1,0:T(8,128)(2,1)}, bf16[768,1536]{1,0:T(8,128)(2,1)}, u32[]{:S(2)}, u32[]{:S(2)}) collective-permute-start(bf16[768,1536]{1,0:T(8,128)(2,1)} %get-tuple-element.276.refs_0_.refs_2_), channel_id=1, source_target_pairs={{0,1},{1,0},{2,3},{3,2},{4,5},{5,4},{6,7},{7,6},{8,9},{9,8},{10,11... | collective-permute-start | bytes 7077896 | tf_op jit(solution)/shard_map/ppermute | solution.py:94
  525.4 30.2 %collective-permute-start.68 = (bf16[3,6,192,256]{3,2,1,0:T(8,128)(2,1)}, bf16[3,6,192,256]{3,2,1,0:T(8,128)(2,1)}, u32[]{:S(2)}, u32[]{:S(2)}) collective-permute-start(bf16[3,6,192,256]{3,2,1,0:T(8,128)(2,1)} %hop_sum.33.refs_0_), channel_id=1, source_target_pairs={{0,8},{10,2},{8,16},{18,10},{16,24},{26,18},{24,28},{30,26},{28,20... | collective-permute-start | bytes 5308424 | tf_op jit(solution)/shard_map/ppermute | solution.py:90
  576.8 36.9 %collective-permute-start.76 = (bf16[1024,384]{1,0:T(8,128)(2,1)S(1)}, bf16[1024,384]{1,0:T(8,128)(2,1)}, u32[]{:S(2)}, u32[]{:S(2)}) collective-permute-start(bf16[1024,384]{1,0:T(8,128)(2,1)S(1)} %copy-done.8), channel_id=1, source_target_pairs={{0,1},{1,0},{2,3},{3,2},{4,5},{5,4},{6,7},{7,6},{8,9},{9,8},{10,11... | collective-permute-start | bytes 2359304 | tf_op jit(solution)/shard_map/ppermute | solution.py:94
  578.6 35.2 %collective-permute-start.73 = (bf16[4,5,192,256]{3,2,1,0:T(8,128)(2,1)}, bf16[4,5,192,256]{3,2,1,0:T(8,128)(2,1)}, u32[]{:S(2)}, u32[]{:S(2)}) collective-permute-start(bf16[4,5,192,256]{3,2,1,0:T(8,128)(2,1)} %get-tuple-element.280), channel_id=1, source_target_pairs={{0,2},{2,0},{1,3},{3,1},{4,6},{6,4},{5,7},{7,5},{8,10},{10,8},{9,1... | collective-permute-start | bytes 5898248 | tf_op jit(solution)/shard_map/ppermute | solution.py:94
  582.7 31.0 %collective-permute-start.74 = (bf16[2,6,192,256]{3,2,1,0:T(8,128)(2,1)}, bf16[2,6,192,256]{3,2,1,0:T(8,128)(2,1)}, u32[]{:S(2)}, u32[]{:S(2)}) collective-permute-start(bf16[2,6,192,256]{3,2,1,0:T(8,128)(2,1)} %hop_sum.37.refs_1_), channel_id=1, source_target_pairs={{0,8},{10,2},{8,16},{18,10},{16,24},{26,18},{24,28},{30,26},{28,20... | collective-permute-start | bytes 3538952 | tf_op jit(solution)/shard_map/ppermute | solution.py:90
  613.7 29.2 %collective-permute-start.81 = (bf16[1024,384]{1,0:T(8,128)(2,1)}, bf16[1024,384]{1,0:T(8,128)(2,1)S(1)}, u32[]{:S(2)}, u32[]{:S(2)}) collective-permute-start(bf16[1024,384]{1,0:T(8,128)(2,1)} %get-tuple-element.289.refs_4_.refs_5_), channel_id=1, source_target_pairs={{0,1},{1,0},{2,3},{3,2},{4,5},{5,4},{6,7},{7,6},{8,9},{9,8},{10,11... | collective-permute-start | bytes 2359304 | tf_op jit(solution)/shard_map/ppermute | solution.py:94
  661.0 42.0 %collective-permute-start.87 = (bf16[1,5,192,256]{3,2,1,0:T(8,128)(2,1)}, bf16[1,5,192,256]{3,2,1,0:T(8,128)(2,1)}, u32[]{:S(2)}, u32[]{:S(2)}) collective-permute-start(bf16[1,5,192,256]{3,2,1,0:T(8,128)(2,1)} %hop_sum.42.refs_1_), channel_id=1, source_target_pairs={{0,8},{10,2},{8,16},{18,10},{16,24},{26,18},{24,28},{30,26},{28,20... | collective-permute-start | bytes 1474568 | tf_op jit(solution)/shard_map/ppermute | solution.py:90
  (71 other events, 879.6 us)
